TPU v7x, 32 devices: a whole 2x2x4 slice. The times are simulated.
32 devices in a mesh: dp: 4 (over y, x), seq: 8 (over z, core).
Axes of the slice: x: 2, y: 2, z: 4, core: 2. Of those that a mesh axis runs over, the one named last changes fastest.
Arguments:
- tokens: bfloat16 [64, 64, 1152], P(('dp', 'seq')), may hold values from -6 to 6
- spatial_qkv: bfloat16 [64, 64, 1728], P(('dp', 'seq')), may hold values from -6 to 6
- wo_spatial: bfloat16 [576, 1152], replicated, may hold values from -0.25 to 0.25
- w_temporal: bfloat16 [1152, 1728], P(None, 'dp'), may hold values from -0.1875 to 0.1875
- wo_temporal: bfloat16 [576, 1152], replicated, may hold values from -0.25 to 0.25
- cotangent: bfloat16 [64, 64, 1152], P(('dp', 'seq')), may hold values from -6 to 6
Outputs:
- block_out: bfloat16 [64, 64, 1152], P(('dp', 'seq'))
- tokens_grad: bfloat16 [64, 64, 1152], P(('dp', 'seq'))
- spatial_qkv_grad: bfloat16 [64, 64, 1728], P(('dp', 'seq'))
- wo_spatial_grad: float32 [576, 1152], P('seq', 'dp')
- wo_temporal_grad: float32 [576, 1152], P('seq', 'dp')
All inputs are finite; a program needn't handle non-finite values.
Results may differ from a plain program's by a relative error of at most 0.038.
Values may be sent and summed in bfloat16 or wider, within the bound.
No kernel may reach another device: no remote copies, remote signals or barrier semaphores. Data moves between devices by JAX's collectives and lax.ppermute only.
A program may use at most 64 MiB of HBM per device.

v0:
```python
import math

import jax
import jax.numpy as jnp
from jax import lax
from jax.sharding import PartitionSpec as P

DH = 72
FRAMES = 16


def split_three(packed):
    inner_width = packed.shape[-1] // 3
    return (
        packed[..., :inner_width],
        packed[..., inner_width : 2 * inner_width],
        packed[..., 2 * inner_width :],
    )


def head_view(matrix):
    batch_size, length, inner_width = matrix.shape
    return matrix.reshape(batch_size, length, inner_width // DH, DH)


def attention_weights_of(query_heads, key_heads):
    scores = jnp.einsum(
        "blhd,bmhd->bhlm", query_heads, key_heads, preferred_element_type=jnp.float32
    ) * (1.0 / math.sqrt(DH))
    return jax.nn.softmax(scores, axis=-1)


def attention(queries, key_rows, values):
    batch_size, length, inner_width = queries.shape
    weights_full = attention_weights_of(head_view(queries), head_view(key_rows))
    rounded = weights_full.astype(jnp.bfloat16)
    output = jnp.einsum(
        "bhlm,bmhd->blhd", rounded, head_view(values), preferred_element_type=jnp.float32
    )
    return output.reshape(batch_size, length, inner_width).astype(jnp.bfloat16)


def attention_grad(queries, key_rows, values, output_grad):
    batch_size, length, inner_width = queries.shape
    query_heads = head_view(queries)
    key_heads = head_view(key_rows)
    value_heads = head_view(values)
    grad_heads = head_view(output_grad)
    weights_full = attention_weights_of(query_heads, key_heads)
    rounded = weights_full.astype(jnp.bfloat16)
    value_grad = jnp.einsum(
        "bhlm,blhd->bmhd", rounded, grad_heads, preferred_element_type=jnp.float32
    )
    weight_grad = jnp.einsum(
        "blhd,bmhd->bhlm", grad_heads, value_heads, preferred_element_type=jnp.float32
    )
    centered = weight_grad - jnp.sum(weights_full * weight_grad, axis=-1, keepdims=True)
    score_grad = (weights_full * centered * (1.0 / math.sqrt(DH))).astype(jnp.bfloat16)
    query_grad = jnp.einsum(
        "bhlm,bmhd->blhd", score_grad, key_heads, preferred_element_type=jnp.float32
    )
    key_grad = jnp.einsum(
        "bhlm,blhd->bmhd", score_grad, query_heads, preferred_element_type=jnp.float32
    )
    joined = [
        part_grad.reshape(batch_size, length, inner_width)
        for part_grad in (query_grad, key_grad, value_grad)
    ]
    return jnp.concatenate(joined, axis=-1).astype(jnp.bfloat16)


def to_clips(matrix, clip_count):
    frame_total, patch_share, channels = matrix.shape
    grouped = matrix.reshape(clip_count, FRAMES, patch_share, channels).transpose(0, 2, 1, 3)
    return grouped.reshape(clip_count * patch_share, FRAMES, channels)


def from_clips(matrix, clip_count):
    batch_rows, frame_count, channels = matrix.shape
    patch_share = batch_rows // clip_count
    grouped = matrix.reshape(clip_count, patch_share, frame_count, channels).transpose(0, 2, 1, 3)
    return grouped.reshape(clip_count * frame_count, patch_share, channels)


def times_transposed(left, right):
    return lax.dot_general(
        left, right, (((1,), (1,)), ((), ())), preferred_element_type=jnp.float32
    )


def transposed_times(left, right):
    return lax.dot_general(
        left, right, (((0,), (0,)), ((), ())), preferred_element_type=jnp.float32
    )


def forward_project(hidden_rows, weight_shard):
    return jnp.dot(
        hidden_rows,
        lax.all_gather(weight_shard, "dp", axis=1, tiled=True),
        preferred_element_type=jnp.float32,
    )


def backward_project(grad_rows, weight_shard):
    return times_transposed(grad_rows, lax.all_gather(weight_shard, "dp", axis=1, tiled=True))


def shards(tokens, spatial_qkv, wo_spatial, w_temporal, wo_temporal, cotangent):
    frames_dev, patches, feature_width = tokens.shape
    row_total = frames_dev * patches
    seq_devices = lax.axis_size("seq")
    clip_count = frames_dev * seq_devices // FRAMES
    spatial_query, spatial_keys, spatial_values = split_three(spatial_qkv)
    spatial_out = attention(spatial_query, spatial_keys, spatial_values)
    spatial_rows = spatial_out.reshape(row_total, -1)
    hidden_rows = (
        tokens.reshape(row_total, feature_width).astype(jnp.float32)
        + jnp.dot(spatial_rows, wo_spatial, preferred_element_type=jnp.float32)
    ).astype(jnp.bfloat16)
    frame_qkv = (
        forward_project(hidden_rows, w_temporal)
        .astype(jnp.bfloat16)
        .reshape(frames_dev, patches, -1)
    )
    patch_qkv = lax.all_to_all(frame_qkv, "seq", split_axis=1, concat_axis=0, tiled=True)
    temporal_query, temporal_keys, temporal_values = split_three(to_clips(patch_qkv, clip_count))
    patch_out = from_clips(attention(temporal_query, temporal_keys, temporal_values), clip_count)
    temporal_out = lax.all_to_all(patch_out, "seq", split_axis=0, concat_axis=1, tiled=True)
    temporal_rows = temporal_out.reshape(row_total, -1)
    block_out = (
        hidden_rows.astype(jnp.float32)
        + jnp.dot(temporal_rows, wo_temporal, preferred_element_type=jnp.float32)
    ).astype(jnp.bfloat16)
    grad_rows = cotangent.reshape(row_total, feature_width)
    out_grad = (
        times_transposed(grad_rows, wo_temporal)
        .astype(jnp.bfloat16)
        .reshape(frames_dev, patches, -1)
    )
    temporal_part = transposed_times(temporal_rows, grad_rows).astype(jnp.bfloat16)
    patch_out_grad = lax.all_to_all(out_grad, "seq", split_axis=1, concat_axis=0, tiled=True)
    clip_qkv_grad = attention_grad(
        temporal_query, temporal_keys, temporal_values, to_clips(patch_out_grad, clip_count)
    )
    patch_qkv_grad = from_clips(clip_qkv_grad, clip_count)
    frame_qkv_grad = lax.all_to_all(patch_qkv_grad, "seq", split_axis=0, concat_axis=1, tiled=True)
    projection_grad = backward_project(frame_qkv_grad.reshape(row_total, -1), w_temporal).astype(
        jnp.bfloat16
    )
    tokens_grad = (grad_rows.astype(jnp.float32) + projection_grad.astype(jnp.float32)).astype(
        jnp.bfloat16
    )
    spatial_out_grad = (
        times_transposed(tokens_grad, wo_spatial)
        .astype(jnp.bfloat16)
        .reshape(frames_dev, patches, -1)
    )
    spatial_part = transposed_times(spatial_rows, tokens_grad).astype(jnp.bfloat16)
    spatial_qkv_grad = attention_grad(spatial_query, spatial_keys, spatial_values, spatial_out_grad)
    seq_sums = (
        lax.psum_scatter(spatial_part, "seq", scatter_dimension=0, tiled=True).astype(jnp.float32),
        lax.psum_scatter(temporal_part, "seq", scatter_dimension=0, tiled=True).astype(jnp.float32),
    )
    spatial_weight_grad, temporal_weight_grad = (
        lax.psum_scatter(
            seq_sums[0].astype(jnp.bfloat16), "dp", scatter_dimension=1, tiled=True
        ).astype(jnp.float32),
        lax.psum_scatter(
            seq_sums[1].astype(jnp.bfloat16), "dp", scatter_dimension=1, tiled=True
        ).astype(jnp.float32),
    )
    return (
        block_out.reshape(frames_dev, patches, feature_width),
        tokens_grad.reshape(frames_dev, patches, feature_width),
        spatial_qkv_grad,
        spatial_weight_grad,
        temporal_weight_grad,
    )


def solution(mesh):
    placed = (
        P(("dp", "seq"), None, None),
        P(("dp", "seq"), None, None),
        P(),
        P(None, "dp"),
        P(),
        P(("dp", "seq"), None, None),
    )
    return jax.shard_map(
        shards,
        mesh=mesh,
        in_specs=placed,
        out_specs=(
            P(("dp", "seq"), None, None),
            P(("dp", "seq"), None, None),
            P(("dp", "seq"), None, None),
            P("seq", "dp"),
            P("seq", "dp"),
        ),
        check_vma=False,
    )
```

profile of v0, /device:TPU:0, one launch (start us, length us, event | category | flops | bytes accessed | tf_op | source)
XLA Modules:
  0.0 259.3 jit_solution(11038089109482344569)
XLA Ops:
  9.3 1.1 fusion.123
  10.5 2.4 fusion.21
  12.8 1.1 copy.60
  14.6 49.0 %all-gather.2.cloned.1.call-done = bf16[1152,1728]{0,1:T(8,128)(2,1)} async-done(((bf16[1152,432]{0,1:T(8,128)(2,1)}), bf16[1152,1728]{0,1:T(8,128)(2,1)}) %all-gather.2.cloned.1.call-update) | async-done | bytes 3981328 | tf_op jit(solution)/shard_map/all_gather | solution.py:100
  63.6 4.1 %convolution_convert_fusion.3 = bf16[128,1728]{0,1:T(8,128)(2,1)} fusion(bf16[128,1152]{1,0:T(8,128)(2,1)S(1)} %fusion.7, bf16[1152,1728]{0,1:T(8,128)(2,1)} %all-gather.2.cloned.1.call-done), kind=kOutput, calls=%fused_computation.11 | convolution fusion | flops 509829120 | bytes 4718592 | tf_op jit(solution)/shard_map/dot_general | solution.py:98
  67.6 1.2 copy.61
  69.3 18.4 %all_to_all.60 = bf16[2,64,1728]{2,0,1:T(2,128)(2,1)S(1)} all-to-all(bf16[2,64,1728]{2,0,1:T(2,128)(2,1)S(1)} %copy.62), channel_id=1, replica_groups=mesh['dp'=4,'seq'=8] {'seq'}, dimensions={1} | all-to-all | bytes 884736 | tf_op jit(solution)/shard_map/all_to_all | solution.py:126
  90.2 2.4 fusion.128
  93.2 2.4 fusion.22
  95.6 1.1 copy.72
  98.5 9.6 %all_to_all.61 = bf16[16,8,576]{2,1,0:T(8,128)(2,1)S(1)} all-to-all(bf16[16,8,576]{2,1,0:T(8,128)(2,1)S(1)} %copy.73), channel_id=1, replica_groups=mesh['dp'=4,'seq'=8] {'seq'}, dimensions={0} | all-to-all | bytes 294912 | tf_op jit(solution)/shard_map/all_to_all | solution.py:129
  108.8 1.6 convolution_convert_fusion
  111.3 13.1 %all_to_all.62 = bf16[2,64,576]{2,0,1:T(2,128)(2,1)S(1)} all-to-all(bf16[2,64,576]{2,0,1:T(2,128)(2,1)S(1)} %copy.76), channel_id=1, replica_groups=mesh['dp'=4,'seq'=8] {'seq'}, dimensions={1} | all-to-all | bytes 294912 | tf_op jit(solution)/shard_map/all_to_all | solution.py:142
  125.2 1.2 reshape.195
  127.1 2.4 fusion.25
  131.4 2.2 fusion.42
  133.7 2.7 %fusion.24 = bf16[8,16,8,72]{3,1,2,0:T(8,128)(2,1)} fusion(f32[8,8,16,16]{2,3,1,0:T(8,128)} %fusion.42, bf16[8,16,8,72]{3,2,0,1:T(8,128)(2,1)} %reshape.193, f32[8,8,16,16]{2,3,1,0:T(8,128)} %get-tuple-element.14, f32[8,8,16]{2,1,0:T(8,128)S(1)} %copy-done.20), kind=kOutput, calls=%fused_computation.40 | convolution fusion | flops 2548751 | bytes 430080 | tf_op jit(solution)/shard_map/bhlm,blhd->bmhd/dot_general | solution.py:62
  138.3 2.8 %fusion.23 = bf16[8,16,8,72]{3,1,2,0:T(8,128)(2,1)} fusion(f32[8,8,16,16]{2,3,1,0:T(8,128)} %fusion.42, bf16[8,16,8,72]{3,2,0,1:T(8,128)(2,1)} %reshape.194, f32[8,8,16,16]{2,3,1,0:T(8,128)} %get-tuple-element.14, f32[8,8,16]{2,1,0:T(8,128)S(1)} %copy-done.20), kind=kOutput, calls=%fused_computation.39 | convolution fusion | flops 2548751 | bytes 430080 | tf_op jit(solution)/shard_map/bhlm,bmhd->blhd/dot_general | solution.py:59
  141.1 1.0 copy.84
  143.0 2.0 concatenate.24
  145.0 1.2 copy.89
  146.1 16.4 %all_to_all.63 = bf16[16,8,1728]{2,1,0:T(8,128)(2,1)S(1)} all-to-all(bf16[16,8,1728]{2,1,0:T(8,128)(2,1)S(1)} %copy.89), channel_id=1, replica_groups=mesh['dp'=4,'seq'=8] {'seq'}, dimensions={0} | all-to-all | bytes 884736 | tf_op jit(solution)/shard_map/all_to_all | solution.py:147
  162.5 3.0 %fusion.6 = bf16[128,1152]{1,0:T(8,128)(2,1)S(1)} fusion(bf16[128,1728]{1,0:T(8,128)(2,1)S(1)} %bitcast.111, bf16[1152,1728]{0,1:T(8,128)(2,1)} %all-gather.2.cloned.1.call-done, bf16[128,1152]{1,0:T(8,128)(2,1)S(1)} %bitcast.108), kind=kOutput, calls=%fused_computation.12 | convolution fusion | flops 510345216 | bytes 5013504 | tf_op jit(solution)/shard_map/dot_general | solution.py:86
  165.5 1.6 convolution_convert_fusion.1
  167.2 1.1 fusion.8
  169.3 1.8 copy.107
  171.5 1.6 fusion.26
  173.1 26.2 %reduce-scatter.17.cloned.1.call-done = bf16[72,1152]{1,0:T(8,128)(2,1)} async-done(((bf16[576,1152]{1,0:T(8,128)(2,1)}), bf16[72,1152]{1,0:T(8,128)(2,1)}) %reduce-scatter.17.cloned.1.call-update) | async-done | bytes 165904
  199.3 1.8 copy.105
  201.1 1.5 fusion.27
  205.1 19.1 %reduce-scatter.15.cloned.1.call-done = bf16[288,72]{1,0:T(8,128)(2,1)} async-done(((bf16[1152,72]{1,0:T(8,128)(2,1)}), bf16[288,72]{1,0:T(8,128)(2,1)}) %reduce-scatter.15.cloned.1.call-update) | async-done | bytes 41488
  225.9 25.2 %reduce-scatter.13.cloned.1.call-done = bf16[288,72]{1,0:T(8,128)(2,1)} async-done(((bf16[1152,72]{1,0:T(8,128)(2,1)}), bf16[288,72]{1,0:T(8,128)(2,1)}) %reduce-scatter.13.cloned.1.call-update) | async-done | bytes 41488
  (100 shorter events, 22.6 us)
Async XLA Ops:
  7.2 103.3 %copy-start = (bf16[576,1152]{1,0:T(8,128)(2,1)S(1)}, bf16[576,1152]{1,0:T(8,128)(2,1)}, u32[]{:S(2)}) copy-start(bf16[576,1152]{1,0:T(8,128)(2,1)} %param.10) | copy-start | bytes 3981316
  7.2 1.1 copy-start.12
  7.2 56.4 %all-gather.2.cloned.1.call-start = ((), (), s32[]{:S(2)}) async-start(), calls=%async_computation.8 | async-start | bytes 4976640 | tf_op jit(solution)/shard_map/all_gather | solution.py:100
  7.9 161.3 %reduce-scatter.19.cloned.1.call-start = ((), (), s32[]{:S(2)}) async-start(), calls=%async_computation.12 | async-start | bytes 1492992
  8.7 1.7 copy-start.14
  9.0 1.4 copy-start.16
  9.3 1.2 copy-start.8
  10.4 2.4 copy-start.21
  10.4 3.7 %copy-start.1 = (bf16[576,1152]{1,0:T(8,128)(2,1)S(1)}, bf16[576,1152]{1,0:T(8,128)(2,1)}, u32[]{:S(2)}) copy-start(bf16[576,1152]{1,0:T(8,128)(2,1)} %param.8) | copy-start | bytes 3981316
  10.5 3.7 %copy-start.13 = (bf16[2,64,1152]{2,1,0:T(8,128)(2,1)S(1)}, bf16[2,64,1152]{2,1,0:T(8,128)(2,1)}, u32[]{:S(2)}) copy-start(bf16[2,64,1152]{2,1,0:T(8,128)(2,1)} %param.6) | copy-start | bytes 884740
  14.2 49.4 %copy-start.4 = (bf16[128,576]{1,0:T(8,128)(2,1)}, bf16[128,576]{1,0:T(8,128)(2,1)S(1)}, u32[]{:S(2)}) copy-start(bf16[128,576]{1,0:T(8,128)(2,1)S(1)} %convert_element_type.106) | copy-start | bytes 442372
  90.1 2.5 copy-start.10
  90.2 3.1 %copy-start.18 = (bf16[8,16,8,72]{3,2,0,1:T(8,128)(2,1)S(1)}, bf16[8,16,8,72]{3,2,0,1:T(8,128)(2,1)}, u32[]{:S(2)}) copy-start(bf16[8,16,8,72]{3,2,0,1:T(8,128)(2,1)} %reshape.194) | copy-start | bytes 442372
  92.6 0.6 copy-start.19
  95.6 13.2 %copy-start.2 = (bf16[2,64,1152]{2,1,0:T(8,128)(2,1)S(1)}, bf16[2,64,1152]{2,1,0:T(8,128)(2,1)}, u32[]{:S(2)}) copy-start(bf16[2,64,1152]{2,1,0:T(8,128)(2,1)} %param.11) | copy-start | bytes 884740
  108.1 0.7 copy-start.6
  110.4 88.8 %reduce-scatter.17.cloned.1.call-start = ((), (), s32[]{:S(2)}) async-start(), calls=%async_computation.11 | async-start | bytes 1492992
  111.2 15.9 %copy-start.20 = (f32[8,8,16]{2,1,0:T(8,128)S(1)}, f32[8,8,16]{2,1,0:T(8,128)}, u32[]{:S(2)}) copy-start(f32[8,8,16]{2,1,0:T(8,128)} %copy-done.19) | copy-start | bytes 12292
  126.4 0.7 copy-start.11
  162.5 3.0 %copy-start.5 = (bf16[128,576]{1,0:T(8,128)(2,1)S(1)}, bf16[128,576]{1,0:T(8,128)(2,1)}, u32[]{:S(2)}) copy-start(bf16[128,576]{1,0:T(8,128)(2,1)} %copy-done.4) | copy-start | bytes 442372
  165.5 2.9 %copy-start.3 = (bf16[128,1152]{1,0:T(8,128)(2,1)}, bf16[128,1152]{1,0:T(8,128)(2,1)S(1)}, u32[]{:S(2)}) copy-start(bf16[128,1152]{1,0:T(8,128)(2,1)S(1)} %fusion.6) | copy-start | bytes 884740
  165.5 1.7 copy-start.7
  167.2 57.1 %reduce-scatter.15.cloned.1.call-start = ((), (), s32[]{:S(2)}) async-start(), calls=%async_computation.10 | async-start | bytes 368640
  168.4 2.8 %copy-start.9 = (bf16[2,64,8,72]{3,2,1,0:T(8,128)(2,1)S(1)}, bf16[2,64,8,72]{3,2,1,0:T(8,128)(2,1)}, u32[]{:S(2)}) copy-start(bf16[2,64,8,72]{3,2,1,0:T(8,128)(2,1)} %copy-done.8) | copy-start | bytes 442372
  168.9 2.6 copy-start.17
  168.9 2.6 copy-start.22
  171.1 80.0 %reduce-scatter.13.cloned.1.call-start = ((), (), s32[]{:S(2)}) async-start(), calls=%async_computation.9 | async-start | bytes 368640
  171.4 29.6 %copy-start.15 = (bf16[2,64,8,72]{3,2,1,0:T(8,128)(2,1)S(1)}, bf16[2,64,8,72]{3,2,1,0:T(8,128)(2,1)}, u32[]{:S(2)}) copy-start(bf16[2,64,8,72]{3,2,1,0:T(8,128)(2,1)} %copy-done.14) | copy-start | bytes 442372
Sparse Core Ops, SparseCore 0:
  9.9 53.6 all-gather.1
  110.5 33.0 reduce-scatter.18
  167.3 31.9 reduce-scatter.16
  201.9 22.3 reduce-scatter.14
  226.9 24.1 reduce-scatter.12
where the time goes:
time: 260 us; the launch traced here: 259 us
  waiting for transfers between devices  120 us (46%)
  blocking collectives  57.4 us (22%)
  matrix products  35.1 us (14%)
  local copies, waits for them, and re-layouts  30.7 us (12%)
  between operations  14.2 us (5%)
    unnamed x9, waiting for transfers between devices  71.3 us
    all_gather x1, waiting for transfers between devices, forward_project(): lax.all_gather(weight_shard, 'dp', axis=1, tiled=True)  49 us
    all_to_all x1, blocking collectives, shards(): lax.all_to_all(frame_qkv, 'seq', split_axis=1, concat_axis=0, tiled=True)  18.4 us
    all_to_all x1, blocking collectives, shards(): lax.all_to_all(patch_qkv_grad, 'seq', split_axis=0, concat_axis=1, tiled=...  16.4 us
    all_to_all x1, blocking collectives, shards(): lax.all_to_all(out_grad, 'seq', split_axis=1, concat_axis=0, tiled=True)  13.1 us
    all_to_all x1, blocking collectives, shards(): lax.all_to_all(patch_out, 'seq', split_axis=0, concat_axis=1, tiled=True)  9.62 us
    unnamed x50, local copies, waits for them, and re-layouts  7.95 us
    concatenate x5, local copies, waits for them, and re-layouts, attention_grad(): return jnp.concatenate(joined, axis=-1).astype(jnp.bfloat16)  5.54 us
  transfers between devices with their start and end apart: 5, of which 4 were waited for; matrix products, arithmetic and copies ran while one was open for 18% of the time, Pallas kernels for 0%

commit v1 on v0

v1 whole, which is shorter than its diff:
```python
import functools
import math

import jax
import jax.numpy as jnp
from jax import lax
from jax.experimental import pallas as pl
from jax.experimental.pallas import tpu as pltpu
from jax.sharding import PartitionSpec as P

DH = 72
FRAMES = 16
LANES = 128
BF16 = jnp.bfloat16
F32 = jnp.float32
VMEM = pl.BlockSpec(memory_space=pltpu.VMEM)
SMEM = pl.BlockSpec(memory_space=pltpu.SMEM)
LIMIT = 40 * 1024 * 1024


def dot(left, right):
    return jnp.dot(left, right, preferred_element_type=F32)


def dot_bt(left, right):
    return lax.dot_general(left, right, (((1,), (1,)), ((), ())), preferred_element_type=F32)


def dot_at(left, right):
    return lax.dot_general(left, right, (((0,), (0,)), ((), ())), preferred_element_type=F32)


def call(body, outs, args, scratch=(), flops=0):
    moved = sum(math.prod(a.shape) * a.dtype.itemsize for a in (*args, *outs))
    return pl.pallas_call(
        body,
        out_shape=outs,
        in_specs=[SMEM if a.dtype == jnp.int32 else VMEM for a in args],
        out_specs=[VMEM] * len(outs),
        scratch_shapes=list(scratch),
        compiler_params=pltpu.CompilerParams(vmem_limit_bytes=LIMIT),
        cost_estimate=pl.CostEstimate(flops=flops, bytes_accessed=moved, transcendentals=0),
    )(*args)


def shape(dims, dtype=BF16):
    return jax.ShapeDtypeStruct(dims, dtype)


def window(head):
    low = head * DH // LANES * LANES
    high = -(-(head + 1) * DH // LANES) * LANES
    return low, high


def head_only(block, head):
    low, high = window(head)
    lane = lax.broadcasted_iota(jnp.int32, (1, high - low), 1) + low
    keep = (lane >= head * DH) & (lane < (head + 1) * DH)
    return jnp.where(keep, block, jnp.zeros_like(block))


def add_tiles(tiles, head, value):
    low, high = window(head)
    for at in range(low // LANES, high // LANES):
        part = value[:, at * LANES - low : (at + 1) * LANES - low]
        tiles[at] = part if tiles[at] is None else tiles[at] + part


def joined(tiles):
    return jnp.concatenate([tile.astype(BF16) for tile in tiles], axis=1)


def same_group(rows, kind):
    row = lax.broadcasted_iota(jnp.int32, (rows, rows), 0)
    col = lax.broadcasted_iota(jnp.int32, (rows, rows), 1)
    how, size = kind
    return row // size == col // size if how == "block" else row % size == col % size


def softmax_forward(q_ref, k_ref, v_ref, p_ref, heads, kind):
    rows = q_ref.shape[0]
    mask = same_group(rows, kind)
    tiles = [None] * (q_ref.shape[1] // LANES)
    for head in range(heads):
        low, high = window(head)
        s = dot_bt(q_ref[:, low:high], head_only(k_ref[:, low:high], head)) * (1.0 / math.sqrt(DH))
        s = jnp.where(mask, s, -jnp.inf)
        e = jnp.exp(s - jnp.max(s, axis=1, keepdims=True))
        p = e / jnp.sum(e, axis=1, keepdims=True)
        p_ref[head] = p
        add_tiles(tiles, head, dot(p.astype(BF16), head_only(v_ref[:, low:high], head)))
    return joined(tiles)


def softmax_backward(q_ref, k_ref, v_ref, g_ref, p_ref, heads):
    count = q_ref.shape[1] // LANES
    dq, dk, dv = [None] * count, [None] * count, [None] * count
    for head in range(heads):
        low, high = window(head)
        p = p_ref[head]
        g = head_only(g_ref[:, low:high], head)
        add_tiles(dv, head, dot_at(p.astype(BF16), g))
        dp = dot_bt(g, v_ref[:, low:high])
        ds = p * (dp - jnp.sum(p * dp, axis=1, keepdims=True)) * (1.0 / math.sqrt(DH))
        ds = ds.astype(BF16)
        add_tiles(dq, head, dot(ds, head_only(k_ref[:, low:high], head)))
        add_tiles(dk, head, dot_at(ds, head_only(q_ref[:, low:high], head)))
    return joined(dq), joined(dk), joined(dv)


def put(ref, value):
    width = value.shape[1]
    ref[:, width // LANES * LANES :] = jnp.zeros(
        (ref.shape[0], ref.shape[1] - width // LANES * LANES), ref.dtype
    )
    ref[:, :width] = value


def two_frames(ref, at, frames):
    return jnp.concatenate([ref[f, at].astype(F32) for f in range(frames)], axis=0).astype(BF16)


def pack_kernel(peers, idx, tok, cot, *outs):
    frames, width = tok.shape[0], tok.shape[3]
    for r in range(peers):
        at = idx[0] ^ r
        outs[r][:, :width] = two_frames(tok, at, frames)
        outs[r][:, width:] = two_frames(cot, at, frames)


def spatial_kernel(peers, patches, qkv, out, by_peer, p_ref, qs, ks, vs):
    inner = out.shape[1]
    rows = out.shape[0]
    x = qkv[...]
    put(qs, x[:, :inner])
    put(ks, x[:, inner : 2 * inner])
    put(vs, x[:, 2 * inner :])
    o = softmax_forward(qs, ks, vs, p_ref, inner // DH, ("block", patches))[:, :inner]
    out[...] = o
    each = patches // peers
    o = o.astype(F32)
    for at in range(peers):
        by_peer[at] = jnp.concatenate(
            [o[f * patches + at * each : f * patches + (at + 1) * each] for f in range(rows // patches)],
            axis=0,
        ).astype(BF16)


def temporal_forward_kernel(peers, shards, group, idx, so, wos, wot, *refs):
    packed, refs = refs[:peers], refs[peers:]
    weights, refs = refs[: len(shards)], refs[len(shards) :]
    q, k, v, g, p_ref, spat, cot, part = refs[:8]
    outs = refs[8 : 8 + peers]
    blocks, tok = refs[8 + peers :]
    width = wos.shape[1]
    inner = wos.shape[0]
    chunk = so.shape[1]
    for r in range(peers):
        rows = slice(r * chunk, (r + 1) * chunk)
        spat[rows] = so[idx[0] ^ r]
        tok[rows] = packed[r][:, :width]
        cot[rows] = packed[r][:, width:]
    hidden = (tok[...].astype(F32) + dot(spat[...], wos[...])).astype(BF16)
    for (place, count), w in zip(shards, weights):
        block = dot_bt(hidden, w[...]).astype(BF16)
        size = block.shape[1] // count
        for i in range(count):
            blocks[place(idx) + i] = block[:, i * size : (i + 1) * size]
    whole = jnp.concatenate([blocks[i] for i in range(blocks.shape[0])], axis=1)
    put(q, whole[:, :inner])
    put(k, whole[:, inner : 2 * inner])
    put(v, whole[:, 2 * inner :])
    o = softmax_forward(q, k, v, p_ref, inner // DH, ("cycle", group))[:, :inner]
    for r in range(peers):
        outs[r][...] = o[r * chunk : (r + 1) * chunk]
    part[...] = dot_at(o, cot[...]).astype(BF16)
    put(g, dot_bt(cot[...], wot[...]).astype(BF16))


def temporal_backward_kernel(peers, shards, idx, q, k, v, g, p_ref, spat, cot, *refs):
    weights, refs = refs[: len(shards)], refs[len(shards) :]
    outs = refs[:peers]
    part, blocks = refs[peers:]
    inner = spat.shape[1]
    chunk = outs[0].shape[0]
    dq, dk, dv = softmax_backward(q, k, v, g, p_ref, inner // DH)
    whole = jnp.concatenate([dq[:, :inner], dk[:, :inner], dv[:, :inner]], axis=1)
    size = blocks.shape[2]
    for i in range(blocks.shape[0]):
        blocks[i] = whole[:, i * size : (i + 1) * size]
    total = jnp.zeros(cot.shape, F32)
    for (place, count), w in zip(shards, weights):
        lhs = jnp.concatenate([blocks[place(idx) + i] for i in range(count)], axis=1)
        total += dot(lhs, w[...])
    grad = (cot[...].astype(F32) + total.astype(BF16).astype(F32)).astype(BF16)
    for r in range(peers):
        outs[r][...] = grad[r * chunk : (r + 1) * chunk]
    part[...] = dot_at(spat[...], grad).astype(BF16)


def block_out_kernel(peers, patches, idx, tok, spat, wos, wot, *refs):
    chunks, (out, rows) = refs[:peers], refs[peers:]
    each = patches // peers
    for r in range(peers):
        for f in range(chunks[r].shape[0] // each):
            low = pl.multiple_of(f * patches + (idx[0] ^ r) * each, each)
            rows[pl.ds(low, each)] = chunks[r][f * each : (f + 1) * each].astype(F32)
    hidden = (tok[...].astype(F32) + dot(spat[...], wos[...])).astype(BF16)
    out[...] = (hidden.astype(F32) + dot(rows[...].astype(BF16), wot[...])).astype(BF16)


def spatial_backward_kernel(peers, patches, idx, qkv, p_ref, wos, *refs):
    chunks, (out, grads, rows, qs, ks, vs, gs) = refs[:peers], refs[peers:]
    inner = wos.shape[0]
    each = patches // peers
    for r in range(peers):
        for f in range(chunks[r].shape[0] // each):
            low = pl.multiple_of(f * patches + (idx[0] ^ r) * each, each)
            rows[pl.ds(low, each)] = chunks[r][f * each : (f + 1) * each].astype(F32)
    grad = rows[...].astype(BF16)
    out[...] = grad
    put(gs, dot_bt(grad, wos[...]).astype(BF16))
    x = qkv[...]
    put(qs, x[:, :inner])
    put(ks, x[:, inner : 2 * inner])
    put(vs, x[:, 2 * inner :])
    dq, dk, dv = softmax_backward(qs, ks, vs, gs, p_ref, inner // DH)
    grads[...] = jnp.concatenate([dq[:, :inner], dk[:, :inner], dv[:, :inner]], axis=1)


def flip(value, axis, bit):
    return lax.ppermute(value, axis, [(i, i ^ bit) for i in range(lax.axis_size(axis))])


def gather_weight(weight, core):
    n = lax.axis_size("dp")
    if n != 4:
        return [lax.all_gather(weight, "dp", axis=0, tiled=True)], [(lambda idx: 0, 1)], 1
    half = weight.shape[0] // 2
    mine = lax.dynamic_slice_in_dim(weight, core * half, half, 0)
    near = [flip(mine, "dp", j) for j in range(1, n)]
    far = [flip(w, "seq", 1) for w in near]
    shards = [(lambda idx: 2 * idx[1], 2)]
    shards += [(lambda idx, j=j: 2 * (idx[1] ^ j) + idx[2], 1) for j in range(1, n)]
    shards += [(lambda idx, j=j: 2 * (idx[1] ^ j) + 1 - idx[2], 1) for j in range(1, n)]
    return [weight, *near, *far], shards, 2 * n


def reduced(part):
    over_seq = lax.psum_scatter(part, "seq", scatter_dimension=0, tiled=True)
    return lax.psum_scatter(over_seq, "dp", scatter_dimension=1, tiled=True).astype(F32)


def shards(tokens, spatial_qkv, wo_spatial, w_temporal, wo_temporal, cotangent):
    frames, patches, width = tokens.shape
    inner = wo_spatial.shape[0]
    heads = inner // DH
    padded = -(-inner // LANES) * LANES
    rows = frames * patches
    peers = FRAMES // frames
    each = patches // peers
    chunk = rows // peers
    n_seq = lax.axis_size("seq")
    seq = lax.axis_index("seq")
    idx = jnp.stack([seq % peers, lax.axis_index("dp"), seq % 2]).astype(jnp.int32)
    wide = pltpu.VMEM((rows, padded), BF16)

    weights, places, count = gather_weight(w_temporal.T, seq % 2)

    packed = call(
        functools.partial(pack_kernel, peers),
        [shape((chunk, 2 * width))] * peers,
        [
            idx,
            tokens.reshape(frames, peers, each, width),
            cotangent.reshape(frames, peers, each, width),
        ],
    )
    packed = [packed[0]] + [flip(packed[r], "seq", r) for r in range(1, peers)]

    qkv_rows = spatial_qkv.reshape(rows, 3 * inner)
    spatial_rows, by_peer, spatial_p = call(
        functools.partial(spatial_kernel, peers, patches),
        [shape((rows, inner)), shape((peers, chunk, inner)), shape((heads, rows, rows), F32)],
        [qkv_rows],
        [wide] * 3,
    )
    groups = None
    if n_seq > peers:
        groups = [list(range(i, i + peers)) for i in range(0, n_seq, peers)]
    by_peer = lax.all_to_all(
        by_peer, "seq", split_axis=0, concat_axis=0, tiled=True, axis_index_groups=groups
    )

    q, k, v, g, temporal_p, spat, cot, temporal_part, *outs = call(
        functools.partial(temporal_forward_kernel, peers, places, each),
        [shape((rows, padded))] * 4
        + [shape((heads, rows, rows), F32), shape((rows, inner)), shape((rows, width))]
        + [shape((inner, width))]
        + [shape((chunk, inner))] * peers,
        [idx, by_peer, wo_spatial, wo_temporal, *packed, *weights],
        [
            pltpu.VMEM((count, rows, 3 * inner // count), BF16),
            pltpu.VMEM((rows, width), BF16),
        ],
    )
    outs = [outs[0]] + [flip(outs[r], "seq", r) for r in range(1, peers)]

    *grads, spatial_part = call(
        functools.partial(temporal_backward_kernel, peers, places),
        [shape((chunk, width))] * peers + [shape((inner, width))],
        [idx, q, k, v, g, temporal_p, spat, cot, *weights],
        [pltpu.VMEM((count, rows, 3 * inner // count), BF16)],
    )
    grads = [grads[0]] + [flip(grads[r], "seq", r) for r in range(1, peers)]

    (block_out,) = call(
        functools.partial(block_out_kernel, peers, patches),
        [shape((rows, width))],
        [idx, tokens.reshape(rows, width), spatial_rows, wo_spatial, wo_temporal, *outs],
        [pltpu.VMEM((rows, inner), F32)],
    )
    tokens_grad, qkv_grad = call(
        functools.partial(spatial_backward_kernel, peers, patches),
        [shape((rows, width)), shape((rows, 3 * inner))],
        [idx, qkv_rows, spatial_p, wo_spatial, *grads],
        [pltpu.VMEM((rows, width), F32)] + [wide] * 4,
    )
    return (
        block_out.reshape(frames, patches, width),
        tokens_grad.reshape(frames, patches, width),
        qkv_grad.reshape(frames, patches, 3 * inner),
        reduced(spatial_part),
        reduced(temporal_part),
    )


def solution(mesh):
    placed = (
        P(("dp", "seq"), None, None),
        P(("dp", "seq"), None, None),
        P(),
        P(None, "dp"),
        P(),
        P(("dp", "seq"), None, None),
    )
    return jax.shard_map(
        shards,
        mesh=mesh,
        in_specs=placed,
        out_specs=(
            P(("dp", "seq"), None, None),
            P(("dp", "seq"), None, None),
            P(("dp", "seq"), None, None),
            P("seq", "dp"),
            P("seq", "dp"),
        ),
        check_vma=False,
    )
```

time: 260 us -> 231 us (0.89)
  blocking collectives: 57.4 us -> 0 us
  matrix products: 35.1 us -> 0 us
  starting transfers between devices: 0.2 us -> 33.2 us
  Pallas kernels: 0 us -> 20.4 us
  waiting for transfers between devices: 120 us -> 129 us
    all_to_all x4 -> x0, blocking collectives: 57.4 us -> none  [the longest x1 18.4 us: shards(): lax.all_to_all(frame_qkv, 'seq', split_axis=1, concat_axis=0, tiled=True)]
    all_gather x1 -> x0, waiting for transfers between devices: 49 us -> none  [forward_project(): lax.all_gather(weight_shard, 'dp', axis=1, tiled=True)]
    ppermute x0 -> x27, waiting for transfers between devices: none -> 39.6 us  [flip(): lax.ppermute(value, axis, [(i, i ^ bit) for i in range(lax.axis_size(axis...]
    dot_general x18 -> x0, matrix products: 31.6 us -> none  [the longest x2 4.73 us: attention(): jnp.einsum('bhlm,bmhd->blhd', rounded, head_view(values), preferred_eleme...]
    ppermute x0 -> x27, starting transfers between devices: none -> 27.8 us  [flip(): lax.ppermute(value, axis, [(i, i ^ bit) for i in range(lax.axis_size(axis...]
    unnamed x50 -> x112, local copies, waits for them, and re-layouts: 7.95 us -> 30.4 us
    pallas_call x0 -> x6, Pallas kernels: none -> 20.4 us  [call(): pl.pallas_call(body, out_shape=outs, in_specs=[SMEM if a.dtype == jnp.int...]
    unnamed x9 -> x8, waiting for transfers between devices: 71.3 us -> 89.6 us
  transfers between devices with their start and end apart: 5 -> 32, of which waited for: 4 -> 14; matrix products, arithmetic and copies ran while one was open for 18% -> 2% of each run, Pallas kernels for 0% -> 4%
where the time goes in v1:
time: 231 us; the launch traced here: 230 us
  waiting for transfers between devices  129 us (56%)
  starting transfers between devices  33.2 us (14%)
  local copies, waits for them, and re-layouts  31.6 us (14%)
  Pallas kernels  20.4 us (9%)
  between operations  14.2 us (6%)
    unnamed x8, waiting for transfers between devices  89.6 us
    ppermute x27, waiting for transfers between devices, flip(): lax.ppermute(value, axis, [(i, i ^ bit) for i in range(lax.axis_size(axis...  39.6 us
    unnamed x112, local copies, waits for them, and re-layouts  30.4 us
    ppermute x27, starting transfers between devices, flip(): lax.ppermute(value, axis, [(i, i ^ bit) for i in range(lax.axis_size(axis...  27.8 us
    pallas_call x6, Pallas kernels, call(): pl.pallas_call(body, out_shape=outs, in_specs=[SMEM if a.dtype == jnp.int...  20.4 us
    all_to_all x1, starting transfers between devices, shards(): lax.all_to_all(by_peer, 'seq', split_axis=0, concat_axis=0, tiled=True, a...  4.99 us
  transfers between devices with their start and end apart: 32, of which 14 were waited for; matrix products, arithmetic and copies ran while one was open for 2% of the time, Pallas kernels for 4%

profile of v1, /device:TPU:0, one launch (start us, length us, event | category | flops | bytes accessed | tf_op | source)
XLA Modules:
  0.0 230.0 jit_solution(16983148298148859334)
XLA Ops:
  7.2 1.2 dynamic-slice_bitcast_fusion
  8.4 3.0 %collective-permute-start.7 = (bf16[216,1152]{1,0:T(8,128)(2,1)S(1)}, bf16[216,1152]{1,0:T(8,128)(2,1)S(1)}, u32[]{:S(2)}, u32[]{:S(2)}) collective-permute-start(bf16[216,1152]{1,0:T(8,128)(2,1)S(1)} %dynamic-slice_bitcast_fusion), channel_id=1, source_target_pairs={{0,8},{8,0},{16,24},{24,16},{1,9},{9,1},{17,25},{25,17},{2,10},{10... | collective-permute-start | bytes 1493000 | tf_op jit(solution)/shard_map/ppermute | solution.py:233
  11.4 1.5 collective-permute-start.8
  13.0 10.6 %collective-permute-done.7.refs_9_.refs_1_ = bf16[216,1152]{1,0:T(8,128)(2,1)S(1)} collective-permute-done((bf16[216,1152]{1,0:T(8,128)(2,1)S(1)}, bf16[216,1152]{1,0:T(8,128)(2,1)S(1)}, u32[]{:S(2)}, u32[]{:S(2)}) %collective-permute-start.7) | collective-permute-done | bytes 497696 | tf_op jit(solution)/shard_map/ppermute | solution.py:233
  23.6 11.3 %collective-permute-done.8.refs_10_.refs_2_ = bf16[216,1152]{1,0:T(8,128)(2,1)S(1)} collective-permute-done((bf16[216,1152]{1,0:T(8,128)(2,1)S(1)}, bf16[216,1152]{1,0:T(8,128)(2,1)S(1)}, u32[]{:S(2)}, u32[]{:S(2)}) %collective-permute-start.8) | collective-permute-done | bytes 497696 | tf_op jit(solution)/shard_map/ppermute | solution.py:233
  37.4 1.2 shard_map.102
  44.1 1.7 shard_map.101
  47.9 5.0 %all-to-all-start = ((bf16[8,16,576]{2,1,0:T(8,128)(2,1)}), bf16[8,16,576]{2,1,0:T(8,128)(2,1)S(1)}, u32[]{:S(2)}, u32[]{:S(2)}) async-start(bf16[8,16,576]{2,1,0:T(8,128)(2,1)} %copy-done.13), calls=%async_computation | async-start | bytes 327680 | tf_op jit(solution)/shard_map/all_to_all | solution.py:292
  52.9 2.0 collective-permute-start.1
  54.9 5.9 %collective-permute-done.1.refs_2_ = bf16[16,2304]{1,0:T(8,128)(2,1)S(1)} collective-permute-done((bf16[16,2304]{1,0:T(8,128)(2,1)}, bf16[16,2304]{1,0:T(8,128)(2,1)S(1)}, u32[]{:S(2)}, u32[]{:S(2)}) %collective-permute-start.1) | collective-permute-done | bytes 73760 | tf_op jit(solution)/shard_map/ppermute | solution.py:233
  61.4 2.4 %collective-permute-start.3 = (bf16[16,2304]{1,0:T(8,128)(2,1)}, bf16[16,2304]{1,0:T(8,128)(2,1)S(1)}, u32[]{:S(2)}, u32[]{:S(2)}) collective-permute-start(bf16[16,2304]{1,0:T(8,128)(2,1)} %copy-done.33), channel_id=1, source_target_pairs={{0,4},{1,5},{2,6},{3,7},{4,0},{5,1},{6,2},{7,3},{8,12},{9,13},{10,... | collective-permute-start | bytes 221192 | tf_op jit(solution)/shard_map/ppermute | solution.py:233
  64.4 2.8 %collective-permute-done.3.refs_4_ = bf16[16,2304]{1,0:T(8,128)(2,1)S(1)} collective-permute-done((bf16[16,2304]{1,0:T(8,128)(2,1)}, bf16[16,2304]{1,0:T(8,128)(2,1)S(1)}, u32[]{:S(2)}, u32[]{:S(2)}) %collective-permute-start.3) | collective-permute-done | bytes 73760 | tf_op jit(solution)/shard_map/ppermute | solution.py:233
  67.8 5.1 %collective-permute-start.5 = (bf16[16,2304]{1,0:T(8,128)(2,1)}, bf16[16,2304]{1,0:T(8,128)(2,1)S(1)}, u32[]{:S(2)}, u32[]{:S(2)}) collective-permute-start(bf16[16,2304]{1,0:T(8,128)(2,1)} %copy-done.31), channel_id=1, source_target_pairs={{0,6},{1,7},{2,4},{3,5},{4,2},{5,3},{6,0},{7,1},{8,14},{9,15},{10,... | collective-permute-start | bytes 221192 | tf_op jit(solution)/shard_map/ppermute | solution.py:233
  73.9 1.9 collective-permute-done.5.refs_6_
  76.4 2.9 %collective-permute-done.6.refs_7_ = bf16[16,2304]{1,0:T(8,128)(2,1)S(1)} collective-permute-done((bf16[16,2304]{1,0:T(8,128)(2,1)}, bf16[16,2304]{1,0:T(8,128)(2,1)S(1)}, u32[]{:S(2)}, u32[]{:S(2)}) %collective-permute-start.6) | collective-permute-done | bytes 73760 | tf_op jit(solution)/shard_map/ppermute | solution.py:233
  80.0 1.3 copy-done.2
  87.5 5.8 %shard_map.103 = (bf16[128,640]{1,0:T(8,128)(2,1)S(1)}, bf16[128,640]{1,0:T(8,128)(2,1)S(1)}, bf16[128,640]{1,0:T(8,128)(2,1)S(1)}, bf16[128,640]{1,0:T(8,128)(2...) custom-call(s32[3]{0:T(128)S(1)} %pad_add_fusion.idx, ...), custom_call_target="tpu_custom_call" | custom-call | bytes 10469388 | tf_op jit(solution)/shard_map/pallas_call | solution.py:35
  94.4 5.5 %shard_map.105 = (bf16[16,1152]{1,0:T(8,128)(2,1)S(1)}, bf16[16,1152]{1,0:T(8,128)(2,1)S(1)}, bf16[16,1152]{1,0:T(8,128)(2,1)S(1)}, bf16[16,1152]{1,0:T(8,128)(2...) custom-call(s32[3]{0:T(128)S(1)} %pad_add_fusion.idx, ...), custom_call_target="tpu_custom_call" | custom-call | bytes 7225356 | tf_op jit(solution)/shard_map/pallas_call | solution.py:35
  103.7 31.5 %reduce-scatter.17.cloned.1.call-done = bf16[72,1152]{1,0:T(8,128)(2,1)} async-done(((bf16[576,1152]{1,0:T(8,128)(2,1)}), bf16[72,1152]{1,0:T(8,128)(2,1)}) %reduce-scatter.17.cloned.1.call-update) | async-done | bytes 165904
  135.2 1.8 copy.11
  137.3 32.6 %reduce-scatter.19.cloned.1.call-done = bf16[72,1152]{1,0:T(8,128)(2,1)} async-done(((bf16[576,1152]{1,0:T(8,128)(2,1)}), bf16[72,1152]{1,0:T(8,128)(2,1)}) %reduce-scatter.19.cloned.1.call-update) | async-done | bytes 165904
  169.8 1.8 copy.13
  171.9 1.8 collective-permute-start.15
  174.7 1.2 collective-permute-done.14.refs_2_
  176.8 1.4 collective-permute-start.18
  178.3 1.9 collective-permute-start.19
  180.3 2.0 collective-permute-done.18.refs_6_
  183.9 1.9 collective-permute-start.25
  185.7 2.8 %collective-permute-start.26 = (bf16[16,1152]{1,0:T(8,128)(2,1)S(1)}, bf16[16,1152]{1,0:T(8,128)(2,1)S(1)}, u32[]{:S(2)}, u32[]{:S(2)}) collective-permute-start(bf16[16,1152]{1,0:T(8,128)(2,1)S(1)} %get-tuple-element.76), channel_id=1, source_target_pairs={{0,7},{1,6},{2,5},{3,4},{4,3},{5,2},{6,1},{7,0},{8,15},{9,14},{10,... | collective-permute-start | bytes 110600 | tf_op jit(solution)/shard_map/ppermute | solution.py:233
  188.6 1.9 shard_map.104
  191.0 4.2 %shard_map.106 = (bf16[128,1152]{1,0:T(8,128)(2,1)}, bf16[128,1728]{1,0:T(8,128)(2,1)}) custom-call(s32[3]{0:T(128)S(1)} %pad_add_fusion.idx, bf16[128,1728]{1,0:T(8,128)(2,1)S(1)} %bitcast.21, f32[8,128,128]{2,1,0:T(8,128)S(1)} %copy-done.11, bf16[576,1152]{1,0:T(8,128)(2,1)S(1)} %copy-done, bf16[16,1152]{1,0:T(8,128)(2,1)S(1)} %get-tuple-element.69.refs_0_, ...), custom_call_target="tpu_custom_call" | custom-call | bytes 3325964 | tf_op jit(solution)/shard_map/pallas_call | solution.py:35
  196.8 25.0 %reduce-scatter.15.cloned.1.call-done = bf16[288,72]{1,0:T(8,128)(2,1)} async-done(((bf16[1152,72]{1,0:T(8,128)(2,1)}), bf16[288,72]{1,0:T(8,128)(2,1)}) %reduce-scatter.15.cloned.1.call-update) | async-done | bytes 41488
  (158 shorter events, 33.0 us)
Async XLA Ops:
  8.4 15.2 %collective-permute-start.7 = (bf16[216,1152]{1,0:T(8,128)(2,1)S(1)}, bf16[216,1152]{1,0:T(8,128)(2,1)S(1)}, u32[]{:S(2)}, u32[]{:S(2)}) collective-permute-start(bf16[216,1152]{1,0:T(8,128)(2,1)S(1)} %dynamic-slice_bitcast_fusion), channel_id=1, source_target_pairs={{0,8},{8,0},{16,24},{24,16},{1,9},{9,1},{17,25},{25,17},{2,10},{10... | collective-permute-start | bytes 1493000 | tf_op jit(solution)/shard_map/ppermute | solution.py:233
  11.4 23.5 %collective-permute-start.8 = (bf16[216,1152]{1,0:T(8,128)(2,1)S(1)}, bf16[216,1152]{1,0:T(8,128)(2,1)S(1)}, u32[]{:S(2)}, u32[]{:S(2)}) collective-permute-start(bf16[216,1152]{1,0:T(8,128)(2,1)S(1)} %dynamic-slice_bitcast_fusion), channel_id=1, source_target_pairs={{0,16},{8,24},{16,0},{24,8},{1,17},{9,25},{17,1},{25,9},{2,18},{10... | collective-permute-start | bytes 1493000 | tf_op jit(solution)/shard_map/ppermute | solution.py:233
  13.0 22.0 %collective-permute-start.9 = (bf16[216,1152]{1,0:T(8,128)(2,1)S(1)}, bf16[216,1152]{1,0:T(8,128)(2,1)}, u32[]{:S(2)}, u32[]{:S(2)}) collective-permute-start(bf16[216,1152]{1,0:T(8,128)(2,1)S(1)} %dynamic-slice_bitcast_fusion), channel_id=1, source_target_pairs={{0,24},{8,16},{16,8},{24,0},{1,25},{9,17},{17,9},{25,1},{2,26},{10... | collective-permute-start | bytes 1493000 | tf_op jit(solution)/shard_map/ppermute | solution.py:233
  23.6 56.3 %collective-permute-start.10 = (bf16[216,1152]{1,0:T(8,128)(2,1)S(1)}, bf16[216,1152]{1,0:T(8,128)(2,1)}, u32[]{:S(2)}, u32[]{:S(2)}) collective-permute-start(bf16[216,1152]{1,0:T(8,128)(2,1)S(1)} %collective-permute-done.7.refs_9_.refs_1_), channel_id=1, source_target_pairs={{0,1},{1,0},{2,3},{3,2},{4,5},{5,4},{6,7},{7,6},{8,9},{9,8},{10,11... | collective-permute-start | bytes 1493000 | tf_op jit(solution)/shard_map/ppermute | solution.py:233
  34.9 45.0 %collective-permute-start.11 = (bf16[216,1152]{1,0:T(8,128)(2,1)S(1)}, bf16[216,1152]{1,0:T(8,128)(2,1)}, u32[]{:S(2)}, u32[]{:S(2)}) collective-permute-start(bf16[216,1152]{1,0:T(8,128)(2,1)S(1)} %collective-permute-done.8.refs_10_.refs_2_), channel_id=1, source_target_pairs={{0,1},{1,0},{2,3},{3,2},{4,5},{5,4},{6,7},{7,6},{8,9},{9,8},{10,11... | collective-permute-start | bytes 1493000 | tf_op jit(solution)/shard_map/ppermute | solution.py:233
  34.9 45.0 %collective-permute-start.12 = (bf16[216,1152]{1,0:T(8,128)(2,1)}, bf16[216,1152]{1,0:T(8,128)(2,1)}, u32[]{:S(2)}, u32[]{:S(2)}) collective-permute-start(bf16[216,1152]{1,0:T(8,128)(2,1)} %collective-permute-done.9.refs_11_.refs_3_), channel_id=1, source_target_pairs={{0,1},{1,0},{2,3},{3,2},{4,5},{5,4},{6,7},{7,6},{8,9},{9,8},{10,11... | collective-permute-start | bytes 1493000 | tf_op jit(solution)/shard_map/ppermute | solution.py:233
  43.0 11.9 %collective-permute-start = (bf16[16,2304]{1,0:T(8,128)(2,1)}, bf16[16,2304]{1,0:T(8,128)(2,1)}, u32[]{:S(2)}, u32[]{:S(2)}) collective-permute-start(bf16[16,2304]{1,0:T(8,128)(2,1)} %get-tuple-element.46), channel_id=1, source_target_pairs={{0,1},{1,0},{2,3},{3,2},{4,5},{5,4},{6,7},{7,6},{8,9},{9,8},{10,11... | collective-permute-start | bytes 221192 | tf_op jit(solution)/shard_map/ppermute | solution.py:233
  47.9 32.0 %all-to-all-start = ((bf16[8,16,576]{2,1,0:T(8,128)(2,1)}), bf16[8,16,576]{2,1,0:T(8,128)(2,1)S(1)}, u32[]{:S(2)}, u32[]{:S(2)}) async-start(bf16[8,16,576]{2,1,0:T(8,128)(2,1)} %copy-done.13), calls=%async_computation | async-start | bytes 327680 | tf_op jit(solution)/shard_map/all_to_all | solution.py:292
  52.9 82.3 %reduce-scatter.17.cloned.1.call-start = ((), (), s32[]{:S(2)}) async-start(), calls=%async_computation.7 | async-start | bytes 1492992
  52.9 7.9 %collective-permute-start.1 = (bf16[16,2304]{1,0:T(8,128)(2,1)}, bf16[16,2304]{1,0:T(8,128)(2,1)S(1)}, u32[]{:S(2)}, u32[]{:S(2)}) collective-permute-start(bf16[16,2304]{1,0:T(8,128)(2,1)} %copy-done.35), channel_id=1, source_target_pairs={{0,2},{1,3},{2,0},{3,1},{4,6},{5,7},{6,4},{7,5},{8,10},{9,11},{10,... | collective-permute-start | bytes 221192 | tf_op jit(solution)/shard_map/ppermute | solution.py:233
  54.9 8.9 %collective-permute-start.2 = (bf16[16,2304]{1,0:T(8,128)(2,1)}, bf16[16,2304]{1,0:T(8,128)(2,1)S(1)}, u32[]{:S(2)}, u32[]{:S(2)}) collective-permute-start(bf16[16,2304]{1,0:T(8,128)(2,1)} %copy-done.34), channel_id=1, source_target_pairs={{0,3},{1,2},{2,1},{3,0},{4,7},{5,6},{6,5},{7,4},{8,11},{9,10},{10,... | collective-permute-start | bytes 221192 | tf_op jit(solution)/shard_map/ppermute | solution.py:233
  61.4 5.8 %collective-permute-start.3 = (bf16[16,2304]{1,0:T(8,128)(2,1)}, bf16[16,2304]{1,0:T(8,128)(2,1)S(1)}, u32[]{:S(2)}, u32[]{:S(2)}) collective-permute-start(bf16[16,2304]{1,0:T(8,128)(2,1)} %copy-done.33), channel_id=1, source_target_pairs={{0,4},{1,5},{2,6},{3,7},{4,0},{5,1},{6,2},{7,3},{8,12},{9,13},{10,... | collective-permute-start | bytes 221192 | tf_op jit(solution)/shard_map/ppermute | solution.py:233
  64.4 8.4 %collective-permute-start.4 = (bf16[16,2304]{1,0:T(8,128)(2,1)}, bf16[16,2304]{1,0:T(8,128)(2,1)S(1)}, u32[]{:S(2)}, u32[]{:S(2)}) collective-permute-start(bf16[16,2304]{1,0:T(8,128)(2,1)} %copy-done.32), channel_id=1, source_target_pairs={{0,5},{1,4},{2,7},{3,6},{4,1},{5,0},{6,3},{7,2},{8,13},{9,12},{10,... | collective-permute-start | bytes 221192 | tf_op jit(solution)/shard_map/ppermute | solution.py:233
  67.8 8.0 %collective-permute-start.5 = (bf16[16,2304]{1,0:T(8,128)(2,1)}, bf16[16,2304]{1,0:T(8,128)(2,1)S(1)}, u32[]{:S(2)}, u32[]{:S(2)}) collective-permute-start(bf16[16,2304]{1,0:T(8,128)(2,1)} %copy-done.31), channel_id=1, source_target_pairs={{0,6},{1,7},{2,4},{3,5},{4,2},{5,3},{6,0},{7,1},{8,14},{9,15},{10,... | collective-permute-start | bytes 221192 | tf_op jit(solution)/shard_map/ppermute | solution.py:233
  73.5 5.8 %collective-permute-start.6 = (bf16[16,2304]{1,0:T(8,128)(2,1)}, bf16[16,2304]{1,0:T(8,128)(2,1)S(1)}, u32[]{:S(2)}, u32[]{:S(2)}) collective-permute-start(bf16[16,2304]{1,0:T(8,128)(2,1)} %copy-done.30), channel_id=1, source_target_pairs={{0,7},{1,6},{2,5},{3,4},{4,3},{5,2},{6,1},{7,0},{8,15},{9,14},{10,... | collective-permute-start | bytes 221192 | tf_op jit(solution)/shard_map/ppermute | solution.py:233
  102.9 66.9 %reduce-scatter.19.cloned.1.call-start = ((), (), s32[]{:S(2)}) async-start(), calls=%async_computation.8 | async-start | bytes 1492992
  103.7 91.5 %reduce-scatter.13.cloned.1.call-start = ((), (), s32[]{:S(2)}) async-start(), calls=%async_computation.5 | async-start | bytes 368640
  137.0 84.8 %reduce-scatter.15.cloned.1.call-start = ((), (), s32[]{:S(2)}) async-start(), calls=%async_computation.6 | async-start | bytes 368640
  171.7 2.4 %collective-permute-start.13 = (bf16[16,576]{1,0:T(8,128)(2,1)}, bf16[16,576]{1,0:T(8,128)(2,1)S(1)}, u32[]{:S(2)}, u32[]{:S(2)}) collective-permute-start(bf16[16,576]{1,0:T(8,128)(2,1)} %copy-done.53), channel_id=1, source_target_pairs={{0,1},{1,0},{2,3},{3,2},{4,5},{5,4},{6,7},{7,6},{8,9},{9,8},{10,11... | collective-permute-start | bytes 55304 | tf_op jit(solution)/shard_map/ppermute | solution.py:233
  171.8 4.1 %collective-permute-start.14 = (bf16[16,576]{1,0:T(8,128)(2,1)}, bf16[16,576]{1,0:T(8,128)(2,1)S(1)}, u32[]{:S(2)}, u32[]{:S(2)}) collective-permute-start(bf16[16,576]{1,0:T(8,128)(2,1)} %copy-done.52), channel_id=1, source_target_pairs={{0,2},{1,3},{2,0},{3,1},{4,6},{5,7},{6,4},{7,5},{8,10},{9,11},{10,... | collective-permute-start | bytes 55304 | tf_op jit(solution)/shard_map/ppermute | solution.py:233
  171.9 4.9 %collective-permute-start.15 = (bf16[16,576]{1,0:T(8,128)(2,1)S(1)}, bf16[16,576]{1,0:T(8,128)(2,1)S(1)}, u32[]{:S(2)}, u32[]{:S(2)}) collective-permute-start(bf16[16,576]{1,0:T(8,128)(2,1)S(1)} %copy-done.51), channel_id=1, source_target_pairs={{0,3},{1,2},{2,1},{3,0},{4,7},{5,6},{6,5},{7,4},{8,11},{9,10},{10,... | collective-permute-start | bytes 55304 | tf_op jit(solution)/shard_map/ppermute | solution.py:233
  173.6 4.7 %collective-permute-start.16 = (bf16[16,576]{1,0:T(8,128)(2,1)S(1)}, bf16[16,576]{1,0:T(8,128)(2,1)S(1)}, u32[]{:S(2)}, u32[]{:S(2)}) collective-permute-start(bf16[16,576]{1,0:T(8,128)(2,1)S(1)} %copy-done.49), channel_id=1, source_target_pairs={{0,4},{1,5},{2,6},{3,7},{4,0},{5,1},{6,2},{7,3},{8,12},{9,13},{10,... | collective-permute-start | bytes 55304 | tf_op jit(solution)/shard_map/ppermute | solution.py:233
  173.6 10.2 %collective-permute-start.20 = (bf16[16,1152]{1,0:T(8,128)(2,1)S(1)}, bf16[16,1152]{1,0:T(8,128)(2,1)S(1)}, u32[]{:S(2)}, u32[]{:S(2)}) collective-permute-start(bf16[16,1152]{1,0:T(8,128)(2,1)S(1)} %copy-done.41), channel_id=1, source_target_pairs={{0,1},{1,0},{2,3},{3,2},{4,5},{5,4},{6,7},{7,6},{8,9},{9,8},{10,11... | collective-permute-start | bytes 110600 | tf_op jit(solution)/shard_map/ppermute | solution.py:233
  174.1 11.7 %collective-permute-start.21 = (bf16[16,1152]{1,0:T(8,128)(2,1)S(1)}, bf16[16,1152]{1,0:T(8,128)(2,1)S(1)}, u32[]{:S(2)}, u32[]{:S(2)}) collective-permute-start(bf16[16,1152]{1,0:T(8,128)(2,1)S(1)} %copy-done.39), channel_id=1, source_target_pairs={{0,2},{1,3},{2,0},{3,1},{4,6},{5,7},{6,4},{7,5},{8,10},{9,11},{10,... | collective-permute-start | bytes 110600 | tf_op jit(solution)/shard_map/ppermute | solution.py:233
  175.8 4.4 %collective-permute-start.17 = (bf16[16,576]{1,0:T(8,128)(2,1)S(1)}, bf16[16,576]{1,0:T(8,128)(2,1)S(1)}, u32[]{:S(2)}, u32[]{:S(2)}) collective-permute-start(bf16[16,576]{1,0:T(8,128)(2,1)S(1)} %copy-done.47), channel_id=1, source_target_pairs={{0,5},{1,4},{2,7},{3,6},{4,1},{5,0},{6,3},{7,2},{8,13},{9,12},{10,... | collective-permute-start | bytes 55304 | tf_op jit(solution)/shard_map/ppermute | solution.py:233
  176.8 5.6 %collective-permute-start.18 = (bf16[16,576]{1,0:T(8,128)(2,1)S(1)}, bf16[16,576]{1,0:T(8,128)(2,1)S(1)}, u32[]{:S(2)}, u32[]{:S(2)}) collective-permute-start(bf16[16,576]{1,0:T(8,128)(2,1)S(1)} %copy-done.45), channel_id=1, source_target_pairs={{0,6},{1,7},{2,4},{3,5},{4,2},{5,3},{6,0},{7,1},{8,14},{9,15},{10,... | collective-permute-start | bytes 55304 | tf_op jit(solution)/shard_map/ppermute | solution.py:233
  178.3 5.1 %collective-permute-start.19 = (bf16[16,576]{1,0:T(8,128)(2,1)S(1)}, bf16[16,576]{1,0:T(8,128)(2,1)S(1)}, u32[]{:S(2)}, u32[]{:S(2)}) collective-permute-start(bf16[16,576]{1,0:T(8,128)(2,1)S(1)} %copy-done.43), channel_id=1, source_target_pairs={{0,7},{1,6},{2,5},{3,4},{4,3},{5,2},{6,1},{7,0},{8,15},{9,14},{10,... | collective-permute-start | bytes 55304 | tf_op jit(solution)/shard_map/ppermute | solution.py:233
  180.2 10.3 %collective-permute-start.22 = (bf16[16,1152]{1,0:T(8,128)(2,1)S(1)}, bf16[16,1152]{1,0:T(8,128)(2,1)S(1)}, u32[]{:S(2)}, u32[]{:S(2)}) collective-permute-start(bf16[16,1152]{1,0:T(8,128)(2,1)S(1)} %copy-done.37), channel_id=1, source_target_pairs={{0,3},{1,2},{2,1},{3,0},{4,7},{5,6},{6,5},{7,4},{8,11},{9,10},{10,... | collective-permute-start | bytes 110600 | tf_op jit(solution)/shard_map/ppermute | solution.py:233
  182.4 8.2 %collective-permute-start.23 = (bf16[16,1152]{1,0:T(8,128)(2,1)S(1)}, bf16[16,1152]{1,0:T(8,128)(2,1)S(1)}, u32[]{:S(2)}, u32[]{:S(2)}) collective-permute-start(bf16[16,1152]{1,0:T(8,128)(2,1)S(1)} %get-tuple-element.73), channel_id=1, source_target_pairs={{0,4},{1,5},{2,6},{3,7},{4,0},{5,1},{6,2},{7,3},{8,12},{9,13},{10,... | collective-permute-start | bytes 110600 | tf_op jit(solution)/shard_map/ppermute | solution.py:233
  183.4 7.1 %collective-permute-start.24 = (bf16[16,1152]{1,0:T(8,128)(2,1)S(1)}, bf16[16,1152]{1,0:T(8,128)(2,1)S(1)}, u32[]{:S(2)}, u32[]{:S(2)}) collective-permute-start(bf16[16,1152]{1,0:T(8,128)(2,1)S(1)} %get-tuple-element.74), channel_id=1, source_target_pairs={{0,5},{1,4},{2,7},{3,6},{4,1},{5,0},{6,3},{7,2},{8,13},{9,12},{10,... | collective-permute-start | bytes 110600 | tf_op jit(solution)/shard_map/ppermute | solution.py:233
  183.9 6.7 %collective-permute-start.25 = (bf16[16,1152]{1,0:T(8,128)(2,1)S(1)}, bf16[16,1152]{1,0:T(8,128)(2,1)S(1)}, u32[]{:S(2)}, u32[]{:S(2)}) collective-permute-start(bf16[16,1152]{1,0:T(8,128)(2,1)S(1)} %get-tuple-element.75), channel_id=1, source_target_pairs={{0,6},{1,7},{2,4},{3,5},{4,2},{5,3},{6,0},{7,1},{8,14},{9,15},{10,... | collective-permute-start | bytes 110600 | tf_op jit(solution)/shard_map/ppermute | solution.py:233
  185.7 5.2 %collective-permute-start.26 = (bf16[16,1152]{1,0:T(8,128)(2,1)S(1)}, bf16[16,1152]{1,0:T(8,128)(2,1)S(1)}, u32[]{:S(2)}, u32[]{:S(2)}) collective-permute-start(bf16[16,1152]{1,0:T(8,128)(2,1)S(1)} %get-tuple-element.76), channel_id=1, source_target_pairs={{0,7},{1,6},{2,5},{3,4},{4,3},{5,2},{6,1},{7,0},{8,15},{9,14},{10,... | collective-permute-start | bytes 110600 | tf_op jit(solution)/shard_map/ppermute | solution.py:233
  (54 other events, 1050.8 us)
Sparse Core Ops, SparseCore 0:
  103.0 32.1 reduce-scatter.16
  137.6 32.1 reduce-scatter.18
  172.6 22.3 reduce-scatter.12
  197.6 24.1 reduce-scatter.14

commit v2 on v1

v2 whole, which is shorter than its diff:
```python
import functools
import math

import jax
import jax.numpy as jnp
from jax import lax
from jax.experimental import pallas as pl
from jax.experimental.pallas import tpu as pltpu
from jax.sharding import PartitionSpec as P

DH = 72
FRAMES = 16
LANES = 128
BF16 = jnp.bfloat16
F32 = jnp.float32
VMEM = pl.BlockSpec(memory_space=pltpu.VMEM)
SMEM = pl.BlockSpec(memory_space=pltpu.SMEM)
LIMIT = 40 * 1024 * 1024


def dot(left, right):
    return jnp.dot(left, right, preferred_element_type=F32)


def dot_bt(left, right):
    return lax.dot_general(left, right, (((1,), (1,)), ((), ())), preferred_element_type=F32)


def dot_at(left, right):
    return lax.dot_general(left, right, (((0,), (0,)), ((), ())), preferred_element_type=F32)


def call(body, outs, args, scratch=(), us=1):
    moved = sum(math.prod(a.shape) * a.dtype.itemsize for a in (*args, *outs))
    return pl.pallas_call(
        body,
        out_shape=outs,
        in_specs=[SMEM if a.dtype == jnp.int32 else VMEM for a in args],
        out_specs=[VMEM] * len(outs),
        scratch_shapes=list(scratch),
        compiler_params=pltpu.CompilerParams(vmem_limit_bytes=LIMIT),
        cost_estimate=pl.CostEstimate(flops=us * 1150000000, bytes_accessed=moved, transcendentals=0),
    )(*args)


def shape(dims, dtype=BF16):
    return jax.ShapeDtypeStruct(dims, dtype)


def window(head):
    low = head * DH // LANES * LANES
    high = -(-(head + 1) * DH // LANES) * LANES
    return low, high


def head_only(block, head):
    low, high = window(head)
    lane = lax.broadcasted_iota(jnp.int32, (1, high - low), 1) + low
    keep = (lane >= head * DH) & (lane < (head + 1) * DH)
    return jnp.where(keep, block, jnp.zeros_like(block))


def add_tiles(tiles, head, value):
    low, high = window(head)
    for at in range(low // LANES, high // LANES):
        part = value[:, at * LANES - low : (at + 1) * LANES - low]
        tiles[at] = part if tiles[at] is None else tiles[at] + part


def joined(tiles):
    return jnp.concatenate([tile.astype(BF16) for tile in tiles], axis=1)


def same_group(rows, kind):
    row = lax.broadcasted_iota(jnp.int32, (rows, rows), 0)
    col = lax.broadcasted_iota(jnp.int32, (rows, rows), 1)
    how, size = kind
    return row // size == col // size if how == "block" else row % size == col % size


def softmax_forward(q_ref, k_ref, v_ref, p_ref, heads, kind):
    rows = q_ref.shape[0]
    mask = same_group(rows, kind)
    tiles = [None] * (q_ref.shape[1] // LANES)
    for head in range(heads):
        low, high = window(head)
        s = dot_bt(q_ref[:, low:high], head_only(k_ref[:, low:high], head)) * (1.0 / math.sqrt(DH))
        s = jnp.where(mask, s, -jnp.inf)
        e = jnp.exp(s - jnp.max(s, axis=1, keepdims=True))
        p = e / jnp.sum(e, axis=1, keepdims=True)
        p_ref[head] = p
        add_tiles(tiles, head, dot(p.astype(BF16), head_only(v_ref[:, low:high], head)))
    return joined(tiles)


def softmax_backward(q_ref, k_ref, v_ref, g_ref, p_ref, heads):
    count = q_ref.shape[1] // LANES
    dq, dk, dv = [None] * count, [None] * count, [None] * count
    for head in range(heads):
        low, high = window(head)
        p = p_ref[head]
        g = head_only(g_ref[:, low:high], head)
        add_tiles(dv, head, dot_at(p.astype(BF16), g))
        dp = dot_bt(g, v_ref[:, low:high])
        ds = p * (dp - jnp.sum(p * dp, axis=1, keepdims=True)) * (1.0 / math.sqrt(DH))
        ds = ds.astype(BF16)
        add_tiles(dq, head, dot(ds, head_only(k_ref[:, low:high], head)))
        add_tiles(dk, head, dot_at(ds, head_only(q_ref[:, low:high], head)))
    return joined(dq), joined(dk), joined(dv)


def put(ref, value):
    width = value.shape[1]
    ref[:, width // LANES * LANES :] = jnp.zeros(
        (ref.shape[0], ref.shape[1] - width // LANES * LANES), ref.dtype
    )
    ref[:, :width] = value


def emit_part(idx, left, right, outs, cols=None, full=None):
    if len(outs) == 1:
        outs[0][...] = dot_at(left, right).astype(BF16)
        return
    count, rows, width = outs[0].shape
    size = width // count
    for r in range(count):
        cols[r] = right[:, r * size : (r + 1) * size]
    for r in range(count):
        full[...] = dot_at(left, cols[idx[0] ^ r])
        for e, out in enumerate(outs):
            blocks = []
            for q in range(count):
                low = pl.multiple_of((idx[2] ^ (2 * q + e)) * rows, rows)
                blocks.append(full[pl.ds(low, rows)])
            out[r] = jnp.concatenate(blocks, axis=1).astype(BF16)


def spatial_kernel(peers, patches, tok, cot, qkv, wos, packed, hid, p_ref, qs, ks, vs):
    rows, width = tok.shape
    inner = wos.shape[0]
    x = qkv[...]
    put(qs, x[:, :inner])
    put(ks, x[:, inner : 2 * inner])
    put(vs, x[:, 2 * inner :])
    o = softmax_forward(qs, ks, vs, p_ref, inner // DH, ("block", patches))[:, :inner]
    hidden = (tok[...].astype(F32) + dot(o, wos[...])).astype(BF16)
    hid[...] = hidden
    each = patches // peers
    low = 0
    for value in (hidden, cot[...], o):
        value = value.astype(F32)
        for at in range(peers):
            cut = [
                value[f * patches + at * each : f * patches + (at + 1) * each]
                for f in range(rows // patches)
            ]
            packed[at, :, low : low + value.shape[1]] = jnp.concatenate(cut, axis=0).astype(BF16)
        low += value.shape[1]


def temporal_forward_kernel(shards, group, parts, idx, packed, wot, *refs):
    weights, refs = refs[: len(shards)], refs[len(shards) :]
    q, k, v, g, p_ref, spat, cot, out = refs[:8]
    part = refs[8 : 8 + parts]
    blocks, hid, *work = refs[8 + parts :]
    inner, width = wot.shape
    chunk = packed.shape[1]
    for at in range(packed.shape[0]):
        rows = slice(at * chunk, (at + 1) * chunk)
        hid[rows] = packed[at, :, :width]
        cot[rows] = packed[at, :, width : 2 * width]
        spat[rows] = packed[at, :, 2 * width :]
    hidden = hid[...]
    for (place, count), w in zip(shards, weights):
        block = dot_bt(hidden, w[...]).astype(BF16)
        size = block.shape[1] // count
        for i in range(count):
            blocks[place(idx) + i] = block[:, i * size : (i + 1) * size]
    whole = jnp.concatenate([blocks[i] for i in range(blocks.shape[0])], axis=1)
    put(q, whole[:, :inner])
    put(k, whole[:, inner : 2 * inner])
    put(v, whole[:, 2 * inner :])
    o = softmax_forward(q, k, v, p_ref, inner // DH, ("cycle", group))[:, :inner]
    out[...] = o
    emit_part(idx, o, cot[...], part, *work)
    put(g, dot_bt(cot[...], wot[...]).astype(BF16))


def temporal_backward_kernel(shards, parts, idx, q, k, v, g, p_ref, spat, cot, out, *refs):
    weights, refs = refs[: len(shards)], refs[len(shards) :]
    packed = refs[0]
    part = refs[1 : 1 + parts]
    blocks, *work = refs[1 + parts :]
    inner = spat.shape[1]
    width = cot.shape[1]
    dq, dk, dv = softmax_backward(q, k, v, g, p_ref, inner // DH)
    whole = jnp.concatenate([dq[:, :inner], dk[:, :inner], dv[:, :inner]], axis=1)
    size = blocks.shape[2]
    for i in range(blocks.shape[0]):
        blocks[i] = whole[:, i * size : (i + 1) * size]
    total = jnp.zeros(cot.shape, F32)
    for (place, count), w in zip(shards, weights):
        lhs = jnp.concatenate([blocks[place(idx) + i] for i in range(count)], axis=1)
        total += dot(lhs, w[...])
    grad = (cot[...].astype(F32) + total.astype(BF16).astype(F32)).astype(BF16)
    chunk = packed.shape[1]
    for at in range(packed.shape[0]):
        rows = slice(at * chunk, (at + 1) * chunk)
        packed[at, :, :width] = grad[rows]
        packed[at, :, width:] = out[rows]
    emit_part(idx, spat[...], grad, part, *work)


def last_kernel(patches, qkv, p_ref, hid, wos, wot, packed, block_out, out, grads, qs, ks, vs, gs):
    inner, width = wos.shape
    peers, chunk, _ = packed.shape
    each = patches // peers
    rows = [packed[at].astype(F32) for at in range(peers)]
    rows = [rows[at][f * each : (f + 1) * each] for f in range(chunk // each) for at in range(peers)]
    rows = jnp.concatenate(rows, axis=0).astype(BF16)
    grad, attended = rows[:, :width], rows[:, width:]
    out[...] = grad
    put(gs, dot_bt(grad, wos[...]).astype(BF16))
    x = qkv[...]
    put(qs, x[:, :inner])
    put(ks, x[:, inner : 2 * inner])
    put(vs, x[:, 2 * inner :])
    dq, dk, dv = softmax_backward(qs, ks, vs, gs, p_ref, inner // DH)
    grads[...] = jnp.concatenate([dq[:, :inner], dk[:, :inner], dv[:, :inner]], axis=1)
    block_out[...] = (hid[...].astype(F32) + dot(attended, wot[...])).astype(BF16)


def sum_cores_kernel(keep, got, own, *outs):
    for r in range(keep.shape[0]):
        total = keep[r].astype(F32) + got[r].astype(F32)
        if r == 0:
            own[...] = total
        else:
            outs[r - 1][...] = total.astype(BF16)


def sum_dp_kernel(own, *refs):
    got, outs = refs[: len(refs) // 2], refs[len(refs) // 2 :]
    total = own[...]
    for part in got:
        total += part[...].astype(F32)
    size = total.shape[1] // len(outs)
    for q, out in enumerate(outs):
        out[...] = total[:, q * size : (q + 1) * size].astype(out.dtype)


def sum_kernel(own, *refs):
    total = own[...]
    for part in refs[:-1]:
        total += part[...].astype(F32)
    refs[-1][...] = total


def flip(value, axis, bit):
    return lax.ppermute(value, axis, [(i, i ^ bit) for i in range(lax.axis_size(axis))])


def gather_weight(weight, core):
    n = lax.axis_size("dp")
    if n != 4:
        return [lax.all_gather(weight, "dp", axis=0, tiled=True)], [(lambda idx: 0, 1)], 1
    half = weight.shape[0] // 2
    mine = lax.dynamic_slice_in_dim(weight, core * half, half, 0)
    near = [flip(mine, "dp", j) for j in range(1, n)]
    far = [flip(w, "seq", 1) for w in near]
    shards = [(lambda idx: 2 * idx[0], 2)]
    shards += [(lambda idx, j=j: 2 * (idx[0] ^ j) + idx[1], 1) for j in range(1, n)]
    shards += [(lambda idx, j=j: 2 * (idx[0] ^ j) + 1 - idx[1], 1) for j in range(1, n)]
    return [weight, *near, *far], shards, 2 * n


def reduced(part):
    if len(part) == 1:
        over_seq = lax.psum_scatter(part[0], "seq", scatter_dimension=0, tiled=True)
        return lax.psum_scatter(over_seq, "dp", scatter_dimension=1, tiled=True).astype(F32)
    keep, send = part
    count, rows, width = keep.shape
    own, *sends = call(
        sum_cores_kernel,
        [shape((rows, width), F32)] + [shape((rows, width))] * (count - 1),
        [keep, flip(send, "seq", 1)],
    )
    got = [flip(value, "dp", r + 1) for r, value in enumerate(sends)]
    block = (rows, width // count)
    own, *sends = call(
        sum_dp_kernel, [shape(block, F32)] + [shape(block)] * (count - 1), [own, *got]
    )
    got = [flip(value, "seq", 2 * (q + 1)) for q, value in enumerate(sends)]
    return call(sum_kernel, [shape(block, F32)], [own, *got])[0]


def shards(tokens, spatial_qkv, wo_spatial, w_temporal, wo_temporal, cotangent):
    frames, patches, width = tokens.shape
    inner = wo_spatial.shape[0]
    heads = inner // DH
    padded = -(-inner // LANES) * LANES
    rows = frames * patches
    peers = FRAMES // frames
    each = patches // peers
    chunk = rows // peers
    n_seq = lax.axis_size("seq")
    n_dp = lax.axis_size("dp")
    seq = lax.axis_index("seq")
    idx = jnp.stack([lax.axis_index("dp"), seq % 2, seq]).astype(jnp.int32)
    wide = pltpu.VMEM((rows, padded), BF16)

    weights, places, count = gather_weight(w_temporal.T, seq % 2)
    blocks = pltpu.VMEM((count, rows, 3 * inner // count), BF16)
    part, work = [shape((inner, width))], []
    if n_dp == 4 and n_seq == 8:
        part = [shape((n_dp, inner // n_seq, width))] * 2
        work = [
            pltpu.VMEM((n_dp, rows, width // n_dp), BF16),
            pltpu.VMEM((inner, width // n_dp), F32),
        ]
    groups = None
    if n_seq > peers:
        groups = [list(range(i, i + peers)) for i in range(0, n_seq, peers)]

    def exchange(value):
        return lax.all_to_all(
            value, "seq", split_axis=0, concat_axis=0, tiled=True, axis_index_groups=groups
        )

    qkv_rows = spatial_qkv.reshape(rows, 3 * inner)
    packed, hidden, spatial_p = call(
        functools.partial(spatial_kernel, peers, patches),
        [
            shape((peers, chunk, 2 * width + inner)),
            shape((rows, width)),
            shape((heads, rows, rows), F32),
        ],
        [tokens.reshape(rows, width), cotangent.reshape(rows, width), qkv_rows, wo_spatial],
        [wide] * 3,
        us=3,
    )
    packed = exchange(packed)

    q, k, v, g, temporal_p, spat, cot, out, *temporal_part = call(
        functools.partial(temporal_forward_kernel, places, each, len(part)),
        [shape((rows, padded))] * 4
        + [shape((heads, rows, rows), F32), shape((rows, inner)), shape((rows, width))]
        + [shape((rows, inner)), *part],
        [idx, packed, wo_temporal, *weights],
        [blocks, pltpu.VMEM((rows, width), BF16), *work],
        us=7,
    )
    back, *spatial_part = call(
        functools.partial(temporal_backward_kernel, places, len(part)),
        [shape((peers, chunk, width + inner)), *part],
        [idx, q, k, v, g, temporal_p, spat, cot, out, *weights],
        [blocks, *work],
        us=7,
    )
    back = exchange(back)
    block_out, tokens_grad, qkv_grad = call(
        functools.partial(last_kernel, patches),
        [shape((rows, width)), shape((rows, width)), shape((rows, 3 * inner))],
        [qkv_rows, spatial_p, hidden, wo_spatial, wo_temporal, back],
        [wide] * 4,
        us=7,
    )
    return (
        block_out.reshape(frames, patches, width),
        tokens_grad.reshape(frames, patches, width),
        qkv_grad.reshape(frames, patches, 3 * inner),
        reduced(spatial_part),
        reduced(temporal_part),
    )


def solution(mesh):
    placed = (
        P(("dp", "seq"), None, None),
        P(("dp", "seq"), None, None),
        P(),
        P(None, "dp"),
        P(),
        P(("dp", "seq"), None, None),
    )
    return jax.shard_map(
        shards,
        mesh=mesh,
        in_specs=placed,
        out_specs=(
            P(("dp", "seq"), None, None),
            P(("dp", "seq"), None, None),
            P(("dp", "seq"), None, None),
            P("seq", "dp"),
            P("seq", "dp"),
        ),
        check_vma=False,
    )
```

time: 231 us -> 104 us (0.45)
  waiting for transfers between devices: 129 us -> 29.6 us
  local copies, waits for them, and re-layouts: 31.6 us -> 13.1 us
  between operations: 14.2 us -> 0.74 us
  Pallas kernels: 20.4 us -> 27.8 us
    unnamed x8 -> x0, waiting for transfers between devices: 89.6 us -> none
    unnamed x112 -> x46, local copies, waits for them, and re-layouts: 30.4 us -> 13 us
    ppermute x27 -> x20, waiting for transfers between devices: 39.6 us -> 28.4 us  [flip(): lax.ppermute(value, axis, [(i, i ^ bit) for i in range(lax.axis_size(axis...]
    pallas_call x6 -> x10, Pallas kernels: 20.4 us -> 27.8 us  [call(): pl.pallas_call(body, out_shape=outs, in_specs=[SMEM if a.dtype == jnp.int...]
    ppermute x27 -> x20, starting transfers between devices: 27.8 us -> 20.6 us  [flip(): lax.ppermute(value, axis, [(i, i ^ bit) for i in range(lax.axis_size(axis...]
    all_to_all x1 -> x2, starting transfers between devices: 4.99 us -> 11.2 us  [exchange(): lax.all_to_all(value, 'seq', split_axis=0, concat_axis=0, tiled=True, axi...]
  transfers between devices with their start and end apart: 32 -> 22, of which waited for: 14 -> 7; matrix products, arithmetic and copies ran while one was open for 2% -> 0% of each run, Pallas kernels for 4% -> 16%
where the time goes in v2:
time: 104 us; the launch traced here: 103 us
  starting transfers between devices  31.8 us (31%)
  waiting for transfers between devices  29.6 us (28%)
  Pallas kernels  27.8 us (27%)
  local copies, waits for them, and re-layouts  13.1 us (13%)
    ppermute x20, waiting for transfers between devices, flip(): lax.ppermute(value, axis, [(i, i ^ bit) for i in range(lax.axis_size(axis...  28.4 us
    pallas_call x10, Pallas kernels, call(): pl.pallas_call(body, out_shape=outs, in_specs=[SMEM if a.dtype == jnp.int...  27.8 us
    ppermute x20, starting transfers between devices, flip(): lax.ppermute(value, axis, [(i, i ^ bit) for i in range(lax.axis_size(axis...  20.6 us
    unnamed x46, local copies, waits for them, and re-layouts  13 us
    all_to_all x2, starting transfers between devices, exchange(): lax.all_to_all(value, 'seq', split_axis=0, concat_axis=0, tiled=True, axi...  11.2 us
  transfers between devices with their start and end apart: 22, of which 7 were waited for; matrix products, arithmetic and copies ran while one was open for 0% of the time, Pallas kernels for 16%

profile of v2, /device:TPU:0, one launch (start us, length us, event | category | flops | bytes accessed | tf_op | source)
XLA Modules:
  0.0 103.0 jit_solution(6022583952975350637)
XLA Ops:
  0.6 1.3 %copy-done.1 = bf16[576,1152]{1,0:T(8,128)(2,1)S(1)} copy-done((bf16[576,1152]{1,0:T(8,128)(2,1)S(1)}, bf16[576,1152]{1,0:T(8,128)(2,1)}, u32[]{:S(2)}) %copy-start.1) | copy-done | bytes 1327128
  2.0 1.0 copy-done.5
  3.0 1.0 copy-done.7
  3.9 1.0 copy-done.8
  4.9 2.9 %shard_map.101 = (bf16[8,16,2880]{2,1,0:T(8,128)(2,1)}, bf16[128,1152]{1,0:T(8,128)(2,1)S(1)}, f32[8,128,128]{2,1,0:T(8,128)S(1)}) custom-call(bf16[128,1152]{1,0:T(8,128)(2,1)S(1)} %bitcast.16, bf16[128,1152]{1,0:T(8,128)(2,1)S(1)} %bitcast.17, bf16[128,1728]{1,0:T(8,128)(2,1)S(1)} %bitcast.14, bf16[576,1152]{1,0:T(8,128)(2,1)S(1)} %copy-done.1), custom_call_target="tpu_custom_call" | custom-call | flops 3449999872 | bytes 3915776 | tf_op jit(solution)/shard_map/pallas_call | solution.py:35
  9.3 6.5 %all-to-all-start = ((bf16[8,16,2880]{2,1,0:T(8,128)(2,1)}), bf16[8,16,2880]{2,1,0:T(8,128)(2,1)S(1)}, u32[]{:S(2)}, u32[]{:S(2)}) async-start(bf16[8,16,2880]{2,1,0:T(8,128)(2,1)} %get-tuple-element.42), calls=%async_computation | async-start | bytes 1507328 | tf_op jit(solution)/shard_map/all_to_all | solution.py:326
  15.9 1.6 %collective-permute-start = (bf16[216,1152]{1,0:T(8,128)(2,1)S(1)}, bf16[216,1152]{1,0:T(8,128)(2,1)}, u32[]{:S(2)}, u32[]{:S(2)}) collective-permute-start(bf16[216,1152]{1,0:T(8,128)(2,1)S(1)} %dynamic-slice_bitcast_fusion), channel_id=1, source_target_pairs={{0,8},{8,0},{16,24},{24,16},{1,9},{9,1},{17,25},{25,17},{2,10},{10... | collective-permute-start | bytes 1493000 | tf_op jit(solution)/shard_map/ppermute | solution.py:260
  17.4 1.5 %collective-permute-start.1 = (bf16[216,1152]{1,0:T(8,128)(2,1)S(1)}, bf16[216,1152]{1,0:T(8,128)(2,1)}, u32[]{:S(2)}, u32[]{:S(2)}) collective-permute-start(bf16[216,1152]{1,0:T(8,128)(2,1)S(1)} %dynamic-slice_bitcast_fusion), channel_id=1, source_target_pairs={{0,16},{8,24},{16,0},{24,8},{1,17},{9,25},{17,1},{25,9},{2,18},{10... | collective-permute-start | bytes 1493000 | tf_op jit(solution)/shard_map/ppermute | solution.py:260
  19.4 10.8 %collective-permute-done.refs_1_ = bf16[216,1152]{1,0:T(8,128)(2,1)} collective-permute-done((bf16[216,1152]{1,0:T(8,128)(2,1)S(1)}, bf16[216,1152]{1,0:T(8,128)(2,1)}, u32[]{:S(2)}, u32[]{:S(2)}) %collective-permute-start) | collective-permute-done | bytes 497696 | tf_op jit(solution)/shard_map/ppermute | solution.py:260
  30.2 11.5 %collective-permute-done.1.refs_2_ = bf16[216,1152]{1,0:T(8,128)(2,1)} collective-permute-done((bf16[216,1152]{1,0:T(8,128)(2,1)S(1)}, bf16[216,1152]{1,0:T(8,128)(2,1)}, u32[]{:S(2)}, u32[]{:S(2)}) %collective-permute-start.1) | collective-permute-done | bytes 497696 | tf_op jit(solution)/shard_map/ppermute | solution.py:260
  42.2 1.6 %collective-permute-done.4.refs_5_ = bf16[216,1152]{1,0:T(8,128)(2,1)} collective-permute-done((bf16[216,1152]{1,0:T(8,128)(2,1)}, bf16[216,1152]{1,0:T(8,128)(2,1)}, u32[]{:S(2)}, u32[]{:S(2)}) %collective-permute-start.4) | collective-permute-done | bytes 497696 | tf_op jit(solution)/shard_map/ppermute | solution.py:260
  44.6 7.5 %shard_map.102 = (bf16[128,640]{1,0:T(8,128)(2,1)S(1)}, bf16[128,640]{1,0:T(8,128)(2,1)S(1)}, bf16[128,640]{1,0:T(8,128)(2,1)S(1)}, bf16[128,640]{1,0:T(8,128)(2...) custom-call(s32[3]{0:T(128)S(1)} %pad_add_fusion.idx, ...), custom_call_target="tpu_custom_call" | custom-call | flops 8049999872 | bytes 9142284 | tf_op jit(solution)/shard_map/pallas_call | solution.py:35
  52.2 7.2 %shard_map.103 = (bf16[8,16,1728]{2,1,0:T(8,128)(2,1)}, bf16[4,72,1152]{2,1,0:T(8,128)(2,1)S(1)}, bf16[4,72,1152]{2,1,0:T(8,128)(2,1)S(1)}) custom-call(s32[3]{0:T(128)S(1)} %pad_add_fusion.idx, bf16[128,640]{1,0:T(8,128)(2,1)S(1)} %get-tuple-element.43.q, bf16[128,640]{1,0:T(8,128)(2,1)S(1)} %get-tuple-element.44.k, ...), custom_call_target="tpu_custom_call" | custom-call | flops 8049999872 | bytes 7520268 | tf_op jit(solution)/shard_map/pallas_call | solution.py:35
  61.1 4.7 %all-to-all-start.1 = ((bf16[8,16,1728]{2,1,0:T(8,128)(2,1)}), bf16[8,16,1728]{2,1,0:T(8,128)(2,1)S(1)}, u32[]{:S(2)}, u32[]{:S(2)}) async-start(bf16[8,16,1728]{2,1,0:T(8,128)(2,1)} %get-tuple-element.51), calls=%async_computation.1 | async-start | bytes 917504 | tf_op jit(solution)/shard_map/all_to_all | solution.py:326
  66.3 1.1 %copy-done.14 = bf16[4,72,1152]{2,1,0:T(8,128)(2,1)S(1)} copy-done((bf16[4,72,1152]{2,1,0:T(8,128)(2,1)S(1)}, bf16[4,72,1152]{2,1,0:T(8,128)(2,1)}, u32[]{:S(2)}) %copy-start.14) | copy-done | bytes 663576
  67.4 1.9 %shard_map.108 = (f32[72,1152]{1,0:T(8,128)S(1)}, bf16[72,1152]{1,0:T(8,128)(2,1)S(1)}, bf16[72,1152]{1,0:T(8,128)(2,1)}, bf16[72,1152]{1,0:T(8,128)(2,1)}) custom-call(bf16[4,72,1152]{2,1,0:T(8,128)(2,1)S(1)} %copy-done.14, bf16[4,72,1152]{2,1,0:T(8,128)(2,1)} %collective-permute-done.13.got), custom_call_target="tpu_custom_call" | custom-call | flops 1150000000 | bytes 2156544 | tf_op jit(solution)/shard_map/pallas_call | solution.py:35
  69.9 1.5 %collective-permute-start.15 = (bf16[72,1152]{1,0:T(8,128)(2,1)}, bf16[72,1152]{1,0:T(8,128)(2,1)}, u32[]{:S(2)}, u32[]{:S(2)}) collective-permute-start(bf16[72,1152]{1,0:T(8,128)(2,1)} %get-tuple-element.69), channel_id=1, source_target_pairs={{0,16},{8,24},{16,0},{24,8},{1,17},{9,25},{17,1},{25,9},{2,18},{10... | collective-permute-start | bytes 497672 | tf_op jit(solution)/shard_map/ppermute | solution.py:260
  71.4 1.4 %collective-permute-start.16 = (bf16[72,1152]{1,0:T(8,128)(2,1)}, bf16[72,1152]{1,0:T(8,128)(2,1)}, u32[]{:S(2)}, u32[]{:S(2)}) collective-permute-start(bf16[72,1152]{1,0:T(8,128)(2,1)} %get-tuple-element.70), channel_id=1, source_target_pairs={{0,24},{8,16},{16,8},{24,0},{1,25},{9,17},{17,9},{25,1},{2,26},{10... | collective-permute-start | bytes 497672 | tf_op jit(solution)/shard_map/ppermute | solution.py:260
  74.9 1.5 %collective-permute-start.8 = (bf16[72,1152]{1,0:T(8,128)(2,1)}, bf16[72,1152]{1,0:T(8,128)(2,1)}, u32[]{:S(2)}, u32[]{:S(2)}) collective-permute-start(bf16[72,1152]{1,0:T(8,128)(2,1)} %get-tuple-element.59), channel_id=1, source_target_pairs={{0,16},{8,24},{16,0},{24,8},{1,17},{9,25},{17,1},{25,9},{2,18},{10... | collective-permute-start | bytes 497672 | tf_op jit(solution)/shard_map/ppermute | solution.py:260
  77.1 1.4 %collective-permute-start.9 = (bf16[72,1152]{1,0:T(8,128)(2,1)S(1)}, bf16[72,1152]{1,0:T(8,128)(2,1)}, u32[]{:S(2)}, u32[]{:S(2)}) collective-permute-start(bf16[72,1152]{1,0:T(8,128)(2,1)S(1)} %get-tuple-element.60), channel_id=1, source_target_pairs={{0,24},{8,16},{16,8},{24,0},{1,25},{9,17},{17,9},{25,1},{2,26},{10... | collective-permute-start | bytes 497672 | tf_op jit(solution)/shard_map/ppermute | solution.py:260
  78.5 1.2 %all-to-all-done.1.packed = bf16[8,16,1728]{2,1,0:T(8,128)(2,1)S(1)} async-done(((bf16[8,16,1728]{2,1,0:T(8,128)(2,1)}), bf16[8,16,1728]{2,1,0:T(8,128)(2,1)S(1)}, u32[]{:S(2)}, u32[]{:S(2)}) %all-to-all-start.1) | async-done | bytes 442400 | tf_op jit(solution)/shard_map/all_to_all | solution.py:326
  79.8 1.0 copy-done.6
  80.8 1.0 %copy-done.20 = f32[8,128,128]{2,1,0:T(8,128)S(1)} copy-done((f32[8,128,128]{2,1,0:T(8,128)S(1)}, f32[8,128,128]{2,1,0:T(8,128)}, u32[]{:S(2)}) %copy-start.20) | copy-done | bytes 524312
  82.8 3.8 %shard_map.104 = (bf16[128,1152]{1,0:T(8,128)(2,1)}, bf16[128,1152]{1,0:T(8,128)(2,1)}, bf16[128,1728]{1,0:T(8,128)(2,1)}) custom-call(bf16[128,1728]{1,0:T(8,128)(2,1)S(1)} %bitcast.15, f32[8,128,128]{2,1,0:T(8,128)S(1)} %copy-done.20, bf16[128,1152]{1,0:T(8,128)(2,1)S(1)} %copy-done.22, bf16[576,1152]{1,0:T(8,128)(2,1)S(1)} %copy-done.2, ...), custom_call_target="tpu_custom_call" | custom-call | flops 8049999872 | bytes 5390336 | tf_op jit(solution)/shard_map/pallas_call | solution.py:35
  86.6 1.2 %shard_map.109 = (f32[72,288]{1,0:T(8,128)S(1)}, bf16[72,288]{1,0:T(8,128)(2,1)S(1)}, bf16[72,288]{1,0:T(8,128)(2,1)S(1)}, bf16[72,288]{1,0:T(8,128)(2,1)S(1)}) custom-call(f32[72,1152]{1,0:T(8,128)S(1)} %copy-done.18, bf16[72,1152]{1,0:T(8,128)(2,1)S(1)} %copy-done.10, bf16[72,1152]{1,0:T(8,128)(2,1)} %collective-permute-done.15.refs_1_, ...), custom_call_target="tpu_custom_call" | custom-call | flops 1150000000 | bytes 1036800 | tf_op jit(solution)/shard_map/pallas_call | solution.py:35
  88.4 2.4 %collective-permute-start.18 = (bf16[72,288]{1,0:T(8,128)(2,1)S(1)}, bf16[72,288]{1,0:T(8,128)(2,1)S(1)}, u32[]{:S(2)}, u32[]{:S(2)}) collective-permute-start(bf16[72,288]{1,0:T(8,128)(2,1)S(1)} %get-tuple-element.73), channel_id=1, source_target_pairs={{0,4},{1,5},{2,6},{3,7},{4,0},{5,1},{6,2},{7,3},{8,12},{9,13},{10,... | collective-permute-start | bytes 124424 | tf_op jit(solution)/shard_map/ppermute | solution.py:260
  90.8 1.5 %collective-permute-start.19 = (bf16[72,288]{1,0:T(8,128)(2,1)S(1)}, bf16[72,288]{1,0:T(8,128)(2,1)S(1)}, u32[]{:S(2)}, u32[]{:S(2)}) collective-permute-start(bf16[72,288]{1,0:T(8,128)(2,1)S(1)} %get-tuple-element.74), channel_id=1, source_target_pairs={{0,6},{1,7},{2,4},{3,5},{4,2},{5,3},{6,0},{7,1},{8,14},{9,15},{10,... | collective-permute-start | bytes 124424 | tf_op jit(solution)/shard_map/ppermute | solution.py:260
  92.3 1.2 %shard_map.106 = (f32[72,288]{1,0:T(8,128)S(1)}, bf16[72,288]{1,0:T(8,128)(2,1)S(1)}, bf16[72,288]{1,0:T(8,128)(2,1)S(1)}, bf16[72,288]{1,0:T(8,128)(2,1)S(1)}) custom-call(f32[72,1152]{1,0:T(8,128)S(1)} %copy-done.16, bf16[72,1152]{1,0:T(8,128)(2,1)S(1)} %collective-permute-done.7.refs_0_, bf16[72,1152]{1,0:T(8,128)(2,1)} %collective-permute-done.8.refs_1_, ...), custom_call_target="tpu_custom_call" | custom-call | flops 1150000000 | bytes 1036800 | tf_op jit(solution)/shard_map/pallas_call | solution.py:35
  93.5 2.9 %collective-permute-start.11 = (bf16[72,288]{1,0:T(8,128)(2,1)S(1)}, bf16[72,288]{1,0:T(8,128)(2,1)S(1)}, u32[]{:S(2)}, u32[]{:S(2)}) collective-permute-start(bf16[72,288]{1,0:T(8,128)(2,1)S(1)} %get-tuple-element.63), channel_id=1, source_target_pairs={{0,4},{1,5},{2,6},{3,7},{4,0},{5,1},{6,2},{7,3},{8,12},{9,13},{10,... | collective-permute-start | bytes 124424 | tf_op jit(solution)/shard_map/ppermute | solution.py:260
  96.4 1.5 %collective-permute-start.12 = (bf16[72,288]{1,0:T(8,128)(2,1)S(1)}, bf16[72,288]{1,0:T(8,128)(2,1)S(1)}, u32[]{:S(2)}, u32[]{:S(2)}) collective-permute-start(bf16[72,288]{1,0:T(8,128)(2,1)S(1)} %get-tuple-element.64), channel_id=1, source_target_pairs={{0,6},{1,7},{2,4},{3,5},{4,2},{5,3},{6,0},{7,1},{8,14},{9,15},{10,... | collective-permute-start | bytes 124424 | tf_op jit(solution)/shard_map/ppermute | solution.py:260
  98.6 1.5 %collective-permute-done.11.refs_1_ = bf16[72,288]{1,0:T(8,128)(2,1)S(1)} collective-permute-done((bf16[72,288]{1,0:T(8,128)(2,1)S(1)}, bf16[72,288]{1,0:T(8,128)(2,1)S(1)}, u32[]{:S(2)}, u32[]{:S(2)}) %collective-permute-start.11) | collective-permute-done | bytes 41504 | tf_op jit(solution)/shard_map/ppermute | solution.py:260
  100.2 2.2 %collective-permute-done.12.refs_2_ = bf16[72,288]{1,0:T(8,128)(2,1)S(1)} collective-permute-done((bf16[72,288]{1,0:T(8,128)(2,1)S(1)}, bf16[72,288]{1,0:T(8,128)(2,1)S(1)}, u32[]{:S(2)}, u32[]{:S(2)}) %collective-permute-start.12) | collective-permute-done | bytes 41504 | tf_op jit(solution)/shard_map/ppermute | solution.py:260
  (70 shorter events, 12.0 us)
Async XLA Ops:
  0.6 1.3 %copy-start.1 = (bf16[576,1152]{1,0:T(8,128)(2,1)S(1)}, bf16[576,1152]{1,0:T(8,128)(2,1)}, u32[]{:S(2)}) copy-start(bf16[576,1152]{1,0:T(8,128)(2,1)} %wos.3) | copy-start | bytes 3981316
  9.3 6.5 %copy-start = (bf16[1152,432]{0,1:T(8,128)(2,1)S(1)}, bf16[1152,432]{0,1:T(8,128)(2,1)}, u32[]{:S(2)}) copy-start(bf16[1152,432]{0,1:T(8,128)(2,1)} %param.9) | copy-start | bytes 2985988
  9.3 35.2 %copy-start.3 = (bf16[576,1152]{1,0:T(8,128)(2,1)S(1)}, bf16[576,1152]{1,0:T(8,128)(2,1)}, u32[]{:S(2)}) copy-start(bf16[576,1152]{1,0:T(8,128)(2,1)} %wot.3) | copy-start | bytes 3981316
  9.3 35.2 %all-to-all-start = ((bf16[8,16,2880]{2,1,0:T(8,128)(2,1)}), bf16[8,16,2880]{2,1,0:T(8,128)(2,1)S(1)}, u32[]{:S(2)}, u32[]{:S(2)}) async-start(bf16[8,16,2880]{2,1,0:T(8,128)(2,1)} %get-tuple-element.42), calls=%async_computation | async-start | bytes 1507328 | tf_op jit(solution)/shard_map/all_to_all | solution.py:326
  15.9 14.3 %collective-permute-start = (bf16[216,1152]{1,0:T(8,128)(2,1)S(1)}, bf16[216,1152]{1,0:T(8,128)(2,1)}, u32[]{:S(2)}, u32[]{:S(2)}) collective-permute-start(bf16[216,1152]{1,0:T(8,128)(2,1)S(1)} %dynamic-slice_bitcast_fusion), channel_id=1, source_target_pairs={{0,8},{8,0},{16,24},{24,16},{1,9},{9,1},{17,25},{25,17},{2,10},{10... | collective-permute-start | bytes 1493000 | tf_op jit(solution)/shard_map/ppermute | solution.py:260
  17.4 24.2 %collective-permute-start.1 = (bf16[216,1152]{1,0:T(8,128)(2,1)S(1)}, bf16[216,1152]{1,0:T(8,128)(2,1)}, u32[]{:S(2)}, u32[]{:S(2)}) collective-permute-start(bf16[216,1152]{1,0:T(8,128)(2,1)S(1)} %dynamic-slice_bitcast_fusion), channel_id=1, source_target_pairs={{0,16},{8,24},{16,0},{24,8},{1,17},{9,25},{17,1},{25,9},{2,18},{10... | collective-permute-start | bytes 1493000 | tf_op jit(solution)/shard_map/ppermute | solution.py:260
  18.9 22.7 %collective-permute-start.2 = (bf16[216,1152]{1,0:T(8,128)(2,1)S(1)}, bf16[216,1152]{1,0:T(8,128)(2,1)}, u32[]{:S(2)}, u32[]{:S(2)}) collective-permute-start(bf16[216,1152]{1,0:T(8,128)(2,1)S(1)} %dynamic-slice_bitcast_fusion), channel_id=1, source_target_pairs={{0,24},{8,16},{16,8},{24,0},{1,25},{9,17},{17,9},{25,1},{2,26},{10... | collective-permute-start | bytes 1493000 | tf_op jit(solution)/shard_map/ppermute | solution.py:260
  30.2 12.1 %collective-permute-start.3 = (bf16[216,1152]{1,0:T(8,128)(2,1)}, bf16[216,1152]{1,0:T(8,128)(2,1)}, u32[]{:S(2)}, u32[]{:S(2)}) collective-permute-start(bf16[216,1152]{1,0:T(8,128)(2,1)} %collective-permute-done.refs_1_), channel_id=1, source_target_pairs={{0,1},{1,0},{2,3},{3,2},{4,5},{5,4},{6,7},{7,6},{8,9},{9,8},{10,11... | collective-permute-start | bytes 1493000 | tf_op jit(solution)/shard_map/ppermute | solution.py:260
  41.7 2.2 %collective-permute-start.4 = (bf16[216,1152]{1,0:T(8,128)(2,1)}, bf16[216,1152]{1,0:T(8,128)(2,1)}, u32[]{:S(2)}, u32[]{:S(2)}) collective-permute-start(bf16[216,1152]{1,0:T(8,128)(2,1)} %collective-permute-done.1.refs_2_), channel_id=1, source_target_pairs={{0,1},{1,0},{2,3},{3,2},{4,5},{5,4},{6,7},{7,6},{8,9},{9,8},{10,11... | collective-permute-start | bytes 1493000 | tf_op jit(solution)/shard_map/ppermute | solution.py:260
  41.7 2.9 %collective-permute-start.5 = (bf16[216,1152]{1,0:T(8,128)(2,1)}, bf16[216,1152]{1,0:T(8,128)(2,1)}, u32[]{:S(2)}, u32[]{:S(2)}) collective-permute-start(bf16[216,1152]{1,0:T(8,128)(2,1)} %collective-permute-done.2.refs_3_), channel_id=1, source_target_pairs={{0,1},{1,0},{2,3},{3,2},{4,5},{5,4},{6,7},{7,6},{8,9},{9,8},{10,11... | collective-permute-start | bytes 1493000 | tf_op jit(solution)/shard_map/ppermute | solution.py:260
  52.0 7.3 %copy-start.13 = (bf16[4,72,1152]{2,1,0:T(8,128)(2,1)}, bf16[4,72,1152]{2,1,0:T(8,128)(2,1)S(1)}, u32[]{:S(2)}) copy-start(bf16[4,72,1152]{2,1,0:T(8,128)(2,1)S(1)} %get-tuple-element.65.keep) | copy-start | bytes 1990660
  52.0 14.3 %collective-permute-start.13 = (bf16[4,72,1152]{2,1,0:T(8,128)(2,1)}, bf16[4,72,1152]{2,1,0:T(8,128)(2,1)}, u32[]{:S(2)}, u32[]{:S(2)}) collective-permute-start(bf16[4,72,1152]{2,1,0:T(8,128)(2,1)} %get-tuple-element.66), channel_id=1, source_target_pairs={{0,1},{1,0},{2,3},{3,2},{4,5},{5,4},{6,7},{7,6},{8,9},{9,8},{10,11... | collective-permute-start | bytes 1990664 | tf_op jit(solution)/shard_map/ppermute | solution.py:260
  61.1 18.7 %all-to-all-start.1 = ((bf16[8,16,1728]{2,1,0:T(8,128)(2,1)}), bf16[8,16,1728]{2,1,0:T(8,128)(2,1)S(1)}, u32[]{:S(2)}, u32[]{:S(2)}) async-start(bf16[8,16,1728]{2,1,0:T(8,128)(2,1)} %get-tuple-element.51), calls=%async_computation.1 | async-start | bytes 917504 | tf_op jit(solution)/shard_map/all_to_all | solution.py:326
  65.8 7.0 %collective-permute-start.6 = (bf16[4,72,1152]{2,1,0:T(8,128)(2,1)}, bf16[4,72,1152]{2,1,0:T(8,128)(2,1)S(1)}, u32[]{:S(2)}, u32[]{:S(2)}) collective-permute-start(bf16[4,72,1152]{2,1,0:T(8,128)(2,1)} %copy-done.4), channel_id=1, source_target_pairs={{0,1},{1,0},{2,3},{3,2},{4,5},{5,4},{6,7},{7,6},{8,9},{9,8},{10,11... | collective-permute-start | bytes 1990664 | tf_op jit(solution)/shard_map/ppermute | solution.py:260
  67.4 5.4 %copy-start.12 = (bf16[4,72,1152]{2,1,0:T(8,128)(2,1)S(1)}, bf16[4,72,1152]{2,1,0:T(8,128)(2,1)}, u32[]{:S(2)}) copy-start(bf16[4,72,1152]{2,1,0:T(8,128)(2,1)} %copy-done.11) | copy-start | bytes 1990660
  69.3 4.3 %copy-start.17 = (f32[72,1152]{1,0:T(8,128)}, f32[72,1152]{1,0:T(8,128)S(1)}, u32[]{:S(2)}) copy-start(f32[72,1152]{1,0:T(8,128)S(1)} %get-tuple-element.67.own) | copy-start | bytes 995332
  69.3 7.1 %collective-permute-start.14 = (bf16[72,1152]{1,0:T(8,128)(2,1)S(1)}, bf16[72,1152]{1,0:T(8,128)(2,1)S(1)}, u32[]{:S(2)}, u32[]{:S(2)}) collective-permute-start(bf16[72,1152]{1,0:T(8,128)(2,1)S(1)} %get-tuple-element.68), channel_id=1, source_target_pairs={{0,8},{8,0},{16,24},{24,16},{1,9},{9,1},{17,25},{25,17},{2,10},{10... | collective-permute-start | bytes 497672 | tf_op jit(solution)/shard_map/ppermute | solution.py:260
  69.9 16.7 %collective-permute-start.15 = (bf16[72,1152]{1,0:T(8,128)(2,1)}, bf16[72,1152]{1,0:T(8,128)(2,1)}, u32[]{:S(2)}, u32[]{:S(2)}) collective-permute-start(bf16[72,1152]{1,0:T(8,128)(2,1)} %get-tuple-element.69), channel_id=1, source_target_pairs={{0,16},{8,24},{16,0},{24,8},{1,17},{9,25},{17,1},{25,9},{2,18},{10... | collective-permute-start | bytes 497672 | tf_op jit(solution)/shard_map/ppermute | solution.py:260
  71.4 15.2 %collective-permute-start.16 = (bf16[72,1152]{1,0:T(8,128)(2,1)}, bf16[72,1152]{1,0:T(8,128)(2,1)}, u32[]{:S(2)}, u32[]{:S(2)}) collective-permute-start(bf16[72,1152]{1,0:T(8,128)(2,1)} %get-tuple-element.70), channel_id=1, source_target_pairs={{0,24},{8,16},{16,8},{24,0},{1,25},{9,17},{17,9},{25,1},{2,26},{10... | collective-permute-start | bytes 497672 | tf_op jit(solution)/shard_map/ppermute | solution.py:260
  72.8 6.9 %copy-start.2 = (bf16[576,1152]{1,0:T(8,128)(2,1)S(1)}, bf16[576,1152]{1,0:T(8,128)(2,1)}, u32[]{:S(2)}) copy-start(bf16[576,1152]{1,0:T(8,128)(2,1)} %wos.3) | copy-start | bytes 3981316
  74.4 16.4 %collective-permute-start.7 = (bf16[72,1152]{1,0:T(8,128)(2,1)}, bf16[72,1152]{1,0:T(8,128)(2,1)S(1)}, u32[]{:S(2)}, u32[]{:S(2)}) collective-permute-start(bf16[72,1152]{1,0:T(8,128)(2,1)} %get-tuple-element.58), channel_id=1, source_target_pairs={{0,8},{8,0},{16,24},{24,16},{1,9},{9,1},{17,25},{25,17},{2,10},{10... | collective-permute-start | bytes 497672 | tf_op jit(solution)/shard_map/ppermute | solution.py:260
  74.9 17.4 %collective-permute-start.8 = (bf16[72,1152]{1,0:T(8,128)(2,1)}, bf16[72,1152]{1,0:T(8,128)(2,1)}, u32[]{:S(2)}, u32[]{:S(2)}) collective-permute-start(bf16[72,1152]{1,0:T(8,128)(2,1)} %get-tuple-element.59), channel_id=1, source_target_pairs={{0,16},{8,24},{16,0},{24,8},{1,17},{9,25},{17,1},{25,9},{2,18},{10... | collective-permute-start | bytes 497672 | tf_op jit(solution)/shard_map/ppermute | solution.py:260
  77.1 15.2 %collective-permute-start.9 = (bf16[72,1152]{1,0:T(8,128)(2,1)S(1)}, bf16[72,1152]{1,0:T(8,128)(2,1)}, u32[]{:S(2)}, u32[]{:S(2)}) collective-permute-start(bf16[72,1152]{1,0:T(8,128)(2,1)S(1)} %get-tuple-element.60), channel_id=1, source_target_pairs={{0,24},{8,16},{16,8},{24,0},{1,25},{9,17},{17,9},{25,1},{2,26},{10... | collective-permute-start | bytes 497672 | tf_op jit(solution)/shard_map/ppermute | solution.py:260
  82.8 3.8 %copy-start.10 = (bf16[72,1152]{1,0:T(8,128)(2,1)S(1)}, bf16[72,1152]{1,0:T(8,128)(2,1)}, u32[]{:S(2)}) copy-start(bf16[72,1152]{1,0:T(8,128)(2,1)} %copy-done.9) | copy-start | bytes 497668
  82.8 3.8 %copy-start.18 = (f32[72,1152]{1,0:T(8,128)S(1)}, f32[72,1152]{1,0:T(8,128)}, u32[]{:S(2)}) copy-start(f32[72,1152]{1,0:T(8,128)} %copy-done.17) | copy-start | bytes 995332
  86.6 5.7 %copy-start.16 = (f32[72,1152]{1,0:T(8,128)S(1)}, f32[72,1152]{1,0:T(8,128)}, u32[]{:S(2)}) copy-start(f32[72,1152]{1,0:T(8,128)} %copy-done.15) | copy-start | bytes 995332
  87.8 8.6 %collective-permute-start.17 = (bf16[72,288]{1,0:T(8,128)(2,1)S(1)}, bf16[72,288]{1,0:T(8,128)(2,1)S(1)}, u32[]{:S(2)}, u32[]{:S(2)}) collective-permute-start(bf16[72,288]{1,0:T(8,128)(2,1)S(1)} %get-tuple-element.72), channel_id=1, source_target_pairs={{0,2},{1,3},{2,0},{3,1},{4,6},{5,7},{6,4},{7,5},{8,10},{9,11},{10,... | collective-permute-start | bytes 124424 | tf_op jit(solution)/shard_map/ppermute | solution.py:260
  88.4 9.5 %collective-permute-start.18 = (bf16[72,288]{1,0:T(8,128)(2,1)S(1)}, bf16[72,288]{1,0:T(8,128)(2,1)S(1)}, u32[]{:S(2)}, u32[]{:S(2)}) collective-permute-start(bf16[72,288]{1,0:T(8,128)(2,1)S(1)} %get-tuple-element.73), channel_id=1, source_target_pairs={{0,4},{1,5},{2,6},{3,7},{4,0},{5,1},{6,2},{7,3},{8,12},{9,13},{10,... | collective-permute-start | bytes 124424 | tf_op jit(solution)/shard_map/ppermute | solution.py:260
  90.8 7.2 %collective-permute-start.19 = (bf16[72,288]{1,0:T(8,128)(2,1)S(1)}, bf16[72,288]{1,0:T(8,128)(2,1)S(1)}, u32[]{:S(2)}, u32[]{:S(2)}) collective-permute-start(bf16[72,288]{1,0:T(8,128)(2,1)S(1)} %get-tuple-element.74), channel_id=1, source_target_pairs={{0,6},{1,7},{2,4},{3,5},{4,2},{5,3},{6,0},{7,1},{8,14},{9,15},{10,... | collective-permute-start | bytes 124424 | tf_op jit(solution)/shard_map/ppermute | solution.py:260
  93.5 5.1 %collective-permute-start.10 = (bf16[72,288]{1,0:T(8,128)(2,1)S(1)}, bf16[72,288]{1,0:T(8,128)(2,1)S(1)}, u32[]{:S(2)}, u32[]{:S(2)}) collective-permute-start(bf16[72,288]{1,0:T(8,128)(2,1)S(1)} %get-tuple-element.62), channel_id=1, source_target_pairs={{0,2},{1,3},{2,0},{3,1},{4,6},{5,7},{6,4},{7,5},{8,10},{9,11},{10,... | collective-permute-start | bytes 124424 | tf_op jit(solution)/shard_map/ppermute | solution.py:260
  93.5 6.6 %collective-permute-start.11 = (bf16[72,288]{1,0:T(8,128)(2,1)S(1)}, bf16[72,288]{1,0:T(8,128)(2,1)S(1)}, u32[]{:S(2)}, u32[]{:S(2)}) collective-permute-start(bf16[72,288]{1,0:T(8,128)(2,1)S(1)} %get-tuple-element.63), channel_id=1, source_target_pairs={{0,4},{1,5},{2,6},{3,7},{4,0},{5,1},{6,2},{7,3},{8,12},{9,13},{10,... | collective-permute-start | bytes 124424 | tf_op jit(solution)/shard_map/ppermute | solution.py:260
  96.4 6.0 %collective-permute-start.12 = (bf16[72,288]{1,0:T(8,128)(2,1)S(1)}, bf16[72,288]{1,0:T(8,128)(2,1)S(1)}, u32[]{:S(2)}, u32[]{:S(2)}) collective-permute-start(bf16[72,288]{1,0:T(8,128)(2,1)S(1)} %get-tuple-element.64), channel_id=1, source_target_pairs={{0,6},{1,7},{2,4},{3,5},{4,2},{5,3},{6,0},{7,1},{8,14},{9,15},{10,... | collective-permute-start | bytes 124424 | tf_op jit(solution)/shard_map/ppermute | solution.py:260
  (13 other events, 11.7 us)

commit v3 on v2

v3 whole, which is shorter than its diff:
```python
import functools
import math

import jax
import jax.numpy as jnp
from jax import lax
from jax.experimental import pallas as pl
from jax.experimental.pallas import tpu as pltpu
from jax.sharding import PartitionSpec as P

DH = 72
FRAMES = 16
LANES = 128
BF16 = jnp.bfloat16
F32 = jnp.float32
VMEM = pl.BlockSpec(memory_space=pltpu.VMEM)
SMEM = pl.BlockSpec(memory_space=pltpu.SMEM)
HBM = pl.BlockSpec(memory_space=pltpu.HBM)
LIMIT = 40 * 1024 * 1024
MOST = 60 * 1024 * 1024


def dot(left, right):
    return jnp.dot(left, right, preferred_element_type=F32)


def dot_bt(left, right):
    return lax.dot_general(left, right, (((1,), (1,)), ((), ())), preferred_element_type=F32)


def dot_at(left, right):
    return lax.dot_general(left, right, (((0,), (0,)), ((), ())), preferred_element_type=F32)


def call(body, outs, args, scratch=(), us=1, far_in=(), far_out=()):
    moved = sum(math.prod(a.shape) * a.dtype.itemsize for a in (*args, *outs))
    near = [SMEM if a.dtype == jnp.int32 else VMEM for a in args]
    return pl.pallas_call(
        body,
        out_shape=outs,
        in_specs=[HBM if i in far_in else spec for i, spec in enumerate(near)],
        out_specs=[HBM if i in far_out else VMEM for i in range(len(outs))],
        scratch_shapes=list(scratch),
        compiler_params=pltpu.CompilerParams(vmem_limit_bytes=MOST if far_in else LIMIT),
        cost_estimate=pl.CostEstimate(
            flops=us * 1150000000, bytes_accessed=moved, transcendentals=0
        ),
    )(*args)


def started(pairs, sems):
    copies = [pltpu.make_async_copy(a, b, sems.at[i]) for i, (a, b) in enumerate(pairs)]
    for copy in copies:
        copy.start()
    return copies


def shape(dims, dtype=BF16):
    return jax.ShapeDtypeStruct(dims, dtype)


def window(head):
    low = head * DH // LANES * LANES
    high = -(-(head + 1) * DH // LANES) * LANES
    return low, high


def head_only(block, head):
    low, high = window(head)
    lane = lax.broadcasted_iota(jnp.int32, (1, high - low), 1) + low
    keep = (lane >= head * DH) & (lane < (head + 1) * DH)
    return jnp.where(keep, block, jnp.zeros_like(block))


def add_tiles(tiles, head, value):
    low, high = window(head)
    for at in range(low // LANES, high // LANES):
        part = value[:, at * LANES - low : (at + 1) * LANES - low]
        tiles[at] = part if tiles[at] is None else tiles[at] + part


def joined(tiles):
    return jnp.concatenate([tile.astype(BF16) for tile in tiles], axis=1)


def same_group(rows, kind):
    row = lax.broadcasted_iota(jnp.int32, (rows, rows), 0)
    col = lax.broadcasted_iota(jnp.int32, (rows, rows), 1)
    how, size = kind
    return row // size == col // size if how == "block" else row % size == col % size


def softmax_forward(q_ref, k_ref, v_ref, p_ref, heads, kind):
    rows = q_ref.shape[0]
    mask = same_group(rows, kind)
    tiles = [None] * (q_ref.shape[1] // LANES)
    for head in range(heads):
        low, high = window(head)
        s = dot_bt(q_ref[:, low:high], head_only(k_ref[:, low:high], head)) * (1.0 / math.sqrt(DH))
        s = jnp.where(mask, s, -jnp.inf)
        e = jnp.exp(s - jnp.max(s, axis=1, keepdims=True))
        p = e / jnp.sum(e, axis=1, keepdims=True)
        p_ref[head] = p
        add_tiles(tiles, head, dot(p.astype(BF16), head_only(v_ref[:, low:high], head)))
    return joined(tiles)


def softmax_backward(q_ref, k_ref, v_ref, g_ref, p_ref, heads):
    count = q_ref.shape[1] // LANES
    dq, dk, dv = [None] * count, [None] * count, [None] * count
    for head in range(heads):
        low, high = window(head)
        p = p_ref[head]
        g = head_only(g_ref[:, low:high], head)
        add_tiles(dv, head, dot_at(p.astype(BF16), g))
        dp = dot_bt(g, v_ref[:, low:high])
        ds = p * (dp - jnp.sum(p * dp, axis=1, keepdims=True)) * (1.0 / math.sqrt(DH))
        ds = ds.astype(BF16)
        add_tiles(dq, head, dot(ds, head_only(k_ref[:, low:high], head)))
        add_tiles(dk, head, dot_at(ds, head_only(q_ref[:, low:high], head)))
    return joined(dq), joined(dk), joined(dv)


def put(ref, value):
    width = value.shape[1]
    ref[:, width // LANES * LANES :] = jnp.zeros(
        (ref.shape[0], ref.shape[1] - width // LANES * LANES), ref.dtype
    )
    ref[:, :width] = value


def chunks_of(value, peers, patches):
    rows = value.shape[0]
    each = patches // peers
    value = value.astype(F32)
    for at in range(peers):
        low = at * each
        cut = [value[low + f : low + f + each] for f in range(0, rows, patches)]
        yield at, jnp.concatenate(cut, axis=0).astype(BF16)


def spatial_kernel(peers, patches, *refs):
    far, (hid_out, back_out, hid_far, p_far), refs = refs[:4], refs[4:8], refs[8:]
    tok, cot, qkv, wos, ahead, behind, hid, p_ref, qs, ks, vs, sems = refs
    width = tok.shape[1]
    inner = wos.shape[0]
    loads = started(zip(far, (tok, cot, qkv, wos)), sems)
    loads[2].wait()
    x = qkv[...]
    put(qs, x[:, :inner])
    put(ks, x[:, inner : 2 * inner])
    put(vs, x[:, 2 * inner :])
    o = softmax_forward(qs, ks, vs, p_ref, inner // DH, ("block", patches))[:, :inner]
    loads[0].wait()
    loads[3].wait()
    hid[...] = (tok[...].astype(F32) + dot(o, wos[...])).astype(BF16)
    for at, rows in chunks_of(hid[...], peers, patches):
        ahead[at] = rows
    stores = started([(ahead, hid_out), (p_ref, p_far), (hid, hid_far)], sems.at[pl.ds(4, 3)])
    loads[1].wait()
    for at, rows in chunks_of(cot[...], peers, patches):
        behind[at, :, :width] = rows
    for at, rows in chunks_of(o, peers, patches):
        behind[at, :, width:] = rows
    stores += started([(behind, back_out)], sems.at[pl.ds(7, 1)])
    for copy in stores:
        copy.wait()


def split_kernel(near_x, near_y, _, from_x, from_y):
    cut = from_y.shape[1]
    from_y[...] = near_y[:, :cut]
    from_x[...] = near_x[:, cut:]


def pieces(shards, weights):
    weights = list(weights)
    for place, count, parts in shards:
        low, held = 0, []
        for _ in range(parts):
            w = weights.pop(0)
            held.append((low, w))
            low += w.shape[1]
        yield place, count, held


def temporal_forward_kernel(shards, total, group, inner, idx, packed, *refs):
    weights, (q, k, v, p_ref, out, blocks, hid) = refs[:total], refs[total:]
    chunk = packed.shape[1]
    for at in range(packed.shape[0]):
        hid[at * chunk : (at + 1) * chunk] = packed[at]
    for place, count, held in pieces(shards, weights):
        block = None
        for low, w in held:
            value = dot_bt(hid[:, low : low + w.shape[1]], w[...])
            block = value if block is None else block + value
        block = block.astype(BF16)
        size = block.shape[1] // count
        for i in range(count):
            blocks[place(idx) + i] = block[:, i * size : (i + 1) * size]
    whole = jnp.concatenate([blocks[i] for i in range(blocks.shape[0])], axis=1)
    put(q, whole[:, :inner])
    put(k, whole[:, inner : 2 * inner])
    put(v, whole[:, 2 * inner :])
    out[...] = softmax_forward(q, k, v, p_ref, inner // DH, ("cycle", group))[:, :inner]


def temporal_backward_kernel(shards, total, idx, q, k, v, p_ref, out, held_back, wot, *refs):
    weights, (packed, mine, blocks, cot, g) = refs[:total], refs[total:]
    inner, width = wot.shape
    chunk = packed.shape[1]
    for at in range(packed.shape[0]):
        rows = slice(at * chunk, (at + 1) * chunk)
        cot[rows] = held_back[at, :, :width]
        mine[rows, inner : 2 * inner] = held_back[at, :, width:]
    put(g, dot_bt(cot[...], wot[...]).astype(BF16))
    dq, dk, dv = softmax_backward(q, k, v, g, p_ref, inner // DH)
    whole = jnp.concatenate([dq[:, :inner], dk[:, :inner], dv[:, :inner]], axis=1)
    size = blocks.shape[2]
    for i in range(blocks.shape[0]):
        blocks[i] = whole[:, i * size : (i + 1) * size]
    grad = jnp.zeros(cot.shape, F32)
    for place, count, held in pieces(shards, weights):
        lhs = jnp.concatenate([blocks[place(idx) + i] for i in range(count)], axis=1)
        grad += jnp.concatenate([dot(lhs, w[...]) for _, w in held], axis=1)
    grad = (cot[...].astype(F32) + grad.astype(BF16).astype(F32)).astype(BF16)
    for at in range(packed.shape[0]):
        rows = slice(at * chunk, (at + 1) * chunk)
        packed[at, :, :width] = grad[rows]
        packed[at, :, width:] = out[rows]
    mine[:, :inner] = out[...]
    mine[:, 2 * inner : 2 * inner + width] = cot[...]
    mine[:, 2 * inner + width :] = grad


def whole_parts_kernel(inner, width, mine, out):
    for i in range(2):
        right = mine[:, 2 * inner + i * width : 2 * inner + (i + 1) * width]
        out[i] = dot_at(mine[:, i * inner : (i + 1) * inner], right).astype(BF16)


def parts_kernel(inner, width, idx, mine, other, own, *refs):
    outs, (heads, cols) = refs[:-2], refs[-2:]
    count = cols.shape[0]
    rows = mine.shape[0]
    size = heads.shape[2]
    wide = cols.shape[2]
    for i in range(2):
        for at, ref in enumerate((mine, other)):
            held = slice(at * rows, (at + 1) * rows)
            for h in range(heads.shape[0]):
                low = i * inner + h * size
                heads[h, held] = ref[:, low : low + size]
            for r in range(count):
                low = 2 * inner + i * width + r * wide
                cols[r, held] = ref[:, low : low + wide]
        left = jnp.concatenate([heads[idx[2] ^ (2 * q)] for q in range(count)], axis=1)
        for r in range(count):
            full = dot_at(left, cols[idx[0] ^ r])
            block = jnp.concatenate([full[q * size : (q + 1) * size] for q in range(count)], axis=1)
            if r == 0:
                own[i] = block
            else:
                outs[r - 1][i] = block.astype(BF16)


def sum_dp_kernel(own, *refs):
    got, outs = refs[: len(refs) // 2], refs[len(refs) // 2 :]
    for i in range(own.shape[0]):
        total = own[i]
        for part in got:
            total += part[i].astype(F32)
        size = total.shape[1] // len(outs)
        for q, out in enumerate(outs):
            out[i] = total[:, q * size : (q + 1) * size].astype(out.dtype)


def sum_kernel(own, *refs):
    got, outs = refs[:-2], refs[-2:]
    for i, out in enumerate(outs):
        total = own[i]
        for part in got:
            total += part[i].astype(F32)
        out[...] = total


def last_kernel(patches, qkv, p_ref, hid, wos, wot, packed, block_out, out, grads, *refs):
    here, (qs, ks, vs, gs, sems) = refs[:5], refs[5:]
    loads = started(zip((wos, qkv, p_ref, wot, hid), here), sems)
    wos, qkv, p_ref, wot, hid = here
    inner, width = wos.shape
    peers, chunk, _ = packed.shape
    each = patches // peers
    rows = [packed[at].astype(F32) for at in range(peers)]
    rows = [rows[at][f * each : (f + 1) * each] for f in range(chunk // each) for at in range(peers)]
    rows = jnp.concatenate(rows, axis=0).astype(BF16)
    grad, attended = rows[:, :width], rows[:, width:]
    out[...] = grad
    loads[0].wait()
    put(gs, dot_bt(grad, wos[...]).astype(BF16))
    loads[1].wait()
    x = qkv[...]
    put(qs, x[:, :inner])
    put(ks, x[:, inner : 2 * inner])
    put(vs, x[:, 2 * inner :])
    loads[2].wait()
    dq, dk, dv = softmax_backward(qs, ks, vs, gs, p_ref, inner // DH)
    grads[...] = jnp.concatenate([dq[:, :inner], dk[:, :inner], dv[:, :inner]], axis=1)
    loads[3].wait()
    loads[4].wait()
    block_out[...] = (hid[...].astype(F32) + dot(attended, wot[...])).astype(BF16)


def flip(value, axis, bit):
    return lax.ppermute(value, axis, [(i, i ^ bit) for i in range(lax.axis_size(axis))])


def gather_weight(weight, core, after):
    n = lax.axis_size("dp")
    if n != 4:
        return [lax.all_gather(weight, "dp", axis=0, tiled=True)], [(lambda idx: 0, 1, 1)], 1
    half, width = weight.shape[0] // 2, weight.shape[1]
    mine = lax.dynamic_slice_in_dim(weight, core * half, half, 0)
    near = [flip(mine, "dp", 1), flip(mine, "dp", 2)]
    cut = width // LANES // 2 * LANES
    from_x, from_y = call(
        split_kernel, [shape((half, width - cut)), shape((half, cut))], [*near, after]
    )
    corner = [flip(from_y, "dp", 1), flip(from_x, "dp", 2)]
    held = near + corner
    far = [flip(w, "seq", 1) for w in held]
    shards = [(lambda idx: 2 * idx[0], 2, 1)]
    for flipped in range(2):
        for j in range(1, n):
            shards.append(
                (
                    lambda idx, j=j, flipped=flipped: 2 * (idx[0] ^ j) + (idx[1] ^ flipped),
                    1,
                    1 if j < 3 else 2,
                )
            )
    return [weight, *held, *far], shards, 2 * n


def reduced(mine, inner, width, idx):
    n_dp, n_seq = lax.axis_size("dp"), lax.axis_size("seq")
    if n_dp != 4 or n_seq != 8:
        (both,) = call(
            functools.partial(whole_parts_kernel, inner, width), [shape((2, inner, width))], [mine]
        )
        both = lax.psum_scatter(both, "seq", scatter_dimension=1, tiled=True)
        both = lax.psum_scatter(both, "dp", scatter_dimension=2, tiled=True).astype(F32)
        return both[0], both[1]
    rows = mine.shape[0]
    size = inner // n_seq
    part = (2, size, width)
    own, *sends = call(
        functools.partial(parts_kernel, inner, width),
        [shape(part, F32)] + [shape(part)] * (n_dp - 1),
        [idx, mine, flip(mine, "seq", 1)],
        [
            pltpu.VMEM((n_seq, 2 * rows, size), BF16),
            pltpu.VMEM((n_dp, 2 * rows, width // n_dp), BF16),
        ],
        us=3,
    )
    got = [flip(value, "dp", r + 1) for r, value in enumerate(sends)]
    block = (2, size, width // n_dp)
    own, *sends = call(
        sum_dp_kernel, [shape(block, F32)] + [shape(block)] * (n_dp - 1), [own, *got]
    )
    got = [flip(value, "seq", 2 * (q + 1)) for q, value in enumerate(sends)]
    return call(sum_kernel, [shape(block[1:], F32)] * 2, [own, *got])


def shards(tokens, spatial_qkv, wo_spatial, w_temporal, wo_temporal, cotangent):
    frames, patches, width = tokens.shape
    inner = wo_spatial.shape[0]
    heads = inner // DH
    padded = -(-inner // LANES) * LANES
    rows = frames * patches
    peers = FRAMES // frames
    each = patches // peers
    chunk = rows // peers
    n_seq = lax.axis_size("seq")
    seq = lax.axis_index("seq")
    idx = jnp.stack([lax.axis_index("dp"), seq % 2, seq]).astype(jnp.int32)
    wide = pltpu.VMEM((rows, padded), BF16)
    weights_of = pltpu.VMEM((heads, rows, rows), F32)
    model = pltpu.VMEM((rows, width), BF16)
    projection = pltpu.VMEM((inner, width), BF16)
    groups = None
    if n_seq > peers:
        groups = [list(range(i, i + peers)) for i in range(0, n_seq, peers)]

    def exchange(value):
        return lax.all_to_all(
            value, "seq", split_axis=0, concat_axis=0, tiled=True, axis_index_groups=groups
        )

    qkv_rows = spatial_qkv.reshape(rows, 3 * inner)
    ahead = (peers, chunk, width)
    behind = (peers, chunk, width + inner)
    ahead_sent, behind_sent, hidden, spatial_p = call(
        functools.partial(spatial_kernel, peers, patches),
        [shape(ahead), shape(behind), shape((rows, width)), shape((heads, rows, rows), F32)],
        [tokens.reshape(rows, width), cotangent.reshape(rows, width), qkv_rows, wo_spatial],
        [model, model, pltpu.VMEM((rows, 3 * inner), BF16), projection]
        + [pltpu.VMEM(ahead, BF16), pltpu.VMEM(behind, BF16), model, weights_of]
        + [wide] * 3
        + [pltpu.SemaphoreType.DMA((8,))],
        us=3,
        far_in=range(4),
        far_out=range(4),
    )
    weights, places, count = gather_weight(w_temporal.T, seq % 2, hidden[:8, :LANES])
    blocks = pltpu.VMEM((count, rows, 3 * inner // count), BF16)
    q, k, v, temporal_p, out = call(
        functools.partial(temporal_forward_kernel, places, len(weights), each, inner),
        [shape((rows, padded))] * 3 + [shape((heads, rows, rows), F32), shape((rows, inner))],
        [idx, exchange(ahead_sent), *weights],
        [blocks, model],
        us=6,
    )
    back, mine = call(
        functools.partial(temporal_backward_kernel, places, len(weights)),
        [shape(behind), shape((rows, 2 * (inner + width)))],
        [idx, q, k, v, temporal_p, out, exchange(behind_sent), wo_temporal, *weights],
        [blocks, model, wide],
        us=6,
    )
    block_out, tokens_grad, qkv_grad = call(
        functools.partial(last_kernel, patches),
        [shape((rows, width)), shape((rows, width)), shape((rows, 3 * inner))],
        [qkv_rows, spatial_p, hidden, wo_spatial, wo_temporal, exchange(back)],
        [projection, pltpu.VMEM((rows, 3 * inner), BF16), weights_of, projection, model]
        + [wide] * 4
        + [pltpu.SemaphoreType.DMA((5,))],
        us=6,
        far_in=range(5),
    )
    temporal_grad, spatial_grad = reduced(mine, inner, width, idx)
    return (
        block_out.reshape(frames, patches, width),
        tokens_grad.reshape(frames, patches, width),
        qkv_grad.reshape(frames, patches, 3 * inner),
        spatial_grad,
        temporal_grad,
    )


def solution(mesh):
    placed = (
        P(("dp", "seq"), None, None),
        P(("dp", "seq"), None, None),
        P(),
        P(None, "dp"),
        P(),
        P(("dp", "seq"), None, None),
    )
    return jax.shard_map(
        shards,
        mesh=mesh,
        in_specs=placed,
        out_specs=(
            P(("dp", "seq"), None, None),
            P(("dp", "seq"), None, None),
            P(("dp", "seq"), None, None),
            P("seq", "dp"),
            P("seq", "dp"),
        ),
        check_vma=False,
    )
```

time: 104 us -> 98 us (0.942)
  waiting for transfers between devices: 29.6 us -> 24.5 us
  starting transfers between devices: 31.8 us -> 28.3 us
  local copies, waits for them, and re-layouts: 13.1 us -> 16.4 us
    ppermute x20 -> x15, waiting for transfers between devices: 28.4 us -> 22.3 us  [flip(): lax.ppermute(value, axis, [(i, i ^ bit) for i in range(lax.axis_size(axis...]
    ppermute x20 -> x15, starting transfers between devices: 20.6 us -> 14.8 us  [flip(): lax.ppermute(value, axis, [(i, i ^ bit) for i in range(lax.axis_size(axis...]
    all_to_all x2 -> x3, starting transfers between devices: 11.2 us -> 13.5 us  [exchange(): lax.all_to_all(value, 'seq', split_axis=0, concat_axis=0, tiled=True, axi...]
    unnamed x46 -> x40, local copies, waits for them, and re-layouts: 13 us -> 14.7 us
    all_to_all x2 -> x3, waiting for transfers between devices: 1.21 us -> 2.18 us  [exchange(): lax.all_to_all(value, 'seq', split_axis=0, concat_axis=0, tiled=True, axi...]
    pallas_call x10 -> x8, Pallas kernels: 27.8 us -> 26.9 us  [call(): pl.pallas_call(body, out_shape=outs, in_specs=[HBM if i in far_in else sp...]
  transfers between devices with their start and end apart: 22 -> 18, of which waited for: 7 -> 6; matrix products, arithmetic and copies ran while one was open for 0% -> 1% of each run, Pallas kernels for 16% -> 20%
where the time goes in v3:
time: 98 us; the launch traced here: 97 us
  starting transfers between devices  28.3 us (29%)
  Pallas kernels  26.9 us (27%)
  waiting for transfers between devices  24.5 us (25%)
  local copies, waits for them, and re-layouts  16.4 us (17%)
    pallas_call x8, Pallas kernels, call(): pl.pallas_call(body, out_shape=outs, in_specs=[HBM if i in far_in else sp...  26.9 us
    ppermute x15, waiting for transfers between devices, flip(): lax.ppermute(value, axis, [(i, i ^ bit) for i in range(lax.axis_size(axis...  22.3 us
    ppermute x15, starting transfers between devices, flip(): lax.ppermute(value, axis, [(i, i ^ bit) for i in range(lax.axis_size(axis...  14.8 us
    unnamed x40, local copies, waits for them, and re-layouts  14.7 us
    all_to_all x3, starting transfers between devices, exchange(): lax.all_to_all(value, 'seq', split_axis=0, concat_axis=0, tiled=True, axi...  13.5 us
    all_to_all x3, waiting for transfers between devices, exchange(): lax.all_to_all(value, 'seq', split_axis=0, concat_axis=0, tiled=True, axi...  2.18 us
  transfers between devices with their start and end apart: 18, of which 6 were waited for; matrix products, arithmetic and copies ran while one was open for 1% of the time, Pallas kernels for 20%

profile of v3, /device:TPU:0, one launch (start us, length us, event | category | flops | bytes accessed | tf_op | source)
XLA Modules:
  0.0 97.0 jit_solution(16676921183794726510)
XLA Ops:
  0.6 1.1 %dynamic-slice_bitcast_fusion = bf16[216,1152]{1,0:T(8,128)(2,1)S(1)} fusion(bf16[1152,432]{0,1:T(8,128)(2,1)} %param.9, s32[]{:T(128)S(6)} %select_n.13), kind=kLoop, calls=%fused_computation | loop fusion | bytes 995332 | tf_op jit(solution)/shard_map/dynamic_slice | solution.py:323
  1.7 3.0 %collective-permute-start.1 = (bf16[216,1152]{1,0:T(8,128)(2,1)S(1)}, bf16[216,1152]{1,0:T(8,128)(2,1)S(1)}, u32[]{:S(2)}, u32[]{:S(2)}) collective-permute-start(bf16[216,1152]{1,0:T(8,128)(2,1)S(1)} %dynamic-slice_bitcast_fusion), channel_id=1, source_target_pairs={{0,16},{8,24},{16,0},{24,8},{1,17},{9,25},{17,1},{25,9},{2,18},{10... | collective-permute-start | bytes 1493000 | tf_op jit(solution)/shard_map/ppermute | solution.py:315
  4.8 1.5 %collective-permute-start = (bf16[216,1152]{1,0:T(8,128)(2,1)S(1)}, bf16[216,1152]{1,0:T(8,128)(2,1)S(1)}, u32[]{:S(2)}, u32[]{:S(2)}) collective-permute-start(bf16[216,1152]{1,0:T(8,128)(2,1)S(1)} %dynamic-slice_bitcast_fusion), channel_id=1, source_target_pairs={{0,8},{8,0},{16,24},{24,16},{1,9},{9,1},{17,25},{25,17},{2,10},{10... | collective-permute-start | bytes 1493000 | tf_op jit(solution)/shard_map/ppermute | solution.py:315
  6.3 4.5 %shard_map.101 = (bf16[8,16,1152]{2,1,0:T(8,128)(2,1)}, bf16[8,16,1728]{2,1,0:T(8,128)(2,1)}, bf16[128,1152]{1,0:T(8,128)(2,1)}, f32[8,128,128]{2,1,0:T(8,128)}) custom-call(bf16[128,1152]{1,0:T(8,128)(2,1)} %bitcast.16, bf16[128,1152]{1,0:T(8,128)(2,1)} %bitcast.17, bf16[128,1728]{1,0:T(8,128)(2,1)} %bitcast.14, bf16[576,1152]{1,0:T(8,128)(2,1)} %wos.1), custom_call_target="tpu_custom_call" | custom-call | flops 3449999872 | bytes 3915776 | tf_op jit(solution)/shard_map/pallas_call | solution.py:38
  10.8 4.9 %all-to-all-start = ((bf16[8,16,1152]{2,1,0:T(8,128)(2,1)}), bf16[8,16,1152]{2,1,0:T(8,128)(2,1)S(1)}, u32[]{:S(2)}, u32[]{:S(2)}) async-start(bf16[8,16,1152]{2,1,0:T(8,128)(2,1)} %get-tuple-element.33), calls=%async_computation | async-start | bytes 589824 | tf_op jit(solution)/shard_map/all_to_all | solution.py:397
  16.4 1.2 %collective-permute-done.near_x.refs_1_ = bf16[216,1152]{1,0:T(8,128)(2,1)S(1)} collective-permute-done((bf16[216,1152]{1,0:T(8,128)(2,1)S(1)}, bf16[216,1152]{1,0:T(8,128)(2,1)S(1)}, u32[]{:S(2)}, u32[]{:S(2)}) %collective-permute-start) | collective-permute-done | bytes 497696 | tf_op jit(solution)/shard_map/ppermute | solution.py:315
  18.6 1.6 %collective-permute-start.2 = (bf16[216,512]{1,0:T(8,128)(2,1)S(1)}, bf16[216,512]{1,0:T(8,128)(2,1)}, u32[]{:S(2)}, u32[]{:S(2)}) collective-permute-start(bf16[216,512]{1,0:T(8,128)(2,1)S(1)} %get-tuple-element.34), channel_id=1, source_target_pairs={{0,8},{8,0},{16,24},{24,16},{1,9},{9,1},{17,25},{25,17},{2,10},{10... | collective-permute-start | bytes 663560 | tf_op jit(solution)/shard_map/ppermute | solution.py:315
  20.2 5.3 %collective-permute-done.3.refs_4_ = bf16[216,640]{1,0:T(8,128)(2,1)S(1)} collective-permute-done((bf16[216,640]{1,0:T(8,128)(2,1)S(1)}, bf16[216,640]{1,0:T(8,128)(2,1)S(1)}, u32[]{:S(2)}, u32[]{:S(2)}) %collective-permute-start.3) | collective-permute-done | bytes 276512 | tf_op jit(solution)/shard_map/ppermute | solution.py:315
  26.3 5.0 %all-to-all-start.1 = ((bf16[8,16,1728]{2,1,0:T(8,128)(2,1)}), bf16[8,16,1728]{2,1,0:T(8,128)(2,1)S(1)}, u32[]{:S(2)}, u32[]{:S(2)}) async-start(bf16[8,16,1728]{2,1,0:T(8,128)(2,1)} %get-tuple-element.41), calls=%async_computation.1 | async-start | bytes 917504 | tf_op jit(solution)/shard_map/all_to_all | solution.py:397
  32.2 1.0 %copy-done.3 = bf16[216,1152]{1,0:T(8,128)(2,1)S(1)} copy-done((bf16[216,1152]{1,0:T(8,128)(2,1)S(1)}, bf16[216,1152]{1,0:T(8,128)(2,1)}, u32[]{:S(2)}) %copy-start.3) | copy-done | bytes 497688
  33.3 1.0 %copy-done.6 = bf16[216,1152]{1,0:T(8,128)(2,1)S(1)} copy-done((bf16[216,1152]{1,0:T(8,128)(2,1)S(1)}, bf16[216,1152]{1,0:T(8,128)(2,1)}, u32[]{:S(2)}) %copy-start.6) | copy-done | bytes 497688
  34.3 1.0 %copy-done.9 = bf16[216,1152]{1,0:T(8,128)(2,1)S(1)} copy-done((bf16[216,1152]{1,0:T(8,128)(2,1)S(1)}, bf16[216,1152]{1,0:T(8,128)(2,1)}, u32[]{:S(2)}) %copy-start.9) | copy-done | bytes 497688
  35.3 5.0 %shard_map.103 = (bf16[128,640]{1,0:T(8,128)(2,1)S(1)}, bf16[128,640]{1,0:T(8,128)(2,1)S(1)}, bf16[128,640]{1,0:T(8,128)(2,1)S(1)}, f32[8,128,128]{2,1,0:T(8,128)S(1)}, bf16[128,576]{1,0:T(8,128)(2,1)S(1)}) custom-call(s32[3]{0:T(128)S(1)} %pad_add_fusion.idx, bf16[8,16,1152]{2,1,0:T(8,128)(2,1)S(1)} %all-to-all-done.packed, bf16[432,1152]{1,0:T(8,128)(2,1)S(1)} %bitcast.12, ...), custom_call_target="tpu_custom_call" | custom-call | flops 6899999744 | bytes 5439500 | tf_op jit(solution)/shard_map/pallas_call | solution.py:38
  43.1 2.2 %all-to-all-done.1.held_back = bf16[8,16,1728]{2,1,0:T(8,128)(2,1)S(1)} async-done(((bf16[8,16,1728]{2,1,0:T(8,128)(2,1)}), bf16[8,16,1728]{2,1,0:T(8,128)(2,1)S(1)}, u32[]{:S(2)}, u32[]{:S(2)}) %all-to-all-start.1) | async-done | bytes 442400 | tf_op jit(solution)/shard_map/all_to_all | solution.py:397
  45.3 1.0 %copy-done.4 = bf16[216,1152]{1,0:T(8,128)(2,1)S(1)} copy-done((bf16[216,1152]{1,0:T(8,128)(2,1)S(1)}, bf16[216,1152]{1,0:T(8,128)(2,1)}, u32[]{:S(2)}) %copy-start.4) | copy-done | bytes 497688
  46.3 1.0 %copy-done.7 = bf16[216,1152]{1,0:T(8,128)(2,1)S(1)} copy-done((bf16[216,1152]{1,0:T(8,128)(2,1)S(1)}, bf16[216,1152]{1,0:T(8,128)(2,1)}, u32[]{:S(2)}) %copy-start.7) | copy-done | bytes 497688
  47.3 1.0 %copy-done.10 = bf16[216,1152]{1,0:T(8,128)(2,1)S(1)} copy-done((bf16[216,1152]{1,0:T(8,128)(2,1)S(1)}, bf16[216,1152]{1,0:T(8,128)(2,1)}, u32[]{:S(2)}) %copy-start.10) | copy-done | bytes 497688
  48.4 1.0 %copy-done.12 = f32[8,128,128]{2,1,0:T(8,128)S(1)} copy-done((f32[8,128,128]{2,1,0:T(8,128)S(1)}, f32[8,128,128]{2,1,0:T(8,128)}, u32[]{:S(2)}) %copy-start.12) | copy-done | bytes 524312
  49.4 0.9 copy-done.14
  50.3 0.9 copy-done.16
  51.3 0.9 copy-done.18
  52.2 6.3 %shard_map.104 = (bf16[8,16,1728]{2,1,0:T(8,128)(2,1)}, bf16[128,3456]{1,0:T(8,128)(2,1)}) custom-call(s32[3]{0:T(128)S(1)} %pad_add_fusion.idx, bf16[128,640]{1,0:T(8,128)(2,1)S(1)} %get-tuple-element.36.q, bf16[128,640]{1,0:T(8,128)(2,1)S(1)} %copy-done.14, bf16[128,640]{1,0:T(8,128)(2,1)S(1)} %copy-done.16, f32[8,128,128]{2,1,0:T(8,128)S(1)} %copy-done.12, ...), custom_call_target="tpu_custom_call" | custom-call | flops 6899999744 | bytes 8241164 | tf_op jit(solution)/shard_map/pallas_call | solution.py:38
  58.4 3.7 %all-to-all-start.2 = ((bf16[8,16,1728]{2,1,0:T(8,128)(2,1)}), bf16[8,16,1728]{2,1,0:T(8,128)(2,1)S(1)}, u32[]{:S(2)}, u32[]{:S(2)}) async-start(bf16[8,16,1728]{2,1,0:T(8,128)(2,1)} %get-tuple-element.42), calls=%async_computation.2 | async-start | bytes 917504 | tf_op jit(solution)/shard_map/all_to_all | solution.py:397
  62.1 3.3 %shard_map.106 = (f32[2,72,1152]{2,1,0:T(8,128)S(1)}, bf16[2,72,1152]{2,1,0:T(8,128)(2,1)S(1)}, bf16[2,72,1152]{2,1,0:T(8,128)(2,1)S(1)}, bf16[2,72,1152]{2,1,0:T(8,128)(2,1)S(1)}) custom-call(s32[3]{0:T(128)S(1)} %pad_add_fusion.idx, bf16[128,3456]{1,0:T(8,128)(2,1)} %get-tuple-element.46.mine, bf16[128,3456]{1,0:T(8,128)(2,1)S(1)} %collective-permute-done.8.other), custom_call_target="tpu_custom_call" | custom-call | flops 3449999872 | bytes 3428364 | tf_op jit(solution)/shard_map/pallas_call | solution.py:38
  65.5 1.6 %collective-permute-start.9 = (bf16[2,72,1152]{2,1,0:T(8,128)(2,1)S(1)}, bf16[2,72,1152]{2,1,0:T(8,128)(2,1)S(1)}, u32[]{:S(2)}, u32[]{:S(2)}) collective-permute-start(bf16[2,72,1152]{2,1,0:T(8,128)(2,1)S(1)} %get-tuple-element.48), channel_id=1, source_target_pairs={{0,8},{8,0},{16,24},{24,16},{1,9},{9,1},{17,25},{25,17},{2,10},{10... | collective-permute-start | bytes 995336 | tf_op jit(solution)/shard_map/ppermute | solution.py:315
  67.0 1.4 %collective-permute-start.10 = (bf16[2,72,1152]{2,1,0:T(8,128)(2,1)S(1)}, bf16[2,72,1152]{2,1,0:T(8,128)(2,1)S(1)}, u32[]{:S(2)}, u32[]{:S(2)}) collective-permute-start(bf16[2,72,1152]{2,1,0:T(8,128)(2,1)S(1)} %get-tuple-element.49), channel_id=1, source_target_pairs={{0,16},{8,24},{16,0},{24,8},{1,17},{9,25},{17,1},{25,9},{2,18},{10... | collective-permute-start | bytes 995336 | tf_op jit(solution)/shard_map/ppermute | solution.py:315
  69.0 7.1 %collective-permute-done.9.refs_0_ = bf16[2,72,1152]{2,1,0:T(8,128)(2,1)S(1)} collective-permute-done((bf16[2,72,1152]{2,1,0:T(8,128)(2,1)S(1)}, bf16[2,72,1152]{2,1,0:T(8,128)(2,1)S(1)}, u32[]{:S(2)}, u32[]{:S(2)}) %collective-permute-start.9) | collective-permute-done | bytes 331808 | tf_op jit(solution)/shard_map/ppermute | solution.py:315
  76.1 7.9 %collective-permute-done.10.refs_1_ = bf16[2,72,1152]{2,1,0:T(8,128)(2,1)S(1)} collective-permute-done((bf16[2,72,1152]{2,1,0:T(8,128)(2,1)S(1)}, bf16[2,72,1152]{2,1,0:T(8,128)(2,1)S(1)}, u32[]{:S(2)}, u32[]{:S(2)}) %collective-permute-start.10) | collective-permute-done | bytes 331808 | tf_op jit(solution)/shard_map/ppermute | solution.py:315
  84.3 1.5 %collective-permute-start.12 = (bf16[2,72,288]{2,1,0:T(8,128)(2,1)S(1)}, bf16[2,72,288]{2,1,0:T(8,128)(2,1)S(1)}, u32[]{:S(2)}, u32[]{:S(2)}) collective-permute-start(bf16[2,72,288]{2,1,0:T(8,128)(2,1)S(1)} %get-tuple-element.52), channel_id=1, source_target_pairs={{0,2},{1,3},{2,0},{3,1},{4,6},{5,7},{6,4},{7,5},{8,10},{9,11},{10,... | collective-permute-start | bytes 248840 | tf_op jit(solution)/shard_map/ppermute | solution.py:315
  85.8 2.4 %collective-permute-start.13 = (bf16[2,72,288]{2,1,0:T(8,128)(2,1)S(1)}, bf16[2,72,288]{2,1,0:T(8,128)(2,1)S(1)}, u32[]{:S(2)}, u32[]{:S(2)}) collective-permute-start(bf16[2,72,288]{2,1,0:T(8,128)(2,1)S(1)} %get-tuple-element.53), channel_id=1, source_target_pairs={{0,4},{1,5},{2,6},{3,7},{4,0},{5,1},{6,2},{7,3},{8,12},{9,13},{10,... | collective-permute-start | bytes 248840 | tf_op jit(solution)/shard_map/ppermute | solution.py:315
  88.7 0.8 copy-done.19
  89.5 6.7 %shard_map.105 = (bf16[128,1152]{1,0:T(8,128)(2,1)}, bf16[128,1152]{1,0:T(8,128)(2,1)}, bf16[128,1728]{1,0:T(8,128)(2,1)}) custom-call(bf16[128,1728]{1,0:T(8,128)(2,1)} %bitcast.15, f32[8,128,128]{2,1,0:T(8,128)} %get-tuple-element.31.p_ref, bf16[128,1152]{1,0:T(8,128)(2,1)} %get-tuple-element.32.hid, bf16[576,1152]{1,0:T(8,128)(2,1)} %wos.1, ...), custom_call_target="tpu_custom_call" | custom-call | flops 6899999744 | bytes 5390336 | tf_op jit(solution)/shard_map/pallas_call | solution.py:38
  (55 shorter events, 8.3 us)
Async XLA Ops:
  1.7 14.6 %collective-permute-start.1 = (bf16[216,1152]{1,0:T(8,128)(2,1)S(1)}, bf16[216,1152]{1,0:T(8,128)(2,1)S(1)}, u32[]{:S(2)}, u32[]{:S(2)}) collective-permute-start(bf16[216,1152]{1,0:T(8,128)(2,1)S(1)} %dynamic-slice_bitcast_fusion), channel_id=1, source_target_pairs={{0,16},{8,24},{16,0},{24,8},{1,17},{9,25},{17,1},{25,9},{2,18},{10... | collective-permute-start | bytes 1493000 | tf_op jit(solution)/shard_map/ppermute | solution.py:315
  4.8 12.8 %collective-permute-start = (bf16[216,1152]{1,0:T(8,128)(2,1)S(1)}, bf16[216,1152]{1,0:T(8,128)(2,1)S(1)}, u32[]{:S(2)}, u32[]{:S(2)}) collective-permute-start(bf16[216,1152]{1,0:T(8,128)(2,1)S(1)} %dynamic-slice_bitcast_fusion), channel_id=1, source_target_pairs={{0,8},{8,0},{16,24},{24,16},{1,9},{9,1},{17,25},{25,17},{2,10},{10... | collective-permute-start | bytes 1493000 | tf_op jit(solution)/shard_map/ppermute | solution.py:315
  10.8 15.5 %all-to-all-start = ((bf16[8,16,1152]{2,1,0:T(8,128)(2,1)}), bf16[8,16,1152]{2,1,0:T(8,128)(2,1)S(1)}, u32[]{:S(2)}, u32[]{:S(2)}) async-start(bf16[8,16,1152]{2,1,0:T(8,128)(2,1)} %get-tuple-element.33), calls=%async_computation | async-start | bytes 589824 | tf_op jit(solution)/shard_map/all_to_all | solution.py:397
  16.4 15.8 %copy-start = (bf16[1152,432]{0,1:T(8,128)(2,1)S(1)}, bf16[1152,432]{0,1:T(8,128)(2,1)}, u32[]{:S(2)}) copy-start(bf16[1152,432]{0,1:T(8,128)(2,1)} %param.9) | copy-start | bytes 2985988
  16.4 1.7 %copy-start.2 = (bf16[216,1152]{1,0:T(8,128)(2,1)}, bf16[216,1152]{1,0:T(8,128)(2,1)S(1)}, u32[]{:S(2)}) copy-start(bf16[216,1152]{1,0:T(8,128)(2,1)S(1)} %collective-permute-done.1.near_y.refs_2_) | copy-start | bytes 1492996
  17.6 0.8 copy-start.5
  17.6 7.9 %collective-permute-start.3 = (bf16[216,640]{1,0:T(8,128)(2,1)S(1)}, bf16[216,640]{1,0:T(8,128)(2,1)S(1)}, u32[]{:S(2)}, u32[]{:S(2)}) collective-permute-start(bf16[216,640]{1,0:T(8,128)(2,1)S(1)} %get-tuple-element.35), channel_id=1, source_target_pairs={{0,16},{8,24},{16,0},{24,8},{1,17},{9,25},{17,1},{25,9},{2,18},{10... | collective-permute-start | bytes 829448 | tf_op jit(solution)/shard_map/ppermute | solution.py:315
  18.0 13.4 %collective-permute-start.5 = (bf16[216,1152]{1,0:T(8,128)(2,1)S(1)}, bf16[216,1152]{1,0:T(8,128)(2,1)S(1)}, u32[]{:S(2)}, u32[]{:S(2)}) collective-permute-start(bf16[216,1152]{1,0:T(8,128)(2,1)S(1)} %collective-permute-done.1.near_y.refs_2_), channel_id=1, source_target_pairs={{0,1},{1,0},{2,3},{3,2},{4,5},{5,4},{6,7},{7,6},{8,9},{9,8},{10,11... | collective-permute-start | bytes 1493000 | tf_op jit(solution)/shard_map/ppermute | solution.py:315
  18.4 13.8 %collective-permute-start.4 = (bf16[216,1152]{1,0:T(8,128)(2,1)S(1)}, bf16[216,1152]{1,0:T(8,128)(2,1)}, u32[]{:S(2)}, u32[]{:S(2)}) collective-permute-start(bf16[216,1152]{1,0:T(8,128)(2,1)S(1)} %collective-permute-done.near_x.refs_1_), channel_id=1, source_target_pairs={{0,1},{1,0},{2,3},{3,2},{4,5},{5,4},{6,7},{7,6},{8,9},{9,8},{10,11... | collective-permute-start | bytes 1493000 | tf_op jit(solution)/shard_map/ppermute | solution.py:315
  18.6 7.8 %collective-permute-start.2 = (bf16[216,512]{1,0:T(8,128)(2,1)S(1)}, bf16[216,512]{1,0:T(8,128)(2,1)}, u32[]{:S(2)}, u32[]{:S(2)}) collective-permute-start(bf16[216,512]{1,0:T(8,128)(2,1)S(1)} %get-tuple-element.34), channel_id=1, source_target_pairs={{0,8},{8,0},{16,24},{24,16},{1,9},{9,1},{17,25},{25,17},{2,10},{10... | collective-permute-start | bytes 663560 | tf_op jit(solution)/shard_map/ppermute | solution.py:315
  25.5 6.7 %collective-permute-start.7 = (bf16[216,640]{1,0:T(8,128)(2,1)S(1)}, bf16[216,640]{1,0:T(8,128)(2,1)}, u32[]{:S(2)}, u32[]{:S(2)}) collective-permute-start(bf16[216,640]{1,0:T(8,128)(2,1)S(1)} %collective-permute-done.3.refs_4_), channel_id=1, source_target_pairs={{0,1},{1,0},{2,3},{3,2},{4,5},{5,4},{6,7},{7,6},{8,9},{9,8},{10,11... | collective-permute-start | bytes 829448 | tf_op jit(solution)/shard_map/ppermute | solution.py:315
  26.3 5.1 %collective-permute-start.6 = (bf16[216,512]{1,0:T(8,128)(2,1)}, bf16[216,512]{1,0:T(8,128)(2,1)}, u32[]{:S(2)}, u32[]{:S(2)}) collective-permute-start(bf16[216,512]{1,0:T(8,128)(2,1)} %collective-permute-done.2.refs_3_), channel_id=1, source_target_pairs={{0,1},{1,0},{2,3},{3,2},{4,5},{5,4},{6,7},{7,6},{8,9},{9,8},{10,11... | collective-permute-start | bytes 663560 | tf_op jit(solution)/shard_map/ppermute | solution.py:315
  26.3 18.9 %all-to-all-start.1 = ((bf16[8,16,1728]{2,1,0:T(8,128)(2,1)}), bf16[8,16,1728]{2,1,0:T(8,128)(2,1)S(1)}, u32[]{:S(2)}, u32[]{:S(2)}) async-start(bf16[8,16,1728]{2,1,0:T(8,128)(2,1)} %get-tuple-element.41), calls=%async_computation.1 | async-start | bytes 917504 | tf_op jit(solution)/shard_map/all_to_all | solution.py:397
  32.2 1.0 %copy-start.3 = (bf16[216,1152]{1,0:T(8,128)(2,1)S(1)}, bf16[216,1152]{1,0:T(8,128)(2,1)}, u32[]{:S(2)}) copy-start(bf16[216,1152]{1,0:T(8,128)(2,1)} %copy-done.2) | copy-start | bytes 1492996
  33.2 1.0 %copy-start.6 = (bf16[216,1152]{1,0:T(8,128)(2,1)S(1)}, bf16[216,1152]{1,0:T(8,128)(2,1)}, u32[]{:S(2)}) copy-start(bf16[216,1152]{1,0:T(8,128)(2,1)} %copy-done.5) | copy-start | bytes 1492996
  34.3 1.0 %copy-start.9 = (bf16[216,1152]{1,0:T(8,128)(2,1)S(1)}, bf16[216,1152]{1,0:T(8,128)(2,1)}, u32[]{:S(2)}) copy-start(bf16[216,1152]{1,0:T(8,128)(2,1)} %copy-done.8) | copy-start | bytes 1492996
  35.3 10.0 %copy-start.1 = (bf16[576,1152]{1,0:T(8,128)(2,1)S(1)}, bf16[576,1152]{1,0:T(8,128)(2,1)}, u32[]{:S(2)}) copy-start(bf16[576,1152]{1,0:T(8,128)(2,1)} %wot.3) | copy-start | bytes 3981316
  45.3 1.0 %copy-start.4 = (bf16[216,1152]{1,0:T(8,128)(2,1)S(1)}, bf16[216,1152]{1,0:T(8,128)(2,1)}, u32[]{:S(2)}) copy-start(bf16[216,1152]{1,0:T(8,128)(2,1)} %copy-done.2) | copy-start | bytes 1492996
  46.3 1.0 %copy-start.7 = (bf16[216,1152]{1,0:T(8,128)(2,1)S(1)}, bf16[216,1152]{1,0:T(8,128)(2,1)}, u32[]{:S(2)}) copy-start(bf16[216,1152]{1,0:T(8,128)(2,1)} %copy-done.5) | copy-start | bytes 1492996
  47.3 1.0 %copy-start.10 = (bf16[216,1152]{1,0:T(8,128)(2,1)S(1)}, bf16[216,1152]{1,0:T(8,128)(2,1)}, u32[]{:S(2)}) copy-start(bf16[216,1152]{1,0:T(8,128)(2,1)} %copy-done.8) | copy-start | bytes 1492996
  48.4 1.0 %copy-start.12 = (f32[8,128,128]{2,1,0:T(8,128)S(1)}, f32[8,128,128]{2,1,0:T(8,128)}, u32[]{:S(2)}) copy-start(f32[8,128,128]{2,1,0:T(8,128)} %copy-done.11) | copy-start | bytes 1572868
  49.4 0.9 copy-start.14
  50.3 0.9 copy-start.16
  51.3 0.9 copy-start.18
  58.4 3.7 %collective-permute-start.8 = (bf16[128,3456]{1,0:T(8,128)(2,1)}, bf16[128,3456]{1,0:T(8,128)(2,1)S(1)}, u32[]{:S(2)}, u32[]{:S(2)}) collective-permute-start(bf16[128,3456]{1,0:T(8,128)(2,1)} %get-tuple-element.46.mine), channel_id=1, source_target_pairs={{0,1},{1,0},{2,3},{3,2},{4,5},{5,4},{6,7},{7,6},{8,9},{9,8},{10,11... | collective-permute-start | bytes 2654216 | tf_op jit(solution)/shard_map/ppermute | solution.py:315
  58.4 30.3 %all-to-all-start.2 = ((bf16[8,16,1728]{2,1,0:T(8,128)(2,1)}), bf16[8,16,1728]{2,1,0:T(8,128)(2,1)S(1)}, u32[]{:S(2)}, u32[]{:S(2)}) async-start(bf16[8,16,1728]{2,1,0:T(8,128)(2,1)} %get-tuple-element.42), calls=%async_computation.2 | async-start | bytes 917504 | tf_op jit(solution)/shard_map/all_to_all | solution.py:397
  65.5 10.7 %collective-permute-start.9 = (bf16[2,72,1152]{2,1,0:T(8,128)(2,1)S(1)}, bf16[2,72,1152]{2,1,0:T(8,128)(2,1)S(1)}, u32[]{:S(2)}, u32[]{:S(2)}) collective-permute-start(bf16[2,72,1152]{2,1,0:T(8,128)(2,1)S(1)} %get-tuple-element.48), channel_id=1, source_target_pairs={{0,8},{8,0},{16,24},{24,16},{1,9},{9,1},{17,25},{25,17},{2,10},{10... | collective-permute-start | bytes 995336 | tf_op jit(solution)/shard_map/ppermute | solution.py:315
  67.0 17.0 %collective-permute-start.10 = (bf16[2,72,1152]{2,1,0:T(8,128)(2,1)S(1)}, bf16[2,72,1152]{2,1,0:T(8,128)(2,1)S(1)}, u32[]{:S(2)}, u32[]{:S(2)}) collective-permute-start(bf16[2,72,1152]{2,1,0:T(8,128)(2,1)S(1)} %get-tuple-element.49), channel_id=1, source_target_pairs={{0,16},{8,24},{16,0},{24,8},{1,17},{9,25},{17,1},{25,9},{2,18},{10... | collective-permute-start | bytes 995336 | tf_op jit(solution)/shard_map/ppermute | solution.py:315
  68.4 15.6 %collective-permute-start.11 = (bf16[2,72,1152]{2,1,0:T(8,128)(2,1)S(1)}, bf16[2,72,1152]{2,1,0:T(8,128)(2,1)S(1)}, u32[]{:S(2)}, u32[]{:S(2)}) collective-permute-start(bf16[2,72,1152]{2,1,0:T(8,128)(2,1)S(1)} %get-tuple-element.50), channel_id=1, source_target_pairs={{0,24},{8,16},{16,8},{24,0},{1,25},{9,17},{17,9},{25,1},{2,26},{10... | collective-permute-start | bytes 995336 | tf_op jit(solution)/shard_map/ppermute | solution.py:315
  84.3 12.0 %collective-permute-start.12 = (bf16[2,72,288]{2,1,0:T(8,128)(2,1)S(1)}, bf16[2,72,288]{2,1,0:T(8,128)(2,1)S(1)}, u32[]{:S(2)}, u32[]{:S(2)}) collective-permute-start(bf16[2,72,288]{2,1,0:T(8,128)(2,1)S(1)} %get-tuple-element.52), channel_id=1, source_target_pairs={{0,2},{1,3},{2,0},{3,1},{4,6},{5,7},{6,4},{7,5},{8,10},{9,11},{10,... | collective-permute-start | bytes 248840 | tf_op jit(solution)/shard_map/ppermute | solution.py:315
  85.8 10.5 %collective-permute-start.13 = (bf16[2,72,288]{2,1,0:T(8,128)(2,1)S(1)}, bf16[2,72,288]{2,1,0:T(8,128)(2,1)S(1)}, u32[]{:S(2)}, u32[]{:S(2)}) collective-permute-start(bf16[2,72,288]{2,1,0:T(8,128)(2,1)S(1)} %get-tuple-element.53), channel_id=1, source_target_pairs={{0,4},{1,5},{2,6},{3,7},{4,0},{5,1},{6,2},{7,3},{8,12},{9,13},{10,... | collective-permute-start | bytes 248840 | tf_op jit(solution)/shard_map/ppermute | solution.py:315
  88.2 8.1 %collective-permute-start.14 = (bf16[2,72,288]{2,1,0:T(8,128)(2,1)S(1)}, bf16[2,72,288]{2,1,0:T(8,128)(2,1)S(1)}, u32[]{:S(2)}, u32[]{:S(2)}) collective-permute-start(bf16[2,72,288]{2,1,0:T(8,128)(2,1)S(1)} %get-tuple-element.54), channel_id=1, source_target_pairs={{0,6},{1,7},{2,4},{3,5},{4,2},{5,3},{6,0},{7,1},{8,14},{9,15},{10,... | collective-permute-start | bytes 248840 | tf_op jit(solution)/shard_map/ppermute | solution.py:315
  (6 other events, 4.4 us)

commit v4 on v3

--- a/solution.py
+++ b/solution.py
@@ -16,7 +16,7 @@
 VMEM = pl.BlockSpec(memory_space=pltpu.VMEM)
 SMEM = pl.BlockSpec(memory_space=pltpu.SMEM)
 HBM = pl.BlockSpec(memory_space=pltpu.HBM)
-LIMIT = 40 * 1024 * 1024
+LIMIT = 16 * 1024 * 1024
 MOST = 60 * 1024 * 1024
 
 
@@ -32,7 +32,7 @@
     return lax.dot_general(left, right, (((0,), (0,)), ((), ())), preferred_element_type=F32)
 
 
-def call(body, outs, args, scratch=(), us=1, far_in=(), far_out=()):
+def call(body, outs, args, scratch=(), us=1, far_in=(), far_out=(), small=False):
     moved = sum(math.prod(a.shape) * a.dtype.itemsize for a in (*args, *outs))
     near = [SMEM if a.dtype == jnp.int32 else VMEM for a in args]
     return pl.pallas_call(
@@ -41,7 +41,7 @@
         in_specs=[HBM if i in far_in else spec for i, spec in enumerate(near)],
         out_specs=[HBM if i in far_out else VMEM for i in range(len(outs))],
         scratch_shapes=list(scratch),
-        compiler_params=pltpu.CompilerParams(vmem_limit_bytes=MOST if far_in else LIMIT),
+        compiler_params=pltpu.CompilerParams(vmem_limit_bytes=LIMIT if small else MOST),
         cost_estimate=pl.CostEstimate(
             flops=us * 1150000000, bytes_accessed=moved, transcendentals=0
         ),
@@ -57,6 +57,9 @@
 
 def shape(dims, dtype=BF16):
     return jax.ShapeDtypeStruct(dims, dtype)
+
+
+TOKEN = shape((8, LANES), F32)
 
 
 def window(head):
@@ -129,40 +132,46 @@
     ref[:, :width] = value
 
 
-def chunks_of(value, peers, patches):
-    rows = value.shape[0]
+def pack(value, out, low, peers, patches):
+    rows, width = value.shape
     each = patches // peers
     value = value.astype(F32)
-    for at in range(peers):
-        low = at * each
-        cut = [value[low + f : low + f + each] for f in range(0, rows, patches)]
-        yield at, jnp.concatenate(cut, axis=0).astype(BF16)
+    cut = [
+        value[f + at * each : f + (at + 1) * each]
+        for at in range(peers)
+        for f in range(0, rows, patches)
+    ]
+    out[:, low : low + width] = jnp.concatenate(cut, axis=0).astype(BF16)
+
+
+def pack_kernel(peers, patches, tok_far, cot_far, out_far, tok, cot, out, sems):
+    width = tok.shape[1]
+    loads = started([(tok_far, tok), (cot_far, cot)], sems)
+    loads[0].wait()
+    pack(tok[...], out, 0, peers, patches)
+    loads[1].wait()
+    pack(cot[...], out, width, peers, patches)
+    started([(out, out_far)], sems.at[pl.ds(2, 1)])[0].wait()
 
 
 def spatial_kernel(peers, patches, *refs):
-    far, (hid_out, back_out, hid_far, p_far), refs = refs[:4], refs[4:8], refs[8:]
-    tok, cot, qkv, wos, ahead, behind, hid, p_ref, qs, ks, vs, sems = refs
-    width = tok.shape[1]
+    far, (packed_far, hid_far, p_far, done), refs = refs[:3], refs[3:7], refs[7:]
+    done[...] = jnp.zeros_like(done)
+    tok, qkv, wos, packed, hid, p_ref, qs, ks, vs, sems = refs
     inner = wos.shape[0]
-    loads = started(zip(far, (tok, cot, qkv, wos)), sems)
-    loads[2].wait()
+    loads = started(zip(far, (tok, qkv, wos)), sems)
+    loads[1].wait()
     x = qkv[...]
     put(qs, x[:, :inner])
     put(ks, x[:, inner : 2 * inner])
     put(vs, x[:, 2 * inner :])
     o = softmax_forward(qs, ks, vs, p_ref, inner // DH, ("block", patches))[:, :inner]
+    pack(o, packed, 0, peers, patches)
+    stores = started([(packed, packed_far), (p_ref, p_far)], sems.at[pl.ds(3, 2)])
     loads[0].wait()
-    loads[3].wait()
+    loads[2].wait()
     hid[...] = (tok[...].astype(F32) + dot(o, wos[...])).astype(BF16)
-    for at, rows in chunks_of(hid[...], peers, patches):
-        ahead[at] = rows
-    stores = started([(ahead, hid_out), (p_ref, p_far), (hid, hid_far)], sems.at[pl.ds(4, 3)])
-    loads[1].wait()
-    for at, rows in chunks_of(cot[...], peers, patches):
-        behind[at, :, :width] = rows
-    for at, rows in chunks_of(o, peers, patches):
-        behind[at, :, width:] = rows
-    stores += started([(behind, back_out)], sems.at[pl.ds(7, 1)])
+    stores += started([(hid, hid_far)], sems.at[pl.ds(5, 1)])
     for copy in stores:
         copy.wait()
 
@@ -173,26 +182,34 @@
     from_x[...] = near_x[:, cut:]
 
 
-def pieces(shards, weights):
-    weights = list(weights)
+def pieces(shards, weights, loads):
+    weights, loads = list(weights), list(loads)
     for place, count, parts in shards:
         low, held = 0, []
         for _ in range(parts):
             w = weights.pop(0)
+            loads.pop(0)()
             held.append((low, w))
             low += w.shape[1]
         yield place, count, held
 
 
-def temporal_forward_kernel(shards, total, group, inner, idx, packed, *refs):
-    weights, (q, k, v, p_ref, out, blocks, hid) = refs[:total], refs[total:]
-    chunk = packed.shape[1]
-    for at in range(packed.shape[0]):
-        hid[at * chunk : (at + 1) * chunk] = packed[at]
-    for place, count, held in pieces(shards, weights):
+def temporal_kernel(shards, total, group, idx, *refs):
+    far, (back_far, mine_far), refs = refs[: 4 + total], refs[4 + total : 6 + total], refs[6 + total :]
+    here, refs = refs[: 4 + total], refs[4 + total :]
+    back, mine, q, k, v, g, p_ref, blocks, sems = refs
+    (packed, so, wos, wot), weights = here[:4], here[4:]
+    inner, width = wos.shape
+    heads = inner // DH
+    loads = started(zip(far, here), sems)
+    for at in range(3):
+        loads[at].wait()
+    mine[:, inner : 2 * inner] = so[...]
+    hidden = (packed[:, :width].astype(F32) + dot(so[...], wos[...])).astype(BF16)
+    for place, count, held in pieces(shards, weights, [copy.wait for copy in loads[4:]]):
         block = None
         for low, w in held:
-            value = dot_bt(hid[:, low : low + w.shape[1]], w[...])
+            value = dot_bt(hidden[:, low : low + w.shape[1]], w[...])
             block = value if block is None else block + value
         block = block.astype(BF16)
         size = block.shape[1] // count
@@ -202,35 +219,27 @@
     put(q, whole[:, :inner])
     put(k, whole[:, inner : 2 * inner])
     put(v, whole[:, 2 * inner :])
-    out[...] = softmax_forward(q, k, v, p_ref, inner // DH, ("cycle", group))[:, :inner]
-
-
-def temporal_backward_kernel(shards, total, idx, q, k, v, p_ref, out, held_back, wot, *refs):
-    weights, (packed, mine, blocks, cot, g) = refs[:total], refs[total:]
-    inner, width = wot.shape
-    chunk = packed.shape[1]
-    for at in range(packed.shape[0]):
-        rows = slice(at * chunk, (at + 1) * chunk)
-        cot[rows] = held_back[at, :, :width]
-        mine[rows, inner : 2 * inner] = held_back[at, :, width:]
-    put(g, dot_bt(cot[...], wot[...]).astype(BF16))
-    dq, dk, dv = softmax_backward(q, k, v, g, p_ref, inner // DH)
+    out = softmax_forward(q, k, v, p_ref, heads, ("cycle", group))[:, :inner]
+    mine[:, :inner] = out
+    back[:, width:] = out
+    cot = packed[:, width:]
+    mine[:, 2 * inner : 2 * inner + width] = cot
+    loads[3].wait()
+    put(g, dot_bt(cot, wot[...]).astype(BF16))
+    dq, dk, dv = softmax_backward(q, k, v, g, p_ref, heads)
     whole = jnp.concatenate([dq[:, :inner], dk[:, :inner], dv[:, :inner]], axis=1)
     size = blocks.shape[2]
     for i in range(blocks.shape[0]):
         blocks[i] = whole[:, i * size : (i + 1) * size]
     grad = jnp.zeros(cot.shape, F32)
-    for place, count, held in pieces(shards, weights):
+    for place, count, held in pieces(shards, weights, [lambda: None] * total):
         lhs = jnp.concatenate([blocks[place(idx) + i] for i in range(count)], axis=1)
         grad += jnp.concatenate([dot(lhs, w[...]) for _, w in held], axis=1)
-    grad = (cot[...].astype(F32) + grad.astype(BF16).astype(F32)).astype(BF16)
-    for at in range(packed.shape[0]):
-        rows = slice(at * chunk, (at + 1) * chunk)
-        packed[at, :, :width] = grad[rows]
-        packed[at, :, width:] = out[rows]
-    mine[:, :inner] = out[...]
-    mine[:, 2 * inner : 2 * inner + width] = cot[...]
+    grad = (cot.astype(F32) + grad.astype(BF16).astype(F32)).astype(BF16)
+    back[:, :width] = grad
     mine[:, 2 * inner + width :] = grad
+    for copy in started([(back, back_far), (mine, mine_far)], sems.at[pl.ds(4 + total, 2)]):
+        copy.wait()
 
 
 def whole_parts_kernel(inner, width, mine, out):
@@ -264,7 +273,7 @@
                 outs[r - 1][i] = block.astype(BF16)
 
 
-def sum_dp_kernel(own, *refs):
+def sum_dp_kernel(_, own, *refs):
     got, outs = refs[: len(refs) // 2], refs[len(refs) // 2 :]
     for i in range(own.shape[0]):
         total = own[i]
@@ -284,31 +293,43 @@
         out[...] = total
 
 
-def last_kernel(patches, qkv, p_ref, hid, wos, wot, packed, block_out, out, grads, *refs):
-    here, (qs, ks, vs, gs, sems) = refs[:5], refs[5:]
-    loads = started(zip((wos, qkv, p_ref, wot, hid), here), sems)
-    wos, qkv, p_ref, wot, hid = here
+def last_kernel(patches, *refs):
+    far, outs_far, done, refs = refs[:6], refs[6:9], refs[9], refs[10:]
+    done[...] = jnp.zeros_like(done)
+    packed, wos, qkv, p_ref, wot, hid, out, block_out, grads, qs, ks, vs, gs, sems = refs
     inner, width = wos.shape
-    peers, chunk, _ = packed.shape
-    each = patches // peers
-    rows = [packed[at].astype(F32) for at in range(peers)]
-    rows = [rows[at][f * each : (f + 1) * each] for f in range(chunk // each) for at in range(peers)]
-    rows = jnp.concatenate(rows, axis=0).astype(BF16)
-    grad, attended = rows[:, :width], rows[:, width:]
+    loads = started(zip(far, refs[:6]), sems)
+    loads[0].wait()
+    rows = packed.shape[0]
+    each = rows // FRAMES
+    frames = rows // patches
+    value = packed[...].astype(F32)
+    cut = [
+        value[(at * frames + f) * each : (at * frames + f + 1) * each]
+        for f in range(frames)
+        for at in range(patches // each)
+    ]
+    value = jnp.concatenate(cut, axis=0).astype(BF16)
+    grad, attended = value[:, :width], value[:, width:]
     out[...] = grad
-    loads[0].wait()
+    stores = started([(out, outs_far[1])], sems.at[pl.ds(6, 1)])
+    loads[1].wait()
     put(gs, dot_bt(grad, wos[...]).astype(BF16))
-    loads[1].wait()
+    loads[2].wait()
     x = qkv[...]
     put(qs, x[:, :inner])
     put(ks, x[:, inner : 2 * inner])
     put(vs, x[:, 2 * inner :])
-    loads[2].wait()
+    loads[4].wait()
+    loads[5].wait()
+    block_out[...] = (hid[...].astype(F32) + dot(attended, wot[...])).astype(BF16)
+    stores += started([(block_out, outs_far[0])], sems.at[pl.ds(7, 1)])
+    loads[3].wait()
     dq, dk, dv = softmax_backward(qs, ks, vs, gs, p_ref, inner // DH)
     grads[...] = jnp.concatenate([dq[:, :inner], dk[:, :inner], dv[:, :inner]], axis=1)
-    loads[3].wait()
-    loads[4].wait()
-    block_out[...] = (hid[...].astype(F32) + dot(attended, wot[...])).astype(BF16)
+    stores += started([(grads, outs_far[2])], sems.at[pl.ds(8, 1)])
+    for copy in stores:
+        copy.wait()
 
 
 def flip(value, axis, bit):
@@ -324,7 +345,8 @@
     near = [flip(mine, "dp", 1), flip(mine, "dp", 2)]
     cut = width // LANES // 2 * LANES
     from_x, from_y = call(
-        split_kernel, [shape((half, width - cut)), shape((half, cut))], [*near, after]
+        split_kernel, [shape((half, width - cut)), shape((half, cut))], [*near, after],
+        small=True,
     )
     corner = [flip(from_y, "dp", 1), flip(from_x, "dp", 2)]
     held = near + corner
@@ -342,7 +364,7 @@
     return [weight, *held, *far], shards, 2 * n
 
 
-def reduced(mine, inner, width, idx):
+def reduced(mine, inner, width, idx, after):
     n_dp, n_seq = lax.axis_size("dp"), lax.axis_size("seq")
     if n_dp != 4 or n_seq != 8:
         (both,) = call(
@@ -363,14 +385,18 @@
             pltpu.VMEM((n_dp, 2 * rows, width // n_dp), BF16),
         ],
         us=3,
+        small=True,
     )
     got = [flip(value, "dp", r + 1) for r, value in enumerate(sends)]
     block = (2, size, width // n_dp)
     own, *sends = call(
-        sum_dp_kernel, [shape(block, F32)] + [shape(block)] * (n_dp - 1), [own, *got]
+        sum_dp_kernel,
+        [shape(block, F32)] + [shape(block)] * (n_dp - 1),
+        [after, own, *got],
+        small=True,
     )
     got = [flip(value, "seq", 2 * (q + 1)) for q, value in enumerate(sends)]
-    return call(sum_kernel, [shape(block[1:], F32)] * 2, [own, *got])
+    return call(sum_kernel, [shape(block[1:], F32)] * 2, [own, *got], small=True)
 
 
 def shards(tokens, spatial_qkv, wo_spatial, w_temporal, wo_temporal, cotangent):
@@ -380,15 +406,9 @@
     padded = -(-inner // LANES) * LANES
     rows = frames * patches
     peers = FRAMES // frames
-    each = patches // peers
-    chunk = rows // peers
     n_seq = lax.axis_size("seq")
     seq = lax.axis_index("seq")
     idx = jnp.stack([lax.axis_index("dp"), seq % 2, seq]).astype(jnp.int32)
-    wide = pltpu.VMEM((rows, padded), BF16)
-    weights_of = pltpu.VMEM((heads, rows, rows), F32)
-    model = pltpu.VMEM((rows, width), BF16)
-    projection = pltpu.VMEM((inner, width), BF16)
     groups = None
     if n_seq > peers:
         groups = [list(range(i, i + peers)) for i in range(0, n_seq, peers)]
@@ -398,48 +418,67 @@
             value, "seq", split_axis=0, concat_axis=0, tiled=True, axis_index_groups=groups
         )
 
+    def held(columns, dtype=BF16):
+        return pltpu.VMEM((rows, columns), dtype)
+
+    def sems(n):
+        return pltpu.SemaphoreType.DMA((n,))
+
+    wide = held(padded)
+    attended = pltpu.VMEM((heads, rows, rows), F32)
+    projection = pltpu.VMEM((inner, width), BF16)
+    token_rows = tokens.reshape(rows, width)
     qkv_rows = spatial_qkv.reshape(rows, 3 * inner)
-    ahead = (peers, chunk, width)
-    behind = (peers, chunk, width + inner)
-    ahead_sent, behind_sent, hidden, spatial_p = call(
+
+    (packed,) = call(
+        functools.partial(pack_kernel, peers, patches),
+        [shape((rows, 2 * width))],
+        [token_rows, cotangent.reshape(rows, width)],
+        [held(width), held(width), held(2 * width), sems(3)],
+        us=2,
+        far_in=range(2),
+        far_out=range(1),
+    )
+    spatial_sent, hidden, spatial_p, spatial_done = call(
         functools.partial(spatial_kernel, peers, patches),
-        [shape(ahead), shape(behind), shape((rows, width)), shape((heads, rows, rows), F32)],
-        [tokens.reshape(rows, width), cotangent.reshape(rows, width), qkv_rows, wo_spatial],
-        [model, model, pltpu.VMEM((rows, 3 * inner), BF16), projection]
-        + [pltpu.VMEM(ahead, BF16), pltpu.VMEM(behind, BF16), model, weights_of]
+        [shape((rows, inner)), shape((rows, width)), shape((heads, rows, rows), F32), TOKEN],
+        [token_rows, qkv_rows, wo_spatial],
+        [held(width), held(3 * inner), projection, held(inner), held(width), attended]
         + [wide] * 3
-        + [pltpu.SemaphoreType.DMA((8,))],
-        us=3,
-        far_in=range(4),
-        far_out=range(4),
-    )
-    weights, places, count = gather_weight(w_temporal.T, seq % 2, hidden[:8, :LANES])
+        + [sems(6)],
+        us=4,
+        far_in=range(3),
+        far_out=range(3),
+    )
+    weights, places, count = gather_weight(w_temporal.T, seq % 2, spatial_done)
     blocks = pltpu.VMEM((count, rows, 3 * inner // count), BF16)
-    q, k, v, temporal_p, out = call(
-        functools.partial(temporal_forward_kernel, places, len(weights), each, inner),
-        [shape((rows, padded))] * 3 + [shape((heads, rows, rows), F32), shape((rows, inner))],
-        [idx, exchange(ahead_sent), *weights],
-        [blocks, model],
+    total = len(weights)
+    back, mine = call(
+        functools.partial(temporal_kernel, places, total, patches // peers),
+        [shape((rows, width + inner)), shape((rows, 2 * (inner + width)))],
+        [idx, exchange(packed), exchange(spatial_sent), wo_spatial, wo_temporal, *weights],
+        [held(2 * width), held(inner), projection, projection]
+        + [pltpu.VMEM(w.shape, BF16) for w in weights]
+        + [held(width + inner), held(2 * (inner + width))]
+        + [wide] * 4
+        + [attended, blocks, sems(6 + total)],
+        us=10,
+        far_in=range(1, 5 + total),
+        far_out=range(2),
+    )
+    block_out, tokens_grad, qkv_grad, last_done = call(
+        functools.partial(last_kernel, patches),
+        [shape((rows, width)), shape((rows, width)), shape((rows, 3 * inner)), TOKEN],
+        [exchange(back), wo_spatial, qkv_rows, spatial_p, wo_temporal, hidden],
+        [held(width + inner), projection, held(3 * inner), attended, projection, held(width)]
+        + [held(width), held(width), held(3 * inner)]
+        + [wide] * 4
+        + [sems(9)],
         us=6,
-    )
-    back, mine = call(
-        functools.partial(temporal_backward_kernel, places, len(weights)),
-        [shape(behind), shape((rows, 2 * (inner + width)))],
-        [idx, q, k, v, temporal_p, out, exchange(behind_sent), wo_temporal, *weights],
-        [blocks, model, wide],
-        us=6,
-    )
-    block_out, tokens_grad, qkv_grad = call(
-        functools.partial(last_kernel, patches),
-        [shape((rows, width)), shape((rows, width)), shape((rows, 3 * inner))],
-        [qkv_rows, spatial_p, hidden, wo_spatial, wo_temporal, exchange(back)],
-        [projection, pltpu.VMEM((rows, 3 * inner), BF16), weights_of, projection, model]
-        + [wide] * 4
-        + [pltpu.SemaphoreType.DMA((5,))],
-        us=6,
-        far_in=range(5),
-    )
-    temporal_grad, spatial_grad = reduced(mine, inner, width, idx)
+        far_in=range(6),
+        far_out=range(3),
+    )
+    temporal_grad, spatial_grad = reduced(mine, inner, width, idx, last_done)
     return (
         block_out.reshape(frames, patches, width),
         tokens_grad.reshape(frames, patches, width),

time: 98 us -> 94.4 us (0.963)
  local copies, waits for them, and re-layouts: 16.4 us -> 2.95 us
  waiting for transfers between devices: 24.5 us -> 31.5 us
  Pallas kernels: 26.9 us -> 30.1 us
    unnamed x40 -> x28, local copies, waits for them, and re-layouts: 14.7 us -> 2.91 us
    all_to_all x3, waiting for transfers between devices: 2.18 us -> 10.5 us  [exchange(): lax.all_to_all(value, 'seq', split_axis=0, concat_axis=0, tiled=True, axi...]
    pallas_call x8, Pallas kernels: 26.9 us -> 30.1 us  [call(): pl.pallas_call(body, out_shape=outs, in_specs=[HBM if i in far_in else sp...]
    ppermute x15, waiting for transfers between devices: 22.3 us -> 21 us  [flip(): lax.ppermute(value, axis, [(i, i ^ bit) for i in range(lax.axis_size(axis...]
    ppermute x15, starting transfers between devices: 14.8 us -> 13.6 us  [flip(): lax.ppermute(value, axis, [(i, i ^ bit) for i in range(lax.axis_size(axis...]
    dynamic_slice x1, local copies, waits for them, and re-layouts: 1.08 us -> 0.05 us  [gather_weight(): mine = lax.dynamic_slice_in_dim(weight, core * half, half, 0)]
  transfers between devices with their start and end apart: 18 -> 18, of which waited for: 6 -> 11; matrix products, arithmetic and copies ran while one was open for 1% -> 1% of each run, Pallas kernels for 20% -> 12%
where the time goes in v4:
time: 94.4 us; the launch traced here: 93.9 us
  waiting for transfers between devices  31.5 us (33%)
  Pallas kernels  30.1 us (32%)
  starting transfers between devices  27.8 us (29%)
  local copies, waits for them, and re-layouts  2.95 us (3%)
    pallas_call x8, Pallas kernels, call(): pl.pallas_call(body, out_shape=outs, in_specs=[HBM if i in far_in else sp...  30.1 us
    ppermute x15, waiting for transfers between devices, flip(): lax.ppermute(value, axis, [(i, i ^ bit) for i in range(lax.axis_size(axis...  21 us
    all_to_all x3, starting transfers between devices, exchange(): lax.all_to_all(value, 'seq', split_axis=0, concat_axis=0, tiled=True, axi...  14.2 us
    ppermute x15, starting transfers between devices, flip(): lax.ppermute(value, axis, [(i, i ^ bit) for i in range(lax.axis_size(axis...  13.6 us
    all_to_all x3, waiting for transfers between devices, exchange(): lax.all_to_all(value, 'seq', split_axis=0, concat_axis=0, tiled=True, axi...  10.5 us
    unnamed x28, local copies, waits for them, and re-layouts  2.91 us
  transfers between devices with their start and end apart: 18, of which 11 were waited for; matrix products, arithmetic and copies ran while one was open for 1% of the time, Pallas kernels for 12%

profile of v4, /device:TPU:0, one launch (start us, length us, event | category | flops | bytes accessed | tf_op | source)
XLA Modules:
  0.0 93.9 jit_solution(18128718843313354784)
XLA Ops:
  0.6 4.7 %shard_map.102 = (bf16[128,576]{1,0:T(8,128)(2,1)}, bf16[128,1152]{1,0:T(8,128)(2,1)}, f32[8,128,128]{2,1,0:T(8,128)}, f32[8,128]{1,0:T(8,128)}) custom-call(bf16[128,1152]{1,0:T(8,128)(2,1)} %bitcast.26, bf16[128,1728]{1,0:T(8,128)(2,1)} %bitcast.24, bf16[576,1152]{1,0:T(8,128)(2,1)} %refs_1_.1), custom_call_target="tpu_custom_call" | custom-call | flops 4600000000 | bytes 3035136 | tf_op jit(solution)/shard_map/pallas_call | solution.py:38
  5.3 6.3 %all-to-all-start.1 = ((bf16[8,16,576]{2,1,0:T(8,128)(2,1)}), bf16[8,16,576]{2,1,0:T(8,128)(2,1)S(1)}, u32[]{:S(2)}, u32[]{:S(2)}) async-start(bf16[8,16,576]{2,1,0:T(8,128)(2,1)} %bitcast.23), calls=%async_computation.1 | async-start | bytes 327680 | tf_op jit(solution)/shard_map/all_to_all | solution.py:417
  11.7 1.6 %collective-permute-start.1 = (bf16[216,1152]{1,0:T(8,128)(2,1)S(1)}, bf16[216,1152]{1,0:T(8,128)(2,1)S(1)}, u32[]{:S(2)}, u32[]{:S(2)}) collective-permute-start(bf16[216,1152]{1,0:T(8,128)(2,1)S(1)} %dynamic-slice_bitcast_fusion), channel_id=1, source_target_pairs={{0,16},{8,24},{16,0},{24,8},{1,17},{9,25},{17,1},{25,9},{2,18},{10... | collective-permute-start | bytes 1493000 | tf_op jit(solution)/shard_map/ppermute | solution.py:336
  13.3 1.5 %collective-permute-start = (bf16[216,1152]{1,0:T(8,128)(2,1)S(1)}, bf16[216,1152]{1,0:T(8,128)(2,1)S(1)}, u32[]{:S(2)}, u32[]{:S(2)}) collective-permute-start(bf16[216,1152]{1,0:T(8,128)(2,1)S(1)} %dynamic-slice_bitcast_fusion), channel_id=1, source_target_pairs={{0,8},{8,0},{16,24},{24,16},{1,9},{9,1},{17,25},{25,17},{2,10},{10... | collective-permute-start | bytes 1493000 | tf_op jit(solution)/shard_map/ppermute | solution.py:336
  14.8 1.9 %shard_map.101 = bf16[128,2304]{1,0:T(8,128)(2,1)} custom-call(bf16[128,1152]{1,0:T(8,128)(2,1)} %bitcast.27, bf16[128,1152]{1,0:T(8,128)(2,1)} %bitcast.28), custom_call_target="tpu_custom_call" | custom-call | flops 2300000000 | bytes 1179648 | tf_op jit(solution)/shard_map/pallas_call | solution.py:38
  16.7 2.1 %all-to-all-done.1 = bf16[8,16,576]{2,1,0:T(8,128)(2,1)S(1)} async-done(((bf16[8,16,576]{2,1,0:T(8,128)(2,1)}), bf16[8,16,576]{2,1,0:T(8,128)(2,1)S(1)}, u32[]{:S(2)}, u32[]{:S(2)}) %all-to-all-start.1) | async-done | bytes 147488 | tf_op jit(solution)/shard_map/all_to_all | solution.py:417
  18.9 3.5 %all-to-all-start = ((bf16[8,16,2304]{2,1,0:T(8,128)(2,1)}), bf16[8,16,2304]{2,1,0:T(8,128)(2,1)S(1)}, u32[]{:S(2)}, u32[]{:S(2)}) async-start(bf16[8,16,2304]{2,1,0:T(8,128)(2,1)} %bitcast.19), calls=%async_computation | async-start | bytes 1179648 | tf_op jit(solution)/shard_map/all_to_all | solution.py:417
  22.4 3.1 %collective-permute-done.1.near_y.refs_6_ = bf16[216,1152]{1,0:T(8,128)(2,1)S(1)} collective-permute-done((bf16[216,1152]{1,0:T(8,128)(2,1)S(1)}, bf16[216,1152]{1,0:T(8,128)(2,1)S(1)}, u32[]{:S(2)}, u32[]{:S(2)}) %collective-permute-start.1) | collective-permute-done | bytes 497696 | tf_op jit(solution)/shard_map/ppermute | solution.py:336
  25.5 1.2 %collective-permute-done.near_x.refs_5_ = bf16[216,1152]{1,0:T(8,128)(2,1)S(1)} collective-permute-done((bf16[216,1152]{1,0:T(8,128)(2,1)S(1)}, bf16[216,1152]{1,0:T(8,128)(2,1)S(1)}, u32[]{:S(2)}, u32[]{:S(2)}) %collective-permute-start) | collective-permute-done | bytes 497696 | tf_op jit(solution)/shard_map/ppermute | solution.py:336
  27.9 1.5 %collective-permute-start.2 = (bf16[216,512]{1,0:T(8,128)(2,1)S(1)}, bf16[216,512]{1,0:T(8,128)(2,1)S(1)}, u32[]{:S(2)}, u32[]{:S(2)}) collective-permute-start(bf16[216,512]{1,0:T(8,128)(2,1)S(1)} %get-tuple-element.29), channel_id=1, source_target_pairs={{0,8},{8,0},{16,24},{24,16},{1,9},{9,1},{17,25},{25,17},{2,10},{10... | collective-permute-start | bytes 663560 | tf_op jit(solution)/shard_map/ppermute | solution.py:336
  29.4 5.4 %collective-permute-done.3.refs_8_ = bf16[216,640]{1,0:T(8,128)(2,1)S(1)} collective-permute-done((bf16[216,640]{1,0:T(8,128)(2,1)S(1)}, bf16[216,640]{1,0:T(8,128)(2,1)S(1)}, u32[]{:S(2)}, u32[]{:S(2)}) %collective-permute-start.3) | collective-permute-done | bytes 276512 | tf_op jit(solution)/shard_map/ppermute | solution.py:336
  34.8 0.6 collective-permute-done.2.refs_7_
  35.4 0.7 pad_add_fusion.idx
  36.1 0.9 collective-permute-done.6.refs_11_
  37.1 2.1 %all-to-all-done = bf16[8,16,2304]{2,1,0:T(8,128)(2,1)S(1)} async-done(((bf16[8,16,2304]{2,1,0:T(8,128)(2,1)}), bf16[8,16,2304]{2,1,0:T(8,128)(2,1)S(1)}, u32[]{:S(2)}, u32[]{:S(2)}) %all-to-all-start) | async-done | bytes 589856 | tf_op jit(solution)/shard_map/all_to_all | solution.py:417
  39.2 0.8 copy-done.6
  40.0 13.3 %shard_map.104 = (bf16[128,1728]{1,0:T(8,128)(2,1)}, bf16[128,3456]{1,0:T(8,128)(2,1)}) custom-call(s32[3]{0:T(128)} %pad_add_fusion.idx, bf16[128,2304]{1,0:T(8,128)(2,1)} %bitcast.18, bf16[128,576]{1,0:T(8,128)(2,1)} %bitcast.22, bf16[576,1152]{1,0:T(8,128)(2,1)} %refs_1_.1, bf16[576,1152]{1,0:T(8,128)(2,1)} %refs_4_.1, bf16[432,1152]{1,0:T(8,128)(2,1)} %bitcast.21, ...), custom_call_target="tpu_custom_call" | custom-call | flops 11500000256 | bytes 8699916 | tf_op jit(solution)/shard_map/pallas_call | solution.py:38
  53.4 4.3 %all-to-all-start.2 = ((bf16[8,16,1728]{2,1,0:T(8,128)(2,1)}), bf16[8,16,1728]{2,1,0:T(8,128)(2,1)}, u32[]{:S(2)}, u32[]{:S(2)}) async-start(bf16[8,16,1728]{2,1,0:T(8,128)(2,1)} %bitcast.20), calls=%async_computation.2 | async-start | bytes 917504 | tf_op jit(solution)/shard_map/all_to_all | solution.py:417
  57.7 1.2 %copy-done.1 = bf16[128,3456]{1,0:T(8,128)(2,1)S(1)} copy-done((bf16[128,3456]{1,0:T(8,128)(2,1)S(1)}, bf16[128,3456]{1,0:T(8,128)(2,1)}, u32[]{:S(2)}) %copy-start.1) | copy-done | bytes 884760
  58.9 2.7 %shard_map.106 = (f32[2,72,1152]{2,1,0:T(8,128)S(1)}, bf16[2,72,1152]{2,1,0:T(8,128)(2,1)S(1)}, bf16[2,72,1152]{2,1,0:T(8,128)(2,1)S(1)}, bf16[2,72,1152]{2,1,0:T(8,128)(2,1)S(1)}) custom-call(s32[3]{0:T(128)S(1)} %copy-done, bf16[128,3456]{1,0:T(8,128)(2,1)S(1)} %copy-done.1, bf16[128,3456]{1,0:T(8,128)(2,1)S(1)} %collective-permute-done.8.other), custom_call_target="tpu_custom_call" | custom-call | flops 3449999872 | bytes 3428364 | tf_op jit(solution)/shard_map/pallas_call | solution.py:38
  61.6 1.5 %collective-permute-start.9 = (bf16[2,72,1152]{2,1,0:T(8,128)(2,1)S(1)}, bf16[2,72,1152]{2,1,0:T(8,128)(2,1)S(1)}, u32[]{:S(2)}, u32[]{:S(2)}) collective-permute-start(bf16[2,72,1152]{2,1,0:T(8,128)(2,1)S(1)} %get-tuple-element.40), channel_id=1, source_target_pairs={{0,8},{8,0},{16,24},{24,16},{1,9},{9,1},{17,25},{25,17},{2,10},{10... | collective-permute-start | bytes 995336 | tf_op jit(solution)/shard_map/ppermute | solution.py:336
  63.1 1.5 %collective-permute-start.10 = (bf16[2,72,1152]{2,1,0:T(8,128)(2,1)S(1)}, bf16[2,72,1152]{2,1,0:T(8,128)(2,1)S(1)}, u32[]{:S(2)}, u32[]{:S(2)}) collective-permute-start(bf16[2,72,1152]{2,1,0:T(8,128)(2,1)S(1)} %get-tuple-element.41), channel_id=1, source_target_pairs={{0,16},{8,24},{16,0},{24,8},{1,17},{9,25},{17,1},{25,9},{2,18},{10... | collective-permute-start | bytes 995336 | tf_op jit(solution)/shard_map/ppermute | solution.py:336
  65.1 6.3 %all-to-all-done.2 = bf16[8,16,1728]{2,1,0:T(8,128)(2,1)} async-done(((bf16[8,16,1728]{2,1,0:T(8,128)(2,1)}), bf16[8,16,1728]{2,1,0:T(8,128)(2,1)}, u32[]{:S(2)}, u32[]{:S(2)}) %all-to-all-start.2) | async-done | bytes 442400 | tf_op jit(solution)/shard_map/all_to_all | solution.py:417
  71.5 6.6 %shard_map.105 = (bf16[128,1152]{1,0:T(8,128)(2,1)}, bf16[128,1152]{1,0:T(8,128)(2,1)}, bf16[128,1728]{1,0:T(8,128)(2,1)}, f32[8,128]{1,0:T(8,128)}) custom-call(bf16[128,1728]{1,0:T(8,128)(2,1)} %bitcast.13.refs_0_, bf16[576,1152]{1,0:T(8,128)(2,1)} %refs_1_.1, bf16[128,1728]{1,0:T(8,128)(2,1)} %bitcast.25, f32[8,128,128]{2,1,0:T(8,128)} %get-tuple-element.32.refs_3_, ...), custom_call_target="tpu_custom_call" | custom-call | flops 6899999744 | bytes 5394432 | tf_op jit(solution)/shard_map/pallas_call | solution.py:38
  78.1 2.0 %collective-permute-done.10.refs_1_ = bf16[2,72,1152]{2,1,0:T(8,128)(2,1)S(1)} collective-permute-done((bf16[2,72,1152]{2,1,0:T(8,128)(2,1)S(1)}, bf16[2,72,1152]{2,1,0:T(8,128)(2,1)S(1)}, u32[]{:S(2)}, u32[]{:S(2)}) %collective-permute-start.10) | collective-permute-done | bytes 331808 | tf_op jit(solution)/shard_map/ppermute | solution.py:336
  80.1 0.7 copy-done.4
  81.0 1.5 %collective-permute-start.12 = (bf16[2,72,288]{2,1,0:T(8,128)(2,1)S(1)}, bf16[2,72,288]{2,1,0:T(8,128)(2,1)S(1)}, u32[]{:S(2)}, u32[]{:S(2)}) collective-permute-start(bf16[2,72,288]{2,1,0:T(8,128)(2,1)S(1)} %get-tuple-element.44), channel_id=1, source_target_pairs={{0,2},{1,3},{2,0},{3,1},{4,6},{5,7},{6,4},{7,5},{8,10},{9,11},{10,... | collective-permute-start | bytes 248840 | tf_op jit(solution)/shard_map/ppermute | solution.py:336
  82.5 2.4 %collective-permute-start.13 = (bf16[2,72,288]{2,1,0:T(8,128)(2,1)S(1)}, bf16[2,72,288]{2,1,0:T(8,128)(2,1)S(1)}, u32[]{:S(2)}, u32[]{:S(2)}) collective-permute-start(bf16[2,72,288]{2,1,0:T(8,128)(2,1)S(1)} %get-tuple-element.45), channel_id=1, source_target_pairs={{0,4},{1,5},{2,6},{3,7},{4,0},{5,1},{6,2},{7,3},{8,12},{9,13},{10,... | collective-permute-start | bytes 248840 | tf_op jit(solution)/shard_map/ppermute | solution.py:336
  84.9 0.6 collective-permute-start.14
  85.5 1.5 %collective-permute-done.12.refs_0_ = bf16[2,72,288]{2,1,0:T(8,128)(2,1)S(1)} collective-permute-done((bf16[2,72,288]{2,1,0:T(8,128)(2,1)S(1)}, bf16[2,72,288]{2,1,0:T(8,128)(2,1)S(1)}, u32[]{:S(2)}, u32[]{:S(2)}) %collective-permute-start.12) | collective-permute-done | bytes 82976 | tf_op jit(solution)/shard_map/ppermute | solution.py:336
  87.0 6.1 %collective-permute-done.13.refs_1_ = bf16[2,72,288]{2,1,0:T(8,128)(2,1)S(1)} collective-permute-done((bf16[2,72,288]{2,1,0:T(8,128)(2,1)S(1)}, bf16[2,72,288]{2,1,0:T(8,128)(2,1)S(1)}, u32[]{:S(2)}, u32[]{:S(2)}) %collective-permute-start.13) | collective-permute-done | bytes 82976 | tf_op jit(solution)/shard_map/ppermute | solution.py:336
  93.2 0.7 shard_map.108
  (42 shorter events, 2.1 us)
Async XLA Ops:
  0.6 11.0 %copy-start.7 = (bf16[1152,432]{0,1:T(8,128)(2,1)S(1)}, bf16[1152,432]{0,1:T(8,128)(2,1)}, u32[]{:S(2)}) copy-start(bf16[1152,432]{0,1:T(8,128)(2,1)} %param.9) | copy-start | bytes 2985988
  5.3 13.6 %all-to-all-start.1 = ((bf16[8,16,576]{2,1,0:T(8,128)(2,1)}), bf16[8,16,576]{2,1,0:T(8,128)(2,1)S(1)}, u32[]{:S(2)}, u32[]{:S(2)}) async-start(bf16[8,16,576]{2,1,0:T(8,128)(2,1)} %bitcast.23), calls=%async_computation.1 | async-start | bytes 327680 | tf_op jit(solution)/shard_map/all_to_all | solution.py:417
  11.7 13.8 %collective-permute-start.1 = (bf16[216,1152]{1,0:T(8,128)(2,1)S(1)}, bf16[216,1152]{1,0:T(8,128)(2,1)S(1)}, u32[]{:S(2)}, u32[]{:S(2)}) collective-permute-start(bf16[216,1152]{1,0:T(8,128)(2,1)S(1)} %dynamic-slice_bitcast_fusion), channel_id=1, source_target_pairs={{0,16},{8,24},{16,0},{24,8},{1,17},{9,25},{17,1},{25,9},{2,18},{10... | collective-permute-start | bytes 1493000 | tf_op jit(solution)/shard_map/ppermute | solution.py:336
  13.3 13.5 %collective-permute-start = (bf16[216,1152]{1,0:T(8,128)(2,1)S(1)}, bf16[216,1152]{1,0:T(8,128)(2,1)S(1)}, u32[]{:S(2)}, u32[]{:S(2)}) collective-permute-start(bf16[216,1152]{1,0:T(8,128)(2,1)S(1)} %dynamic-slice_bitcast_fusion), channel_id=1, source_target_pairs={{0,8},{8,0},{16,24},{24,16},{1,9},{9,1},{17,25},{25,17},{2,10},{10... | collective-permute-start | bytes 1493000 | tf_op jit(solution)/shard_map/ppermute | solution.py:336
  14.8 12.0 %copy-start.5 = (f32[8,128]{1,0:T(8,128)S(1)}, f32[8,128]{1,0:T(8,128)}, u32[]{:S(2)}) copy-start(f32[8,128]{1,0:T(8,128)} %get-tuple-element.28._) | copy-start | bytes 12292
  18.9 7.9 %copy-start.8 = (bf16[8,16,576]{2,1,0:T(8,128)(2,1)}, bf16[8,16,576]{2,1,0:T(8,128)(2,1)S(1)}, u32[]{:S(2)}) copy-start(bf16[8,16,576]{2,1,0:T(8,128)(2,1)S(1)} %all-to-all-done.1) | copy-start | bytes 442372
  18.9 20.2 %all-to-all-start = ((bf16[8,16,2304]{2,1,0:T(8,128)(2,1)}), bf16[8,16,2304]{2,1,0:T(8,128)(2,1)S(1)}, u32[]{:S(2)}, u32[]{:S(2)}) async-start(bf16[8,16,2304]{2,1,0:T(8,128)(2,1)} %bitcast.19), calls=%async_computation | async-start | bytes 1179648 | tf_op jit(solution)/shard_map/all_to_all | solution.py:417
  25.5 1.9 %copy-start.2 = (bf16[216,1152]{1,0:T(8,128)(2,1)}, bf16[216,1152]{1,0:T(8,128)(2,1)S(1)}, u32[]{:S(2)}) copy-start(bf16[216,1152]{1,0:T(8,128)(2,1)S(1)} %collective-permute-done.1.near_y.refs_6_) | copy-start | bytes 1492996
  26.8 0.8 copy-start.3
  26.8 8.0 %collective-permute-start.3 = (bf16[216,640]{1,0:T(8,128)(2,1)S(1)}, bf16[216,640]{1,0:T(8,128)(2,1)S(1)}, u32[]{:S(2)}, u32[]{:S(2)}) collective-permute-start(bf16[216,640]{1,0:T(8,128)(2,1)S(1)} %get-tuple-element.30), channel_id=1, source_target_pairs={{0,16},{8,24},{16,0},{24,8},{1,17},{9,25},{17,1},{25,9},{2,18},{10... | collective-permute-start | bytes 829448 | tf_op jit(solution)/shard_map/ppermute | solution.py:336
  27.4 9.6 %collective-permute-start.5 = (bf16[216,1152]{1,0:T(8,128)(2,1)S(1)}, bf16[216,1152]{1,0:T(8,128)(2,1)S(1)}, u32[]{:S(2)}, u32[]{:S(2)}) collective-permute-start(bf16[216,1152]{1,0:T(8,128)(2,1)S(1)} %collective-permute-done.1.near_y.refs_6_), channel_id=1, source_target_pairs={{0,1},{1,0},{2,3},{3,2},{4,5},{5,4},{6,7},{7,6},{8,9},{9,8},{10,11... | collective-permute-start | bytes 1493000 | tf_op jit(solution)/shard_map/ppermute | solution.py:336
  27.6 9.5 %collective-permute-start.4 = (bf16[216,1152]{1,0:T(8,128)(2,1)S(1)}, bf16[216,1152]{1,0:T(8,128)(2,1)S(1)}, u32[]{:S(2)}, u32[]{:S(2)}) collective-permute-start(bf16[216,1152]{1,0:T(8,128)(2,1)S(1)} %collective-permute-done.near_x.refs_5_), channel_id=1, source_target_pairs={{0,1},{1,0},{2,3},{3,2},{4,5},{5,4},{6,7},{7,6},{8,9},{9,8},{10,11... | collective-permute-start | bytes 1493000 | tf_op jit(solution)/shard_map/ppermute | solution.py:336
  27.9 7.5 %collective-permute-start.2 = (bf16[216,512]{1,0:T(8,128)(2,1)S(1)}, bf16[216,512]{1,0:T(8,128)(2,1)S(1)}, u32[]{:S(2)}, u32[]{:S(2)}) collective-permute-start(bf16[216,512]{1,0:T(8,128)(2,1)S(1)} %get-tuple-element.29), channel_id=1, source_target_pairs={{0,8},{8,0},{16,24},{24,16},{1,9},{9,1},{17,25},{25,17},{2,10},{10... | collective-permute-start | bytes 663560 | tf_op jit(solution)/shard_map/ppermute | solution.py:336
  34.8 4.3 %copy-start.11 = (bf16[216,640]{1,0:T(8,128)(2,1)}, bf16[216,640]{1,0:T(8,128)(2,1)S(1)}, u32[]{:S(2)}) copy-start(bf16[216,640]{1,0:T(8,128)(2,1)S(1)} %collective-permute-done.3.refs_8_) | copy-start | bytes 829444
  34.8 4.3 %collective-permute-start.7 = (bf16[216,640]{1,0:T(8,128)(2,1)S(1)}, bf16[216,640]{1,0:T(8,128)(2,1)S(1)}, u32[]{:S(2)}, u32[]{:S(2)}) collective-permute-start(bf16[216,640]{1,0:T(8,128)(2,1)S(1)} %collective-permute-done.3.refs_8_), channel_id=1, source_target_pairs={{0,1},{1,0},{2,3},{3,2},{4,5},{5,4},{6,7},{7,6},{8,9},{9,8},{10,11... | collective-permute-start | bytes 829448 | tf_op jit(solution)/shard_map/ppermute | solution.py:336
  35.4 3.7 %copy-start.13 = (bf16[216,512]{1,0:T(8,128)(2,1)}, bf16[216,512]{1,0:T(8,128)(2,1)S(1)}, u32[]{:S(2)}) copy-start(bf16[216,512]{1,0:T(8,128)(2,1)S(1)} %collective-permute-done.2.refs_7_) | copy-start | bytes 663556
  35.4 1.6 %collective-permute-start.6 = (bf16[216,512]{1,0:T(8,128)(2,1)S(1)}, bf16[216,512]{1,0:T(8,128)(2,1)}, u32[]{:S(2)}, u32[]{:S(2)}) collective-permute-start(bf16[216,512]{1,0:T(8,128)(2,1)S(1)} %collective-permute-done.2.refs_7_), channel_id=1, source_target_pairs={{0,1},{1,0},{2,3},{3,2},{4,5},{5,4},{6,7},{7,6},{8,9},{9,8},{10,11... | collective-permute-start | bytes 663560 | tf_op jit(solution)/shard_map/ppermute | solution.py:336
  37.0 2.1 %copy-start.9 = (bf16[216,1152]{1,0:T(8,128)(2,1)}, bf16[216,1152]{1,0:T(8,128)(2,1)S(1)}, u32[]{:S(2)}) copy-start(bf16[216,1152]{1,0:T(8,128)(2,1)S(1)} %collective-permute-done.5.refs_10_) | copy-start | bytes 1492996
  37.0 2.1 %copy-start.10 = (bf16[216,1152]{1,0:T(8,128)(2,1)}, bf16[216,1152]{1,0:T(8,128)(2,1)S(1)}, u32[]{:S(2)}) copy-start(bf16[216,1152]{1,0:T(8,128)(2,1)S(1)} %collective-permute-done.4.refs_9_) | copy-start | bytes 1492996
  39.1 0.8 copy-start.6
  39.1 0.9 copy-start.12
  40.0 17.7 %copy-start = (s32[3]{0:T(128)S(1)}, s32[3]{0:T(128)}, u32[]{:S(2)}) copy-start(s32[3]{0:T(128)} %pad_add_fusion.idx) | copy-start | bytes 40
  53.3 4.4 %collective-permute-start.8 = (bf16[128,3456]{1,0:T(8,128)(2,1)}, bf16[128,3456]{1,0:T(8,128)(2,1)S(1)}, u32[]{:S(2)}, u32[]{:S(2)}) collective-permute-start(bf16[128,3456]{1,0:T(8,128)(2,1)} %get-tuple-element.38.mine), channel_id=1, source_target_pairs={{0,1},{1,0},{2,3},{3,2},{4,5},{5,4},{6,7},{7,6},{8,9},{9,8},{10,11... | collective-permute-start | bytes 2654216 | tf_op jit(solution)/shard_map/ppermute | solution.py:336
  53.4 18.1 %all-to-all-start.2 = ((bf16[8,16,1728]{2,1,0:T(8,128)(2,1)}), bf16[8,16,1728]{2,1,0:T(8,128)(2,1)}, u32[]{:S(2)}, u32[]{:S(2)}) async-start(bf16[8,16,1728]{2,1,0:T(8,128)(2,1)} %bitcast.20), calls=%async_computation.2 | async-start | bytes 917504 | tf_op jit(solution)/shard_map/all_to_all | solution.py:417
  57.7 1.2 %copy-start.1 = (bf16[128,3456]{1,0:T(8,128)(2,1)S(1)}, bf16[128,3456]{1,0:T(8,128)(2,1)}, u32[]{:S(2)}) copy-start(bf16[128,3456]{1,0:T(8,128)(2,1)} %get-tuple-element.38.mine) | copy-start | bytes 2654212
  61.6 16.5 %collective-permute-start.9 = (bf16[2,72,1152]{2,1,0:T(8,128)(2,1)S(1)}, bf16[2,72,1152]{2,1,0:T(8,128)(2,1)S(1)}, u32[]{:S(2)}, u32[]{:S(2)}) collective-permute-start(bf16[2,72,1152]{2,1,0:T(8,128)(2,1)S(1)} %get-tuple-element.40), channel_id=1, source_target_pairs={{0,8},{8,0},{16,24},{24,16},{1,9},{9,1},{17,25},{25,17},{2,10},{10... | collective-permute-start | bytes 995336 | tf_op jit(solution)/shard_map/ppermute | solution.py:336
  63.1 17.0 %collective-permute-start.10 = (bf16[2,72,1152]{2,1,0:T(8,128)(2,1)S(1)}, bf16[2,72,1152]{2,1,0:T(8,128)(2,1)S(1)}, u32[]{:S(2)}, u32[]{:S(2)}) collective-permute-start(bf16[2,72,1152]{2,1,0:T(8,128)(2,1)S(1)} %get-tuple-element.41), channel_id=1, source_target_pairs={{0,16},{8,24},{16,0},{24,8},{1,17},{9,25},{17,1},{25,9},{2,18},{10... | collective-permute-start | bytes 995336 | tf_op jit(solution)/shard_map/ppermute | solution.py:336
  64.7 15.5 %collective-permute-start.11 = (bf16[2,72,1152]{2,1,0:T(8,128)(2,1)S(1)}, bf16[2,72,1152]{2,1,0:T(8,128)(2,1)S(1)}, u32[]{:S(2)}, u32[]{:S(2)}) collective-permute-start(bf16[2,72,1152]{2,1,0:T(8,128)(2,1)S(1)} %get-tuple-element.42), channel_id=1, source_target_pairs={{0,24},{8,16},{16,8},{24,0},{1,25},{9,17},{17,9},{25,1},{2,26},{10... | collective-permute-start | bytes 995336 | tf_op jit(solution)/shard_map/ppermute | solution.py:336
  80.1 0.7 copy-start.4
  81.0 6.0 %collective-permute-start.12 = (bf16[2,72,288]{2,1,0:T(8,128)(2,1)S(1)}, bf16[2,72,288]{2,1,0:T(8,128)(2,1)S(1)}, u32[]{:S(2)}, u32[]{:S(2)}) collective-permute-start(bf16[2,72,288]{2,1,0:T(8,128)(2,1)S(1)} %get-tuple-element.44), channel_id=1, source_target_pairs={{0,2},{1,3},{2,0},{3,1},{4,6},{5,7},{6,4},{7,5},{8,10},{9,11},{10,... | collective-permute-start | bytes 248840 | tf_op jit(solution)/shard_map/ppermute | solution.py:336
  82.5 10.6 %collective-permute-start.13 = (bf16[2,72,288]{2,1,0:T(8,128)(2,1)S(1)}, bf16[2,72,288]{2,1,0:T(8,128)(2,1)S(1)}, u32[]{:S(2)}, u32[]{:S(2)}) collective-permute-start(bf16[2,72,288]{2,1,0:T(8,128)(2,1)S(1)} %get-tuple-element.45), channel_id=1, source_target_pairs={{0,4},{1,5},{2,6},{3,7},{4,0},{5,1},{6,2},{7,3},{8,12},{9,13},{10,... | collective-permute-start | bytes 248840 | tf_op jit(solution)/shard_map/ppermute | solution.py:336
  84.9 8.2 %collective-permute-start.14 = (bf16[2,72,288]{2,1,0:T(8,128)(2,1)S(1)}, bf16[2,72,288]{2,1,0:T(8,128)(2,1)S(1)}, u32[]{:S(2)}, u32[]{:S(2)}) collective-permute-start(bf16[2,72,288]{2,1,0:T(8,128)(2,1)S(1)} %get-tuple-element.46), channel_id=1, source_target_pairs={{0,6},{1,7},{2,4},{3,5},{4,2},{5,3},{6,0},{7,1},{8,14},{9,15},{10,... | collective-permute-start | bytes 248840 | tf_op jit(solution)/shard_map/ppermute | solution.py:336

commit v5 on v3

v5 whole, which is shorter than its diff:
```python
import functools
import math

import jax
import jax.numpy as jnp
from jax import lax
from jax.experimental import pallas as pl
from jax.experimental.pallas import tpu as pltpu
from jax.sharding import PartitionSpec as P

DH = 72
FRAMES = 16
LANES = 128
BF16 = jnp.bfloat16
F32 = jnp.float32
VMEM = pl.BlockSpec(memory_space=pltpu.VMEM)
SMEM = pl.BlockSpec(memory_space=pltpu.SMEM)
HBM = pl.BlockSpec(memory_space=pltpu.HBM)
LIMIT = 16 * 1024 * 1024
MOST = 60 * 1024 * 1024


def dot(left, right):
    return jnp.dot(left, right, preferred_element_type=F32)


def dot_bt(left, right):
    return lax.dot_general(left, right, (((1,), (1,)), ((), ())), preferred_element_type=F32)


def dot_at(left, right):
    return lax.dot_general(left, right, (((0,), (0,)), ((), ())), preferred_element_type=F32)


def call(body, outs, args, scratch=(), us=0, far_in=(), far_out=(), small=False):
    moved = sum(math.prod(a.shape) * a.dtype.itemsize for a in (*args, *outs))
    near = [SMEM if a.dtype == jnp.int32 else VMEM for a in args]
    return pl.pallas_call(
        body,
        out_shape=outs,
        in_specs=[HBM if i in far_in else spec for i, spec in enumerate(near)],
        out_specs=[HBM if i in far_out else VMEM for i in range(len(outs))],
        scratch_shapes=list(scratch),
        compiler_params=pltpu.CompilerParams(vmem_limit_bytes=LIMIT if small else MOST),
        cost_estimate=pl.CostEstimate(
            flops=us * 1150000000, bytes_accessed=moved if us else 0, transcendentals=0
        ),
    )(*args)


def started(pairs, sems):
    copies = [pltpu.make_async_copy(a, b, sems.at[i]) for i, (a, b) in enumerate(pairs)]
    for copy in copies:
        copy.start()
    return copies


def shape(dims, dtype=BF16):
    return jax.ShapeDtypeStruct(dims, dtype)


TOKEN = shape((8, LANES), F32)


def window(head):
    low = head * DH // LANES * LANES
    high = -(-(head + 1) * DH // LANES) * LANES
    return low, high


def head_only(block, head):
    low, high = window(head)
    lane = lax.broadcasted_iota(jnp.int32, (1, high - low), 1) + low
    keep = (lane >= head * DH) & (lane < (head + 1) * DH)
    return jnp.where(keep, block, jnp.zeros_like(block))


def add_tiles(tiles, head, value):
    low, high = window(head)
    for at in range(low // LANES, high // LANES):
        part = value[:, at * LANES - low : (at + 1) * LANES - low]
        tiles[at] = part if tiles[at] is None else tiles[at] + part


def joined(tiles):
    return jnp.concatenate([tile.astype(BF16) for tile in tiles], axis=1)


def same_group(rows, kind):
    row = lax.broadcasted_iota(jnp.int32, (rows, rows), 0)
    col = lax.broadcasted_iota(jnp.int32, (rows, rows), 1)
    how, size = kind
    return row // size == col // size if how == "block" else row % size == col % size


def softmax_forward(q_ref, k_ref, v_ref, p_ref, heads, kind):
    rows = q_ref.shape[0]
    mask = same_group(rows, kind)
    tiles = [None] * (q_ref.shape[1] // LANES)
    for head in range(heads):
        low, high = window(head)
        s = dot_bt(q_ref[:, low:high], head_only(k_ref[:, low:high], head)) * (1.0 / math.sqrt(DH))
        s = jnp.where(mask, s, -jnp.inf)
        e = jnp.exp(s - jnp.max(s, axis=1, keepdims=True))
        p = e / jnp.sum(e, axis=1, keepdims=True)
        p_ref[head] = p
        add_tiles(tiles, head, dot(p.astype(BF16), head_only(v_ref[:, low:high], head)))
    return joined(tiles)


def softmax_backward(q_ref, k_ref, v_ref, g_ref, p_ref, heads):
    count = q_ref.shape[1] // LANES
    dq, dk, dv = [None] * count, [None] * count, [None] * count
    for head in range(heads):
        low, high = window(head)
        p = p_ref[head]
        g = head_only(g_ref[:, low:high], head)
        add_tiles(dv, head, dot_at(p.astype(BF16), g))
        dp = dot_bt(g, v_ref[:, low:high])
        ds = p * (dp - jnp.sum(p * dp, axis=1, keepdims=True)) * (1.0 / math.sqrt(DH))
        ds = ds.astype(BF16)
        add_tiles(dq, head, dot(ds, head_only(k_ref[:, low:high], head)))
        add_tiles(dk, head, dot_at(ds, head_only(q_ref[:, low:high], head)))
    return joined(dq), joined(dk), joined(dv)


def put(ref, value):
    width = value.shape[1]
    ref[:, width // LANES * LANES :] = jnp.zeros(
        (ref.shape[0], ref.shape[1] - width // LANES * LANES), ref.dtype
    )
    ref[:, :width] = value


def spatial_kernel(chips, patches, idx, *refs):
    far, outs, refs = refs[:4], refs[4 : 4 + chips], refs[4 + chips :]
    hid_far, p_far, done, tok, cot, qkv, wos, held, hid, p_ref, qs, ks, vs, sems = refs
    done[...] = jnp.zeros_like(done)
    inner, width = wos.shape
    count, block, _ = held.shape
    loads = started(zip(far, (qkv, tok, wos, cot)), sems)
    loads[0].wait()
    x = qkv[...]
    put(qs, x[:, :inner])
    put(ks, x[:, inner : 2 * inner])
    put(vs, x[:, 2 * inner :])
    o = softmax_forward(qs, ks, vs, p_ref, inner // DH, ("block", patches))[:, :inner]
    stores = started([(p_ref, p_far)], sems.at[pl.ds(4, 1)])
    for at in range(3):
        loads[1 + at].wait()
    hid[...] = (tok[...].astype(F32) + dot(o, wos[...])).astype(BF16)
    for at in range(count):
        rows = slice(at * block, (at + 1) * block)
        held[at, :, :width] = hid[rows]
        held[at, :, width : 2 * width] = cot[rows]
        held[at, :, 2 * width :] = o[rows]
    pairs = [(hid, hid_far)]
    for q in range(chips):
        for f in range(count // chips):
            rows = pl.ds(f * block, block)
            pairs.append((held.at[f * chips + (idx[2] ^ q)], outs[q].at[rows]))
    stores += started(pairs, sems.at[pl.ds(5, len(pairs))])
    for copy in stores:
        copy.wait()


def own_patches(refs, core, block):
    value = jnp.concatenate([ref[...] for ref in refs], axis=0)
    rows, width = value.shape
    value = value.astype(F32).reshape(rows // block, block, width)
    value = jnp.where(core == 0, value[:, : block // 2], value[:, block // 2 :])
    return value.reshape(rows // 2, width)


def all_patches(mine, other, core, block):
    rows, width = mine.shape
    mine = mine.astype(F32).reshape(2 * rows // block, block // 2, width)
    other = other.astype(F32).reshape(2 * rows // block, block // 2, width)
    first, second = jnp.where(core == 0, mine, other), jnp.where(core == 0, other, mine)
    return jnp.concatenate([first, second], axis=1).reshape(2 * rows, width).astype(BF16)


def split_kernel(near_x, near_y, _, from_x, from_y):
    cut = from_y.shape[1]
    from_y[...] = near_y[:, :cut]
    from_x[...] = near_x[:, cut:]


def pieces(shards, weights):
    weights = list(weights)
    for place, count, parts in shards:
        low, held = 0, []
        for _ in range(parts):
            w = weights.pop(0)
            held.append((low, w))
            low += w.shape[1]
        yield place, count, held


def temporal_kernel(shards, total, chips, group, idx, *refs):
    near, far, wot, refs = refs[:chips], refs[chips : 2 * chips], refs[2 * chips], refs[2 * chips + 1 :]
    weights, (mine, cot, q, k, v, g, p_ref, blocks) = refs[:total], refs[total:]
    inner, width = wot.shape
    heads = inner // DH
    value = [own_patches(refs, idx[1], 2 * group) for refs in (near, far)]
    value = jnp.concatenate(value, axis=0).astype(BF16)
    hidden = value[:, :width]
    cot[...] = value[:, width : 2 * width]
    for place, count, held in pieces(shards, weights):
        block = None
        for low, w in held:
            value = dot_bt(hidden[:, low : low + w.shape[1]], w[...])
            block = value if block is None else block + value
        block = block.astype(BF16)
        size = block.shape[1] // count
        for i in range(count):
            blocks[place(idx) + i] = block[:, i * size : (i + 1) * size]
    whole = jnp.concatenate([blocks[i] for i in range(blocks.shape[0])], axis=1)
    put(q, whole[:, :inner])
    put(k, whole[:, inner : 2 * inner])
    put(v, whole[:, 2 * inner :])
    mine[:, width:] = softmax_forward(q, k, v, p_ref, heads, ("cycle", group))[:, :inner]
    put(g, dot_bt(cot[...], wot[...]).astype(BF16))
    dq, dk, dv = softmax_backward(q, k, v, g, p_ref, heads)
    whole = jnp.concatenate([dq[:, :inner], dk[:, :inner], dv[:, :inner]], axis=1)
    size = blocks.shape[2]
    for i in range(blocks.shape[0]):
        blocks[i] = whole[:, i * size : (i + 1) * size]
    grad = jnp.zeros(cot.shape, F32)
    for place, count, held in pieces(shards, weights):
        lhs = jnp.concatenate([blocks[place(idx) + i] for i in range(count)], axis=1)
        grad += jnp.concatenate([dot(lhs, w[...]) for _, w in held], axis=1)
    mine[:, :width] = (cot[...].astype(F32) + grad.astype(BF16).astype(F32)).astype(BF16)


def whole_return_kernel(chips, block, inner, width, idx, mine, other, *refs):
    held, outs, part = refs[:chips], refs[chips : 2 * chips], refs[2 * chips]
    held = jnp.concatenate([ref[...] for ref in held], axis=0)
    cot, so = held[:, width : 2 * width], held[:, 2 * width :]
    half = mine.shape[0] // 2
    near = all_patches(mine[:half], other[half:], idx[1], block)
    for q, out in enumerate(outs):
        out[...] = near[q * out.shape[0] : (q + 1) * out.shape[0]]
    part[0] = dot_at(near[:, width:], cot).astype(BF16)
    part[1] = dot_at(so, near[:, :width]).astype(BF16)


def return_kernel(chips, block, inner, width, idx, mine, other, *refs):
    sent, refs = (refs[:chips], refs[chips : 2 * chips]), refs[2 * chips :]
    sent = [jnp.concatenate([ref[...] for ref in parts], axis=0) for parts in sent]
    outs, (keep, send_x, send_y, heads, cols) = refs[:chips], refs[chips:]
    half = mine.shape[0] // 2
    near = all_patches(mine[:half], other[half:], idx[1], block)
    for q, out in enumerate(outs):
        out[...] = near[q * out.shape[0] : (q + 1) * out.shape[0]]
    far = all_patches(mine[half:], other[:half], idx[1], block)
    rows = near.shape[0]
    size = heads.shape[2]
    count, _, wide = cols.shape
    for i in range(2):
        if i == 0:
            lefts = [near[:, width:], far[:, width:]]
            rights = [part[:, width : 2 * width] for part in sent]
        else:
            lefts = [part[:, 2 * width :] for part in sent]
            rights = [near[:, :width], far[:, :width]]
        for at in range(2):
            held = slice(at * rows, (at + 1) * rows)
            for h in range(heads.shape[0]):
                heads[h, held] = lefts[at][:, h * size : (h + 1) * size]
            for r in range(count):
                cols[r, held] = rights[at][:, r * wide : (r + 1) * wide]
        left = jnp.concatenate([heads[idx[3] ^ (2 * q)] for q in range(chips)], axis=1)
        first = 1 if i == 0 else 2
        for r in range(count):
            full = dot_at(left, cols[idx[0] ^ r])
            value = jnp.concatenate([full[q * size : (q + 1) * size] for q in range(chips)], axis=1)
            if r & first:
                (send_x, send_y)[i][r // 2 if i == 0 else r - 2] = value.astype(BF16)
            else:
                keep[2 * i + (r > 0)] = value


def sum_first_kernel(keep, got_x, got_y, own, send_y, send_x):
    for i, (got, send) in enumerate(((got_x, send_y), (got_y, send_x))):
        own[i] = keep[2 * i] + got[0].astype(F32)
        send[...] = (keep[2 * i + 1] + got[1].astype(F32)).astype(BF16)


def sum_second_kernel(own, got_y, got_x, kept, *outs):
    totals = [own[0] + got_y[...].astype(F32), own[1] + got_x[...].astype(F32)]
    size = totals[0].shape[1] // (1 + len(outs))
    for q, out in enumerate((kept, *outs)):
        cut = [total[:, q * size : (q + 1) * size] for total in totals]
        out[...] = jnp.concatenate(cut, axis=1).astype(out.dtype)


def sum_kernel(own, *refs):
    got, outs = refs[:-2], refs[-2:]
    total = own[...]
    for part in got:
        total += part[...].astype(F32)
    size = outs[0].shape[1]
    for i, out in enumerate(outs):
        out[...] = total[:, i * size : (i + 1) * size]


def last_kernel(chips, patches, idx, *refs):
    loaded = 5 + chips
    far, (block_far, out_far, grads_far), refs = refs[:loaded], refs[loaded : loaded + 3], refs[loaded + 3 :]
    rows, wos, qkv, p_ref, wot, hid, block_out, grads, qs, ks, vs, gs, sems = refs
    inner, width = wos.shape
    frames = rows.shape[0] // patches
    block = patches // chips
    pairs = list(zip(far[chips:], (wos, qkv, p_ref, wot, hid)))
    for q in range(chips):
        for f in range(frames):
            low = pl.multiple_of(f * patches + (idx[2] ^ q) * block, block)
            pairs.append((far[q].at[pl.ds(f * block, block)], rows.at[pl.ds(low, block)]))
    loads = started(pairs, sems)
    for copy in loads[5:]:
        copy.wait()
    value = rows[...]
    grad, attended = value[:, :width], value[:, width:]
    base = len(pairs)
    stores = started([(rows.at[:, pl.ds(0, width)], out_far)], sems.at[pl.ds(base, 1)])
    loads[0].wait()
    put(gs, dot_bt(grad, wos[...]).astype(BF16))
    loads[1].wait()
    x = qkv[...]
    put(qs, x[:, :inner])
    put(ks, x[:, inner : 2 * inner])
    put(vs, x[:, 2 * inner :])
    loads[3].wait()
    loads[4].wait()
    block_out[...] = (hid[...].astype(F32) + dot(attended, wot[...])).astype(BF16)
    stores += started([(block_out, block_far)], sems.at[pl.ds(base + 1, 1)])
    loads[2].wait()
    dq, dk, dv = softmax_backward(qs, ks, vs, gs, p_ref, inner // DH)
    grads[...] = jnp.concatenate([dq[:, :inner], dk[:, :inner], dv[:, :inner]], axis=1)
    stores += started([(grads, grads_far)], sems.at[pl.ds(base + 2, 1)])
    for copy in stores:
        copy.wait()


def flip(value, axis, bit):
    return lax.ppermute(value, axis, [(i, i ^ bit) for i in range(lax.axis_size(axis))])


def sems(n):
    return pltpu.SemaphoreType.DMA((n,))


def gather_weight(weight, core, after):
    n = lax.axis_size("dp")
    if n != 4:
        return [lax.all_gather(weight, "dp", axis=0, tiled=True)], [(lambda idx: 0, 1, 1)], 1
    half, width = weight.shape[0] // 2, weight.shape[1]
    mine = lax.dynamic_slice_in_dim(weight, core * half, half, 0)
    near = [flip(mine, "dp", 1), flip(mine, "dp", 2)]
    cut = width // LANES // 2 * LANES
    from_x, from_y = call(
        split_kernel,
        [shape((half, width - cut)), shape((half, cut))],
        [*near, after],
        small=True,
    )
    corner = [flip(from_y, "dp", 1), flip(from_x, "dp", 2)]
    held = near + corner
    far = [flip(w, "seq", 1) for w in held]
    shards = [(lambda idx: 2 * idx[0], 2, 1)]
    for flipped in range(2):
        for j in range(1, n):
            shards.append(
                (
                    lambda idx, j=j, flipped=flipped: 2 * (idx[0] ^ j) + (idx[1] ^ flipped),
                    1,
                    1 if j < 3 else 2,
                )
            )
    return [weight, *held, *far], shards, 2 * n


def from_chips(parts):
    return [parts[0]] + [flip(parts[q], "seq", 2 * q) for q in range(1, len(parts))]


def reduced(keep, send_x, send_y):
    _, size, width = keep.shape
    step = shape((size, width))
    own, send_t, send_s = call(
        sum_first_kernel,
        [shape((2, size, width), F32), step, step],
        [keep, flip(send_x, "dp", 1), flip(send_y, "dp", 2)],
        small=True,
    )
    n = lax.axis_size("seq") // 2
    block = (size, 2 * width // n)
    own, *sends = call(
        sum_second_kernel,
        [shape(block, F32)] + [shape(block)] * (n - 1),
        [own, flip(send_t, "dp", 2), flip(send_s, "dp", 1)],
        small=True,
    )
    got = [flip(value, "seq", 2 * (q + 1)) for q, value in enumerate(sends)]
    return call(sum_kernel, [shape((size, width // n), F32)] * 2, [own, *got], small=True)


def shards(tokens, spatial_qkv, wo_spatial, w_temporal, wo_temporal, cotangent):
    frames, patches, width = tokens.shape
    inner = wo_spatial.shape[0]
    heads = inner // DH
    padded = -(-inner // LANES) * LANES
    rows = frames * patches
    peers = FRAMES // frames
    chips = peers // 2
    group = patches // peers
    block = 2 * group
    n_dp, n_seq = lax.axis_size("dp"), lax.axis_size("seq")
    seq = lax.axis_index("seq")
    idx = jnp.stack([lax.axis_index("dp"), seq % 2, seq % peers // 2, seq]).astype(jnp.int32)

    def held(columns, dtype=BF16):
        return pltpu.VMEM((rows, columns), dtype)

    wide = held(padded)
    attended = pltpu.VMEM((heads, rows, rows), F32)
    projection = pltpu.VMEM((inner, width), BF16)
    per_chip = rows // chips
    qkv_rows = spatial_qkv.reshape(rows, 3 * inner)
    sent = 2 * width + inner
    *near, hidden, spatial_p, done = call(
        functools.partial(spatial_kernel, chips, patches),
        [shape((per_chip, sent))] * chips
        + [shape((rows, width)), shape((heads, rows, rows), F32), TOKEN],
        [idx, qkv_rows, tokens.reshape(rows, width), wo_spatial, cotangent.reshape(rows, width)],
        [held(width), held(width), held(3 * inner), projection]
        + [pltpu.VMEM((frames * chips, block, sent), BF16), held(width), attended]
        + [wide] * 3
        + [sems(6 + chips * frames)],
        us=4,
        far_in=range(1, 5),
        far_out=range(chips + 2),
    )
    weights, places, count = gather_weight(w_temporal.T, seq % 2, done)
    near = from_chips(near)
    far = [flip(value, "seq", 1) for value in near]
    blocks = pltpu.VMEM((count, rows, 3 * inner // count), BF16)
    (mine,) = call(
        functools.partial(temporal_kernel, places, len(weights), chips, group),
        [shape((rows, width + inner))],
        [idx, *near, *far, wo_temporal, *weights],
        [held(width)] + [wide] * 4 + [attended, blocks],
        us=10,
        small=True,
    )
    other = flip(mine, "seq", 1)
    back = [shape((per_chip, width + inner))] * chips
    if n_dp == 4 and n_seq == peers:
        size = inner // n_seq
        *back, keep, send_x, send_y = call(
            functools.partial(return_kernel, chips, block, inner, width),
            back
            + [shape((n_dp, size, width), F32)]
            + [shape((2, size, width))] * 2,
            [idx, mine, other, *near, *far],
            [
                pltpu.VMEM((n_seq, 2 * rows, size), BF16),
                pltpu.VMEM((n_dp, 2 * rows, width // n_dp), BF16),
            ],
            us=0,
            small=True,
        )
        temporal_grad, spatial_grad = reduced(keep, send_x, send_y)
    else:
        *back, both = call(
            functools.partial(whole_return_kernel, chips, block, inner, width),
            back + [shape((2, inner, width))],
            [idx, mine, other, *near],
            us=0,
            small=True,
        )
        both = lax.psum_scatter(both, "seq", scatter_dimension=1, tiled=True)
        both = lax.psum_scatter(both, "dp", scatter_dimension=2, tiled=True).astype(F32)
        temporal_grad, spatial_grad = both[0], both[1]
    block_out, tokens_grad, qkv_grad = call(
        functools.partial(last_kernel, chips, patches),
        [shape((rows, width)), shape((rows, width)), shape((rows, 3 * inner))],
        [idx, *from_chips(back), wo_spatial, qkv_rows, spatial_p, wo_temporal, hidden],
        [held(width + inner), projection, held(3 * inner), attended, projection, held(width)]
        + [held(width), held(3 * inner)]
        + [wide] * 4
        + [sems(8 + chips * frames)],
        us=6,
        far_in=range(1, 6 + chips),
        far_out=range(3),
    )
    return (
        block_out.reshape(frames, patches, width),
        tokens_grad.reshape(frames, patches, width),
        qkv_grad.reshape(frames, patches, 3 * inner),
        spatial_grad,
        temporal_grad,
    )


def solution(mesh):
    placed = (
        P(("dp", "seq"), None, None),
        P(("dp", "seq"), None, None),
        P(),
        P(None, "dp"),
        P(),
        P(("dp", "seq"), None, None),
    )
    return jax.shard_map(
        shards,
        mesh=mesh,
        in_specs=placed,
        out_specs=(
            P(("dp", "seq"), None, None),
            P(("dp", "seq"), None, None),
            P(("dp", "seq"), None, None),
            P("seq", "dp"),
            P("seq", "dp"),
        ),
        check_vma=False,
    )
```

time: 98 us -> 94.1 us (0.960)
  the two profiles are of different devices: /device:TPU:0 before, /device:TPU:8 now
where the time goes in v5:
time: 94.1 us; the launch traced here: 93.9 us
  waiting for transfers between devices  43.1 us (46%)
  Pallas kernels  24.9 us (26%)
  starting transfers between devices  19.7 us (21%)
  local copies, waits for them, and re-layouts  4.78 us (5%)
    ppermute x26, waiting for transfers between devices, flip(): lax.ppermute(value, axis, [(i, i ^ bit) for i in range(lax.axis_size(axis...  43.1 us
    pallas_call x8, Pallas kernels, call(): pl.pallas_call(body, out_shape=outs, in_specs=[HBM if i in far_in else sp...  24.9 us
    ppermute x26, starting transfers between devices, flip(): lax.ppermute(value, axis, [(i, i ^ bit) for i in range(lax.axis_size(axis...  19.7 us
    unnamed x18, local copies, waits for them, and re-layouts  2.9 us
  transfers between devices with their start and end apart: 26, of which 11 were waited for; matrix products, arithmetic and copies ran while one was open for 1% of the time, Pallas kernels for 14%

profile of v5, /device:TPU:8, one launch (start us, length us, event | category | flops | bytes accessed | tf_op | source)
XLA Modules:
  0.0 93.9 jit_solution(11013195631419620927)
XLA Ops:
  0.6 1.9 %dynamic-slice_bitcast_fusion = bf16[216,1152]{1,0:T(8,128)(2,1)} fusion(bf16[1152,432]{0,1:T(8,128)(2,1)} %param.9, s32[]{:T(128)S(6)} %select_n.23), kind=kLoop, calls=%fused_computation | loop fusion | bytes 995332 | tf_op jit(solution)/shard_map/dynamic_slice | solution.py:359
  2.5 1.5 %collective-permute-start.8 = (bf16[216,1152]{1,0:T(8,128)(2,1)}, bf16[216,1152]{1,0:T(8,128)(2,1)S(1)}, u32[]{:S(2)}, u32[]{:S(2)}) collective-permute-start(bf16[216,1152]{1,0:T(8,128)(2,1)} %dynamic-slice_bitcast_fusion), channel_id=1, source_target_pairs={{0,16},{8,24},{16,0},{24,8},{1,17},{9,25},{17,1},{25,9},{2,18},{10... | collective-permute-start | bytes 1493000 | tf_op jit(solution)/shard_map/ppermute | solution.py:347
  4.0 1.5 %collective-permute-start.7 = (bf16[216,1152]{1,0:T(8,128)(2,1)}, bf16[216,1152]{1,0:T(8,128)(2,1)S(1)}, u32[]{:S(2)}, u32[]{:S(2)}) collective-permute-start(bf16[216,1152]{1,0:T(8,128)(2,1)} %dynamic-slice_bitcast_fusion), channel_id=1, source_target_pairs={{0,8},{8,0},{16,24},{24,16},{1,9},{9,1},{17,25},{25,17},{2,10},{10... | collective-permute-start | bytes 1493000 | tf_op jit(solution)/shard_map/ppermute | solution.py:347
  5.5 0.7 pad_add_fusion.idx
  6.2 5.6 %shard_map.101 = (bf16[32,2880]{1,0:T(8,128)(2,1)}, bf16[32,2880]{1,0:T(8,128)(2,1)}, bf16[32,2880]{1,0:T(8,128)(2,1)}, bf16[32,2880]{1,0:T(8,128)(2,1)}, bf16[1...) custom-call(s32[4]{0:T(128)} %pad_add_fusion.idx, bf16[128,1728]{1,0:T(8,128)(2,1)} %bitcast.14, ...), custom_call_target="tpu_custom_call" | custom-call | flops 4600000000 | bytes 3919888 | tf_op jit(solution)/shard_map/pallas_call | solution.py:38
  11.8 0.5 collective-permute-start
  12.3 2.6 %collective-permute-start.1 = (bf16[32,2880]{1,0:T(8,128)(2,1)}, bf16[32,2880]{1,0:T(8,128)(2,1)S(1)}, u32[]{:S(2)}, u32[]{:S(2)}) collective-permute-start(bf16[32,2880]{1,0:T(8,128)(2,1)} %get-tuple-element.35), channel_id=1, source_target_pairs={{0,4},{1,5},{2,6},{3,7},{4,0},{5,1},{6,2},{7,3},{8,12},{9,13},{10,... | collective-permute-start | bytes 552968 | tf_op jit(solution)/shard_map/ppermute | solution.py:347
  15.4 4.4 %collective-permute-done.refs_1_ = bf16[32,2880]{1,0:T(8,128)(2,1)S(1)} collective-permute-done((bf16[32,2880]{1,0:T(8,128)(2,1)}, bf16[32,2880]{1,0:T(8,128)(2,1)S(1)}, u32[]{:S(2)}, u32[]{:S(2)}) %collective-permute-start) | collective-permute-done | bytes 184352 | tf_op jit(solution)/shard_map/ppermute | solution.py:347
  20.3 0.7 copy-done.2
  21.0 0.6 collective-permute-start.10
  21.6 6.5 %collective-permute-done.1.refs_2_ = bf16[32,2880]{1,0:T(8,128)(2,1)S(1)} collective-permute-done((bf16[32,2880]{1,0:T(8,128)(2,1)}, bf16[32,2880]{1,0:T(8,128)(2,1)S(1)}, u32[]{:S(2)}, u32[]{:S(2)}) %collective-permute-start.1) | collective-permute-done | bytes 184352 | tf_op jit(solution)/shard_map/ppermute | solution.py:347
  28.0 3.3 %collective-permute-done.2.refs_3_ = bf16[32,2880]{1,0:T(8,128)(2,1)S(1)} collective-permute-done((bf16[32,2880]{1,0:T(8,128)(2,1)}, bf16[32,2880]{1,0:T(8,128)(2,1)S(1)}, u32[]{:S(2)}, u32[]{:S(2)}) %collective-permute-start.2) | collective-permute-done | bytes 184352 | tf_op jit(solution)/shard_map/ppermute | solution.py:347
  31.4 0.5 collective-permute-start.9
  32.4 6.8 %collective-permute-done.9.refs_12_ = bf16[216,512]{1,0:T(8,128)(2,1)S(1)} collective-permute-done((bf16[216,512]{1,0:T(8,128)(2,1)S(1)}, bf16[216,512]{1,0:T(8,128)(2,1)S(1)}, u32[]{:S(2)}, u32[]{:S(2)}) %collective-permute-start.9) | collective-permute-done | bytes 221216 | tf_op jit(solution)/shard_map/ppermute | solution.py:347
  39.7 1.2 %collective-permute-done.6.refs_7_ = bf16[32,2880]{1,0:T(8,128)(2,1)S(1)} collective-permute-done((bf16[32,2880]{1,0:T(8,128)(2,1)S(1)}, bf16[32,2880]{1,0:T(8,128)(2,1)S(1)}, u32[]{:S(2)}, u32[]{:S(2)}) %collective-permute-start.6) | collective-permute-done | bytes 184352 | tf_op jit(solution)/shard_map/ppermute | solution.py:347
  41.0 0.9 copy-done.1
  41.9 8.0 %shard_map.103.mine = bf16[128,1728]{1,0:T(8,128)(2,1)S(1)} custom-call(s32[4]{0:T(128)S(1)} %copy-done.3, bf16[32,2880]{1,0:T(8,128)(2,1)S(1)} %copy-done.1, bf16[32,2880]{1,0:T(8,128)(2,1)S(1)} %collective-permute-done.refs_1_, bf16[32,2880]{1,0:T(8,128)(2,1)S(1)} %collective-permute-done.1.refs_2_, bf16[32,2880]{1,0:T(8,128)(2,1)S(1)} %collective-permute-done.2.refs_3_, ...), custom_call_target="tpu_custom_call" | custom-call | flops 11500000256 | bytes 7225360 | tf_op jit(solution)/shard_map/pallas_call | solution.py:38
  50.2 1.6 %collective-permute-done.15.other = bf16[128,1728]{1,0:T(8,128)(2,1)S(1)} collective-permute-done((bf16[128,1728]{1,0:T(8,128)(2,1)S(1)}, bf16[128,1728]{1,0:T(8,128)(2,1)S(1)}, u32[]{:S(2)}, u32[]{:S(2)}) %collective-permute-start.15) | collective-permute-done | bytes 442400 | tf_op jit(solution)/shard_map/ppermute | solution.py:347
  51.8 2.8 %shard_map.104 = (bf16[32,1728]{1,0:T(8,128)(2,1)S(1)}, bf16[32,1728]{1,0:T(8,128)(2,1)S(1)}, bf16[32,1728]{1,0:T(8,128)(2,1)S(1)}, bf16[32,1728]{1,0:T(8,128)(2...) custom-call(s32[4]{0:T(128)S(1)} %copy-done.3, ...), custom_call_target="tpu_custom_call" | custom-call | tf_op jit(solution)/shard_map/pallas_call | solution.py:38
  54.7 0.6 copy-done.5
  55.3 0.5 collective-permute-start.19
  56.4 8.8 %collective-permute-done.19.got_x = bf16[2,72,1152]{2,1,0:T(8,128)(2,1)S(1)} collective-permute-done((bf16[2,72,1152]{2,1,0:T(8,128)(2,1)S(1)}, bf16[2,72,1152]{2,1,0:T(8,128)(2,1)S(1)}, u32[]{:S(2)}, u32[]{:S(2)}) %collective-permute-start.19) | collective-permute-done | bytes 331808 | tf_op jit(solution)/shard_map/ppermute | solution.py:347
  65.6 0.6 collective-permute-start.21
  66.2 1.5 %collective-permute-start.22 = (bf16[72,1152]{1,0:T(8,128)(2,1)S(1)}, bf16[72,1152]{1,0:T(8,128)(2,1)S(1)}, u32[]{:S(2)}, u32[]{:S(2)}) collective-permute-start(bf16[72,1152]{1,0:T(8,128)(2,1)S(1)} %get-tuple-element.54), channel_id=1, source_target_pairs={{0,8},{8,0},{16,24},{24,16},{1,9},{9,1},{17,25},{25,17},{2,10},{10... | collective-permute-start | bytes 497672 | tf_op jit(solution)/shard_map/ppermute | solution.py:347
  67.7 3.0 %collective-permute-start.17 = (bf16[32,1728]{1,0:T(8,128)(2,1)S(1)}, bf16[32,1728]{1,0:T(8,128)(2,1)S(1)}, u32[]{:S(2)}, u32[]{:S(2)}) collective-permute-start(bf16[32,1728]{1,0:T(8,128)(2,1)S(1)} %get-tuple-element.42), channel_id=1, source_target_pairs={{0,4},{1,5},{2,6},{3,7},{4,0},{5,1},{6,2},{7,3},{8,12},{9,13},{10,... | collective-permute-start | bytes 331784 | tf_op jit(solution)/shard_map/ppermute | solution.py:347
  71.7 0.7 collective-permute-start.23
  72.4 2.4 %collective-permute-start.24 = (bf16[72,576]{1,0:T(8,128)(2,1)S(1)}, bf16[72,576]{1,0:T(8,128)(2,1)S(1)}, u32[]{:S(2)}, u32[]{:S(2)}) collective-permute-start(bf16[72,576]{1,0:T(8,128)(2,1)S(1)} %get-tuple-element.57), channel_id=1, source_target_pairs={{0,4},{1,5},{2,6},{3,7},{4,0},{5,1},{6,2},{7,3},{8,12},{9,13},{10,... | collective-permute-start | bytes 248840 | tf_op jit(solution)/shard_map/ppermute | solution.py:347
  75.3 3.7 %collective-permute-done.17.refs_2_ = bf16[32,1728]{1,0:T(8,128)(2,1)S(1)} collective-permute-done((bf16[32,1728]{1,0:T(8,128)(2,1)S(1)}, bf16[32,1728]{1,0:T(8,128)(2,1)S(1)}, u32[]{:S(2)}, u32[]{:S(2)}) %collective-permute-start.17) | collective-permute-done | bytes 110624 | tf_op jit(solution)/shard_map/ppermute | solution.py:347
  79.0 6.0 %collective-permute-done.18.refs_3_ = bf16[32,1728]{1,0:T(8,128)(2,1)S(1)} collective-permute-done((bf16[32,1728]{1,0:T(8,128)(2,1)S(1)}, bf16[32,1728]{1,0:T(8,128)(2,1)S(1)}, u32[]{:S(2)}, u32[]{:S(2)}) %collective-permute-start.18) | collective-permute-done | bytes 110624 | tf_op jit(solution)/shard_map/ppermute | solution.py:347
  85.1 0.6 copy-done.8
  85.7 7.3 %shard_map.105 = (bf16[128,1152]{1,0:T(8,128)(2,1)}, bf16[128,1152]{1,0:T(8,128)(2,1)}, bf16[128,1728]{1,0:T(8,128)(2,1)}) custom-call(s32[4]{0:T(128)} %pad_add_fusion.idx, bf16[32,1728]{1,0:T(8,128)(2,1)} %copy-done.5, bf16[32,1728]{1,0:T(8,128)(2,1)} %copy-done.6, bf16[32,1728]{1,0:T(8,128)(2,1)} %copy-done.7, bf16[32,1728]{1,0:T(8,128)(2,1)} %copy-done.8, ...), custom_call_target="tpu_custom_call" | custom-call | flops 6899999744 | bytes 5390352 | tf_op jit(solution)/shard_map/pallas_call | solution.py:38
  93.1 0.8 shard_map.108
  (48 shorter events, 4.8 us)
Async XLA Ops:
  2.5 17.2 %collective-permute-start.8 = (bf16[216,1152]{1,0:T(8,128)(2,1)}, bf16[216,1152]{1,0:T(8,128)(2,1)S(1)}, u32[]{:S(2)}, u32[]{:S(2)}) collective-permute-start(bf16[216,1152]{1,0:T(8,128)(2,1)} %dynamic-slice_bitcast_fusion), channel_id=1, source_target_pairs={{0,16},{8,24},{16,0},{24,8},{1,17},{9,25},{17,1},{25,9},{2,18},{10... | collective-permute-start | bytes 1493000 | tf_op jit(solution)/shard_map/ppermute | solution.py:347
  4.0 16.2 %collective-permute-start.7 = (bf16[216,1152]{1,0:T(8,128)(2,1)}, bf16[216,1152]{1,0:T(8,128)(2,1)S(1)}, u32[]{:S(2)}, u32[]{:S(2)}) collective-permute-start(bf16[216,1152]{1,0:T(8,128)(2,1)} %dynamic-slice_bitcast_fusion), channel_id=1, source_target_pairs={{0,8},{8,0},{16,24},{24,16},{1,9},{9,1},{17,25},{25,17},{2,10},{10... | collective-permute-start | bytes 1493000 | tf_op jit(solution)/shard_map/ppermute | solution.py:347
  6.2 34.8 %copy-start = (bf16[1152,432]{0,1:T(8,128)(2,1)S(1)}, bf16[1152,432]{0,1:T(8,128)(2,1)}, u32[]{:S(2)}) copy-start(bf16[1152,432]{0,1:T(8,128)(2,1)} %param.9) | copy-start | bytes 2985988
  6.2 34.8 %copy-start.3 = (s32[4]{0:T(128)S(1)}, s32[4]{0:T(128)}, u32[]{:S(2)}) copy-start(s32[4]{0:T(128)} %pad_add_fusion.idx) | copy-start | bytes 52
  6.2 34.8 %copy-start.4 = (bf16[576,1152]{1,0:T(8,128)(2,1)S(1)}, bf16[576,1152]{1,0:T(8,128)(2,1)}, u32[]{:S(2)}) copy-start(bf16[576,1152]{1,0:T(8,128)(2,1)} %refs_7_.1) | copy-start | bytes 3981316
  11.8 7.9 %collective-permute-start = (bf16[32,2880]{1,0:T(8,128)(2,1)}, bf16[32,2880]{1,0:T(8,128)(2,1)S(1)}, u32[]{:S(2)}, u32[]{:S(2)}) collective-permute-start(bf16[32,2880]{1,0:T(8,128)(2,1)} %get-tuple-element.34), channel_id=1, source_target_pairs={{0,2},{1,3},{2,0},{3,1},{4,6},{5,7},{6,4},{7,5},{8,10},{9,11},{10,... | collective-permute-start | bytes 552968 | tf_op jit(solution)/shard_map/ppermute | solution.py:347
  12.3 15.7 %collective-permute-start.1 = (bf16[32,2880]{1,0:T(8,128)(2,1)}, bf16[32,2880]{1,0:T(8,128)(2,1)S(1)}, u32[]{:S(2)}, u32[]{:S(2)}) collective-permute-start(bf16[32,2880]{1,0:T(8,128)(2,1)} %get-tuple-element.35), channel_id=1, source_target_pairs={{0,4},{1,5},{2,6},{3,7},{4,0},{5,1},{6,2},{7,3},{8,12},{9,13},{10,... | collective-permute-start | bytes 552968 | tf_op jit(solution)/shard_map/ppermute | solution.py:347
  14.9 16.4 %collective-permute-start.2 = (bf16[32,2880]{1,0:T(8,128)(2,1)}, bf16[32,2880]{1,0:T(8,128)(2,1)S(1)}, u32[]{:S(2)}, u32[]{:S(2)}) collective-permute-start(bf16[32,2880]{1,0:T(8,128)(2,1)} %get-tuple-element.36), channel_id=1, source_target_pairs={{0,6},{1,7},{2,4},{3,5},{4,2},{5,3},{6,0},{7,1},{8,14},{9,15},{10,... | collective-permute-start | bytes 552968 | tf_op jit(solution)/shard_map/ppermute | solution.py:347
  19.7 11.6 %collective-permute-start.3 = (bf16[32,2880]{1,0:T(8,128)(2,1)}, bf16[32,2880]{1,0:T(8,128)(2,1)S(1)}, u32[]{:S(2)}, u32[]{:S(2)}) collective-permute-start(bf16[32,2880]{1,0:T(8,128)(2,1)} %get-tuple-element.33.refs_0_), channel_id=1, source_target_pairs={{0,1},{1,0},{2,3},{3,2},{4,5},{5,4},{6,7},{7,6},{8,9},{9,8},{10,11... | collective-permute-start | bytes 552968 | tf_op jit(solution)/shard_map/ppermute | solution.py:347
  19.7 12.2 %collective-permute-start.4 = (bf16[32,2880]{1,0:T(8,128)(2,1)S(1)}, bf16[32,2880]{1,0:T(8,128)(2,1)S(1)}, u32[]{:S(2)}, u32[]{:S(2)}) collective-permute-start(bf16[32,2880]{1,0:T(8,128)(2,1)S(1)} %collective-permute-done.refs_1_), channel_id=1, source_target_pairs={{0,1},{1,0},{2,3},{3,2},{4,5},{5,4},{6,7},{7,6},{8,9},{9,8},{10,11... | collective-permute-start | bytes 552968 | tf_op jit(solution)/shard_map/ppermute | solution.py:347
  21.0 11.1 %collective-permute-start.10 = (bf16[216,640]{1,0:T(8,128)(2,1)S(1)}, bf16[216,640]{1,0:T(8,128)(2,1)S(1)}, u32[]{:S(2)}, u32[]{:S(2)}) collective-permute-start(bf16[216,640]{1,0:T(8,128)(2,1)S(1)} %get-tuple-element.39), channel_id=1, source_target_pairs={{0,16},{8,24},{16,0},{24,8},{1,17},{9,25},{17,1},{25,9},{2,18},{10... | collective-permute-start | bytes 829448 | tf_op jit(solution)/shard_map/ppermute | solution.py:347
  28.0 12.9 %collective-permute-start.12 = (bf16[216,1152]{1,0:T(8,128)(2,1)S(1)}, bf16[216,1152]{1,0:T(8,128)(2,1)S(1)}, u32[]{:S(2)}, u32[]{:S(2)}) collective-permute-start(bf16[216,1152]{1,0:T(8,128)(2,1)S(1)} %collective-permute-done.8.near_y.refs_11_), channel_id=1, source_target_pairs={{0,1},{1,0},{2,3},{3,2},{4,5},{5,4},{6,7},{7,6},{8,9},{9,8},{10,11... | collective-permute-start | bytes 1493000 | tf_op jit(solution)/shard_map/ppermute | solution.py:347
  31.3 9.6 %collective-permute-start.11 = (bf16[216,1152]{1,0:T(8,128)(2,1)S(1)}, bf16[216,1152]{1,0:T(8,128)(2,1)S(1)}, u32[]{:S(2)}, u32[]{:S(2)}) collective-permute-start(bf16[216,1152]{1,0:T(8,128)(2,1)S(1)} %collective-permute-done.7.near_x.refs_10_), channel_id=1, source_target_pairs={{0,1},{1,0},{2,3},{3,2},{4,5},{5,4},{6,7},{7,6},{8,9},{9,8},{10,11... | collective-permute-start | bytes 1493000 | tf_op jit(solution)/shard_map/ppermute | solution.py:347
  31.4 7.8 %collective-permute-start.9 = (bf16[216,512]{1,0:T(8,128)(2,1)S(1)}, bf16[216,512]{1,0:T(8,128)(2,1)S(1)}, u32[]{:S(2)}, u32[]{:S(2)}) collective-permute-start(bf16[216,512]{1,0:T(8,128)(2,1)S(1)} %get-tuple-element.38), channel_id=1, source_target_pairs={{0,8},{8,0},{16,24},{24,16},{1,9},{9,1},{17,25},{25,17},{2,10},{10... | collective-permute-start | bytes 663560 | tf_op jit(solution)/shard_map/ppermute | solution.py:347
  31.9 7.3 %collective-permute-start.5 = (bf16[32,2880]{1,0:T(8,128)(2,1)S(1)}, bf16[32,2880]{1,0:T(8,128)(2,1)S(1)}, u32[]{:S(2)}, u32[]{:S(2)}) collective-permute-start(bf16[32,2880]{1,0:T(8,128)(2,1)S(1)} %collective-permute-done.1.refs_2_), channel_id=1, source_target_pairs={{0,1},{1,0},{2,3},{3,2},{4,5},{5,4},{6,7},{7,6},{8,9},{9,8},{10,11... | collective-permute-start | bytes 552968 | tf_op jit(solution)/shard_map/ppermute | solution.py:347
  32.1 8.8 %collective-permute-start.14 = (bf16[216,640]{1,0:T(8,128)(2,1)S(1)}, bf16[216,640]{1,0:T(8,128)(2,1)S(1)}, u32[]{:S(2)}, u32[]{:S(2)}) collective-permute-start(bf16[216,640]{1,0:T(8,128)(2,1)S(1)} %collective-permute-done.10.refs_13_), channel_id=1, source_target_pairs={{0,1},{1,0},{2,3},{3,2},{4,5},{5,4},{6,7},{7,6},{8,9},{9,8},{10,11... | collective-permute-start | bytes 829448 | tf_op jit(solution)/shard_map/ppermute | solution.py:347
  39.2 1.8 %collective-permute-start.13 = (bf16[216,512]{1,0:T(8,128)(2,1)S(1)}, bf16[216,512]{1,0:T(8,128)(2,1)S(1)}, u32[]{:S(2)}, u32[]{:S(2)}) collective-permute-start(bf16[216,512]{1,0:T(8,128)(2,1)S(1)} %collective-permute-done.9.refs_12_), channel_id=1, source_target_pairs={{0,1},{1,0},{2,3},{3,2},{4,5},{5,4},{6,7},{7,6},{8,9},{9,8},{10,11... | collective-permute-start | bytes 663560 | tf_op jit(solution)/shard_map/ppermute | solution.py:347
  39.2 1.7 %collective-permute-start.6 = (bf16[32,2880]{1,0:T(8,128)(2,1)S(1)}, bf16[32,2880]{1,0:T(8,128)(2,1)S(1)}, u32[]{:S(2)}, u32[]{:S(2)}) collective-permute-start(bf16[32,2880]{1,0:T(8,128)(2,1)S(1)} %collective-permute-done.2.refs_3_), channel_id=1, source_target_pairs={{0,1},{1,0},{2,3},{3,2},{4,5},{5,4},{6,7},{7,6},{8,9},{9,8},{10,11... | collective-permute-start | bytes 552968 | tf_op jit(solution)/shard_map/ppermute | solution.py:347
  41.0 0.9 copy-start.1
  49.9 1.9 %collective-permute-start.15 = (bf16[128,1728]{1,0:T(8,128)(2,1)S(1)}, bf16[128,1728]{1,0:T(8,128)(2,1)S(1)}, u32[]{:S(2)}, u32[]{:S(2)}) collective-permute-start(bf16[128,1728]{1,0:T(8,128)(2,1)S(1)} %shard_map.103.mine), channel_id=1, source_target_pairs={{0,1},{1,0},{2,3},{3,2},{4,5},{5,4},{6,7},{7,6},{8,9},{9,8},{10,11... | collective-permute-start | bytes 1327112 | tf_op jit(solution)/shard_map/ppermute | solution.py:347
  55.3 9.9 %collective-permute-start.19 = (bf16[2,72,1152]{2,1,0:T(8,128)(2,1)S(1)}, bf16[2,72,1152]{2,1,0:T(8,128)(2,1)S(1)}, u32[]{:S(2)}, u32[]{:S(2)}) collective-permute-start(bf16[2,72,1152]{2,1,0:T(8,128)(2,1)S(1)} %get-tuple-element.50), channel_id=1, source_target_pairs={{0,8},{8,0},{16,24},{24,16},{1,9},{9,1},{17,25},{25,17},{2,10},{10... | collective-permute-start | bytes 995336 | tf_op jit(solution)/shard_map/ppermute | solution.py:347
  55.9 9.6 %collective-permute-start.20 = (bf16[2,72,1152]{2,1,0:T(8,128)(2,1)S(1)}, bf16[2,72,1152]{2,1,0:T(8,128)(2,1)S(1)}, u32[]{:S(2)}, u32[]{:S(2)}) collective-permute-start(bf16[2,72,1152]{2,1,0:T(8,128)(2,1)S(1)} %get-tuple-element.51), channel_id=1, source_target_pairs={{0,16},{8,24},{16,0},{24,8},{1,17},{9,25},{17,1},{25,9},{2,18},{10... | collective-permute-start | bytes 995336 | tf_op jit(solution)/shard_map/ppermute | solution.py:347
  65.6 5.6 %collective-permute-start.21 = (bf16[72,1152]{1,0:T(8,128)(2,1)S(1)}, bf16[72,1152]{1,0:T(8,128)(2,1)S(1)}, u32[]{:S(2)}, u32[]{:S(2)}) collective-permute-start(bf16[72,1152]{1,0:T(8,128)(2,1)S(1)} %get-tuple-element.53), channel_id=1, source_target_pairs={{0,16},{8,24},{16,0},{24,8},{1,17},{9,25},{17,1},{25,9},{2,18},{10... | collective-permute-start | bytes 497672 | tf_op jit(solution)/shard_map/ppermute | solution.py:347
  66.2 5.3 %collective-permute-start.22 = (bf16[72,1152]{1,0:T(8,128)(2,1)S(1)}, bf16[72,1152]{1,0:T(8,128)(2,1)S(1)}, u32[]{:S(2)}, u32[]{:S(2)}) collective-permute-start(bf16[72,1152]{1,0:T(8,128)(2,1)S(1)} %get-tuple-element.54), channel_id=1, source_target_pairs={{0,8},{8,0},{16,24},{24,16},{1,9},{9,1},{17,25},{25,17},{2,10},{10... | collective-permute-start | bytes 497672 | tf_op jit(solution)/shard_map/ppermute | solution.py:347
  67.7 7.1 %collective-permute-start.16 = (bf16[32,1728]{1,0:T(8,128)(2,1)S(1)}, bf16[32,1728]{1,0:T(8,128)(2,1)S(1)}, u32[]{:S(2)}, u32[]{:S(2)}) collective-permute-start(bf16[32,1728]{1,0:T(8,128)(2,1)S(1)} %get-tuple-element.41), channel_id=1, source_target_pairs={{0,2},{1,3},{2,0},{3,1},{4,6},{5,7},{6,4},{7,5},{8,10},{9,11},{10,... | collective-permute-start | bytes 331784 | tf_op jit(solution)/shard_map/ppermute | solution.py:347
  67.7 11.4 %collective-permute-start.17 = (bf16[32,1728]{1,0:T(8,128)(2,1)S(1)}, bf16[32,1728]{1,0:T(8,128)(2,1)S(1)}, u32[]{:S(2)}, u32[]{:S(2)}) collective-permute-start(bf16[32,1728]{1,0:T(8,128)(2,1)S(1)} %get-tuple-element.42), channel_id=1, source_target_pairs={{0,4},{1,5},{2,6},{3,7},{4,0},{5,1},{6,2},{7,3},{8,12},{9,13},{10,... | collective-permute-start | bytes 331784 | tf_op jit(solution)/shard_map/ppermute | solution.py:347
  70.7 14.4 %collective-permute-start.18 = (bf16[32,1728]{1,0:T(8,128)(2,1)S(1)}, bf16[32,1728]{1,0:T(8,128)(2,1)S(1)}, u32[]{:S(2)}, u32[]{:S(2)}) collective-permute-start(bf16[32,1728]{1,0:T(8,128)(2,1)S(1)} %get-tuple-element.43), channel_id=1, source_target_pairs={{0,6},{1,7},{2,4},{3,5},{4,2},{5,3},{6,0},{7,1},{8,14},{9,15},{10,... | collective-permute-start | bytes 331784 | tf_op jit(solution)/shard_map/ppermute | solution.py:347
  71.7 21.3 %collective-permute-start.23 = (bf16[72,576]{1,0:T(8,128)(2,1)S(1)}, bf16[72,576]{1,0:T(8,128)(2,1)S(1)}, u32[]{:S(2)}, u32[]{:S(2)}) collective-permute-start(bf16[72,576]{1,0:T(8,128)(2,1)S(1)} %get-tuple-element.56), channel_id=1, source_target_pairs={{0,2},{1,3},{2,0},{3,1},{4,6},{5,7},{6,4},{7,5},{8,10},{9,11},{10,... | collective-permute-start | bytes 248840 | tf_op jit(solution)/shard_map/ppermute | solution.py:347
  72.4 20.6 %collective-permute-start.24 = (bf16[72,576]{1,0:T(8,128)(2,1)S(1)}, bf16[72,576]{1,0:T(8,128)(2,1)S(1)}, u32[]{:S(2)}, u32[]{:S(2)}) collective-permute-start(bf16[72,576]{1,0:T(8,128)(2,1)S(1)} %get-tuple-element.57), channel_id=1, source_target_pairs={{0,4},{1,5},{2,6},{3,7},{4,0},{5,1},{6,2},{7,3},{8,12},{9,13},{10,... | collective-permute-start | bytes 248840 | tf_op jit(solution)/shard_map/ppermute | solution.py:347
  74.8 10.3 %copy-start.6 = (bf16[32,1728]{1,0:T(8,128)(2,1)}, bf16[32,1728]{1,0:T(8,128)(2,1)S(1)}, u32[]{:S(2)}) copy-start(bf16[32,1728]{1,0:T(8,128)(2,1)S(1)} %collective-permute-done.16.refs_1_) | copy-start | bytes 331780
  74.8 18.3 %collective-permute-start.25 = (bf16[72,576]{1,0:T(8,128)(2,1)S(1)}, bf16[72,576]{1,0:T(8,128)(2,1)S(1)}, u32[]{:S(2)}, u32[]{:S(2)}) collective-permute-start(bf16[72,576]{1,0:T(8,128)(2,1)S(1)} %get-tuple-element.58), channel_id=1, source_target_pairs={{0,6},{1,7},{2,4},{3,5},{4,2},{5,3},{6,0},{7,1},{8,14},{9,15},{10,... | collective-permute-start | bytes 248840 | tf_op jit(solution)/shard_map/ppermute | solution.py:347
  79.0 6.0 %copy-start.7 = (bf16[32,1728]{1,0:T(8,128)(2,1)}, bf16[32,1728]{1,0:T(8,128)(2,1)S(1)}, u32[]{:S(2)}) copy-start(bf16[32,1728]{1,0:T(8,128)(2,1)S(1)} %collective-permute-done.17.refs_2_) | copy-start | bytes 331780
  (3 other events, 2.0 us)

commit v6 on v5

--- a/solution.py
+++ b/solution.py
@@ -39,7 +39,10 @@
         body,
         out_shape=outs,
         in_specs=[HBM if i in far_in else spec for i, spec in enumerate(near)],
-        out_specs=[HBM if i in far_out else VMEM for i in range(len(outs))],
+        out_specs=[
+            HBM if i in far_out else SMEM if out.dtype == jnp.int32 else VMEM
+            for i, out in enumerate(outs)
+        ],
         scratch_shapes=list(scratch),
         compiler_params=pltpu.CompilerParams(vmem_limit_bytes=LIMIT if small else MOST),
         cost_estimate=pl.CostEstimate(
@@ -59,7 +62,7 @@
     return jax.ShapeDtypeStruct(dims, dtype)
 
 
-TOKEN = shape((8, LANES), F32)
+TOKEN = shape((1,), jnp.int32)
 
 
 def window(head):
@@ -132,10 +135,15 @@
     ref[:, :width] = value
 
 
-def spatial_kernel(chips, patches, idx, *refs):
+def place(chips):
+    seq = lax.axis_index("seq")
+    return lax.axis_index("dp"), seq % 2, seq % (2 * chips) // 2, seq
+
+
+def spatial_kernel(chips, patches, *refs):
+    idx = place(chips)
     far, outs, refs = refs[:4], refs[4 : 4 + chips], refs[4 + chips :]
-    hid_far, p_far, done, tok, cot, qkv, wos, held, hid, p_ref, qs, ks, vs, sems = refs
-    done[...] = jnp.zeros_like(done)
+    hid_far, p_far, tok, cot, qkv, wos, held, hid, p_ref, qs, ks, vs, sems = refs
     inner, width = wos.shape
     count, block, _ = held.shape
     loads = started(zip(far, (qkv, tok, wos, cot)), sems)
@@ -153,21 +161,19 @@
         rows = slice(at * block, (at + 1) * block)
         held[at, :, :width] = hid[rows]
         held[at, :, width : 2 * width] = cot[rows]
-        held[at, :, 2 * width :] = o[rows]
-    pairs = [(hid, hid_far)]
+        held[at, :, 2 * width : 2 * width + inner] = o[rows]
+    stores += started([(hid, hid_far)], sems.at[pl.ds(5, 1)])
     for q in range(chips):
         for f in range(count // chips):
-            rows = pl.ds(f * block, block)
-            pairs.append((held.at[f * chips + (idx[2] ^ q)], outs[q].at[rows]))
-    stores += started(pairs, sems.at[pl.ds(5, len(pairs))])
+            rows = slice(f * block, (f + 1) * block)
+            outs[q][rows] = held[f * chips + (idx[2] ^ q)]
     for copy in stores:
         copy.wait()
 
 
-def own_patches(refs, core, block):
-    value = jnp.concatenate([ref[...] for ref in refs], axis=0)
-    rows, width = value.shape
-    value = value.astype(F32).reshape(rows // block, block, width)
+def own_patches(ref, core, block):
+    rows, width = ref.shape
+    value = ref[...].astype(F32).reshape(rows // block, block, width)
     value = jnp.where(core == 0, value[:, : block // 2], value[:, block // 2 :])
     return value.reshape(rows // 2, width)
 
@@ -180,41 +186,61 @@
     return jnp.concatenate([first, second], axis=1).reshape(2 * rows, width).astype(BF16)
 
 
-def split_kernel(near_x, near_y, _, from_x, from_y):
-    cut = from_y.shape[1]
-    from_y[...] = near_y[:, :cut]
-    from_x[...] = near_x[:, cut:]
-
-
-def pieces(shards, weights):
-    weights = list(weights)
-    for place, count, parts in shards:
-        low, held = 0, []
-        for _ in range(parts):
-            w = weights.pop(0)
-            held.append((low, w))
-            low += w.shape[1]
-        yield place, count, held
-
-
-def temporal_kernel(shards, total, chips, group, idx, *refs):
-    near, far, wot, refs = refs[:chips], refs[chips : 2 * chips], refs[2 * chips], refs[2 * chips + 1 :]
-    weights, (mine, cot, q, k, v, g, p_ref, blocks) = refs[:total], refs[total:]
+def cut_kernel(chips, whole, out, left, right, sem):
+    copy = pltpu.make_async_copy(whole.at[place(chips)[1]], out, sem.at[0])
+    copy.start()
+    copy.wait()
+    cut = left.shape[1]
+    left[...] = out[:, :cut]
+    right[...] = out[:, cut:]
+
+
+def second_kernel(mine, got_x, got_y, own, left, right, kept):
+    half, cut = got_x.shape
+    left[:half] = mine[:, :cut]
+    left[half:] = got_x[...]
+    right[:half] = mine[:, cut:]
+    right[half:] = got_y[...]
+    kept[...] = own[...]
+
+
+def join_rows_kernel(*refs):
+    out, rows = refs[-1], refs[0].shape[0]
+    for at, ref in enumerate(refs[:-1]):
+        out[at * rows : (at + 1) * rows] = ref[...]
+
+
+def projected(hidden, shards, weights, idx, blocks, sums):
+    size = blocks.shape[2]
+    sums[...] = jnp.zeros_like(sums)
+    for held, w in zip(shards, weights):
+        low = held[0][1]
+        value = dot_bt(hidden[:, low : low + w.shape[1]], w[...])
+        for at, _, i in held:
+            sums[at(idx)] += value if i is None else value[:, i * size : (i + 1) * size]
+    blocks[...] = sums[...].astype(BF16)
+
+
+def projected_back(blocks, shards, weights, idx, total):
+    total[...] = jnp.zeros_like(total)
+    for held, w in zip(shards, weights):
+        low = held[0][1]
+        lhs = jnp.concatenate([blocks[at(idx)] for at, _, _ in held], axis=1)
+        total[:, low : low + w.shape[1]] += dot(lhs, w[...])
+
+
+def temporal_kernel(shards, chips, group, near, far, wot, *refs):
+    idx = place(chips)
+    weights, refs = refs[: len(shards)], refs[len(shards) :]
+    mine, cot, q, k, v, g, p_ref, blocks, sums, total = refs
     inner, width = wot.shape
     heads = inner // DH
-    value = [own_patches(refs, idx[1], 2 * group) for refs in (near, far)]
+    value = [own_patches(ref, idx[1], 2 * group) for ref in (near, far)]
     value = jnp.concatenate(value, axis=0).astype(BF16)
     hidden = value[:, :width]
     cot[...] = value[:, width : 2 * width]
-    for place, count, held in pieces(shards, weights):
-        block = None
-        for low, w in held:
-            value = dot_bt(hidden[:, low : low + w.shape[1]], w[...])
-            block = value if block is None else block + value
-        block = block.astype(BF16)
-        size = block.shape[1] // count
-        for i in range(count):
-            blocks[place(idx) + i] = block[:, i * size : (i + 1) * size]
+    size = blocks.shape[2]
+    projected(hidden, shards, weights, idx, blocks, sums)
     whole = jnp.concatenate([blocks[i] for i in range(blocks.shape[0])], axis=1)
     put(q, whole[:, :inner])
     put(k, whole[:, inner : 2 * inner])
@@ -223,20 +249,17 @@
     put(g, dot_bt(cot[...], wot[...]).astype(BF16))
     dq, dk, dv = softmax_backward(q, k, v, g, p_ref, heads)
     whole = jnp.concatenate([dq[:, :inner], dk[:, :inner], dv[:, :inner]], axis=1)
-    size = blocks.shape[2]
     for i in range(blocks.shape[0]):
         blocks[i] = whole[:, i * size : (i + 1) * size]
-    grad = jnp.zeros(cot.shape, F32)
-    for place, count, held in pieces(shards, weights):
-        lhs = jnp.concatenate([blocks[place(idx) + i] for i in range(count)], axis=1)
-        grad += jnp.concatenate([dot(lhs, w[...]) for _, w in held], axis=1)
+    projected_back(blocks, shards, weights, idx, total)
+    grad = total[...]
     mine[:, :width] = (cot[...].astype(F32) + grad.astype(BF16).astype(F32)).astype(BF16)
 
 
-def whole_return_kernel(chips, block, inner, width, idx, mine, other, *refs):
-    held, outs, part = refs[:chips], refs[chips : 2 * chips], refs[2 * chips]
-    held = jnp.concatenate([ref[...] for ref in held], axis=0)
-    cot, so = held[:, width : 2 * width], held[:, 2 * width :]
+def whole_return_kernel(chips, block, inner, width, mine, other, *refs):
+    idx = place(chips)
+    held, outs, part = refs[0], refs[1 : 1 + chips], refs[1 + chips]
+    cot, so = held[:, width : 2 * width], held[:, 2 * width : 2 * width + inner]
     half = mine.shape[0] // 2
     near = all_patches(mine[:half], other[half:], idx[1], block)
     for q, out in enumerate(outs):
@@ -245,14 +268,18 @@
     part[1] = dot_at(so, near[:, :width]).astype(BF16)
 
 
-def return_kernel(chips, block, inner, width, idx, mine, other, *refs):
-    sent, refs = (refs[:chips], refs[chips : 2 * chips]), refs[2 * chips :]
-    sent = [jnp.concatenate([ref[...] for ref in parts], axis=0) for parts in sent]
-    outs, (keep, send_x, send_y, heads, cols) = refs[:chips], refs[chips:]
+def return_kernel(chips, block, inner, width, mine, other, *refs):
+    idx = place(chips)
+    sent, refs = refs[:2], refs[2:]
+    outs, (keep, send_x, send_y, heads, cols, kept, sem) = refs[:chips], refs[chips:]
     half = mine.shape[0] // 2
     near = all_patches(mine[:half], other[half:], idx[1], block)
-    for q, out in enumerate(outs):
-        out[...] = near[q * out.shape[0] : (q + 1) * out.shape[0]]
+    rows = kept.shape[0]
+    kept[...] = near[:rows]
+    copy = pltpu.make_async_copy(kept, outs[0], sem.at[0])
+    copy.start()
+    for q in range(1, chips):
+        outs[q][...] = near[q * rows : (q + 1) * rows]
     far = all_patches(mine[half:], other[:half], idx[1], block)
     rows = near.shape[0]
     size = heads.shape[2]
@@ -262,7 +289,7 @@
             lefts = [near[:, width:], far[:, width:]]
             rights = [part[:, width : 2 * width] for part in sent]
         else:
-            lefts = [part[:, 2 * width :] for part in sent]
+            lefts = [part[:, 2 * width : 2 * width + inner] for part in sent]
             rights = [near[:, :width], far[:, :width]]
         for at in range(2):
             held = slice(at * rows, (at + 1) * rows)
@@ -279,9 +306,10 @@
                 (send_x, send_y)[i][r // 2 if i == 0 else r - 2] = value.astype(BF16)
             else:
                 keep[2 * i + (r > 0)] = value
-
-
-def sum_first_kernel(keep, got_x, got_y, own, send_y, send_x):
+    copy.wait()
+
+
+def sum_first_kernel(_, keep, got_x, got_y, own, send_y, send_x):
     for i, (got, send) in enumerate(((got_x, send_y), (got_y, send_x))):
         own[i] = keep[2 * i] + got[0].astype(F32)
         send[...] = (keep[2 * i + 1] + got[1].astype(F32)).astype(BF16)
@@ -305,9 +333,12 @@
         out[...] = total[:, i * size : (i + 1) * size]
 
 
-def last_kernel(chips, patches, idx, *refs):
+def last_kernel(chips, patches, *refs):
+    idx = place(chips)
     loaded = 5 + chips
-    far, (block_far, out_far, grads_far), refs = refs[:loaded], refs[loaded : loaded + 3], refs[loaded + 3 :]
+    far, outs, refs = refs[:loaded], refs[loaded : loaded + 4], refs[loaded + 4 :]
+    block_far, out_far, grads_far, done = outs
+    done[0] = 0
     rows, wos, qkv, p_ref, wot, hid, block_out, grads, qs, ks, vs, gs, sems = refs
     inner, width = wos.shape
     frames = rows.shape[0] // patches
@@ -351,47 +382,56 @@
     return pltpu.SemaphoreType.DMA((n,))
 
 
-def gather_weight(weight, core, after):
+def gather(weight, parts, chips):
     n = lax.axis_size("dp")
+    rows, sent = parts[0].shape
+    whole = [shape((len(parts) * rows, sent))]
     if n != 4:
-        return [lax.all_gather(weight, "dp", axis=0, tiled=True)], [(lambda idx: 0, 1, 1)], 1
+        (near,) = call(join_rows_kernel, whole, from_chips(parts), small=True)
+        weights = [lax.all_gather(weight, "dp", axis=0, tiled=True)]
+        return near, flip(near, "seq", 1), weights, [[(lambda idx: 0, 0, None)]], 1
     half, width = weight.shape[0] // 2, weight.shape[1]
-    mine = lax.dynamic_slice_in_dim(weight, core * half, half, 0)
-    near = [flip(mine, "dp", 1), flip(mine, "dp", 2)]
-    cut = width // LANES // 2 * LANES
-    from_x, from_y = call(
-        split_kernel,
-        [shape((half, width - cut)), shape((half, cut))],
-        [*near, after],
+    cut = -(-width // LANES // 2) * LANES
+    mine, left, right = call(
+        functools.partial(cut_kernel, chips),
+        [shape((half, width)), shape((half, cut)), shape((half, width - cut))],
+        [weight.reshape(2, half, width)],
+        [sems(1)],
+        far_in=range(1),
+    )
+    got_x, got_y = flip(left, "dp", 1), flip(right, "dp", 2)
+    left, right, own = call(
+        second_kernel,
+        [shape((2 * half, cut)), shape((2 * half, width - cut)), shape((rows, sent))],
+        [mine, got_x, got_y, parts[0]],
         small=True,
     )
-    corner = [flip(from_y, "dp", 1), flip(from_x, "dp", 2)]
-    held = near + corner
-    far = [flip(w, "seq", 1) for w in held]
-    shards = [(lambda idx: 2 * idx[0], 2, 1)]
-    for flipped in range(2):
-        for j in range(1, n):
-            shards.append(
-                (
-                    lambda idx, j=j, flipped=flipped: 2 * (idx[0] ^ j) + (idx[1] ^ flipped),
-                    1,
-                    1 if j < 3 else 2,
-                )
-            )
-    return [weight, *held, *far], shards, 2 * n
+    (near,) = call(join_rows_kernel, whole, [own, *from_chips(parts)[1:]], small=True)
+    held = [got_x, got_y, flip(left, "dp", 2), flip(right, "dp", 1)]
+    weights = [weight, *held, *[flip(w, "seq", 1) for w in held]]
+
+    def block(j, other):
+        return lambda idx: 2 * (idx[0] ^ j) + (idx[1] ^ other)
+
+    shards = [[(lambda idx: 2 * idx[0], 0, 0), (lambda idx: 2 * idx[0] + 1, 0, 1)]]
+    for other in (0, 1):
+        shards += [[(block(1, other), 0, None)], [(block(2, other), cut, None)]]
+        shards.append([(block(2, other), 0, 0), (block(3, other), 0, 1)])
+        shards.append([(block(1, other), cut, 0), (block(3, other), cut, 1)])
+    return near, flip(near, "seq", 1), weights, shards, 2 * n
 
 
 def from_chips(parts):
     return [parts[0]] + [flip(parts[q], "seq", 2 * q) for q in range(1, len(parts))]
 
 
-def reduced(keep, send_x, send_y):
+def reduced(keep, send_x, send_y, after):
     _, size, width = keep.shape
     step = shape((size, width))
     own, send_t, send_s = call(
         sum_first_kernel,
         [shape((2, size, width), F32), step, step],
-        [keep, flip(send_x, "dp", 1), flip(send_y, "dp", 2)],
+        [after, keep, flip(send_x, "dp", 1), flip(send_y, "dp", 2)],
         small=True,
     )
     n = lax.axis_size("seq") // 2
@@ -417,8 +457,6 @@
     group = patches // peers
     block = 2 * group
     n_dp, n_seq = lax.axis_size("dp"), lax.axis_size("seq")
-    seq = lax.axis_index("seq")
-    idx = jnp.stack([lax.axis_index("dp"), seq % 2, seq % peers // 2, seq]).astype(jnp.int32)
 
     def held(columns, dtype=BF16):
         return pltpu.VMEM((rows, columns), dtype)
@@ -428,30 +466,29 @@
     projection = pltpu.VMEM((inner, width), BF16)
     per_chip = rows // chips
     qkv_rows = spatial_qkv.reshape(rows, 3 * inner)
-    sent = 2 * width + inner
-    *near, hidden, spatial_p, done = call(
+    sent = -(-(2 * width + inner) // LANES) * LANES
+    *near, hidden, spatial_p = call(
         functools.partial(spatial_kernel, chips, patches),
         [shape((per_chip, sent))] * chips
-        + [shape((rows, width)), shape((heads, rows, rows), F32), TOKEN],
-        [idx, qkv_rows, tokens.reshape(rows, width), wo_spatial, cotangent.reshape(rows, width)],
+        + [shape((rows, width)), shape((heads, rows, rows), F32)],
+        [qkv_rows, tokens.reshape(rows, width), wo_spatial, cotangent.reshape(rows, width)],
         [held(width), held(width), held(3 * inner), projection]
         + [pltpu.VMEM((frames * chips, block, sent), BF16), held(width), attended]
         + [wide] * 3
-        + [sems(6 + chips * frames)],
-        us=4,
-        far_in=range(1, 5),
-        far_out=range(chips + 2),
-    )
-    weights, places, count = gather_weight(w_temporal.T, seq % 2, done)
-    near = from_chips(near)
-    far = [flip(value, "seq", 1) for value in near]
-    blocks = pltpu.VMEM((count, rows, 3 * inner // count), BF16)
+        + [sems(6)],
+        far_in=range(4),
+        far_out=(chips, chips + 1),
+    )
+    near, far, weights, places, count = gather(w_temporal.T, near, chips)
+
+    def blocks(dtype):
+        return pltpu.VMEM((count, rows, 3 * inner // count), dtype)
+
     (mine,) = call(
-        functools.partial(temporal_kernel, places, len(weights), chips, group),
+        functools.partial(temporal_kernel, places, chips, group),
         [shape((rows, width + inner))],
-        [idx, *near, *far, wo_temporal, *weights],
-        [held(width)] + [wide] * 4 + [attended, blocks],
-        us=10,
+        [near, far, wo_temporal, *weights],
+        [held(width)] + [wide] * 4 + [attended, blocks(BF16), blocks(F32), held(width, F32)],
         small=True,
     )
     other = flip(mine, "seq", 1)
@@ -463,38 +500,40 @@
             back
             + [shape((n_dp, size, width), F32)]
             + [shape((2, size, width))] * 2,
-            [idx, mine, other, *near, *far],
+            [mine, other, near, far],
             [
                 pltpu.VMEM((n_seq, 2 * rows, size), BF16),
                 pltpu.VMEM((n_dp, 2 * rows, width // n_dp), BF16),
+                pltpu.VMEM((per_chip, width + inner), BF16),
+                sems(1),
             ],
-            us=0,
+            far_out=range(1),
             small=True,
         )
-        temporal_grad, spatial_grad = reduced(keep, send_x, send_y)
     else:
         *back, both = call(
             functools.partial(whole_return_kernel, chips, block, inner, width),
             back + [shape((2, inner, width))],
-            [idx, mine, other, *near],
-            us=0,
+            [mine, other, near],
             small=True,
         )
-        both = lax.psum_scatter(both, "seq", scatter_dimension=1, tiled=True)
-        both = lax.psum_scatter(both, "dp", scatter_dimension=2, tiled=True).astype(F32)
-        temporal_grad, spatial_grad = both[0], both[1]
-    block_out, tokens_grad, qkv_grad = call(
+    block_out, tokens_grad, qkv_grad, done = call(
         functools.partial(last_kernel, chips, patches),
-        [shape((rows, width)), shape((rows, width)), shape((rows, 3 * inner))],
-        [idx, *from_chips(back), wo_spatial, qkv_rows, spatial_p, wo_temporal, hidden],
+        [shape((rows, width)), shape((rows, width)), shape((rows, 3 * inner)), TOKEN],
+        [*from_chips(back), wo_spatial, qkv_rows, spatial_p, wo_temporal, hidden],
         [held(width + inner), projection, held(3 * inner), attended, projection, held(width)]
         + [held(width), held(3 * inner)]
         + [wide] * 4
         + [sems(8 + chips * frames)],
-        us=6,
-        far_in=range(1, 6 + chips),
+        far_in=range(5 + chips),
         far_out=range(3),
     )
+    if n_dp == 4 and n_seq == peers:
+        temporal_grad, spatial_grad = reduced(keep, send_x, send_y, done)
+    else:
+        both = lax.psum_scatter(both, "seq", scatter_dimension=1, tiled=True)
+        both = lax.psum_scatter(both, "dp", scatter_dimension=2, tiled=True).astype(F32)
+        temporal_grad, spatial_grad = both[0], both[1]
     return (
         block_out.reshape(frames, patches, width),
         tokens_grad.reshape(frames, patches, width),

time: 94.1 us -> 92.8 us (0.986)
  the two profiles are of different devices: /device:TPU:8 before, /device:TPU:0 now
where the time goes in v6:
time: 92.8 us; the launch traced here: 92.6 us
  waiting for transfers between devices  36.8 us (40%)
  starting transfers between devices  27 us (29%)
  Pallas kernels  25.8 us (28%)
  local copies, waits for them, and re-layouts  2.26 us (2%)
    ppermute x23, waiting for transfers between devices, flip(): lax.ppermute(value, axis, [(i, i ^ bit) for i in range(lax.axis_size(axis...  36.8 us
    ppermute x23, starting transfers between devices, flip(): lax.ppermute(value, axis, [(i, i ^ bit) for i in range(lax.axis_size(axis...  27 us
    pallas_call x10, Pallas kernels, call(): pl.pallas_call(body, out_shape=outs, in_specs=[HBM if i in far_in else sp...  25.8 us
    unnamed x16, local copies, waits for them, and re-layouts  2.26 us
  transfers between devices with their start and end apart: 23, of which 11 were waited for; matrix products, arithmetic and copies ran while one was open for 0% of the time, Pallas kernels for 13%

profile of v6, /device:TPU:0, one launch (start us, length us, event | category | flops | bytes accessed | tf_op | source)
XLA Modules:
  0.0 92.6 jit_solution(5678534145620796888)
XLA Ops:
  0.6 2.0 %shard_map.101 = (bf16[216,1152]{1,0:T(8,128)(2,1)}, bf16[216,640]{1,0:T(8,128)(2,1)}, bf16[216,512]{1,0:T(8,128)(2,1)}) custom-call(bf16[2,216,1152]{2,1,0:T(8,128)(2,1)} %bitcast.9), custom_call_target="tpu_custom_call" | custom-call | tf_op jit(solution)/shard_map/pallas_call | solution.py:38
  2.6 3.0 %collective-permute-start = (bf16[216,640]{1,0:T(8,128)(2,1)}, bf16[216,640]{1,0:T(8,128)(2,1)S(1)}, u32[]{:S(2)}, u32[]{:S(2)}) collective-permute-start(bf16[216,640]{1,0:T(8,128)(2,1)} %get-tuple-element.38), channel_id=1, source_target_pairs={{0,8},{8,0},{16,24},{24,16},{1,9},{9,1},{17,25},{25,17},{2,10},{10... | collective-permute-start | bytes 829448 | tf_op jit(solution)/shard_map/ppermute | solution.py:378
  5.6 1.5 %collective-permute-start.1 = (bf16[216,512]{1,0:T(8,128)(2,1)}, bf16[216,512]{1,0:T(8,128)(2,1)S(1)}, u32[]{:S(2)}, u32[]{:S(2)}) collective-permute-start(bf16[216,512]{1,0:T(8,128)(2,1)} %get-tuple-element.39), channel_id=1, source_target_pairs={{0,16},{8,24},{16,0},{24,8},{1,17},{9,25},{17,1},{25,9},{2,18},{10... | collective-permute-start | bytes 663560 | tf_op jit(solution)/shard_map/ppermute | solution.py:378
  7.2 4.8 %shard_map.102 = (bf16[32,2944]{1,0:T(8,128)(2,1)}, bf16[32,2944]{1,0:T(8,128)(2,1)}, bf16[32,2944]{1,0:T(8,128)(2,1)}, bf16[32,2944]{1,0:T(8,128)(2,1)}, bf16[1...) custom-call(bf16[128,1728]{1,0:T(8,128)(2,1)} %bitcast.11, bf16[128,1152]{1,0:T(8,128)(2,1)} %bitcast.13, ...), custom_call_target="tpu_custom_call" | custom-call | tf_op jit(solution)/shard_map/pallas_call | solution.py:38
  12.0 0.8 collective-permute-done.1.got_y.refs_2_
  12.8 0.9 copy-done.3
  13.8 1.6 %collective-permute-start.6 = (bf16[432,640]{1,0:T(8,128)(2,1)S(1)}, bf16[432,640]{1,0:T(8,128)(2,1)S(1)}, u32[]{:S(2)}, u32[]{:S(2)}) collective-permute-start(bf16[432,640]{1,0:T(8,128)(2,1)S(1)} %get-tuple-element.45), channel_id=1, source_target_pairs={{0,16},{8,24},{16,0},{24,8},{1,17},{9,25},{17,1},{25,9},{2,18},{10... | collective-permute-start | bytes 1658888 | tf_op jit(solution)/shard_map/ppermute | solution.py:378
  15.4 1.6 %collective-permute-start.2 = (bf16[32,2944]{1,0:T(8,128)(2,1)}, bf16[32,2944]{1,0:T(8,128)(2,1)S(1)}, u32[]{:S(2)}, u32[]{:S(2)}) collective-permute-start(bf16[32,2944]{1,0:T(8,128)(2,1)} %get-tuple-element.42), channel_id=1, source_target_pairs={{0,2},{1,3},{2,0},{3,1},{4,6},{5,7},{6,4},{7,5},{8,10},{9,11},{10,... | collective-permute-start | bytes 565256 | tf_op jit(solution)/shard_map/ppermute | solution.py:378
  16.9 2.6 %collective-permute-start.3 = (bf16[32,2944]{1,0:T(8,128)(2,1)}, bf16[32,2944]{1,0:T(8,128)(2,1)S(1)}, u32[]{:S(2)}, u32[]{:S(2)}) collective-permute-start(bf16[32,2944]{1,0:T(8,128)(2,1)} %get-tuple-element.43), channel_id=1, source_target_pairs={{0,4},{1,5},{2,6},{3,7},{4,0},{5,1},{6,2},{7,3},{8,12},{9,13},{10,... | collective-permute-start | bytes 565256 | tf_op jit(solution)/shard_map/ppermute | solution.py:378
  19.7 1.5 %collective-permute-start.7 = (bf16[432,512]{1,0:T(8,128)(2,1)S(1)}, bf16[432,512]{1,0:T(8,128)(2,1)S(1)}, u32[]{:S(2)}, u32[]{:S(2)}) collective-permute-start(bf16[432,512]{1,0:T(8,128)(2,1)S(1)} %get-tuple-element.46), channel_id=1, source_target_pairs={{0,8},{8,0},{16,24},{24,16},{1,9},{9,1},{17,25},{25,17},{2,10},{10... | collective-permute-start | bytes 1327112 | tf_op jit(solution)/shard_map/ppermute | solution.py:378
  21.2 2.3 %collective-permute-done.2.refs_1_ = bf16[32,2944]{1,0:T(8,128)(2,1)S(1)} collective-permute-done((bf16[32,2944]{1,0:T(8,128)(2,1)}, bf16[32,2944]{1,0:T(8,128)(2,1)S(1)}, u32[]{:S(2)}, u32[]{:S(2)}) %collective-permute-start.2) | collective-permute-done | bytes 188448 | tf_op jit(solution)/shard_map/ppermute | solution.py:378
  23.5 9.7 %collective-permute-done.3.refs_2_ = bf16[32,2944]{1,0:T(8,128)(2,1)S(1)} collective-permute-done((bf16[32,2944]{1,0:T(8,128)(2,1)}, bf16[32,2944]{1,0:T(8,128)(2,1)S(1)}, u32[]{:S(2)}, u32[]{:S(2)}) %collective-permute-start.3) | collective-permute-done | bytes 188448 | tf_op jit(solution)/shard_map/ppermute | solution.py:378
  34.4 3.3 %collective-permute-done.9.refs_6_ = bf16[216,512]{1,0:T(8,128)(2,1)S(1)} collective-permute-done((bf16[216,512]{1,0:T(8,128)(2,1)S(1)}, bf16[216,512]{1,0:T(8,128)(2,1)S(1)}, u32[]{:S(2)}, u32[]{:S(2)}) %collective-permute-start.9) | collective-permute-done | bytes 221216 | tf_op jit(solution)/shard_map/ppermute | solution.py:378
  37.7 7.1 %shard_map.105.mine = bf16[128,1728]{1,0:T(8,128)(2,1)S(1)} custom-call(bf16[128,2944]{1,0:T(8,128)(2,1)S(1)} %shard_map.104.near.refs_0_, bf16[128,2944]{1,0:T(8,128)(2,1)S(1)} %collective-permute-done.5.far.refs_1_, bf16[576,1152]{1,0:T(8,128)(2,1)S(1)} %copy-done, bf16[432,1152]{1,0:T(8,128)(2,1)S(1)} %bitcast.10, ...), custom_call_target="tpu_custom_call" | custom-call | tf_op jit(solution)/shard_map/pallas_call | solution.py:38
  45.0 1.7 %collective-permute-done.12.other = bf16[128,1728]{1,0:T(8,128)(2,1)S(1)} collective-permute-done((bf16[128,1728]{1,0:T(8,128)(2,1)S(1)}, bf16[128,1728]{1,0:T(8,128)(2,1)S(1)}, u32[]{:S(2)}, u32[]{:S(2)}) %collective-permute-start.12) | collective-permute-done | bytes 442400 | tf_op jit(solution)/shard_map/ppermute | solution.py:378
  46.7 2.9 %shard_map.106 = (bf16[32,1728]{1,0:T(8,128)(2,1)S(1)}, bf16[32,1728]{1,0:T(8,128)(2,1)S(1)}, bf16[32,1728]{1,0:T(8,128)(2,1)S(1)}, bf16[32,1728]{1,0:T(8,128)(2...) custom-call(bf16[128,1728]{1,0:T(8,128)(2,1)S(1)} %shard_map.105.mine, ...), custom_call_target="tpu_custom_call" | custom-call | tf_op jit(solution)/shard_map/pallas_call | solution.py:38
  50.2 1.5 %collective-permute-start.16 = (bf16[2,72,1152]{2,1,0:T(8,128)(2,1)S(1)}, bf16[2,72,1152]{2,1,0:T(8,128)(2,1)S(1)}, u32[]{:S(2)}, u32[]{:S(2)}) collective-permute-start(bf16[2,72,1152]{2,1,0:T(8,128)(2,1)S(1)} %get-tuple-element.58), channel_id=1, source_target_pairs={{0,8},{8,0},{16,24},{24,16},{1,9},{9,1},{17,25},{25,17},{2,10},{10... | collective-permute-start | bytes 995336 | tf_op jit(solution)/shard_map/ppermute | solution.py:378
  52.2 2.6 %collective-permute-start.13 = (bf16[32,1728]{1,0:T(8,128)(2,1)S(1)}, bf16[32,1728]{1,0:T(8,128)(2,1)S(1)}, u32[]{:S(2)}, u32[]{:S(2)}) collective-permute-start(bf16[32,1728]{1,0:T(8,128)(2,1)S(1)} %get-tuple-element.48), channel_id=1, source_target_pairs={{0,2},{1,3},{2,0},{3,1},{4,6},{5,7},{6,4},{7,5},{8,10},{9,11},{10,... | collective-permute-start | bytes 331784 | tf_op jit(solution)/shard_map/ppermute | solution.py:378
  54.8 1.0 %collective-permute-start.14 = (bf16[32,1728]{1,0:T(8,128)(2,1)S(1)}, bf16[32,1728]{1,0:T(8,128)(2,1)S(1)}, u32[]{:S(2)}, u32[]{:S(2)}) collective-permute-start(bf16[32,1728]{1,0:T(8,128)(2,1)S(1)} %get-tuple-element.49), channel_id=1, source_target_pairs={{0,4},{1,5},{2,6},{3,7},{4,0},{5,1},{6,2},{7,3},{8,12},{9,13},{10,... | collective-permute-start | bytes 331784 | tf_op jit(solution)/shard_map/ppermute | solution.py:378
  55.9 1.5 %collective-permute-start.15 = (bf16[32,1728]{1,0:T(8,128)(2,1)S(1)}, bf16[32,1728]{1,0:T(8,128)(2,1)S(1)}, u32[]{:S(2)}, u32[]{:S(2)}) collective-permute-start(bf16[32,1728]{1,0:T(8,128)(2,1)S(1)} %get-tuple-element.50), channel_id=1, source_target_pairs={{0,6},{1,7},{2,4},{3,5},{4,2},{5,3},{6,0},{7,1},{8,14},{9,15},{10,... | collective-permute-start | bytes 331784 | tf_op jit(solution)/shard_map/ppermute | solution.py:378
  57.3 1.1 %collective-permute-done.13.refs_1_ = bf16[32,1728]{1,0:T(8,128)(2,1)S(1)} collective-permute-done((bf16[32,1728]{1,0:T(8,128)(2,1)S(1)}, bf16[32,1728]{1,0:T(8,128)(2,1)S(1)}, u32[]{:S(2)}, u32[]{:S(2)}) %collective-permute-start.13) | collective-permute-done | bytes 110624 | tf_op jit(solution)/shard_map/ppermute | solution.py:378
  58.4 7.8 %collective-permute-done.14.refs_2_ = bf16[32,1728]{1,0:T(8,128)(2,1)S(1)} collective-permute-done((bf16[32,1728]{1,0:T(8,128)(2,1)S(1)}, bf16[32,1728]{1,0:T(8,128)(2,1)S(1)}, u32[]{:S(2)}, u32[]{:S(2)}) %collective-permute-start.14) | collective-permute-done | bytes 110624 | tf_op jit(solution)/shard_map/ppermute | solution.py:378
  67.0 7.2 %shard_map.107 = (bf16[128,1152]{1,0:T(8,128)(2,1)}, bf16[128,1152]{1,0:T(8,128)(2,1)}, bf16[128,1728]{1,0:T(8,128)(2,1)}, s32[1]{0:T(128)}) custom-call(bf16[32,1728]{1,0:T(8,128)(2,1)} %copy-done.4, bf16[32,1728]{1,0:T(8,128)(2,1)} %copy-done.5, bf16[32,1728]{1,0:T(8,128)(2,1)} %copy-done.6, bf16[32,1728]{1,0:T(8,128)(2,1)} %copy-done.7, ...), custom_call_target="tpu_custom_call" | custom-call | tf_op jit(solution)/shard_map/pallas_call | solution.py:38
  74.2 0.8 shard_map.108
  74.9 1.6 %collective-permute-start.18 = (bf16[72,1152]{1,0:T(8,128)(2,1)S(1)}, bf16[72,1152]{1,0:T(8,128)(2,1)S(1)}, u32[]{:S(2)}, u32[]{:S(2)}) collective-permute-start(bf16[72,1152]{1,0:T(8,128)(2,1)S(1)} %get-tuple-element.61), channel_id=1, source_target_pairs={{0,16},{8,24},{16,0},{24,8},{1,17},{9,25},{17,1},{25,9},{2,18},{10... | collective-permute-start | bytes 497672 | tf_op jit(solution)/shard_map/ppermute | solution.py:378
  77.0 3.3 %collective-permute-done.18.got_y = bf16[72,1152]{1,0:T(8,128)(2,1)S(1)} collective-permute-done((bf16[72,1152]{1,0:T(8,128)(2,1)S(1)}, bf16[72,1152]{1,0:T(8,128)(2,1)S(1)}, u32[]{:S(2)}, u32[]{:S(2)}) %collective-permute-start.18) | collective-permute-done | bytes 165920 | tf_op jit(solution)/shard_map/ppermute | solution.py:378
  80.3 1.5 %collective-permute-done.19.got_x = bf16[72,1152]{1,0:T(8,128)(2,1)S(1)} collective-permute-done((bf16[72,1152]{1,0:T(8,128)(2,1)S(1)}, bf16[72,1152]{1,0:T(8,128)(2,1)S(1)}, u32[]{:S(2)}, u32[]{:S(2)}) %collective-permute-start.19) | collective-permute-done | bytes 165920 | tf_op jit(solution)/shard_map/ppermute | solution.py:378
  82.1 1.8 %collective-permute-start.20 = (bf16[72,576]{1,0:T(8,128)(2,1)S(1)}, bf16[72,576]{1,0:T(8,128)(2,1)S(1)}, u32[]{:S(2)}, u32[]{:S(2)}) collective-permute-start(bf16[72,576]{1,0:T(8,128)(2,1)S(1)} %get-tuple-element.64), channel_id=1, source_target_pairs={{0,2},{1,3},{2,0},{3,1},{4,6},{5,7},{6,4},{7,5},{8,10},{9,11},{10,... | collective-permute-start | bytes 248840 | tf_op jit(solution)/shard_map/ppermute | solution.py:378
  83.9 1.0 %collective-permute-start.21 = (bf16[72,576]{1,0:T(8,128)(2,1)S(1)}, bf16[72,576]{1,0:T(8,128)(2,1)S(1)}, u32[]{:S(2)}, u32[]{:S(2)}) collective-permute-start(bf16[72,576]{1,0:T(8,128)(2,1)S(1)} %get-tuple-element.65), channel_id=1, source_target_pairs={{0,4},{1,5},{2,6},{3,7},{4,0},{5,1},{6,2},{7,3},{8,12},{9,13},{10,... | collective-permute-start | bytes 248840 | tf_op jit(solution)/shard_map/ppermute | solution.py:378
  84.8 1.7 %collective-permute-start.22 = (bf16[72,576]{1,0:T(8,128)(2,1)S(1)}, bf16[72,576]{1,0:T(8,128)(2,1)S(1)}, u32[]{:S(2)}, u32[]{:S(2)}) collective-permute-start(bf16[72,576]{1,0:T(8,128)(2,1)S(1)} %get-tuple-element.66), channel_id=1, source_target_pairs={{0,6},{1,7},{2,4},{3,5},{4,2},{5,3},{6,0},{7,1},{8,14},{9,15},{10,... | collective-permute-start | bytes 248840 | tf_op jit(solution)/shard_map/ppermute | solution.py:378
  86.7 5.2 %collective-permute-done.21.refs_1_ = bf16[72,576]{1,0:T(8,128)(2,1)S(1)} collective-permute-done((bf16[72,576]{1,0:T(8,128)(2,1)S(1)}, bf16[72,576]{1,0:T(8,128)(2,1)S(1)}, u32[]{:S(2)}, u32[]{:S(2)}) %collective-permute-start.21) | collective-permute-done | bytes 82976 | tf_op jit(solution)/shard_map/ppermute | solution.py:378
  91.8 0.8 shard_map.110
  (40 shorter events, 4.5 us)
Async XLA Ops:
  2.6 10.1 %copy-start.2 = (bf16[216,1152]{1,0:T(8,128)(2,1)S(1)}, bf16[216,1152]{1,0:T(8,128)(2,1)}, u32[]{:S(2)}) copy-start(bf16[216,1152]{1,0:T(8,128)(2,1)} %get-tuple-element.37.mine) | copy-start | bytes 1492996
  2.6 10.1 %collective-permute-start = (bf16[216,640]{1,0:T(8,128)(2,1)}, bf16[216,640]{1,0:T(8,128)(2,1)S(1)}, u32[]{:S(2)}, u32[]{:S(2)}) collective-permute-start(bf16[216,640]{1,0:T(8,128)(2,1)} %get-tuple-element.38), channel_id=1, source_target_pairs={{0,8},{8,0},{16,24},{24,16},{1,9},{9,1},{17,25},{25,17},{2,10},{10... | collective-permute-start | bytes 829448 | tf_op jit(solution)/shard_map/ppermute | solution.py:378
  5.6 7.1 %collective-permute-start.1 = (bf16[216,512]{1,0:T(8,128)(2,1)}, bf16[216,512]{1,0:T(8,128)(2,1)S(1)}, u32[]{:S(2)}, u32[]{:S(2)}) collective-permute-start(bf16[216,512]{1,0:T(8,128)(2,1)} %get-tuple-element.39), channel_id=1, source_target_pairs={{0,16},{8,24},{16,0},{24,8},{1,17},{9,25},{17,1},{25,9},{2,18},{10... | collective-permute-start | bytes 663560 | tf_op jit(solution)/shard_map/ppermute | solution.py:378
  12.7 0.9 %copy-start.3 = (bf16[32,2944]{1,0:T(8,128)(2,1)S(1)}, bf16[32,2944]{1,0:T(8,128)(2,1)}, u32[]{:S(2)}) copy-start(bf16[32,2944]{1,0:T(8,128)(2,1)} %get-tuple-element.40.own) | copy-start | bytes 565252
  13.7 24.0 %copy-start = (bf16[576,1152]{1,0:T(8,128)(2,1)S(1)}, bf16[576,1152]{1,0:T(8,128)(2,1)}, u32[]{:S(2)}) copy-start(bf16[576,1152]{1,0:T(8,128)(2,1)} %refs_7_.1) | copy-start | bytes 3981316
  13.7 24.0 %copy-start.1 = (bf16[1152,432]{0,1:T(8,128)(2,1)S(1)}, bf16[1152,432]{0,1:T(8,128)(2,1)}, u32[]{:S(2)}) copy-start(bf16[1152,432]{0,1:T(8,128)(2,1)} %param.9) | copy-start | bytes 2985988
  13.8 19.5 %collective-permute-start.6 = (bf16[432,640]{1,0:T(8,128)(2,1)S(1)}, bf16[432,640]{1,0:T(8,128)(2,1)S(1)}, u32[]{:S(2)}, u32[]{:S(2)}) collective-permute-start(bf16[432,640]{1,0:T(8,128)(2,1)S(1)} %get-tuple-element.45), channel_id=1, source_target_pairs={{0,16},{8,24},{16,0},{24,8},{1,17},{9,25},{17,1},{25,9},{2,18},{10... | collective-permute-start | bytes 1658888 | tf_op jit(solution)/shard_map/ppermute | solution.py:378
  15.4 8.1 %collective-permute-start.2 = (bf16[32,2944]{1,0:T(8,128)(2,1)}, bf16[32,2944]{1,0:T(8,128)(2,1)S(1)}, u32[]{:S(2)}, u32[]{:S(2)}) collective-permute-start(bf16[32,2944]{1,0:T(8,128)(2,1)} %get-tuple-element.42), channel_id=1, source_target_pairs={{0,2},{1,3},{2,0},{3,1},{4,6},{5,7},{6,4},{7,5},{8,10},{9,11},{10,... | collective-permute-start | bytes 565256 | tf_op jit(solution)/shard_map/ppermute | solution.py:378
  16.9 16.2 %collective-permute-start.3 = (bf16[32,2944]{1,0:T(8,128)(2,1)}, bf16[32,2944]{1,0:T(8,128)(2,1)S(1)}, u32[]{:S(2)}, u32[]{:S(2)}) collective-permute-start(bf16[32,2944]{1,0:T(8,128)(2,1)} %get-tuple-element.43), channel_id=1, source_target_pairs={{0,4},{1,5},{2,6},{3,7},{4,0},{5,1},{6,2},{7,3},{8,12},{9,13},{10,... | collective-permute-start | bytes 565256 | tf_op jit(solution)/shard_map/ppermute | solution.py:378
  19.5 13.6 %collective-permute-start.4 = (bf16[32,2944]{1,0:T(8,128)(2,1)}, bf16[32,2944]{1,0:T(8,128)(2,1)S(1)}, u32[]{:S(2)}, u32[]{:S(2)}) collective-permute-start(bf16[32,2944]{1,0:T(8,128)(2,1)} %get-tuple-element.44), channel_id=1, source_target_pairs={{0,6},{1,7},{2,4},{3,5},{4,2},{5,3},{6,0},{7,1},{8,14},{9,15},{10,... | collective-permute-start | bytes 565256 | tf_op jit(solution)/shard_map/ppermute | solution.py:378
  19.7 14.1 %collective-permute-start.7 = (bf16[432,512]{1,0:T(8,128)(2,1)S(1)}, bf16[432,512]{1,0:T(8,128)(2,1)S(1)}, u32[]{:S(2)}, u32[]{:S(2)}) collective-permute-start(bf16[432,512]{1,0:T(8,128)(2,1)S(1)} %get-tuple-element.46), channel_id=1, source_target_pairs={{0,8},{8,0},{16,24},{24,16},{1,9},{9,1},{17,25},{25,17},{2,10},{10... | collective-permute-start | bytes 1327112 | tf_op jit(solution)/shard_map/ppermute | solution.py:378
  33.2 4.4 %collective-permute-start.5 = (bf16[128,2944]{1,0:T(8,128)(2,1)S(1)}, bf16[128,2944]{1,0:T(8,128)(2,1)S(1)}, u32[]{:S(2)}, u32[]{:S(2)}) collective-permute-start(bf16[128,2944]{1,0:T(8,128)(2,1)S(1)} %shard_map.104.near.refs_0_), channel_id=1, source_target_pairs={{0,1},{1,0},{2,3},{3,2},{4,5},{5,4},{6,7},{7,6},{8,9},{9,8},{10,11... | collective-permute-start | bytes 2261000 | tf_op jit(solution)/shard_map/ppermute | solution.py:378
  33.3 4.4 %collective-permute-start.10 = (bf16[432,640]{1,0:T(8,128)(2,1)S(1)}, bf16[432,640]{1,0:T(8,128)(2,1)S(1)}, u32[]{:S(2)}, u32[]{:S(2)}) collective-permute-start(bf16[432,640]{1,0:T(8,128)(2,1)S(1)} %collective-permute-done.6.refs_3_), channel_id=1, source_target_pairs={{0,1},{1,0},{2,3},{3,2},{4,5},{5,4},{6,7},{7,6},{8,9},{9,8},{10,11... | collective-permute-start | bytes 1658888 | tf_op jit(solution)/shard_map/ppermute | solution.py:378
  33.8 3.9 %collective-permute-start.11 = (bf16[432,512]{1,0:T(8,128)(2,1)S(1)}, bf16[432,512]{1,0:T(8,128)(2,1)S(1)}, u32[]{:S(2)}, u32[]{:S(2)}) collective-permute-start(bf16[432,512]{1,0:T(8,128)(2,1)S(1)} %collective-permute-done.7.refs_4_), channel_id=1, source_target_pairs={{0,1},{1,0},{2,3},{3,2},{4,5},{5,4},{6,7},{7,6},{8,9},{9,8},{10,11... | collective-permute-start | bytes 1327112 | tf_op jit(solution)/shard_map/ppermute | solution.py:378
  33.9 3.8 %collective-permute-start.8 = (bf16[216,640]{1,0:T(8,128)(2,1)S(1)}, bf16[216,640]{1,0:T(8,128)(2,1)S(1)}, u32[]{:S(2)}, u32[]{:S(2)}) collective-permute-start(bf16[216,640]{1,0:T(8,128)(2,1)S(1)} %collective-permute-done.got_x.refs_1_), channel_id=1, source_target_pairs={{0,1},{1,0},{2,3},{3,2},{4,5},{5,4},{6,7},{7,6},{8,9},{9,8},{10,11... | collective-permute-start | bytes 829448 | tf_op jit(solution)/shard_map/ppermute | solution.py:378
  34.3 3.3 %collective-permute-start.9 = (bf16[216,512]{1,0:T(8,128)(2,1)S(1)}, bf16[216,512]{1,0:T(8,128)(2,1)S(1)}, u32[]{:S(2)}, u32[]{:S(2)}) collective-permute-start(bf16[216,512]{1,0:T(8,128)(2,1)S(1)} %collective-permute-done.1.got_y.refs_2_), channel_id=1, source_target_pairs={{0,1},{1,0},{2,3},{3,2},{4,5},{5,4},{6,7},{7,6},{8,9},{9,8},{10,11... | collective-permute-start | bytes 663560 | tf_op jit(solution)/shard_map/ppermute | solution.py:378
  44.8 1.9 %collective-permute-start.12 = (bf16[128,1728]{1,0:T(8,128)(2,1)S(1)}, bf16[128,1728]{1,0:T(8,128)(2,1)S(1)}, u32[]{:S(2)}, u32[]{:S(2)}) collective-permute-start(bf16[128,1728]{1,0:T(8,128)(2,1)S(1)} %shard_map.105.mine), channel_id=1, source_target_pairs={{0,1},{1,0},{2,3},{3,2},{4,5},{5,4},{6,7},{7,6},{8,9},{9,8},{10,11... | collective-permute-start | bytes 1327112 | tf_op jit(solution)/shard_map/ppermute | solution.py:378
  49.6 0.6 copy-start.4
  50.2 23.9 %collective-permute-start.16 = (bf16[2,72,1152]{2,1,0:T(8,128)(2,1)S(1)}, bf16[2,72,1152]{2,1,0:T(8,128)(2,1)S(1)}, u32[]{:S(2)}, u32[]{:S(2)}) collective-permute-start(bf16[2,72,1152]{2,1,0:T(8,128)(2,1)S(1)} %get-tuple-element.58), channel_id=1, source_target_pairs={{0,8},{8,0},{16,24},{24,16},{1,9},{9,1},{17,25},{25,17},{2,10},{10... | collective-permute-start | bytes 995336 | tf_op jit(solution)/shard_map/ppermute | solution.py:378
  51.7 22.4 %collective-permute-start.17 = (bf16[2,72,1152]{2,1,0:T(8,128)(2,1)S(1)}, bf16[2,72,1152]{2,1,0:T(8,128)(2,1)S(1)}, u32[]{:S(2)}, u32[]{:S(2)}) collective-permute-start(bf16[2,72,1152]{2,1,0:T(8,128)(2,1)S(1)} %get-tuple-element.59), channel_id=1, source_target_pairs={{0,16},{8,24},{16,0},{24,8},{1,17},{9,25},{17,1},{25,9},{2,18},{10... | collective-permute-start | bytes 995336 | tf_op jit(solution)/shard_map/ppermute | solution.py:378
  52.2 6.2 %collective-permute-start.13 = (bf16[32,1728]{1,0:T(8,128)(2,1)S(1)}, bf16[32,1728]{1,0:T(8,128)(2,1)S(1)}, u32[]{:S(2)}, u32[]{:S(2)}) collective-permute-start(bf16[32,1728]{1,0:T(8,128)(2,1)S(1)} %get-tuple-element.48), channel_id=1, source_target_pairs={{0,2},{1,3},{2,0},{3,1},{4,6},{5,7},{6,4},{7,5},{8,10},{9,11},{10,... | collective-permute-start | bytes 331784 | tf_op jit(solution)/shard_map/ppermute | solution.py:378
  54.8 11.4 %collective-permute-start.14 = (bf16[32,1728]{1,0:T(8,128)(2,1)S(1)}, bf16[32,1728]{1,0:T(8,128)(2,1)S(1)}, u32[]{:S(2)}, u32[]{:S(2)}) collective-permute-start(bf16[32,1728]{1,0:T(8,128)(2,1)S(1)} %get-tuple-element.49), channel_id=1, source_target_pairs={{0,4},{1,5},{2,6},{3,7},{4,0},{5,1},{6,2},{7,3},{8,12},{9,13},{10,... | collective-permute-start | bytes 331784 | tf_op jit(solution)/shard_map/ppermute | solution.py:378
  55.9 10.4 %collective-permute-start.15 = (bf16[32,1728]{1,0:T(8,128)(2,1)S(1)}, bf16[32,1728]{1,0:T(8,128)(2,1)S(1)}, u32[]{:S(2)}, u32[]{:S(2)}) collective-permute-start(bf16[32,1728]{1,0:T(8,128)(2,1)S(1)} %get-tuple-element.50), channel_id=1, source_target_pairs={{0,6},{1,7},{2,4},{3,5},{4,2},{5,3},{6,0},{7,1},{8,14},{9,15},{10,... | collective-permute-start | bytes 331784 | tf_op jit(solution)/shard_map/ppermute | solution.py:378
  58.4 7.9 %copy-start.5 = (bf16[32,1728]{1,0:T(8,128)(2,1)}, bf16[32,1728]{1,0:T(8,128)(2,1)S(1)}, u32[]{:S(2)}) copy-start(bf16[32,1728]{1,0:T(8,128)(2,1)S(1)} %collective-permute-done.13.refs_1_) | copy-start | bytes 331780
  66.3 0.6 copy-start.6
  66.3 0.7 copy-start.7
  74.9 5.4 %collective-permute-start.18 = (bf16[72,1152]{1,0:T(8,128)(2,1)S(1)}, bf16[72,1152]{1,0:T(8,128)(2,1)S(1)}, u32[]{:S(2)}, u32[]{:S(2)}) collective-permute-start(bf16[72,1152]{1,0:T(8,128)(2,1)S(1)} %get-tuple-element.61), channel_id=1, source_target_pairs={{0,16},{8,24},{16,0},{24,8},{1,17},{9,25},{17,1},{25,9},{2,18},{10... | collective-permute-start | bytes 497672 | tf_op jit(solution)/shard_map/ppermute | solution.py:378
  76.5 5.3 %collective-permute-start.19 = (bf16[72,1152]{1,0:T(8,128)(2,1)S(1)}, bf16[72,1152]{1,0:T(8,128)(2,1)S(1)}, u32[]{:S(2)}, u32[]{:S(2)}) collective-permute-start(bf16[72,1152]{1,0:T(8,128)(2,1)S(1)} %get-tuple-element.62), channel_id=1, source_target_pairs={{0,8},{8,0},{16,24},{24,16},{1,9},{9,1},{17,25},{25,17},{2,10},{10... | collective-permute-start | bytes 497672 | tf_op jit(solution)/shard_map/ppermute | solution.py:378
  82.1 4.6 %collective-permute-start.20 = (bf16[72,576]{1,0:T(8,128)(2,1)S(1)}, bf16[72,576]{1,0:T(8,128)(2,1)S(1)}, u32[]{:S(2)}, u32[]{:S(2)}) collective-permute-start(bf16[72,576]{1,0:T(8,128)(2,1)S(1)} %get-tuple-element.64), channel_id=1, source_target_pairs={{0,2},{1,3},{2,0},{3,1},{4,6},{5,7},{6,4},{7,5},{8,10},{9,11},{10,... | collective-permute-start | bytes 248840 | tf_op jit(solution)/shard_map/ppermute | solution.py:378
  83.9 8.0 %collective-permute-start.21 = (bf16[72,576]{1,0:T(8,128)(2,1)S(1)}, bf16[72,576]{1,0:T(8,128)(2,1)S(1)}, u32[]{:S(2)}, u32[]{:S(2)}) collective-permute-start(bf16[72,576]{1,0:T(8,128)(2,1)S(1)} %get-tuple-element.65), channel_id=1, source_target_pairs={{0,4},{1,5},{2,6},{3,7},{4,0},{5,1},{6,2},{7,3},{8,12},{9,13},{10,... | collective-permute-start | bytes 248840 | tf_op jit(solution)/shard_map/ppermute | solution.py:378
  84.8 7.0 %collective-permute-start.22 = (bf16[72,576]{1,0:T(8,128)(2,1)S(1)}, bf16[72,576]{1,0:T(8,128)(2,1)S(1)}, u32[]{:S(2)}, u32[]{:S(2)}) collective-permute-start(bf16[72,576]{1,0:T(8,128)(2,1)S(1)} %get-tuple-element.66), channel_id=1, source_target_pairs={{0,6},{1,7},{2,4},{3,5},{4,2},{5,3},{6,0},{7,1},{8,14},{9,15},{10,... | collective-permute-start | bytes 248840 | tf_op jit(solution)/shard_map/ppermute | solution.py:378

commit v7 on v6

--- a/solution.py
+++ b/solution.py
@@ -16,6 +16,7 @@
 VMEM = pl.BlockSpec(memory_space=pltpu.VMEM)
 SMEM = pl.BlockSpec(memory_space=pltpu.SMEM)
 HBM = pl.BlockSpec(memory_space=pltpu.HBM)
+PAD = 8 * LANES
 LIMIT = 16 * 1024 * 1024
 MOST = 60 * 1024 * 1024
 
@@ -186,28 +187,28 @@
     return jnp.concatenate([first, second], axis=1).reshape(2 * rows, width).astype(BF16)
 
 
-def cut_kernel(chips, whole, out, left, right, sem):
-    copy = pltpu.make_async_copy(whole.at[place(chips)[1]], out, sem.at[0])
-    copy.start()
-    copy.wait()
-    cut = left.shape[1]
-    left[...] = out[:, :cut]
-    right[...] = out[:, cut:]
-
-
-def second_kernel(mine, got_x, got_y, own, left, right, kept):
-    half, cut = got_x.shape
-    left[:half] = mine[:, :cut]
+def cut_kernel(chips, whole, left, right, sem):
+    core, cut = place(chips)[1], left.shape[1]
+    pairs = [(whole.at[core, :, pl.ds(0, cut)], left)]
+    pairs.append((whole.at[core, :, pl.ds(cut, right.shape[1])], right))
+    for copy in started(pairs, sem):
+        copy.wait()
+
+
+def second_kernel(own_left, own_right, got_x, got_y, own, left, right, kept):
+    half = got_x.shape[0]
+    left[:half] = own_left[...]
     left[half:] = got_x[...]
-    right[:half] = mine[:, cut:]
+    right[:half] = own_right[...]
     right[half:] = got_y[...]
     kept[...] = own[...]
 
 
 def join_rows_kernel(*refs):
-    out, rows = refs[-1], refs[0].shape[0]
-    for at, ref in enumerate(refs[:-1]):
-        out[at * rows : (at + 1) * rows] = ref[...]
+    out, low = refs[-1], 0
+    for ref in refs[:-1]:
+        out[low : low + ref.shape[0], : ref.shape[1]] = ref[...]
+        low += ref.shape[0]
 
 
 def projected(hidden, shards, weights, idx, blocks, sums):
@@ -309,7 +310,7 @@
     copy.wait()
 
 
-def sum_first_kernel(_, keep, got_x, got_y, own, send_y, send_x):
+def sum_first_kernel(keep, got_x, got_y, _, own, send_y, send_x):
     for i, (got, send) in enumerate(((got_x, send_y), (got_y, send_x))):
         own[i] = keep[2 * i] + got[0].astype(F32)
         send[...] = (keep[2 * i + 1] + got[1].astype(F32)).astype(BF16)
@@ -336,40 +337,41 @@
 def last_kernel(chips, patches, *refs):
     idx = place(chips)
     loaded = 5 + chips
-    far, outs, refs = refs[:loaded], refs[loaded : loaded + 4], refs[loaded + 4 :]
-    block_far, out_far, grads_far, done = outs
-    done[0] = 0
+    far, outs, refs = refs[:loaded], refs[loaded : loaded + 3], refs[loaded + 3 :]
+    block_far, out_far, grads_far = outs
     rows, wos, qkv, p_ref, wot, hid, block_out, grads, qs, ks, vs, gs, sems = refs
     inner, width = wos.shape
     frames = rows.shape[0] // patches
     block = patches // chips
-    pairs = list(zip(far[chips:], (wos, qkv, p_ref, wot, hid)))
+    pairs = []
     for q in range(chips):
         for f in range(frames):
             low = pl.multiple_of(f * patches + (idx[2] ^ q) * block, block)
             pairs.append((far[q].at[pl.ds(f * block, block)], rows.at[pl.ds(low, block)]))
+    first = len(pairs)
+    pairs += zip(far[chips:], (wos, qkv, p_ref, wot, hid))
     loads = started(pairs, sems)
-    for copy in loads[5:]:
+    for copy in loads[:first]:
         copy.wait()
     value = rows[...]
     grad, attended = value[:, :width], value[:, width:]
     base = len(pairs)
     stores = started([(rows.at[:, pl.ds(0, width)], out_far)], sems.at[pl.ds(base, 1)])
-    loads[0].wait()
+    loads[first].wait()
     put(gs, dot_bt(grad, wos[...]).astype(BF16))
-    loads[1].wait()
+    loads[first + 1].wait()
     x = qkv[...]
     put(qs, x[:, :inner])
     put(ks, x[:, inner : 2 * inner])
     put(vs, x[:, 2 * inner :])
-    loads[3].wait()
-    loads[4].wait()
-    block_out[...] = (hid[...].astype(F32) + dot(attended, wot[...])).astype(BF16)
-    stores += started([(block_out, block_far)], sems.at[pl.ds(base + 1, 1)])
-    loads[2].wait()
+    loads[first + 2].wait()
     dq, dk, dv = softmax_backward(qs, ks, vs, gs, p_ref, inner // DH)
     grads[...] = jnp.concatenate([dq[:, :inner], dk[:, :inner], dv[:, :inner]], axis=1)
     stores += started([(grads, grads_far)], sems.at[pl.ds(base + 2, 1)])
+    loads[first + 3].wait()
+    loads[first + 4].wait()
+    block_out[...] = (hid[...].astype(F32) + dot(attended, wot[...])).astype(BF16)
+    stores += started([(block_out, block_far)], sems.at[pl.ds(base + 1, 1)])
     for copy in stores:
         copy.wait()
 
@@ -385,29 +387,36 @@
 def gather(weight, parts, chips):
     n = lax.axis_size("dp")
     rows, sent = parts[0].shape
-    whole = [shape((len(parts) * rows, sent))]
+    whole = [shape((len(parts) * rows, sent + PAD))]
     if n != 4:
         (near,) = call(join_rows_kernel, whole, from_chips(parts), small=True)
         weights = [lax.all_gather(weight, "dp", axis=0, tiled=True)]
         return near, flip(near, "seq", 1), weights, [[(lambda idx: 0, 0, None)]], 1
     half, width = weight.shape[0] // 2, weight.shape[1]
     cut = -(-width // LANES // 2) * LANES
-    mine, left, right = call(
+    left, right = call(
         functools.partial(cut_kernel, chips),
-        [shape((half, width)), shape((half, cut)), shape((half, width - cut))],
+        [shape((half, cut)), shape((half, width - cut))],
         [weight.reshape(2, half, width)],
-        [sems(1)],
+        [sems(2)],
         far_in=range(1),
+        far_out=range(2),
     )
     got_x, got_y = flip(left, "dp", 1), flip(right, "dp", 2)
     left, right, own = call(
         second_kernel,
         [shape((2 * half, cut)), shape((2 * half, width - cut)), shape((rows, sent))],
-        [mine, got_x, got_y, parts[0]],
+        [left, right, got_x, got_y, parts[0]],
         small=True,
     )
     (near,) = call(join_rows_kernel, whole, [own, *from_chips(parts)[1:]], small=True)
-    held = [got_x, got_y, flip(left, "dp", 2), flip(right, "dp", 1)]
+    (right,) = call(
+        join_rows_kernel,
+        [shape((3 * half, width - cut))],
+        [got_y, flip(right, "dp", 1)],
+        small=True,
+    )
+    held = [got_x, flip(left, "dp", 2), right]
     weights = [weight, *held, *[flip(w, "seq", 1) for w in held]]
 
     def block(j, other):
@@ -415,9 +424,9 @@
 
     shards = [[(lambda idx: 2 * idx[0], 0, 0), (lambda idx: 2 * idx[0] + 1, 0, 1)]]
     for other in (0, 1):
-        shards += [[(block(1, other), 0, None)], [(block(2, other), cut, None)]]
+        shards += [[(block(1, other), 0, None)]]
         shards.append([(block(2, other), 0, 0), (block(3, other), 0, 1)])
-        shards.append([(block(1, other), cut, 0), (block(3, other), cut, 1)])
+        shards.append([(block(j, other), cut, i) for i, j in enumerate((2, 1, 3))])
     return near, flip(near, "seq", 1), weights, shards, 2 * n
 
 
@@ -431,7 +440,7 @@
     own, send_t, send_s = call(
         sum_first_kernel,
         [shape((2, size, width), F32), step, step],
-        [after, keep, flip(send_x, "dp", 1), flip(send_y, "dp", 2)],
+        [keep, flip(send_x, "dp", 1), flip(send_y, "dp", 2), after],
         small=True,
     )
     n = lax.axis_size("seq") // 2
@@ -517,10 +526,11 @@
             [mine, other, near],
             small=True,
         )
-    block_out, tokens_grad, qkv_grad, done = call(
+    back = from_chips(back)
+    block_out, tokens_grad, qkv_grad = call(
         functools.partial(last_kernel, chips, patches),
-        [shape((rows, width)), shape((rows, width)), shape((rows, 3 * inner)), TOKEN],
-        [*from_chips(back), wo_spatial, qkv_rows, spatial_p, wo_temporal, hidden],
+        [shape((rows, width)), shape((rows, width)), shape((rows, 3 * inner))],
+        [*back, wo_spatial, qkv_rows, spatial_p, wo_temporal, hidden],
         [held(width + inner), projection, held(3 * inner), attended, projection, held(width)]
         + [held(width), held(3 * inner)]
         + [wide] * 4
@@ -529,7 +539,7 @@
         far_out=range(3),
     )
     if n_dp == 4 and n_seq == peers:
-        temporal_grad, spatial_grad = reduced(keep, send_x, send_y, done)
+        temporal_grad, spatial_grad = reduced(keep, send_x, send_y, back[1])
     else:
         both = lax.psum_scatter(both, "seq", scatter_dimension=1, tiled=True)
         both = lax.psum_scatter(both, "dp", scatter_dimension=2, tiled=True).astype(F32)

time: 92.8 us -> 97.4 us (1.050)
  the two profiles are of different devices: /device:TPU:0 before, /device:TPU:12 now
where the time goes in v7:
time: 97.4 us; the launch traced here: 97.2 us
  Pallas kernels  38.7 us (40%)
  waiting for transfers between devices  36.7 us (38%)
  starting transfers between devices  19.4 us (20%)
  local copies, waits for them, and re-layouts  1.59 us (2%)
    pallas_call x11, Pallas kernels, call(): pl.pallas_call(body, out_shape=outs, in_specs=[HBM if i in far_in else sp...  38.7 us
    ppermute x22, waiting for transfers between devices, flip(): lax.ppermute(value, axis, [(i, i ^ bit) for i in range(lax.axis_size(axis...  36.7 us
    ppermute x22, starting transfers between devices, flip(): lax.ppermute(value, axis, [(i, i ^ bit) for i in range(lax.axis_size(axis...  19.4 us
  transfers between devices with their start and end apart: 22, of which 12 were waited for; matrix products, arithmetic and copies ran while one was open for 0% of the time, Pallas kernels for 12%

profile of v7, /device:TPU:12, one launch (start us, length us, event | category | flops | bytes accessed | tf_op | source)
XLA Modules:
  0.0 97.2 jit_solution(17145508912794311767)
XLA Ops:
  0.6 16.2 %shard_map.101 = (bf16[216,640]{1,0:T(8,128)(2,1)}, bf16[216,512]{1,0:T(8,128)(2,1)}) custom-call(bf16[2,216,1152]{2,1,0:T(8,128)(2,1)} %bitcast.9), custom_call_target="tpu_custom_call" | custom-call | tf_op jit(solution)/shard_map/pallas_call | solution.py:39
  16.9 1.6 %collective-permute-start = (bf16[216,640]{1,0:T(8,128)(2,1)}, bf16[216,640]{1,0:T(8,128)(2,1)S(1)}, u32[]{:S(2)}, u32[]{:S(2)}) collective-permute-start(bf16[216,640]{1,0:T(8,128)(2,1)} %get-tuple-element.35.own_left), channel_id=1, source_target_pairs={{0,8},{8,0},{16,24},{24,16},{1,9},{9,1},{17,25},{25,17},{2,10},{10... | collective-permute-start | bytes 829448 | tf_op jit(solution)/shard_map/ppermute | solution.py:380
  18.9 4.8 %shard_map.102 = (bf16[32,2944]{1,0:T(8,128)(2,1)}, bf16[32,2944]{1,0:T(8,128)(2,1)}, bf16[32,2944]{1,0:T(8,128)(2,1)}, bf16[32,2944]{1,0:T(8,128)(2,1)}, bf16[1...) custom-call(bf16[128,1728]{1,0:T(8,128)(2,1)} %bitcast.11, bf16[128,1152]{1,0:T(8,128)(2,1)} %bitcast.13, ...), custom_call_target="tpu_custom_call" | custom-call | tf_op jit(solution)/shard_map/pallas_call | solution.py:39
  23.8 0.5 collective-permute-start.2
  24.3 2.6 %collective-permute-start.3 = (bf16[32,2944]{1,0:T(8,128)(2,1)}, bf16[32,2944]{1,0:T(8,128)(2,1)S(1)}, u32[]{:S(2)}, u32[]{:S(2)}) collective-permute-start(bf16[32,2944]{1,0:T(8,128)(2,1)} %get-tuple-element.40), channel_id=1, source_target_pairs={{0,4},{1,5},{2,6},{3,7},{4,0},{5,1},{6,2},{7,3},{8,12},{9,13},{10,... | collective-permute-start | bytes 565256 | tf_op jit(solution)/shard_map/ppermute | solution.py:380
  27.4 0.9 copy-done.5
  28.4 1.6 %collective-permute-start.6 = (bf16[432,640]{1,0:T(8,128)(2,1)S(1)}, bf16[432,640]{1,0:T(8,128)(2,1)S(1)}, u32[]{:S(2)}, u32[]{:S(2)}) collective-permute-start(bf16[432,640]{1,0:T(8,128)(2,1)S(1)} %get-tuple-element.42), channel_id=1, source_target_pairs={{0,16},{8,24},{16,0},{24,8},{1,17},{9,25},{17,1},{25,9},{2,18},{10... | collective-permute-start | bytes 1658888 | tf_op jit(solution)/shard_map/ppermute | solution.py:380
  30.0 0.5 collective-permute-start.7
  30.5 1.2 %collective-permute-done.2.refs_1_ = bf16[32,2944]{1,0:T(8,128)(2,1)S(1)} collective-permute-done((bf16[32,2944]{1,0:T(8,128)(2,1)}, bf16[32,2944]{1,0:T(8,128)(2,1)S(1)}, u32[]{:S(2)}, u32[]{:S(2)}) %collective-permute-start.2) | collective-permute-done | bytes 188448 | tf_op jit(solution)/shard_map/ppermute | solution.py:380
  31.7 8.3 %collective-permute-done.3.refs_2_ = bf16[32,2944]{1,0:T(8,128)(2,1)S(1)} collective-permute-done((bf16[32,2944]{1,0:T(8,128)(2,1)}, bf16[32,2944]{1,0:T(8,128)(2,1)S(1)}, u32[]{:S(2)}, u32[]{:S(2)}) %collective-permute-start.3) | collective-permute-done | bytes 188448 | tf_op jit(solution)/shard_map/ppermute | solution.py:380
  40.0 3.3 %collective-permute-done.4.refs_3_ = bf16[32,2944]{1,0:T(8,128)(2,1)S(1)} collective-permute-done((bf16[32,2944]{1,0:T(8,128)(2,1)}, bf16[32,2944]{1,0:T(8,128)(2,1)S(1)}, u32[]{:S(2)}, u32[]{:S(2)}) %collective-permute-start.4) | collective-permute-done | bytes 188448 | tf_op jit(solution)/shard_map/ppermute | solution.py:380
  43.5 0.5 collective-permute-start.10
  44.6 3.6 %collective-permute-done.8.refs_4_ = bf16[216,640]{1,0:T(8,128)(2,1)S(1)} collective-permute-done((bf16[216,640]{1,0:T(8,128)(2,1)S(1)}, bf16[216,640]{1,0:T(8,128)(2,1)S(1)}, u32[]{:S(2)}, u32[]{:S(2)}) %collective-permute-start.8) | collective-permute-done | bytes 276512 | tf_op jit(solution)/shard_map/ppermute | solution.py:380
  48.2 7.5 %shard_map.106.mine = bf16[128,1728]{1,0:T(8,128)(2,1)S(1)} custom-call(bf16[128,3968]{1,0:T(8,128)(2,1)S(1)} %shard_map.104.near.refs_0_, bf16[128,3968]{1,0:T(8,128)(2,1)S(1)} %collective-permute-done.5.far.refs_1_, bf16[576,1152]{1,0:T(8,128)(2,1)S(1)} %copy-done, bf16[432,1152]{1,0:T(8,128)(2,1)S(1)} %bitcast.10, ...), custom_call_target="tpu_custom_call" | custom-call | tf_op jit(solution)/shard_map/pallas_call | solution.py:39
  55.9 1.7 %collective-permute-done.11.other = bf16[128,1728]{1,0:T(8,128)(2,1)S(1)} collective-permute-done((bf16[128,1728]{1,0:T(8,128)(2,1)S(1)}, bf16[128,1728]{1,0:T(8,128)(2,1)S(1)}, u32[]{:S(2)}, u32[]{:S(2)}) %collective-permute-start.11) | collective-permute-done | bytes 442400 | tf_op jit(solution)/shard_map/ppermute | solution.py:380
  57.6 2.9 %shard_map.107 = (bf16[32,1728]{1,0:T(8,128)(2,1)S(1)}, bf16[32,1728]{1,0:T(8,128)(2,1)S(1)}, bf16[32,1728]{1,0:T(8,128)(2,1)S(1)}, bf16[32,1728]{1,0:T(8,128)(2...) custom-call(bf16[128,1728]{1,0:T(8,128)(2,1)S(1)} %shard_map.106.mine, ...), custom_call_target="tpu_custom_call" | custom-call | tf_op jit(solution)/shard_map/pallas_call | solution.py:39
  60.5 0.6 collective-permute-start.15
  61.1 1.5 %collective-permute-start.16 = (bf16[2,72,1152]{2,1,0:T(8,128)(2,1)S(1)}, bf16[2,72,1152]{2,1,0:T(8,128)(2,1)S(1)}, u32[]{:S(2)}, u32[]{:S(2)}) collective-permute-start(bf16[2,72,1152]{2,1,0:T(8,128)(2,1)S(1)} %get-tuple-element.55), channel_id=1, source_target_pairs={{0,16},{8,24},{16,0},{24,8},{1,17},{9,25},{17,1},{25,9},{2,18},{10... | collective-permute-start | bytes 995336 | tf_op jit(solution)/shard_map/ppermute | solution.py:380
  62.6 4.8 %collective-permute-done.12.refs_1_._ = bf16[32,1728]{1,0:T(8,128)(2,1)S(1)} collective-permute-done((bf16[32,1728]{1,0:T(8,128)(2,1)S(1)}, bf16[32,1728]{1,0:T(8,128)(2,1)S(1)}, u32[]{:S(2)}, u32[]{:S(2)}) %collective-permute-start.12) | collective-permute-done | bytes 110624 | tf_op jit(solution)/shard_map/ppermute | solution.py:380
  67.4 3.0 %collective-permute-done.15.got_x = bf16[2,72,1152]{2,1,0:T(8,128)(2,1)S(1)} collective-permute-done((bf16[2,72,1152]{2,1,0:T(8,128)(2,1)S(1)}, bf16[2,72,1152]{2,1,0:T(8,128)(2,1)S(1)}, u32[]{:S(2)}, u32[]{:S(2)}) %collective-permute-start.15) | collective-permute-done | bytes 331808 | tf_op jit(solution)/shard_map/ppermute | solution.py:380
  70.8 1.6 %collective-permute-start.17 = (bf16[72,1152]{1,0:T(8,128)(2,1)S(1)}, bf16[72,1152]{1,0:T(8,128)(2,1)S(1)}, u32[]{:S(2)}, u32[]{:S(2)}) collective-permute-start(bf16[72,1152]{1,0:T(8,128)(2,1)S(1)} %get-tuple-element.57), channel_id=1, source_target_pairs={{0,16},{8,24},{16,0},{24,8},{1,17},{9,25},{17,1},{25,9},{2,18},{10... | collective-permute-start | bytes 497672 | tf_op jit(solution)/shard_map/ppermute | solution.py:380
  72.4 1.5 %collective-permute-start.18 = (bf16[72,1152]{1,0:T(8,128)(2,1)S(1)}, bf16[72,1152]{1,0:T(8,128)(2,1)S(1)}, u32[]{:S(2)}, u32[]{:S(2)}) collective-permute-start(bf16[72,1152]{1,0:T(8,128)(2,1)S(1)} %get-tuple-element.58), channel_id=1, source_target_pairs={{0,8},{8,0},{16,24},{24,16},{1,9},{9,1},{17,25},{25,17},{2,10},{10... | collective-permute-start | bytes 497672 | tf_op jit(solution)/shard_map/ppermute | solution.py:380
  73.9 1.6 %collective-permute-start.14 = (bf16[32,1728]{1,0:T(8,128)(2,1)S(1)}, bf16[32,1728]{1,0:T(8,128)(2,1)S(1)}, u32[]{:S(2)}, u32[]{:S(2)}) collective-permute-start(bf16[32,1728]{1,0:T(8,128)(2,1)S(1)} %get-tuple-element.47), channel_id=1, source_target_pairs={{0,6},{1,7},{2,4},{3,5},{4,2},{5,3},{6,0},{7,1},{8,14},{9,15},{10,... | collective-permute-start | bytes 331784 | tf_op jit(solution)/shard_map/ppermute | solution.py:380
  75.4 0.8 collective-permute-done.17.got_y
  76.2 1.5 %collective-permute-done.18.got_x = bf16[72,1152]{1,0:T(8,128)(2,1)S(1)} collective-permute-done((bf16[72,1152]{1,0:T(8,128)(2,1)S(1)}, bf16[72,1152]{1,0:T(8,128)(2,1)S(1)}, u32[]{:S(2)}, u32[]{:S(2)}) %collective-permute-start.18) | collective-permute-done | bytes 165920 | tf_op jit(solution)/shard_map/ppermute | solution.py:380
  77.9 0.6 collective-permute-start.19
  78.5 2.5 %collective-permute-start.20 = (bf16[72,576]{1,0:T(8,128)(2,1)S(1)}, bf16[72,576]{1,0:T(8,128)(2,1)S(1)}, u32[]{:S(2)}, u32[]{:S(2)}) collective-permute-start(bf16[72,576]{1,0:T(8,128)(2,1)S(1)} %get-tuple-element.61), channel_id=1, source_target_pairs={{0,4},{1,5},{2,6},{3,7},{4,0},{5,1},{6,2},{7,3},{8,12},{9,13},{10,... | collective-permute-start | bytes 248840 | tf_op jit(solution)/shard_map/ppermute | solution.py:380
  81.5 2.5 %collective-permute-done.13.refs_2_ = bf16[32,1728]{1,0:T(8,128)(2,1)S(1)} collective-permute-done((bf16[32,1728]{1,0:T(8,128)(2,1)S(1)}, bf16[32,1728]{1,0:T(8,128)(2,1)S(1)}, u32[]{:S(2)}, u32[]{:S(2)}) %collective-permute-start.13) | collective-permute-done | bytes 110624 | tf_op jit(solution)/shard_map/ppermute | solution.py:380
  84.0 5.8 %collective-permute-done.14.refs_3_ = bf16[32,1728]{1,0:T(8,128)(2,1)S(1)} collective-permute-done((bf16[32,1728]{1,0:T(8,128)(2,1)S(1)}, bf16[32,1728]{1,0:T(8,128)(2,1)S(1)}, u32[]{:S(2)}, u32[]{:S(2)}) %collective-permute-start.14) | collective-permute-done | bytes 110624 | tf_op jit(solution)/shard_map/ppermute | solution.py:380
  89.7 0.6 copy-done.8
  90.4 6.1 %shard_map.108 = (bf16[128,1152]{1,0:T(8,128)(2,1)}, bf16[128,1152]{1,0:T(8,128)(2,1)}, bf16[128,1728]{1,0:T(8,128)(2,1)}) custom-call(bf16[32,1728]{1,0:T(8,128)(2,1)} %copy-done.6, bf16[32,1728]{1,0:T(8,128)(2,1)} %copy-done.2, bf16[32,1728]{1,0:T(8,128)(2,1)} %copy-done.7, bf16[32,1728]{1,0:T(8,128)(2,1)} %copy-done.8, bf16[576,1152]{1,0:T(8,128)(2,1)} %refs_4_.1, ...), custom_call_target="tpu_custom_call" | custom-call | tf_op jit(solution)/shard_map/pallas_call | solution.py:39
  96.5 0.8 shard_map.111
  (41 shorter events, 3.0 us)
Async XLA Ops:
  16.8 10.5 %copy-start.3 = (bf16[216,640]{1,0:T(8,128)(2,1)S(1)}, bf16[216,640]{1,0:T(8,128)(2,1)}, u32[]{:S(2)}) copy-start(bf16[216,640]{1,0:T(8,128)(2,1)} %get-tuple-element.35.own_left) | copy-start | bytes 829444
  16.9 10.5 %copy-start.4 = (bf16[216,512]{1,0:T(8,128)(2,1)S(1)}, bf16[216,512]{1,0:T(8,128)(2,1)}, u32[]{:S(2)}) copy-start(bf16[216,512]{1,0:T(8,128)(2,1)} %get-tuple-element.36.own_right) | copy-start | bytes 663556
  16.9 10.5 %collective-permute-start = (bf16[216,640]{1,0:T(8,128)(2,1)}, bf16[216,640]{1,0:T(8,128)(2,1)S(1)}, u32[]{:S(2)}, u32[]{:S(2)}) collective-permute-start(bf16[216,640]{1,0:T(8,128)(2,1)} %get-tuple-element.35.own_left), channel_id=1, source_target_pairs={{0,8},{8,0},{16,24},{24,16},{1,9},{9,1},{17,25},{25,17},{2,10},{10... | collective-permute-start | bytes 829448 | tf_op jit(solution)/shard_map/ppermute | solution.py:380
  18.4 8.9 %collective-permute-start.1 = (bf16[216,512]{1,0:T(8,128)(2,1)}, bf16[216,512]{1,0:T(8,128)(2,1)S(1)}, u32[]{:S(2)}, u32[]{:S(2)}) collective-permute-start(bf16[216,512]{1,0:T(8,128)(2,1)} %get-tuple-element.36.own_right), channel_id=1, source_target_pairs={{0,16},{8,24},{16,0},{24,8},{1,17},{9,25},{17,1},{25,9},{2,18},{10... | collective-permute-start | bytes 663560 | tf_op jit(solution)/shard_map/ppermute | solution.py:380
  23.8 7.9 %collective-permute-start.2 = (bf16[32,2944]{1,0:T(8,128)(2,1)}, bf16[32,2944]{1,0:T(8,128)(2,1)S(1)}, u32[]{:S(2)}, u32[]{:S(2)}) collective-permute-start(bf16[32,2944]{1,0:T(8,128)(2,1)} %get-tuple-element.39), channel_id=1, source_target_pairs={{0,2},{1,3},{2,0},{3,1},{4,6},{5,7},{6,4},{7,5},{8,10},{9,11},{10,... | collective-permute-start | bytes 565256 | tf_op jit(solution)/shard_map/ppermute | solution.py:380
  24.3 15.7 %collective-permute-start.3 = (bf16[32,2944]{1,0:T(8,128)(2,1)}, bf16[32,2944]{1,0:T(8,128)(2,1)S(1)}, u32[]{:S(2)}, u32[]{:S(2)}) collective-permute-start(bf16[32,2944]{1,0:T(8,128)(2,1)} %get-tuple-element.40), channel_id=1, source_target_pairs={{0,4},{1,5},{2,6},{3,7},{4,0},{5,1},{6,2},{7,3},{8,12},{9,13},{10,... | collective-permute-start | bytes 565256 | tf_op jit(solution)/shard_map/ppermute | solution.py:380
  26.9 16.4 %collective-permute-start.4 = (bf16[32,2944]{1,0:T(8,128)(2,1)}, bf16[32,2944]{1,0:T(8,128)(2,1)S(1)}, u32[]{:S(2)}, u32[]{:S(2)}) collective-permute-start(bf16[32,2944]{1,0:T(8,128)(2,1)} %get-tuple-element.41), channel_id=1, source_target_pairs={{0,6},{1,7},{2,4},{3,5},{4,2},{5,3},{6,0},{7,1},{8,14},{9,15},{10,... | collective-permute-start | bytes 565256 | tf_op jit(solution)/shard_map/ppermute | solution.py:380
  27.4 0.9 copy-start.5
  28.4 15.7 %collective-permute-start.6 = (bf16[432,640]{1,0:T(8,128)(2,1)S(1)}, bf16[432,640]{1,0:T(8,128)(2,1)S(1)}, u32[]{:S(2)}, u32[]{:S(2)}) collective-permute-start(bf16[432,640]{1,0:T(8,128)(2,1)S(1)} %get-tuple-element.42), channel_id=1, source_target_pairs={{0,16},{8,24},{16,0},{24,8},{1,17},{9,25},{17,1},{25,9},{2,18},{10... | collective-permute-start | bytes 1658888 | tf_op jit(solution)/shard_map/ppermute | solution.py:380
  30.0 13.5 %collective-permute-start.7 = (bf16[432,512]{1,0:T(8,128)(2,1)S(1)}, bf16[432,512]{1,0:T(8,128)(2,1)S(1)}, u32[]{:S(2)}, u32[]{:S(2)}) collective-permute-start(bf16[432,512]{1,0:T(8,128)(2,1)S(1)} %get-tuple-element.43), channel_id=1, source_target_pairs={{0,8},{8,0},{16,24},{24,16},{1,9},{9,1},{17,25},{25,17},{2,10},{10... | collective-permute-start | bytes 1327112 | tf_op jit(solution)/shard_map/ppermute | solution.py:380
  43.3 4.9 %copy-start = (bf16[576,1152]{1,0:T(8,128)(2,1)S(1)}, bf16[576,1152]{1,0:T(8,128)(2,1)}, u32[]{:S(2)}) copy-start(bf16[576,1152]{1,0:T(8,128)(2,1)} %refs_7_.1) | copy-start | bytes 3981316
  43.3 4.9 %copy-start.1 = (bf16[1152,432]{0,1:T(8,128)(2,1)S(1)}, bf16[1152,432]{0,1:T(8,128)(2,1)}, u32[]{:S(2)}) copy-start(bf16[1152,432]{0,1:T(8,128)(2,1)} %param.9) | copy-start | bytes 2985988
  43.4 4.8 %collective-permute-start.5 = (bf16[128,3968]{1,0:T(8,128)(2,1)S(1)}, bf16[128,3968]{1,0:T(8,128)(2,1)S(1)}, u32[]{:S(2)}, u32[]{:S(2)}) collective-permute-start(bf16[128,3968]{1,0:T(8,128)(2,1)S(1)} %shard_map.104.near.refs_0_), channel_id=1, source_target_pairs={{0,1},{1,0},{2,3},{3,2},{4,5},{5,4},{6,7},{7,6},{8,9},{9,8},{10,11... | collective-permute-start | bytes 3047432 | tf_op jit(solution)/shard_map/ppermute | solution.py:380
  43.5 4.7 %collective-permute-start.10 = (bf16[648,512]{1,0:T(8,128)(2,1)S(1)}, bf16[648,512]{1,0:T(8,128)(2,1)S(1)}, u32[]{:S(2)}, u32[]{:S(2)}) collective-permute-start(bf16[648,512]{1,0:T(8,128)(2,1)S(1)} %shard_map.105.refs_3_), channel_id=1, source_target_pairs={{0,1},{1,0},{2,3},{3,2},{4,5},{5,4},{6,7},{7,6},{8,9},{9,8},{10,11... | collective-permute-start | bytes 1990664 | tf_op jit(solution)/shard_map/ppermute | solution.py:380
  44.1 4.1 %collective-permute-start.9 = (bf16[432,640]{1,0:T(8,128)(2,1)S(1)}, bf16[432,640]{1,0:T(8,128)(2,1)S(1)}, u32[]{:S(2)}, u32[]{:S(2)}) collective-permute-start(bf16[432,640]{1,0:T(8,128)(2,1)S(1)} %collective-permute-done.6.refs_2_), channel_id=1, source_target_pairs={{0,1},{1,0},{2,3},{3,2},{4,5},{5,4},{6,7},{7,6},{8,9},{9,8},{10,11... | collective-permute-start | bytes 1658888 | tf_op jit(solution)/shard_map/ppermute | solution.py:380
  44.1 4.0 %collective-permute-start.8 = (bf16[216,640]{1,0:T(8,128)(2,1)S(1)}, bf16[216,640]{1,0:T(8,128)(2,1)S(1)}, u32[]{:S(2)}, u32[]{:S(2)}) collective-permute-start(bf16[216,640]{1,0:T(8,128)(2,1)S(1)} %collective-permute-done.got_x.refs_1_), channel_id=1, source_target_pairs={{0,1},{1,0},{2,3},{3,2},{4,5},{5,4},{6,7},{7,6},{8,9},{9,8},{10,11... | collective-permute-start | bytes 829448 | tf_op jit(solution)/shard_map/ppermute | solution.py:380
  55.7 1.9 %collective-permute-start.11 = (bf16[128,1728]{1,0:T(8,128)(2,1)S(1)}, bf16[128,1728]{1,0:T(8,128)(2,1)S(1)}, u32[]{:S(2)}, u32[]{:S(2)}) collective-permute-start(bf16[128,1728]{1,0:T(8,128)(2,1)S(1)} %shard_map.106.mine), channel_id=1, source_target_pairs={{0,1},{1,0},{2,3},{3,2},{4,5},{5,4},{6,7},{7,6},{8,9},{9,8},{10,11... | collective-permute-start | bytes 1327112 | tf_op jit(solution)/shard_map/ppermute | solution.py:380
  60.5 17.4 %copy-start.6 = (bf16[32,1728]{1,0:T(8,128)(2,1)}, bf16[32,1728]{1,0:T(8,128)(2,1)S(1)}, u32[]{:S(2)}) copy-start(bf16[32,1728]{1,0:T(8,128)(2,1)S(1)} %get-tuple-element.44.refs_0_) | copy-start | bytes 331780
  60.5 9.9 %collective-permute-start.15 = (bf16[2,72,1152]{2,1,0:T(8,128)(2,1)S(1)}, bf16[2,72,1152]{2,1,0:T(8,128)(2,1)S(1)}, u32[]{:S(2)}, u32[]{:S(2)}) collective-permute-start(bf16[2,72,1152]{2,1,0:T(8,128)(2,1)S(1)} %get-tuple-element.54), channel_id=1, source_target_pairs={{0,8},{8,0},{16,24},{24,16},{1,9},{9,1},{17,25},{25,17},{2,10},{10... | collective-permute-start | bytes 995336 | tf_op jit(solution)/shard_map/ppermute | solution.py:380
  61.1 9.6 %collective-permute-start.16 = (bf16[2,72,1152]{2,1,0:T(8,128)(2,1)S(1)}, bf16[2,72,1152]{2,1,0:T(8,128)(2,1)S(1)}, u32[]{:S(2)}, u32[]{:S(2)}) collective-permute-start(bf16[2,72,1152]{2,1,0:T(8,128)(2,1)S(1)} %get-tuple-element.55), channel_id=1, source_target_pairs={{0,16},{8,24},{16,0},{24,8},{1,17},{9,25},{17,1},{25,9},{2,18},{10... | collective-permute-start | bytes 995336 | tf_op jit(solution)/shard_map/ppermute | solution.py:380
  62.6 4.8 %collective-permute-start.12 = (bf16[32,1728]{1,0:T(8,128)(2,1)S(1)}, bf16[32,1728]{1,0:T(8,128)(2,1)S(1)}, u32[]{:S(2)}, u32[]{:S(2)}) collective-permute-start(bf16[32,1728]{1,0:T(8,128)(2,1)S(1)} %get-tuple-element.45), channel_id=1, source_target_pairs={{0,2},{1,3},{2,0},{3,1},{4,6},{5,7},{6,4},{7,5},{8,10},{9,11},{10,... | collective-permute-start | bytes 331784 | tf_op jit(solution)/shard_map/ppermute | solution.py:380
  67.4 10.5 %copy-start.2 = (bf16[32,1728]{1,0:T(8,128)(2,1)}, bf16[32,1728]{1,0:T(8,128)(2,1)S(1)}, u32[]{:S(2)}) copy-start(bf16[32,1728]{1,0:T(8,128)(2,1)S(1)} %collective-permute-done.12.refs_1_._) | copy-start | bytes 331780
  70.8 5.4 %collective-permute-start.17 = (bf16[72,1152]{1,0:T(8,128)(2,1)S(1)}, bf16[72,1152]{1,0:T(8,128)(2,1)S(1)}, u32[]{:S(2)}, u32[]{:S(2)}) collective-permute-start(bf16[72,1152]{1,0:T(8,128)(2,1)S(1)} %get-tuple-element.57), channel_id=1, source_target_pairs={{0,16},{8,24},{16,0},{24,8},{1,17},{9,25},{17,1},{25,9},{2,18},{10... | collective-permute-start | bytes 497672 | tf_op jit(solution)/shard_map/ppermute | solution.py:380
  72.4 5.3 %collective-permute-start.18 = (bf16[72,1152]{1,0:T(8,128)(2,1)S(1)}, bf16[72,1152]{1,0:T(8,128)(2,1)S(1)}, u32[]{:S(2)}, u32[]{:S(2)}) collective-permute-start(bf16[72,1152]{1,0:T(8,128)(2,1)S(1)} %get-tuple-element.58), channel_id=1, source_target_pairs={{0,8},{8,0},{16,24},{24,16},{1,9},{9,1},{17,25},{25,17},{2,10},{10... | collective-permute-start | bytes 497672 | tf_op jit(solution)/shard_map/ppermute | solution.py:380
  73.9 10.1 %collective-permute-start.13 = (bf16[32,1728]{1,0:T(8,128)(2,1)S(1)}, bf16[32,1728]{1,0:T(8,128)(2,1)S(1)}, u32[]{:S(2)}, u32[]{:S(2)}) collective-permute-start(bf16[32,1728]{1,0:T(8,128)(2,1)S(1)} %get-tuple-element.46), channel_id=1, source_target_pairs={{0,4},{1,5},{2,6},{3,7},{4,0},{5,1},{6,2},{7,3},{8,12},{9,13},{10,... | collective-permute-start | bytes 331784 | tf_op jit(solution)/shard_map/ppermute | solution.py:380
  73.9 15.9 %collective-permute-start.14 = (bf16[32,1728]{1,0:T(8,128)(2,1)S(1)}, bf16[32,1728]{1,0:T(8,128)(2,1)S(1)}, u32[]{:S(2)}, u32[]{:S(2)}) collective-permute-start(bf16[32,1728]{1,0:T(8,128)(2,1)S(1)} %get-tuple-element.47), channel_id=1, source_target_pairs={{0,6},{1,7},{2,4},{3,5},{4,2},{5,3},{6,0},{7,1},{8,14},{9,15},{10,... | collective-permute-start | bytes 331784 | tf_op jit(solution)/shard_map/ppermute | solution.py:380
  77.9 18.5 %collective-permute-start.19 = (bf16[72,576]{1,0:T(8,128)(2,1)S(1)}, bf16[72,576]{1,0:T(8,128)(2,1)S(1)}, u32[]{:S(2)}, u32[]{:S(2)}) collective-permute-start(bf16[72,576]{1,0:T(8,128)(2,1)S(1)} %get-tuple-element.60), channel_id=1, source_target_pairs={{0,2},{1,3},{2,0},{3,1},{4,6},{5,7},{6,4},{7,5},{8,10},{9,11},{10,... | collective-permute-start | bytes 248840 | tf_op jit(solution)/shard_map/ppermute | solution.py:380
  78.5 17.9 %collective-permute-start.20 = (bf16[72,576]{1,0:T(8,128)(2,1)S(1)}, bf16[72,576]{1,0:T(8,128)(2,1)S(1)}, u32[]{:S(2)}, u32[]{:S(2)}) collective-permute-start(bf16[72,576]{1,0:T(8,128)(2,1)S(1)} %get-tuple-element.61), channel_id=1, source_target_pairs={{0,4},{1,5},{2,6},{3,7},{4,0},{5,1},{6,2},{7,3},{8,12},{9,13},{10,... | collective-permute-start | bytes 248840 | tf_op jit(solution)/shard_map/ppermute | solution.py:380
  81.0 15.4 %collective-permute-start.21 = (bf16[72,576]{1,0:T(8,128)(2,1)S(1)}, bf16[72,576]{1,0:T(8,128)(2,1)S(1)}, u32[]{:S(2)}, u32[]{:S(2)}) collective-permute-start(bf16[72,576]{1,0:T(8,128)(2,1)S(1)} %get-tuple-element.62), channel_id=1, source_target_pairs={{0,6},{1,7},{2,4},{3,5},{4,2},{5,3},{6,0},{7,1},{8,14},{9,15},{10,... | collective-permute-start | bytes 248840 | tf_op jit(solution)/shard_map/ppermute | solution.py:380
  84.0 5.8 %copy-start.7 = (bf16[32,1728]{1,0:T(8,128)(2,1)}, bf16[32,1728]{1,0:T(8,128)(2,1)S(1)}, u32[]{:S(2)}) copy-start(bf16[32,1728]{1,0:T(8,128)(2,1)S(1)} %collective-permute-done.13.refs_2_) | copy-start | bytes 331780
  89.7 0.6 copy-start.8

commit v8 on v7

--- a/solution.py
+++ b/solution.py
@@ -336,42 +336,28 @@
 
 def last_kernel(chips, patches, *refs):
     idx = place(chips)
-    loaded = 5 + chips
-    far, outs, refs = refs[:loaded], refs[loaded : loaded + 3], refs[loaded + 3 :]
-    block_far, out_far, grads_far = outs
-    rows, wos, qkv, p_ref, wot, hid, block_out, grads, qs, ks, vs, gs, sems = refs
+    held, (wos, qkv, p_ref, wot, hid), refs = refs[:chips], refs[chips : chips + 5], refs[chips + 5 :]
+    block_far, out_far, grads_far, rows, block_out, grads, qs, ks, vs, gs, sems = refs
     inner, width = wos.shape
     frames = rows.shape[0] // patches
     block = patches // chips
-    pairs = []
     for q in range(chips):
         for f in range(frames):
             low = pl.multiple_of(f * patches + (idx[2] ^ q) * block, block)
-            pairs.append((far[q].at[pl.ds(f * block, block)], rows.at[pl.ds(low, block)]))
-    first = len(pairs)
-    pairs += zip(far[chips:], (wos, qkv, p_ref, wot, hid))
-    loads = started(pairs, sems)
-    for copy in loads[:first]:
-        copy.wait()
+            rows[pl.ds(low, block)] = held[q][f * block : (f + 1) * block]
     value = rows[...]
     grad, attended = value[:, :width], value[:, width:]
-    base = len(pairs)
-    stores = started([(rows.at[:, pl.ds(0, width)], out_far)], sems.at[pl.ds(base, 1)])
-    loads[first].wait()
+    stores = started([(rows.at[:, pl.ds(0, width)], out_far)], sems.at[pl.ds(0, 1)])
+    block_out[...] = (hid[...].astype(F32) + dot(attended, wot[...])).astype(BF16)
+    stores += started([(block_out, block_far)], sems.at[pl.ds(1, 1)])
     put(gs, dot_bt(grad, wos[...]).astype(BF16))
-    loads[first + 1].wait()
     x = qkv[...]
     put(qs, x[:, :inner])
     put(ks, x[:, inner : 2 * inner])
     put(vs, x[:, 2 * inner :])
-    loads[first + 2].wait()
     dq, dk, dv = softmax_backward(qs, ks, vs, gs, p_ref, inner // DH)
     grads[...] = jnp.concatenate([dq[:, :inner], dk[:, :inner], dv[:, :inner]], axis=1)
-    stores += started([(grads, grads_far)], sems.at[pl.ds(base + 2, 1)])
-    loads[first + 3].wait()
-    loads[first + 4].wait()
-    block_out[...] = (hid[...].astype(F32) + dot(attended, wot[...])).astype(BF16)
-    stores += started([(block_out, block_far)], sems.at[pl.ds(base + 1, 1)])
+    stores += started([(grads, grads_far)], sems.at[pl.ds(2, 1)])
     for copy in stores:
         copy.wait()
 
@@ -400,7 +386,6 @@
         [weight.reshape(2, half, width)],
         [sems(2)],
         far_in=range(1),
-        far_out=range(2),
     )
     got_x, got_y = flip(left, "dp", 1), flip(right, "dp", 2)
     left, right, own = call(
@@ -409,7 +394,7 @@
         [left, right, got_x, got_y, parts[0]],
         small=True,
     )
-    (near,) = call(join_rows_kernel, whole, [own, *from_chips(parts)[1:]], small=True)
+    (near,) = call(join_rows_kernel, whole, from_chips(parts), small=True)
     (right,) = call(
         join_rows_kernel,
         [shape((3 * half, width - cut))],
@@ -531,12 +516,9 @@
         functools.partial(last_kernel, chips, patches),
         [shape((rows, width)), shape((rows, width)), shape((rows, 3 * inner))],
         [*back, wo_spatial, qkv_rows, spatial_p, wo_temporal, hidden],
-        [held(width + inner), projection, held(3 * inner), attended, projection, held(width)]
-        + [held(width), held(3 * inner)]
-        + [wide] * 4
-        + [sems(8 + chips * frames)],
-        far_in=range(5 + chips),
+        [held(width + inner), held(width), held(3 * inner)] + [wide] * 4 + [sems(3)],
         far_out=range(3),
+        small=True,
     )
     if n_dp == 4 and n_seq == peers:
         temporal_grad, spatial_grad = reduced(keep, send_x, send_y, back[1])

time: 97.4 us -> 80.5 us (0.83)
  the two profiles are of different devices: /device:TPU:12 before, /device:TPU:0 now
where the time goes in v8:
time: 80.5 us; the launch traced here: 80.3 us
  waiting for transfers between devices  29.3 us (36%)
  starting transfers between devices  26.3 us (33%)
  Pallas kernels  22.9 us (28%)
  local copies, waits for them, and re-layouts  0.95 us (1%)
  between operations  0.82 us (1%)
    ppermute x22, waiting for transfers between devices, flip(): lax.ppermute(value, axis, [(i, i ^ bit) for i in range(lax.axis_size(axis...  29.3 us
    ppermute x22, starting transfers between devices, flip(): lax.ppermute(value, axis, [(i, i ^ bit) for i in range(lax.axis_size(axis...  26.3 us
    pallas_call x11, Pallas kernels, call(): pl.pallas_call(body, out_shape=outs, in_specs=[HBM if i in far_in else sp...  22.9 us
  transfers between devices with their start and end apart: 22, of which 9 were waited for; matrix products, arithmetic and copies ran while one was open for 0% of the time, Pallas kernels for 12%

profile of v8, /device:TPU:0, one launch (start us, length us, event | category | flops | bytes accessed | tf_op | source)
XLA Modules:
  0.0 80.3 jit_solution(9534874026592297128)
XLA Ops:
  0.6 1.8 %shard_map.103 = (bf16[216,640]{1,0:T(8,128)(2,1)}, bf16[216,512]{1,0:T(8,128)(2,1)}) custom-call(bf16[2,216,1152]{2,1,0:T(8,128)(2,1)} %bitcast.9), custom_call_target="tpu_custom_call" | custom-call | tf_op jit(solution)/shard_map/pallas_call | solution.py:39
  2.5 3.0 %collective-permute-start.4 = (bf16[216,640]{1,0:T(8,128)(2,1)}, bf16[216,640]{1,0:T(8,128)(2,1)S(1)}, u32[]{:S(2)}, u32[]{:S(2)}) collective-permute-start(bf16[216,640]{1,0:T(8,128)(2,1)} %get-tuple-element.38.own_left), channel_id=1, source_target_pairs={{0,8},{8,0},{16,24},{24,16},{1,9},{9,1},{17,25},{25,17},{2,10},{10... | collective-permute-start | bytes 829448 | tf_op jit(solution)/shard_map/ppermute | solution.py:366
  5.5 1.5 %collective-permute-start.5 = (bf16[216,512]{1,0:T(8,128)(2,1)}, bf16[216,512]{1,0:T(8,128)(2,1)S(1)}, u32[]{:S(2)}, u32[]{:S(2)}) collective-permute-start(bf16[216,512]{1,0:T(8,128)(2,1)} %get-tuple-element.39.own_right), channel_id=1, source_target_pairs={{0,16},{8,24},{16,0},{24,8},{1,17},{9,25},{17,1},{25,9},{2,18},{10... | collective-permute-start | bytes 663560 | tf_op jit(solution)/shard_map/ppermute | solution.py:366
  7.0 4.8 %shard_map.101 = (bf16[32,2944]{1,0:T(8,128)(2,1)}, bf16[32,2944]{1,0:T(8,128)(2,1)}, bf16[32,2944]{1,0:T(8,128)(2,1)}, bf16[32,2944]{1,0:T(8,128)(2,1)}, bf16[1...) custom-call(bf16[128,1728]{1,0:T(8,128)(2,1)} %bitcast.11, bf16[128,1152]{1,0:T(8,128)(2,1)} %bitcast.13, ...), custom_call_target="tpu_custom_call" | custom-call | tf_op jit(solution)/shard_map/pallas_call | solution.py:39
  11.9 1.6 %collective-permute-start = (bf16[32,2944]{1,0:T(8,128)(2,1)}, bf16[32,2944]{1,0:T(8,128)(2,1)S(1)}, u32[]{:S(2)}, u32[]{:S(2)}) collective-permute-start(bf16[32,2944]{1,0:T(8,128)(2,1)} %get-tuple-element.35), channel_id=1, source_target_pairs={{0,2},{1,3},{2,0},{3,1},{4,6},{5,7},{6,4},{7,5},{8,10},{9,11},{10,... | collective-permute-start | bytes 565256 | tf_op jit(solution)/shard_map/ppermute | solution.py:366
  13.5 2.6 %collective-permute-start.1 = (bf16[32,2944]{1,0:T(8,128)(2,1)}, bf16[32,2944]{1,0:T(8,128)(2,1)S(1)}, u32[]{:S(2)}, u32[]{:S(2)}) collective-permute-start(bf16[32,2944]{1,0:T(8,128)(2,1)} %get-tuple-element.36), channel_id=1, source_target_pairs={{0,4},{1,5},{2,6},{3,7},{4,0},{5,1},{6,2},{7,3},{8,12},{9,13},{10,... | collective-permute-start | bytes 565256 | tf_op jit(solution)/shard_map/ppermute | solution.py:366
  16.4 0.9 %copy-done.4 = bf16[32,2944]{1,0:T(8,128)(2,1)S(1)} copy-done((bf16[32,2944]{1,0:T(8,128)(2,1)S(1)}, bf16[32,2944]{1,0:T(8,128)(2,1)}, u32[]{:S(2)}) %copy-start.4) | copy-done | bytes 188440
  17.3 0.8 shard_map.104
  18.0 0.5 collective-permute-start.6
  18.9 1.8 %collective-permute-done.refs_1_ = bf16[32,2944]{1,0:T(8,128)(2,1)S(1)} collective-permute-done((bf16[32,2944]{1,0:T(8,128)(2,1)}, bf16[32,2944]{1,0:T(8,128)(2,1)S(1)}, u32[]{:S(2)}, u32[]{:S(2)}) %collective-permute-start) | collective-permute-done | bytes 188448 | tf_op jit(solution)/shard_map/ppermute | solution.py:366
  20.7 9.7 %collective-permute-done.1.refs_2_ = bf16[32,2944]{1,0:T(8,128)(2,1)S(1)} collective-permute-done((bf16[32,2944]{1,0:T(8,128)(2,1)}, bf16[32,2944]{1,0:T(8,128)(2,1)S(1)}, u32[]{:S(2)}, u32[]{:S(2)}) %collective-permute-start.1) | collective-permute-done | bytes 188448 | tf_op jit(solution)/shard_map/ppermute | solution.py:366
  30.6 0.5 collective-permute-start.10
  31.6 3.6 %collective-permute-done.8.refs_4_ = bf16[216,640]{1,0:T(8,128)(2,1)S(1)} collective-permute-done((bf16[216,640]{1,0:T(8,128)(2,1)S(1)}, bf16[216,640]{1,0:T(8,128)(2,1)S(1)}, u32[]{:S(2)}, u32[]{:S(2)}) %collective-permute-start.8) | collective-permute-done | bytes 276512 | tf_op jit(solution)/shard_map/ppermute | solution.py:366
  35.3 7.5 %shard_map.106.mine = bf16[128,1728]{1,0:T(8,128)(2,1)S(1)} custom-call(bf16[128,3968]{1,0:T(8,128)(2,1)S(1)} %shard_map.102.near.refs_0_, bf16[128,3968]{1,0:T(8,128)(2,1)S(1)} %collective-permute-done.3.far.refs_1_, bf16[576,1152]{1,0:T(8,128)(2,1)S(1)} %copy-done.1, bf16[432,1152]{1,0:T(8,128)(2,1)S(1)} %bitcast.10, ...), custom_call_target="tpu_custom_call" | custom-call | tf_op jit(solution)/shard_map/pallas_call | solution.py:39
  42.9 1.7 %collective-permute-done.11.other = bf16[128,1728]{1,0:T(8,128)(2,1)S(1)} collective-permute-done((bf16[128,1728]{1,0:T(8,128)(2,1)S(1)}, bf16[128,1728]{1,0:T(8,128)(2,1)S(1)}, u32[]{:S(2)}, u32[]{:S(2)}) %collective-permute-start.11) | collective-permute-done | bytes 442400 | tf_op jit(solution)/shard_map/ppermute | solution.py:366
  44.6 2.9 %shard_map.107 = (bf16[32,1728]{1,0:T(8,128)(2,1)S(1)}, bf16[32,1728]{1,0:T(8,128)(2,1)S(1)}, bf16[32,1728]{1,0:T(8,128)(2,1)S(1)}, bf16[32,1728]{1,0:T(8,128)(2...) custom-call(bf16[128,1728]{1,0:T(8,128)(2,1)S(1)} %shard_map.106.mine, ...), custom_call_target="tpu_custom_call" | custom-call | tf_op jit(solution)/shard_map/pallas_call | solution.py:39
  47.5 0.6 collective-permute-start.15
  48.1 0.5 collective-permute-start.16
  48.6 2.6 %collective-permute-start.12 = (bf16[32,1728]{1,0:T(8,128)(2,1)S(1)}, bf16[32,1728]{1,0:T(8,128)(2,1)S(1)}, u32[]{:S(2)}, u32[]{:S(2)}) collective-permute-start(bf16[32,1728]{1,0:T(8,128)(2,1)S(1)} %get-tuple-element.43), channel_id=1, source_target_pairs={{0,2},{1,3},{2,0},{3,1},{4,6},{5,7},{6,4},{7,5},{8,10},{9,11},{10,... | collective-permute-start | bytes 331784 | tf_op jit(solution)/shard_map/ppermute | solution.py:366
  51.2 2.9 %collective-permute-done.12.refs_1_._ = bf16[32,1728]{1,0:T(8,128)(2,1)S(1)} collective-permute-done((bf16[32,1728]{1,0:T(8,128)(2,1)S(1)}, bf16[32,1728]{1,0:T(8,128)(2,1)S(1)}, u32[]{:S(2)}, u32[]{:S(2)}) %collective-permute-start.12) | collective-permute-done | bytes 110624 | tf_op jit(solution)/shard_map/ppermute | solution.py:366
  54.1 3.3 %collective-permute-done.15.got_x = bf16[2,72,1152]{2,1,0:T(8,128)(2,1)S(1)} collective-permute-done((bf16[2,72,1152]{2,1,0:T(8,128)(2,1)S(1)}, bf16[2,72,1152]{2,1,0:T(8,128)(2,1)S(1)}, u32[]{:S(2)}, u32[]{:S(2)}) %collective-permute-start.15) | collective-permute-done | bytes 331808 | tf_op jit(solution)/shard_map/ppermute | solution.py:366
  57.8 0.6 collective-permute-start.17
  58.4 1.5 %collective-permute-start.18 = (bf16[72,1152]{1,0:T(8,128)(2,1)S(1)}, bf16[72,1152]{1,0:T(8,128)(2,1)S(1)}, u32[]{:S(2)}, u32[]{:S(2)}) collective-permute-start(bf16[72,1152]{1,0:T(8,128)(2,1)S(1)} %get-tuple-element.56), channel_id=1, source_target_pairs={{0,8},{8,0},{16,24},{24,16},{1,9},{9,1},{17,25},{25,17},{2,10},{10... | collective-permute-start | bytes 497672 | tf_op jit(solution)/shard_map/ppermute | solution.py:366
  59.9 3.6 %collective-permute-start.13 = (bf16[32,1728]{1,0:T(8,128)(2,1)S(1)}, bf16[32,1728]{1,0:T(8,128)(2,1)S(1)}, u32[]{:S(2)}, u32[]{:S(2)}) collective-permute-start(bf16[32,1728]{1,0:T(8,128)(2,1)S(1)} %get-tuple-element.44), channel_id=1, source_target_pairs={{0,4},{1,5},{2,6},{3,7},{4,0},{5,1},{6,2},{7,3},{8,12},{9,13},{10,... | collective-permute-start | bytes 331784 | tf_op jit(solution)/shard_map/ppermute | solution.py:366
  63.5 1.3 %collective-permute-start.14 = (bf16[32,1728]{1,0:T(8,128)(2,1)S(1)}, bf16[32,1728]{1,0:T(8,128)(2,1)S(1)}, u32[]{:S(2)}, u32[]{:S(2)}) collective-permute-start(bf16[32,1728]{1,0:T(8,128)(2,1)S(1)} %get-tuple-element.45), channel_id=1, source_target_pairs={{0,6},{1,7},{2,4},{3,5},{4,2},{5,3},{6,0},{7,1},{8,14},{9,15},{10,... | collective-permute-start | bytes 331784 | tf_op jit(solution)/shard_map/ppermute | solution.py:366
  65.1 1.6 %collective-permute-start.19 = (bf16[72,576]{1,0:T(8,128)(2,1)S(1)}, bf16[72,576]{1,0:T(8,128)(2,1)S(1)}, u32[]{:S(2)}, u32[]{:S(2)}) collective-permute-start(bf16[72,576]{1,0:T(8,128)(2,1)S(1)} %get-tuple-element.58), channel_id=1, source_target_pairs={{0,2},{1,3},{2,0},{3,1},{4,6},{5,7},{6,4},{7,5},{8,10},{9,11},{10,... | collective-permute-start | bytes 248840 | tf_op jit(solution)/shard_map/ppermute | solution.py:366
  66.6 1.5 %collective-permute-start.20 = (bf16[72,576]{1,0:T(8,128)(2,1)S(1)}, bf16[72,576]{1,0:T(8,128)(2,1)S(1)}, u32[]{:S(2)}, u32[]{:S(2)}) collective-permute-start(bf16[72,576]{1,0:T(8,128)(2,1)S(1)} %get-tuple-element.59), channel_id=1, source_target_pairs={{0,4},{1,5},{2,6},{3,7},{4,0},{5,1},{6,2},{7,3},{8,12},{9,13},{10,... | collective-permute-start | bytes 248840 | tf_op jit(solution)/shard_map/ppermute | solution.py:366
  68.2 1.3 %collective-permute-start.21 = (bf16[72,576]{1,0:T(8,128)(2,1)S(1)}, bf16[72,576]{1,0:T(8,128)(2,1)S(1)}, u32[]{:S(2)}, u32[]{:S(2)}) collective-permute-start(bf16[72,576]{1,0:T(8,128)(2,1)S(1)} %get-tuple-element.60), channel_id=1, source_target_pairs={{0,6},{1,7},{2,4},{3,5},{4,2},{5,3},{6,0},{7,1},{8,14},{9,15},{10,... | collective-permute-start | bytes 248840 | tf_op jit(solution)/shard_map/ppermute | solution.py:366
  69.5 3.1 %collective-permute-done.13.refs_2_ = bf16[32,1728]{1,0:T(8,128)(2,1)S(1)} collective-permute-done((bf16[32,1728]{1,0:T(8,128)(2,1)S(1)}, bf16[32,1728]{1,0:T(8,128)(2,1)S(1)}, u32[]{:S(2)}, u32[]{:S(2)}) %collective-permute-start.13) | collective-permute-done | bytes 110624 | tf_op jit(solution)/shard_map/ppermute | solution.py:366
  72.7 3.9 %shard_map.108 = (bf16[128,1152]{1,0:T(8,128)(2,1)}, bf16[128,1152]{1,0:T(8,128)(2,1)}, bf16[128,1728]{1,0:T(8,128)(2,1)}) custom-call(bf16[32,1728]{1,0:T(8,128)(2,1)S(1)} %get-tuple-element.42.refs_0_, bf16[32,1728]{1,0:T(8,128)(2,1)S(1)} %collective-permute-done.12.refs_1_._, bf16[32,1728]{1,0:T(8,128)(2,1)S(1)} %collective-permute-done.13.refs_2_, ...), custom_call_target="tpu_custom_call" | custom-call | tf_op jit(solution)/shard_map/pallas_call | solution.py:39
  76.6 3.0 %collective-permute-done.20.refs_1_ = bf16[72,576]{1,0:T(8,128)(2,1)S(1)} collective-permute-done((bf16[72,576]{1,0:T(8,128)(2,1)S(1)}, bf16[72,576]{1,0:T(8,128)(2,1)S(1)}, u32[]{:S(2)}, u32[]{:S(2)}) %collective-permute-start.20) | collective-permute-done | bytes 82976 | tf_op jit(solution)/shard_map/ppermute | solution.py:366
  79.5 0.8 shard_map.111
  (41 shorter events, 2.1 us)
Async XLA Ops:
  2.5 13.9 %copy-start.7 = (bf16[216,640]{1,0:T(8,128)(2,1)S(1)}, bf16[216,640]{1,0:T(8,128)(2,1)}, u32[]{:S(2)}) copy-start(bf16[216,640]{1,0:T(8,128)(2,1)} %get-tuple-element.38.own_left) | copy-start | bytes 829444
  2.5 13.9 %copy-start.8 = (bf16[216,512]{1,0:T(8,128)(2,1)S(1)}, bf16[216,512]{1,0:T(8,128)(2,1)}, u32[]{:S(2)}) copy-start(bf16[216,512]{1,0:T(8,128)(2,1)} %get-tuple-element.39.own_right) | copy-start | bytes 663556
  2.5 13.8 %collective-permute-start.4 = (bf16[216,640]{1,0:T(8,128)(2,1)}, bf16[216,640]{1,0:T(8,128)(2,1)S(1)}, u32[]{:S(2)}, u32[]{:S(2)}) collective-permute-start(bf16[216,640]{1,0:T(8,128)(2,1)} %get-tuple-element.38.own_left), channel_id=1, source_target_pairs={{0,8},{8,0},{16,24},{24,16},{1,9},{9,1},{17,25},{25,17},{2,10},{10... | collective-permute-start | bytes 829448 | tf_op jit(solution)/shard_map/ppermute | solution.py:366
  5.5 10.8 %collective-permute-start.5 = (bf16[216,512]{1,0:T(8,128)(2,1)}, bf16[216,512]{1,0:T(8,128)(2,1)S(1)}, u32[]{:S(2)}, u32[]{:S(2)}) collective-permute-start(bf16[216,512]{1,0:T(8,128)(2,1)} %get-tuple-element.39.own_right), channel_id=1, source_target_pairs={{0,16},{8,24},{16,0},{24,8},{1,17},{9,25},{17,1},{25,9},{2,18},{10... | collective-permute-start | bytes 663560 | tf_op jit(solution)/shard_map/ppermute | solution.py:366
  11.9 8.8 %collective-permute-start = (bf16[32,2944]{1,0:T(8,128)(2,1)}, bf16[32,2944]{1,0:T(8,128)(2,1)S(1)}, u32[]{:S(2)}, u32[]{:S(2)}) collective-permute-start(bf16[32,2944]{1,0:T(8,128)(2,1)} %get-tuple-element.35), channel_id=1, source_target_pairs={{0,2},{1,3},{2,0},{3,1},{4,6},{5,7},{6,4},{7,5},{8,10},{9,11},{10,... | collective-permute-start | bytes 565256 | tf_op jit(solution)/shard_map/ppermute | solution.py:366
  13.5 16.8 %collective-permute-start.1 = (bf16[32,2944]{1,0:T(8,128)(2,1)}, bf16[32,2944]{1,0:T(8,128)(2,1)S(1)}, u32[]{:S(2)}, u32[]{:S(2)}) collective-permute-start(bf16[32,2944]{1,0:T(8,128)(2,1)} %get-tuple-element.36), channel_id=1, source_target_pairs={{0,4},{1,5},{2,6},{3,7},{4,0},{5,1},{6,2},{7,3},{8,12},{9,13},{10,... | collective-permute-start | bytes 565256 | tf_op jit(solution)/shard_map/ppermute | solution.py:366
  16.1 14.3 %collective-permute-start.2 = (bf16[32,2944]{1,0:T(8,128)(2,1)}, bf16[32,2944]{1,0:T(8,128)(2,1)S(1)}, u32[]{:S(2)}, u32[]{:S(2)}) collective-permute-start(bf16[32,2944]{1,0:T(8,128)(2,1)} %get-tuple-element.37), channel_id=1, source_target_pairs={{0,6},{1,7},{2,4},{3,5},{4,2},{5,3},{6,0},{7,1},{8,14},{9,15},{10,... | collective-permute-start | bytes 565256 | tf_op jit(solution)/shard_map/ppermute | solution.py:366
  16.3 0.9 %copy-start.4 = (bf16[32,2944]{1,0:T(8,128)(2,1)S(1)}, bf16[32,2944]{1,0:T(8,128)(2,1)}, u32[]{:S(2)}) copy-start(bf16[32,2944]{1,0:T(8,128)(2,1)} %get-tuple-element.34.refs_0_.own) | copy-start | bytes 565252
  18.0 13.1 %collective-permute-start.6 = (bf16[432,640]{1,0:T(8,128)(2,1)S(1)}, bf16[432,640]{1,0:T(8,128)(2,1)S(1)}, u32[]{:S(2)}, u32[]{:S(2)}) collective-permute-start(bf16[432,640]{1,0:T(8,128)(2,1)S(1)} %get-tuple-element.40), channel_id=1, source_target_pairs={{0,16},{8,24},{16,0},{24,8},{1,17},{9,25},{17,1},{25,9},{2,18},{10... | collective-permute-start | bytes 1658888 | tf_op jit(solution)/shard_map/ppermute | solution.py:366
  18.5 16.7 %copy-start.1 = (bf16[576,1152]{1,0:T(8,128)(2,1)S(1)}, bf16[576,1152]{1,0:T(8,128)(2,1)}, u32[]{:S(2)}) copy-start(bf16[576,1152]{1,0:T(8,128)(2,1)} %refs_7_.1) | copy-start | bytes 3981316
  18.5 16.7 %copy-start.2 = (bf16[1152,432]{0,1:T(8,128)(2,1)S(1)}, bf16[1152,432]{0,1:T(8,128)(2,1)}, u32[]{:S(2)}) copy-start(bf16[1152,432]{0,1:T(8,128)(2,1)} %param.9) | copy-start | bytes 2985988
  18.5 12.0 %collective-permute-start.7 = (bf16[432,512]{1,0:T(8,128)(2,1)S(1)}, bf16[432,512]{1,0:T(8,128)(2,1)S(1)}, u32[]{:S(2)}, u32[]{:S(2)}) collective-permute-start(bf16[432,512]{1,0:T(8,128)(2,1)S(1)} %get-tuple-element.41), channel_id=1, source_target_pairs={{0,8},{8,0},{16,24},{24,16},{1,9},{9,1},{17,25},{25,17},{2,10},{10... | collective-permute-start | bytes 1327112 | tf_op jit(solution)/shard_map/ppermute | solution.py:366
  30.4 4.8 %collective-permute-start.3 = (bf16[128,3968]{1,0:T(8,128)(2,1)S(1)}, bf16[128,3968]{1,0:T(8,128)(2,1)S(1)}, u32[]{:S(2)}, u32[]{:S(2)}) collective-permute-start(bf16[128,3968]{1,0:T(8,128)(2,1)S(1)} %shard_map.102.near.refs_0_), channel_id=1, source_target_pairs={{0,1},{1,0},{2,3},{3,2},{4,5},{5,4},{6,7},{7,6},{8,9},{9,8},{10,11... | collective-permute-start | bytes 3047432 | tf_op jit(solution)/shard_map/ppermute | solution.py:366
  30.6 4.7 %collective-permute-start.10 = (bf16[648,512]{1,0:T(8,128)(2,1)S(1)}, bf16[648,512]{1,0:T(8,128)(2,1)S(1)}, u32[]{:S(2)}, u32[]{:S(2)}) collective-permute-start(bf16[648,512]{1,0:T(8,128)(2,1)S(1)} %shard_map.105.refs_3_), channel_id=1, source_target_pairs={{0,1},{1,0},{2,3},{3,2},{4,5},{5,4},{6,7},{7,6},{8,9},{9,8},{10,11... | collective-permute-start | bytes 1990664 | tf_op jit(solution)/shard_map/ppermute | solution.py:366
  31.1 4.1 %collective-permute-start.9 = (bf16[432,640]{1,0:T(8,128)(2,1)S(1)}, bf16[432,640]{1,0:T(8,128)(2,1)S(1)}, u32[]{:S(2)}, u32[]{:S(2)}) collective-permute-start(bf16[432,640]{1,0:T(8,128)(2,1)S(1)} %collective-permute-done.6.refs_2_), channel_id=1, source_target_pairs={{0,1},{1,0},{2,3},{3,2},{4,5},{5,4},{6,7},{7,6},{8,9},{9,8},{10,11... | collective-permute-start | bytes 1658888 | tf_op jit(solution)/shard_map/ppermute | solution.py:366
  31.2 4.0 %collective-permute-start.8 = (bf16[216,640]{1,0:T(8,128)(2,1)S(1)}, bf16[216,640]{1,0:T(8,128)(2,1)S(1)}, u32[]{:S(2)}, u32[]{:S(2)}) collective-permute-start(bf16[216,640]{1,0:T(8,128)(2,1)S(1)} %collective-permute-done.4.got_x.refs_1_), channel_id=1, source_target_pairs={{0,1},{1,0},{2,3},{3,2},{4,5},{5,4},{6,7},{7,6},{8,9},{9,8},{10,11... | collective-permute-start | bytes 829448 | tf_op jit(solution)/shard_map/ppermute | solution.py:366
  42.7 1.9 %collective-permute-start.11 = (bf16[128,1728]{1,0:T(8,128)(2,1)S(1)}, bf16[128,1728]{1,0:T(8,128)(2,1)S(1)}, u32[]{:S(2)}, u32[]{:S(2)}) collective-permute-start(bf16[128,1728]{1,0:T(8,128)(2,1)S(1)} %shard_map.106.mine), channel_id=1, source_target_pairs={{0,1},{1,0},{2,3},{3,2},{4,5},{5,4},{6,7},{7,6},{8,9},{9,8},{10,11... | collective-permute-start | bytes 1327112 | tf_op jit(solution)/shard_map/ppermute | solution.py:366
  47.5 9.9 %collective-permute-start.15 = (bf16[2,72,1152]{2,1,0:T(8,128)(2,1)S(1)}, bf16[2,72,1152]{2,1,0:T(8,128)(2,1)S(1)}, u32[]{:S(2)}, u32[]{:S(2)}) collective-permute-start(bf16[2,72,1152]{2,1,0:T(8,128)(2,1)S(1)} %get-tuple-element.52), channel_id=1, source_target_pairs={{0,8},{8,0},{16,24},{24,16},{1,9},{9,1},{17,25},{25,17},{2,10},{10... | collective-permute-start | bytes 995336 | tf_op jit(solution)/shard_map/ppermute | solution.py:366
  48.1 9.6 %collective-permute-start.16 = (bf16[2,72,1152]{2,1,0:T(8,128)(2,1)S(1)}, bf16[2,72,1152]{2,1,0:T(8,128)(2,1)S(1)}, u32[]{:S(2)}, u32[]{:S(2)}) collective-permute-start(bf16[2,72,1152]{2,1,0:T(8,128)(2,1)S(1)} %get-tuple-element.53), channel_id=1, source_target_pairs={{0,16},{8,24},{16,0},{24,8},{1,17},{9,25},{17,1},{25,9},{2,18},{10... | collective-permute-start | bytes 995336 | tf_op jit(solution)/shard_map/ppermute | solution.py:366
  48.6 5.5 %collective-permute-start.12 = (bf16[32,1728]{1,0:T(8,128)(2,1)S(1)}, bf16[32,1728]{1,0:T(8,128)(2,1)S(1)}, u32[]{:S(2)}, u32[]{:S(2)}) collective-permute-start(bf16[32,1728]{1,0:T(8,128)(2,1)S(1)} %get-tuple-element.43), channel_id=1, source_target_pairs={{0,2},{1,3},{2,0},{3,1},{4,6},{5,7},{6,4},{7,5},{8,10},{9,11},{10,... | collective-permute-start | bytes 331784 | tf_op jit(solution)/shard_map/ppermute | solution.py:366
  57.7 15.0 %copy-start = (bf16[576,1152]{1,0:T(8,128)(2,1)S(1)}, bf16[576,1152]{1,0:T(8,128)(2,1)}, u32[]{:S(2)}) copy-start(bf16[576,1152]{1,0:T(8,128)(2,1)} %refs_4_.1) | copy-start | bytes 3981316
  57.7 15.0 %copy-start.3 = (bf16[2,64,1728]{2,1,0:T(8,128)(2,1)S(1)}, bf16[2,64,1728]{2,1,0:T(8,128)(2,1)}, u32[]{:S(2)}) copy-start(bf16[2,64,1728]{2,1,0:T(8,128)(2,1)} %param.7) | copy-start | bytes 1327108
  57.7 15.0 %copy-start.5 = (f32[8,128,128]{2,1,0:T(8,128)S(1)}, f32[8,128,128]{2,1,0:T(8,128)}, u32[]{:S(2)}) copy-start(f32[8,128,128]{2,1,0:T(8,128)} %get-tuple-element.46.refs_6_) | copy-start | bytes 1572868
  57.7 15.0 %copy-start.6 = (bf16[128,1152]{1,0:T(8,128)(2,1)S(1)}, bf16[128,1152]{1,0:T(8,128)(2,1)}, u32[]{:S(2)}) copy-start(bf16[128,1152]{1,0:T(8,128)(2,1)} %get-tuple-element.47.refs_8_) | copy-start | bytes 884740
  57.8 7.0 %collective-permute-start.17 = (bf16[72,1152]{1,0:T(8,128)(2,1)S(1)}, bf16[72,1152]{1,0:T(8,128)(2,1)S(1)}, u32[]{:S(2)}, u32[]{:S(2)}) collective-permute-start(bf16[72,1152]{1,0:T(8,128)(2,1)S(1)} %get-tuple-element.55), channel_id=1, source_target_pairs={{0,16},{8,24},{16,0},{24,8},{1,17},{9,25},{17,1},{25,9},{2,18},{10... | collective-permute-start | bytes 497672 | tf_op jit(solution)/shard_map/ppermute | solution.py:366
  58.4 6.5 %collective-permute-start.18 = (bf16[72,1152]{1,0:T(8,128)(2,1)S(1)}, bf16[72,1152]{1,0:T(8,128)(2,1)S(1)}, u32[]{:S(2)}, u32[]{:S(2)}) collective-permute-start(bf16[72,1152]{1,0:T(8,128)(2,1)S(1)} %get-tuple-element.56), channel_id=1, source_target_pairs={{0,8},{8,0},{16,24},{24,16},{1,9},{9,1},{17,25},{25,17},{2,10},{10... | collective-permute-start | bytes 497672 | tf_op jit(solution)/shard_map/ppermute | solution.py:366
  59.9 12.7 %collective-permute-start.13 = (bf16[32,1728]{1,0:T(8,128)(2,1)S(1)}, bf16[32,1728]{1,0:T(8,128)(2,1)S(1)}, u32[]{:S(2)}, u32[]{:S(2)}) collective-permute-start(bf16[32,1728]{1,0:T(8,128)(2,1)S(1)} %get-tuple-element.44), channel_id=1, source_target_pairs={{0,4},{1,5},{2,6},{3,7},{4,0},{5,1},{6,2},{7,3},{8,12},{9,13},{10,... | collective-permute-start | bytes 331784 | tf_op jit(solution)/shard_map/ppermute | solution.py:366
  63.5 9.1 %collective-permute-start.14 = (bf16[32,1728]{1,0:T(8,128)(2,1)S(1)}, bf16[32,1728]{1,0:T(8,128)(2,1)S(1)}, u32[]{:S(2)}, u32[]{:S(2)}) collective-permute-start(bf16[32,1728]{1,0:T(8,128)(2,1)S(1)} %get-tuple-element.45), channel_id=1, source_target_pairs={{0,6},{1,7},{2,4},{3,5},{4,2},{5,3},{6,0},{7,1},{8,14},{9,15},{10,... | collective-permute-start | bytes 331784 | tf_op jit(solution)/shard_map/ppermute | solution.py:366
  65.1 11.5 %collective-permute-start.19 = (bf16[72,576]{1,0:T(8,128)(2,1)S(1)}, bf16[72,576]{1,0:T(8,128)(2,1)S(1)}, u32[]{:S(2)}, u32[]{:S(2)}) collective-permute-start(bf16[72,576]{1,0:T(8,128)(2,1)S(1)} %get-tuple-element.58), channel_id=1, source_target_pairs={{0,2},{1,3},{2,0},{3,1},{4,6},{5,7},{6,4},{7,5},{8,10},{9,11},{10,... | collective-permute-start | bytes 248840 | tf_op jit(solution)/shard_map/ppermute | solution.py:366
  66.6 12.9 %collective-permute-start.20 = (bf16[72,576]{1,0:T(8,128)(2,1)S(1)}, bf16[72,576]{1,0:T(8,128)(2,1)S(1)}, u32[]{:S(2)}, u32[]{:S(2)}) collective-permute-start(bf16[72,576]{1,0:T(8,128)(2,1)S(1)} %get-tuple-element.59), channel_id=1, source_target_pairs={{0,4},{1,5},{2,6},{3,7},{4,0},{5,1},{6,2},{7,3},{8,12},{9,13},{10,... | collective-permute-start | bytes 248840 | tf_op jit(solution)/shard_map/ppermute | solution.py:366
  68.2 11.4 %collective-permute-start.21 = (bf16[72,576]{1,0:T(8,128)(2,1)S(1)}, bf16[72,576]{1,0:T(8,128)(2,1)S(1)}, u32[]{:S(2)}, u32[]{:S(2)}) collective-permute-start(bf16[72,576]{1,0:T(8,128)(2,1)S(1)} %get-tuple-element.60), channel_id=1, source_target_pairs={{0,6},{1,7},{2,4},{3,5},{4,2},{5,3},{6,0},{7,1},{8,14},{9,15},{10,... | collective-permute-start | bytes 248840 | tf_op jit(solution)/shard_map/ppermute | solution.py:366

commit v9 on v8

--- a/solution.py
+++ b/solution.py
@@ -16,7 +16,7 @@
 VMEM = pl.BlockSpec(memory_space=pltpu.VMEM)
 SMEM = pl.BlockSpec(memory_space=pltpu.SMEM)
 HBM = pl.BlockSpec(memory_space=pltpu.HBM)
-PAD = 8 * LANES
+PAD = 2 * LANES
 LIMIT = 16 * 1024 * 1024
 MOST = 60 * 1024 * 1024
 
@@ -187,20 +187,10 @@
     return jnp.concatenate([first, second], axis=1).reshape(2 * rows, width).astype(BF16)
 
 
-def cut_kernel(chips, whole, left, right, sem):
-    core, cut = place(chips)[1], left.shape[1]
-    pairs = [(whole.at[core, :, pl.ds(0, cut)], left)]
-    pairs.append((whole.at[core, :, pl.ds(cut, right.shape[1])], right))
-    for copy in started(pairs, sem):
-        copy.wait()
-
-
-def second_kernel(own_left, own_right, got_x, got_y, own, left, right, kept):
-    half = got_x.shape[0]
-    left[:half] = own_left[...]
-    left[half:] = got_x[...]
-    right[:half] = own_right[...]
-    right[half:] = got_y[...]
+def half_kernel(chips, got, own, half, kept):
+    rows = half.shape[0]
+    core = place(chips)[1]
+    half[...] = jnp.where(core == 0, got[:rows].astype(F32), got[rows:].astype(F32)).astype(BF16)
     kept[...] = own[...]
 
 
@@ -211,29 +201,10 @@
         low += ref.shape[0]
 
 
-def projected(hidden, shards, weights, idx, blocks, sums):
-    size = blocks.shape[2]
-    sums[...] = jnp.zeros_like(sums)
-    for held, w in zip(shards, weights):
-        low = held[0][1]
-        value = dot_bt(hidden[:, low : low + w.shape[1]], w[...])
-        for at, _, i in held:
-            sums[at(idx)] += value if i is None else value[:, i * size : (i + 1) * size]
-    blocks[...] = sums[...].astype(BF16)
-
-
-def projected_back(blocks, shards, weights, idx, total):
-    total[...] = jnp.zeros_like(total)
-    for held, w in zip(shards, weights):
-        low = held[0][1]
-        lhs = jnp.concatenate([blocks[at(idx)] for at, _, _ in held], axis=1)
-        total[:, low : low + w.shape[1]] += dot(lhs, w[...])
-
-
 def temporal_kernel(shards, chips, group, near, far, wot, *refs):
     idx = place(chips)
     weights, refs = refs[: len(shards)], refs[len(shards) :]
-    mine, cot, q, k, v, g, p_ref, blocks, sums, total = refs
+    mine, cot, q, k, v, g, p_ref, blocks = refs
     inner, width = wot.shape
     heads = inner // DH
     value = [own_patches(ref, idx[1], 2 * group) for ref in (near, far)]
@@ -241,7 +212,10 @@
     hidden = value[:, :width]
     cot[...] = value[:, width : 2 * width]
     size = blocks.shape[2]
-    projected(hidden, shards, weights, idx, blocks, sums)
+    for at, w in zip(shards, weights):
+        value = dot_bt(hidden, w[...]).astype(BF16)
+        for i, block in enumerate(at(idx)):
+            blocks[block] = value[:, i * size : (i + 1) * size]
     whole = jnp.concatenate([blocks[i] for i in range(blocks.shape[0])], axis=1)
     put(q, whole[:, :inner])
     put(k, whole[:, inner : 2 * inner])
@@ -252,8 +226,10 @@
     whole = jnp.concatenate([dq[:, :inner], dk[:, :inner], dv[:, :inner]], axis=1)
     for i in range(blocks.shape[0]):
         blocks[i] = whole[:, i * size : (i + 1) * size]
-    projected_back(blocks, shards, weights, idx, total)
-    grad = total[...]
+    grad = jnp.zeros(cot.shape, F32)
+    for at, w in zip(shards, weights):
+        lhs = jnp.concatenate([blocks[block] for block in at(idx)], axis=1)
+        grad += dot(lhs, w[...])
     mine[:, :width] = (cot[...].astype(F32) + grad.astype(BF16).astype(F32)).astype(BF16)
 
 
@@ -370,6 +346,14 @@
     return pltpu.SemaphoreType.DMA((n,))
 
 
+def across(value, bits):
+    n = lax.axis_size("seq")
+    pairs = [
+        (d * n + i, (d ^ bits[i % 2]) * n + i) for d in range(lax.axis_size("dp")) for i in range(n)
+    ]
+    return lax.ppermute(value, ("dp", "seq"), pairs)
+
+
 def gather(weight, parts, chips):
     n = lax.axis_size("dp")
     rows, sent = parts[0].shape
@@ -377,41 +361,29 @@
     if n != 4:
         (near,) = call(join_rows_kernel, whole, from_chips(parts), small=True)
         weights = [lax.all_gather(weight, "dp", axis=0, tiled=True)]
-        return near, flip(near, "seq", 1), weights, [[(lambda idx: 0, 0, None)]], 1
+        return near, flip(near, "seq", 1), weights, [lambda idx: [0]], 1
     half, width = weight.shape[0] // 2, weight.shape[1]
-    cut = -(-width // LANES // 2) * LANES
-    left, right = call(
-        functools.partial(cut_kernel, chips),
-        [shape((half, cut)), shape((half, width - cut))],
-        [weight.reshape(2, half, width)],
-        [sems(2)],
-        far_in=range(1),
-    )
-    got_x, got_y = flip(left, "dp", 1), flip(right, "dp", 2)
-    left, right, own = call(
-        second_kernel,
-        [shape((2 * half, cut)), shape((2 * half, width - cut)), shape((rows, sent))],
-        [left, right, got_x, got_y, parts[0]],
+    side = across(weight, (1, 2))
+    corner, own = call(
+        functools.partial(half_kernel, chips),
+        [shape((half, width)), shape((rows, sent))],
+        [side, parts[0]],
         small=True,
     )
-    (near,) = call(join_rows_kernel, whole, from_chips(parts), small=True)
-    (right,) = call(
-        join_rows_kernel,
-        [shape((3 * half, width - cut))],
-        [got_y, flip(right, "dp", 1)],
-        small=True,
-    )
-    held = [got_x, flip(left, "dp", 2), right]
-    weights = [weight, *held, *[flip(w, "seq", 1) for w in held]]
-
-    def block(j, other):
-        return lambda idx: 2 * (idx[0] ^ j) + (idx[1] ^ other)
-
-    shards = [[(lambda idx: 2 * idx[0], 0, 0), (lambda idx: 2 * idx[0] + 1, 0, 1)]]
-    for other in (0, 1):
-        shards += [[(block(1, other), 0, None)]]
-        shards.append([(block(2, other), 0, 0), (block(3, other), 0, 1)])
-        shards.append([(block(j, other), cut, i) for i, j in enumerate((2, 1, 3))])
+    corner = across(corner, (2, 1))
+    (near,) = call(join_rows_kernel, whole, [own, *from_chips(parts)[1:]], small=True)
+    weights = [weight, side, flip(side, "seq", 1), corner, flip(corner, "seq", 1)]
+
+    def both(shard):
+        return lambda idx: [2 * shard(idx), 2 * shard(idx) + 1]
+
+    shards = [
+        both(lambda idx: idx[0]),
+        both(lambda idx: idx[0] ^ (1 + idx[1])),
+        both(lambda idx: idx[0] ^ (2 - idx[1])),
+        lambda idx: [2 * (idx[0] ^ 3) + idx[1]],
+        lambda idx: [2 * (idx[0] ^ 3) + 1 - idx[1]],
+    ]
     return near, flip(near, "seq", 1), weights, shards, 2 * n
 
 
@@ -474,15 +446,12 @@
         far_out=(chips, chips + 1),
     )
     near, far, weights, places, count = gather(w_temporal.T, near, chips)
-
-    def blocks(dtype):
-        return pltpu.VMEM((count, rows, 3 * inner // count), dtype)
-
+    blocks = pltpu.VMEM((count, rows, 3 * inner // count), BF16)
     (mine,) = call(
         functools.partial(temporal_kernel, places, chips, group),
         [shape((rows, width + inner))],
         [near, far, wo_temporal, *weights],
-        [held(width)] + [wide] * 4 + [attended, blocks(BF16), blocks(F32), held(width, F32)],
+        [held(width)] + [wide] * 4 + [attended, blocks],
         small=True,
     )
     other = flip(mine, "seq", 1)

time: 80.5 us -> 75.5 us (0.938)
  waiting for transfers between devices: 29.3 us -> 25.8 us
  Pallas kernels: 22.9 us -> 20.1 us
  starting transfers between devices: 26.3 us -> 27.7 us
    ppermute x22 -> x17, waiting for transfers between devices: 29.3 us -> 22.7 us  [flip(): lax.ppermute(value, axis, [(i, i ^ bit) for i in range(lax.axis_size(axis...]
    ppermute x0 -> x2, starting transfers between devices: none -> 5.12 us  [across(): return lax.ppermute(value, ('dp', 'seq'), pairs)]
    ppermute x22 -> x17, starting transfers between devices: 26.3 us -> 22.6 us  [flip(): lax.ppermute(value, axis, [(i, i ^ bit) for i in range(lax.axis_size(axis...]
    ppermute x0 -> x2, waiting for transfers between devices: none -> 3.15 us  [across(): return lax.ppermute(value, ('dp', 'seq'), pairs)]
    pallas_call x11 -> x9, Pallas kernels: 22.9 us -> 20.1 us  [call(): pl.pallas_call(body, out_shape=outs, in_specs=[HBM if i in far_in else sp...]
  transfers between devices with their start and end apart: 22 -> 19, of which waited for: 9 -> 10; matrix products, arithmetic and copies ran while one was open for 0% -> 0% of each run, Pallas kernels for 12% -> 12%
where the time goes in v9:
time: 75.5 us; the launch traced here: 75.3 us
  starting transfers between devices  27.7 us (37%)
  waiting for transfers between devices  25.8 us (34%)
  Pallas kernels  20.1 us (27%)
  local copies, waits for them, and re-layouts  0.95 us (1%)
    ppermute x17, waiting for transfers between devices, flip(): lax.ppermute(value, axis, [(i, i ^ bit) for i in range(lax.axis_size(axis...  22.7 us
    ppermute x17, starting transfers between devices, flip(): lax.ppermute(value, axis, [(i, i ^ bit) for i in range(lax.axis_size(axis...  22.6 us
    pallas_call x9, Pallas kernels, call(): pl.pallas_call(body, out_shape=outs, in_specs=[HBM if i in far_in else sp...  20.1 us
    ppermute x2, starting transfers between devices, across(): return lax.ppermute(value, ('dp', 'seq'), pairs)  5.12 us
    ppermute x2, waiting for transfers between devices, across(): return lax.ppermute(value, ('dp', 'seq'), pairs)  3.15 us
  transfers between devices with their start and end apart: 19, of which 10 were waited for; matrix products, arithmetic and copies ran while one was open for 0% of the time, Pallas kernels for 12%

profile of v9, /device:TPU:0, one launch (start us, length us, event | category | flops | bytes accessed | tf_op | source)
XLA Modules:
  0.0 75.3 jit_solution(8641098290511786931)
XLA Ops:
  0.6 3.0 %collective-permute-start = (bf16[432,1152]{1,0:T(8,128)(2,1)}, bf16[432,1152]{1,0:T(8,128)(2,1)S(1)}, u32[]{:S(2)}, u32[]{:S(2)}) collective-permute-start(bf16[432,1152]{1,0:T(8,128)(2,1)} %bitcast.9), channel_id=1, source_target_pairs={{0,8},{1,17},{2,10},{3,19},{4,12},{5,21},{6,14},{7,23},{8,0},{9,25... | collective-permute-start | bytes 2985992 | tf_op jit(solution)/shard_map/ppermute | solution.py:354
  3.6 4.8 %shard_map.101 = (bf16[32,2944]{1,0:T(8,128)(2,1)}, bf16[32,2944]{1,0:T(8,128)(2,1)}, bf16[32,2944]{1,0:T(8,128)(2,1)}, bf16[32,2944]{1,0:T(8,128)(2,1)}, bf16[1...) custom-call(bf16[128,1728]{1,0:T(8,128)(2,1)} %bitcast.7, bf16[128,1152]{1,0:T(8,128)(2,1)} %bitcast.11, ...), custom_call_target="tpu_custom_call" | custom-call | tf_op jit(solution)/shard_map/pallas_call | solution.py:39
  8.5 1.6 %collective-permute-start.1 = (bf16[32,2944]{1,0:T(8,128)(2,1)}, bf16[32,2944]{1,0:T(8,128)(2,1)S(1)}, u32[]{:S(2)}, u32[]{:S(2)}) collective-permute-start(bf16[32,2944]{1,0:T(8,128)(2,1)} %get-tuple-element.34), channel_id=1, source_target_pairs={{0,2},{1,3},{2,0},{3,1},{4,6},{5,7},{6,4},{7,5},{8,10},{9,11},{10,... | collective-permute-start | bytes 565256 | tf_op jit(solution)/shard_map/ppermute | solution.py:342
  10.1 2.6 %collective-permute-start.2 = (bf16[32,2944]{1,0:T(8,128)(2,1)}, bf16[32,2944]{1,0:T(8,128)(2,1)S(1)}, u32[]{:S(2)}, u32[]{:S(2)}) collective-permute-start(bf16[32,2944]{1,0:T(8,128)(2,1)} %get-tuple-element.35), channel_id=1, source_target_pairs={{0,4},{1,5},{2,6},{3,7},{4,0},{5,1},{6,2},{7,3},{8,12},{9,13},{10,... | collective-permute-start | bytes 565256 | tf_op jit(solution)/shard_map/ppermute | solution.py:342
  12.7 0.2 collective-permute-start.3
  12.9 3.1 %collective-permute-done.got.refs_1_ = bf16[432,1152]{1,0:T(8,128)(2,1)S(1)} collective-permute-done((bf16[432,1152]{1,0:T(8,128)(2,1)}, bf16[432,1152]{1,0:T(8,128)(2,1)S(1)}, u32[]{:S(2)}, u32[]{:S(2)}) %collective-permute-start) | collective-permute-done | bytes 995360 | tf_op jit(solution)/shard_map/ppermute | solution.py:354
  16.1 0.9 %copy-done.6 = bf16[32,2944]{1,0:T(8,128)(2,1)S(1)} copy-done((bf16[32,2944]{1,0:T(8,128)(2,1)S(1)}, bf16[32,2944]{1,0:T(8,128)(2,1)}, u32[]{:S(2)}) %copy-start.6) | copy-done | bytes 188440
  17.1 2.1 %collective-permute-start.6 = (bf16[216,1152]{1,0:T(8,128)(2,1)S(1)}, bf16[216,1152]{1,0:T(8,128)(2,1)S(1)}, u32[]{:S(2)}, u32[]{:S(2)}) collective-permute-start(bf16[216,1152]{1,0:T(8,128)(2,1)S(1)} %get-tuple-element.37), channel_id=1, source_target_pairs={{0,16},{1,9},{2,18},{3,11},{4,20},{5,13},{6,22},{7,15},{8,24},{9,1... | collective-permute-start | bytes 1493000 | tf_op jit(solution)/shard_map/ppermute | solution.py:354
  19.2 7.7 %collective-permute-done.2.refs_2_ = bf16[32,2944]{1,0:T(8,128)(2,1)S(1)} collective-permute-done((bf16[32,2944]{1,0:T(8,128)(2,1)}, bf16[32,2944]{1,0:T(8,128)(2,1)S(1)}, u32[]{:S(2)}, u32[]{:S(2)}) %collective-permute-start.2) | collective-permute-done | bytes 188448 | tf_op jit(solution)/shard_map/ppermute | solution.py:342
  27.1 0.5 collective-permute-start.7
  27.6 1.8 %collective-permute-done.4.far.refs_1_ = bf16[128,3200]{1,0:T(8,128)(2,1)S(1)} collective-permute-done((bf16[128,3200]{1,0:T(8,128)(2,1)S(1)}, bf16[128,3200]{1,0:T(8,128)(2,1)S(1)}, u32[]{:S(2)}, u32[]{:S(2)}) %collective-permute-start.4) | collective-permute-done | bytes 819232 | tf_op jit(solution)/shard_map/ppermute | solution.py:342
  29.4 0.7 collective-permute-done.7.refs_4_
  30.1 7.2 %shard_map.104.mine = bf16[128,1728]{1,0:T(8,128)(2,1)S(1)} custom-call(bf16[128,3200]{1,0:T(8,128)(2,1)S(1)} %shard_map.103.near.refs_0_, bf16[128,3200]{1,0:T(8,128)(2,1)S(1)} %collective-permute-done.4.far.refs_1_, bf16[576,1152]{1,0:T(8,128)(2,1)S(1)} %copy-done, bf16[432,1152]{1,0:T(8,128)(2,1)S(1)} %bitcast.10, ...), custom_call_target="tpu_custom_call" | custom-call | tf_op jit(solution)/shard_map/pallas_call | solution.py:39
  37.4 0.2 collective-permute-start.8
  37.6 1.7 %collective-permute-done.8.other = bf16[128,1728]{1,0:T(8,128)(2,1)S(1)} collective-permute-done((bf16[128,1728]{1,0:T(8,128)(2,1)S(1)}, bf16[128,1728]{1,0:T(8,128)(2,1)S(1)}, u32[]{:S(2)}, u32[]{:S(2)}) %collective-permute-start.8) | collective-permute-done | bytes 442400 | tf_op jit(solution)/shard_map/ppermute | solution.py:342
  39.2 2.9 %shard_map.105 = (bf16[32,1728]{1,0:T(8,128)(2,1)S(1)}, bf16[32,1728]{1,0:T(8,128)(2,1)S(1)}, bf16[32,1728]{1,0:T(8,128)(2,1)S(1)}, bf16[32,1728]{1,0:T(8,128)(2...) custom-call(bf16[128,1728]{1,0:T(8,128)(2,1)S(1)} %shard_map.104.mine, ...), custom_call_target="tpu_custom_call" | custom-call | tf_op jit(solution)/shard_map/pallas_call | solution.py:39
  42.1 0.5 collective-permute-start.12
  42.7 1.6 %collective-permute-start.13 = (bf16[2,72,1152]{2,1,0:T(8,128)(2,1)S(1)}, bf16[2,72,1152]{2,1,0:T(8,128)(2,1)S(1)}, u32[]{:S(2)}, u32[]{:S(2)}) collective-permute-start(bf16[2,72,1152]{2,1,0:T(8,128)(2,1)S(1)} %get-tuple-element.49), channel_id=1, source_target_pairs={{0,16},{8,24},{16,0},{24,8},{1,17},{9,25},{17,1},{25,9},{2,18},{10... | collective-permute-start | bytes 995336 | tf_op jit(solution)/shard_map/ppermute | solution.py:342
  44.3 2.9 %collective-permute-start.9 = (bf16[32,1728]{1,0:T(8,128)(2,1)S(1)}, bf16[32,1728]{1,0:T(8,128)(2,1)S(1)}, u32[]{:S(2)}, u32[]{:S(2)}) collective-permute-start(bf16[32,1728]{1,0:T(8,128)(2,1)S(1)} %get-tuple-element.39), channel_id=1, source_target_pairs={{0,2},{1,3},{2,0},{3,1},{4,6},{5,7},{6,4},{7,5},{8,10},{9,11},{10,... | collective-permute-start | bytes 331784 | tf_op jit(solution)/shard_map/ppermute | solution.py:342
  47.1 2.9 %collective-permute-done.9.refs_1_._ = bf16[32,1728]{1,0:T(8,128)(2,1)S(1)} collective-permute-done((bf16[32,1728]{1,0:T(8,128)(2,1)S(1)}, bf16[32,1728]{1,0:T(8,128)(2,1)S(1)}, u32[]{:S(2)}, u32[]{:S(2)}) %collective-permute-start.9) | collective-permute-done | bytes 110624 | tf_op jit(solution)/shard_map/ppermute | solution.py:342
  50.0 2.0 %collective-permute-done.12.got_x = bf16[2,72,1152]{2,1,0:T(8,128)(2,1)S(1)} collective-permute-done((bf16[2,72,1152]{2,1,0:T(8,128)(2,1)S(1)}, bf16[2,72,1152]{2,1,0:T(8,128)(2,1)S(1)}, u32[]{:S(2)}, u32[]{:S(2)}) %collective-permute-start.12) | collective-permute-done | bytes 331808 | tf_op jit(solution)/shard_map/ppermute | solution.py:342
  52.4 1.7 %collective-permute-start.14 = (bf16[72,1152]{1,0:T(8,128)(2,1)S(1)}, bf16[72,1152]{1,0:T(8,128)(2,1)S(1)}, u32[]{:S(2)}, u32[]{:S(2)}) collective-permute-start(bf16[72,1152]{1,0:T(8,128)(2,1)S(1)} %get-tuple-element.51), channel_id=1, source_target_pairs={{0,16},{8,24},{16,0},{24,8},{1,17},{9,25},{17,1},{25,9},{2,18},{10... | collective-permute-start | bytes 497672 | tf_op jit(solution)/shard_map/ppermute | solution.py:342
  54.1 0.8 %collective-permute-start.15 = (bf16[72,1152]{1,0:T(8,128)(2,1)S(1)}, bf16[72,1152]{1,0:T(8,128)(2,1)S(1)}, u32[]{:S(2)}, u32[]{:S(2)}) collective-permute-start(bf16[72,1152]{1,0:T(8,128)(2,1)S(1)} %get-tuple-element.52), channel_id=1, source_target_pairs={{0,8},{8,0},{16,24},{24,16},{1,9},{9,1},{17,25},{25,17},{2,10},{10... | collective-permute-start | bytes 497672 | tf_op jit(solution)/shard_map/ppermute | solution.py:342
  54.8 3.6 %collective-permute-start.10 = (bf16[32,1728]{1,0:T(8,128)(2,1)S(1)}, bf16[32,1728]{1,0:T(8,128)(2,1)S(1)}, u32[]{:S(2)}, u32[]{:S(2)}) collective-permute-start(bf16[32,1728]{1,0:T(8,128)(2,1)S(1)} %get-tuple-element.40), channel_id=1, source_target_pairs={{0,4},{1,5},{2,6},{3,7},{4,0},{5,1},{6,2},{7,3},{8,12},{9,13},{10,... | collective-permute-start | bytes 331784 | tf_op jit(solution)/shard_map/ppermute | solution.py:342
  58.4 1.3 %collective-permute-start.11 = (bf16[32,1728]{1,0:T(8,128)(2,1)S(1)}, bf16[32,1728]{1,0:T(8,128)(2,1)S(1)}, u32[]{:S(2)}, u32[]{:S(2)}) collective-permute-start(bf16[32,1728]{1,0:T(8,128)(2,1)S(1)} %get-tuple-element.41), channel_id=1, source_target_pairs={{0,6},{1,7},{2,4},{3,5},{4,2},{5,3},{6,0},{7,1},{8,14},{9,15},{10,... | collective-permute-start | bytes 331784 | tf_op jit(solution)/shard_map/ppermute | solution.py:342
  60.0 2.5 %collective-permute-start.16 = (bf16[72,576]{1,0:T(8,128)(2,1)S(1)}, bf16[72,576]{1,0:T(8,128)(2,1)S(1)}, u32[]{:S(2)}, u32[]{:S(2)}) collective-permute-start(bf16[72,576]{1,0:T(8,128)(2,1)S(1)} %get-tuple-element.54), channel_id=1, source_target_pairs={{0,2},{1,3},{2,0},{3,1},{4,6},{5,7},{6,4},{7,5},{8,10},{9,11},{10,... | collective-permute-start | bytes 248840 | tf_op jit(solution)/shard_map/ppermute | solution.py:342
  62.5 1.1 %collective-permute-start.17 = (bf16[72,576]{1,0:T(8,128)(2,1)S(1)}, bf16[72,576]{1,0:T(8,128)(2,1)S(1)}, u32[]{:S(2)}, u32[]{:S(2)}) collective-permute-start(bf16[72,576]{1,0:T(8,128)(2,1)S(1)} %get-tuple-element.55), channel_id=1, source_target_pairs={{0,4},{1,5},{2,6},{3,7},{4,0},{5,1},{6,2},{7,3},{8,12},{9,13},{10,... | collective-permute-start | bytes 248840 | tf_op jit(solution)/shard_map/ppermute | solution.py:342
  63.6 1.4 %collective-permute-start.18 = (bf16[72,576]{1,0:T(8,128)(2,1)S(1)}, bf16[72,576]{1,0:T(8,128)(2,1)S(1)}, u32[]{:S(2)}, u32[]{:S(2)}) collective-permute-start(bf16[72,576]{1,0:T(8,128)(2,1)S(1)} %get-tuple-element.56), channel_id=1, source_target_pairs={{0,6},{1,7},{2,4},{3,5},{4,2},{5,3},{6,0},{7,1},{8,14},{9,15},{10,... | collective-permute-start | bytes 248840 | tf_op jit(solution)/shard_map/ppermute | solution.py:342
  65.0 2.8 %collective-permute-done.10.refs_2_ = bf16[32,1728]{1,0:T(8,128)(2,1)S(1)} collective-permute-done((bf16[32,1728]{1,0:T(8,128)(2,1)S(1)}, bf16[32,1728]{1,0:T(8,128)(2,1)S(1)}, u32[]{:S(2)}, u32[]{:S(2)}) %collective-permute-start.10) | collective-permute-done | bytes 110624 | tf_op jit(solution)/shard_map/ppermute | solution.py:342
  67.8 3.9 %shard_map.106 = (bf16[128,1152]{1,0:T(8,128)(2,1)}, bf16[128,1152]{1,0:T(8,128)(2,1)}, bf16[128,1728]{1,0:T(8,128)(2,1)}) custom-call(bf16[32,1728]{1,0:T(8,128)(2,1)S(1)} %get-tuple-element.38.refs_0_, bf16[32,1728]{1,0:T(8,128)(2,1)S(1)} %collective-permute-done.9.refs_1_._, bf16[32,1728]{1,0:T(8,128)(2,1)S(1)} %collective-permute-done.10.refs_2_, ...), custom_call_target="tpu_custom_call" | custom-call | tf_op jit(solution)/shard_map/pallas_call | solution.py:39
  71.8 2.8 %collective-permute-done.17.refs_1_ = bf16[72,576]{1,0:T(8,128)(2,1)S(1)} collective-permute-done((bf16[72,576]{1,0:T(8,128)(2,1)S(1)}, bf16[72,576]{1,0:T(8,128)(2,1)S(1)}, u32[]{:S(2)}, u32[]{:S(2)}) %collective-permute-start.17) | collective-permute-done | bytes 82976 | tf_op jit(solution)/shard_map/ppermute | solution.py:342
  74.6 0.8 %shard_map.109 = (f32[72,288]{1,0:T(8,128)}, f32[72,288]{1,0:T(8,128)}) custom-call(f32[72,576]{1,0:T(8,128)S(1)} %get-tuple-element.53.own, bf16[72,576]{1,0:T(8,128)(2,1)S(1)} %collective-permute-done.16.refs_0_, bf16[72,576]{1,0:T(8,128)(2,1)S(1)} %collective-permute-done.17.refs_1_, bf16[72,576]{1,0:T(8,128)(2,1)S(1)} %collective-permute-done.18.refs_2_), custom_call_target="tpu_custom_call" | custom-call | tf_op jit(solution)/shard_map/pallas_call | solution.py:39
  (29 shorter events, 0.8 us)
Async XLA Ops:
  0.6 15.4 %collective-permute-start = (bf16[432,1152]{1,0:T(8,128)(2,1)}, bf16[432,1152]{1,0:T(8,128)(2,1)S(1)}, u32[]{:S(2)}, u32[]{:S(2)}) collective-permute-start(bf16[432,1152]{1,0:T(8,128)(2,1)} %bitcast.9), channel_id=1, source_target_pairs={{0,8},{1,17},{2,10},{3,19},{4,12},{5,21},{6,14},{7,23},{8,0},{9,25... | collective-permute-start | bytes 2985992 | tf_op jit(solution)/shard_map/ppermute | solution.py:354
  8.5 10.8 %collective-permute-start.1 = (bf16[32,2944]{1,0:T(8,128)(2,1)}, bf16[32,2944]{1,0:T(8,128)(2,1)S(1)}, u32[]{:S(2)}, u32[]{:S(2)}) collective-permute-start(bf16[32,2944]{1,0:T(8,128)(2,1)} %get-tuple-element.34), channel_id=1, source_target_pairs={{0,2},{1,3},{2,0},{3,1},{4,6},{5,7},{6,4},{7,5},{8,10},{9,11},{10,... | collective-permute-start | bytes 565256 | tf_op jit(solution)/shard_map/ppermute | solution.py:342
  10.1 16.9 %collective-permute-start.2 = (bf16[32,2944]{1,0:T(8,128)(2,1)}, bf16[32,2944]{1,0:T(8,128)(2,1)S(1)}, u32[]{:S(2)}, u32[]{:S(2)}) collective-permute-start(bf16[32,2944]{1,0:T(8,128)(2,1)} %get-tuple-element.35), channel_id=1, source_target_pairs={{0,4},{1,5},{2,6},{3,7},{4,0},{5,1},{6,2},{7,3},{8,12},{9,13},{10,... | collective-permute-start | bytes 565256 | tf_op jit(solution)/shard_map/ppermute | solution.py:342
  12.7 14.3 %collective-permute-start.3 = (bf16[32,2944]{1,0:T(8,128)(2,1)}, bf16[32,2944]{1,0:T(8,128)(2,1)S(1)}, u32[]{:S(2)}, u32[]{:S(2)}) collective-permute-start(bf16[32,2944]{1,0:T(8,128)(2,1)} %get-tuple-element.36), channel_id=1, source_target_pairs={{0,6},{1,7},{2,4},{3,5},{4,2},{5,3},{6,0},{7,1},{8,14},{9,15},{10,... | collective-permute-start | bytes 565256 | tf_op jit(solution)/shard_map/ppermute | solution.py:342
  16.1 0.9 %copy-start.6 = (bf16[32,2944]{1,0:T(8,128)(2,1)S(1)}, bf16[32,2944]{1,0:T(8,128)(2,1)}, u32[]{:S(2)}) copy-start(bf16[32,2944]{1,0:T(8,128)(2,1)} %get-tuple-element.32.own) | copy-start | bytes 565252
  17.0 13.1 %copy-start = (bf16[576,1152]{1,0:T(8,128)(2,1)S(1)}, bf16[576,1152]{1,0:T(8,128)(2,1)}, u32[]{:S(2)}) copy-start(bf16[576,1152]{1,0:T(8,128)(2,1)} %refs_7_.1) | copy-start | bytes 3981316
  17.0 13.1 %copy-start.3 = (bf16[1152,432]{0,1:T(8,128)(2,1)S(1)}, bf16[1152,432]{0,1:T(8,128)(2,1)}, u32[]{:S(2)}) copy-start(bf16[1152,432]{0,1:T(8,128)(2,1)} %param.9) | copy-start | bytes 2985988
  17.1 10.0 %collective-permute-start.6 = (bf16[216,1152]{1,0:T(8,128)(2,1)S(1)}, bf16[216,1152]{1,0:T(8,128)(2,1)S(1)}, u32[]{:S(2)}, u32[]{:S(2)}) collective-permute-start(bf16[216,1152]{1,0:T(8,128)(2,1)S(1)} %get-tuple-element.37), channel_id=1, source_target_pairs={{0,16},{1,9},{2,18},{3,11},{4,20},{5,13},{6,22},{7,15},{8,24},{9,1... | collective-permute-start | bytes 1493000 | tf_op jit(solution)/shard_map/ppermute | solution.py:354
  19.2 10.2 %collective-permute-start.5 = (bf16[432,1152]{1,0:T(8,128)(2,1)S(1)}, bf16[432,1152]{1,0:T(8,128)(2,1)S(1)}, u32[]{:S(2)}, u32[]{:S(2)}) collective-permute-start(bf16[432,1152]{1,0:T(8,128)(2,1)S(1)} %collective-permute-done.got.refs_1_), channel_id=1, source_target_pairs={{0,1},{1,0},{2,3},{3,2},{4,5},{5,4},{6,7},{7,6},{8,9},{9,8},{10,11... | collective-permute-start | bytes 2985992 | tf_op jit(solution)/shard_map/ppermute | solution.py:342
  27.0 2.4 %collective-permute-start.4 = (bf16[128,3200]{1,0:T(8,128)(2,1)S(1)}, bf16[128,3200]{1,0:T(8,128)(2,1)S(1)}, u32[]{:S(2)}, u32[]{:S(2)}) collective-permute-start(bf16[128,3200]{1,0:T(8,128)(2,1)S(1)} %shard_map.103.near.refs_0_), channel_id=1, source_target_pairs={{0,1},{1,0},{2,3},{3,2},{4,5},{5,4},{6,7},{7,6},{8,9},{9,8},{10,11... | collective-permute-start | bytes 2457608 | tf_op jit(solution)/shard_map/ppermute | solution.py:342
  27.1 3.0 %collective-permute-start.7 = (bf16[216,1152]{1,0:T(8,128)(2,1)S(1)}, bf16[216,1152]{1,0:T(8,128)(2,1)S(1)}, u32[]{:S(2)}, u32[]{:S(2)}) collective-permute-start(bf16[216,1152]{1,0:T(8,128)(2,1)S(1)} %collective-permute-done.6.refs_3_), channel_id=1, source_target_pairs={{0,1},{1,0},{2,3},{3,2},{4,5},{5,4},{6,7},{7,6},{8,9},{9,8},{10,11... | collective-permute-start | bytes 1493000 | tf_op jit(solution)/shard_map/ppermute | solution.py:342
  37.4 1.9 %collective-permute-start.8 = (bf16[128,1728]{1,0:T(8,128)(2,1)S(1)}, bf16[128,1728]{1,0:T(8,128)(2,1)S(1)}, u32[]{:S(2)}, u32[]{:S(2)}) collective-permute-start(bf16[128,1728]{1,0:T(8,128)(2,1)S(1)} %shard_map.104.mine), channel_id=1, source_target_pairs={{0,1},{1,0},{2,3},{3,2},{4,5},{5,4},{6,7},{7,6},{8,9},{9,8},{10,11... | collective-permute-start | bytes 1327112 | tf_op jit(solution)/shard_map/ppermute | solution.py:342
  42.1 9.9 %collective-permute-start.12 = (bf16[2,72,1152]{2,1,0:T(8,128)(2,1)S(1)}, bf16[2,72,1152]{2,1,0:T(8,128)(2,1)S(1)}, u32[]{:S(2)}, u32[]{:S(2)}) collective-permute-start(bf16[2,72,1152]{2,1,0:T(8,128)(2,1)S(1)} %get-tuple-element.48), channel_id=1, source_target_pairs={{0,8},{8,0},{16,24},{24,16},{1,9},{9,1},{17,25},{25,17},{2,10},{10... | collective-permute-start | bytes 995336 | tf_op jit(solution)/shard_map/ppermute | solution.py:342
  42.7 9.6 %collective-permute-start.13 = (bf16[2,72,1152]{2,1,0:T(8,128)(2,1)S(1)}, bf16[2,72,1152]{2,1,0:T(8,128)(2,1)S(1)}, u32[]{:S(2)}, u32[]{:S(2)}) collective-permute-start(bf16[2,72,1152]{2,1,0:T(8,128)(2,1)S(1)} %get-tuple-element.49), channel_id=1, source_target_pairs={{0,16},{8,24},{16,0},{24,8},{1,17},{9,25},{17,1},{25,9},{2,18},{10... | collective-permute-start | bytes 995336 | tf_op jit(solution)/shard_map/ppermute | solution.py:342
  44.3 5.7 %collective-permute-start.9 = (bf16[32,1728]{1,0:T(8,128)(2,1)S(1)}, bf16[32,1728]{1,0:T(8,128)(2,1)S(1)}, u32[]{:S(2)}, u32[]{:S(2)}) collective-permute-start(bf16[32,1728]{1,0:T(8,128)(2,1)S(1)} %get-tuple-element.39), channel_id=1, source_target_pairs={{0,2},{1,3},{2,0},{3,1},{4,6},{5,7},{6,4},{7,5},{8,10},{9,11},{10,... | collective-permute-start | bytes 331784 | tf_op jit(solution)/shard_map/ppermute | solution.py:342
  52.2 15.6 %copy-start.1 = (bf16[576,1152]{1,0:T(8,128)(2,1)S(1)}, bf16[576,1152]{1,0:T(8,128)(2,1)}, u32[]{:S(2)}) copy-start(bf16[576,1152]{1,0:T(8,128)(2,1)} %refs_4_.1) | copy-start | bytes 3981316
  52.2 15.6 %copy-start.2 = (bf16[2,64,1728]{2,1,0:T(8,128)(2,1)S(1)}, bf16[2,64,1728]{2,1,0:T(8,128)(2,1)}, u32[]{:S(2)}) copy-start(bf16[2,64,1728]{2,1,0:T(8,128)(2,1)} %param.7) | copy-start | bytes 1327108
  52.2 15.6 %copy-start.4 = (f32[8,128,128]{2,1,0:T(8,128)S(1)}, f32[8,128,128]{2,1,0:T(8,128)}, u32[]{:S(2)}) copy-start(f32[8,128,128]{2,1,0:T(8,128)} %get-tuple-element.42.refs_6_) | copy-start | bytes 1572868
  52.2 15.6 %copy-start.5 = (bf16[128,1152]{1,0:T(8,128)(2,1)S(1)}, bf16[128,1152]{1,0:T(8,128)(2,1)}, u32[]{:S(2)}) copy-start(bf16[128,1152]{1,0:T(8,128)(2,1)} %get-tuple-element.43.refs_8_) | copy-start | bytes 884740
  52.4 7.4 %collective-permute-start.14 = (bf16[72,1152]{1,0:T(8,128)(2,1)S(1)}, bf16[72,1152]{1,0:T(8,128)(2,1)S(1)}, u32[]{:S(2)}, u32[]{:S(2)}) collective-permute-start(bf16[72,1152]{1,0:T(8,128)(2,1)S(1)} %get-tuple-element.51), channel_id=1, source_target_pairs={{0,16},{8,24},{16,0},{24,8},{1,17},{9,25},{17,1},{25,9},{2,18},{10... | collective-permute-start | bytes 497672 | tf_op jit(solution)/shard_map/ppermute | solution.py:342
  54.1 5.7 %collective-permute-start.15 = (bf16[72,1152]{1,0:T(8,128)(2,1)S(1)}, bf16[72,1152]{1,0:T(8,128)(2,1)S(1)}, u32[]{:S(2)}, u32[]{:S(2)}) collective-permute-start(bf16[72,1152]{1,0:T(8,128)(2,1)S(1)} %get-tuple-element.52), channel_id=1, source_target_pairs={{0,8},{8,0},{16,24},{24,16},{1,9},{9,1},{17,25},{25,17},{2,10},{10... | collective-permute-start | bytes 497672 | tf_op jit(solution)/shard_map/ppermute | solution.py:342
  54.8 13.0 %collective-permute-start.10 = (bf16[32,1728]{1,0:T(8,128)(2,1)S(1)}, bf16[32,1728]{1,0:T(8,128)(2,1)S(1)}, u32[]{:S(2)}, u32[]{:S(2)}) collective-permute-start(bf16[32,1728]{1,0:T(8,128)(2,1)S(1)} %get-tuple-element.40), channel_id=1, source_target_pairs={{0,4},{1,5},{2,6},{3,7},{4,0},{5,1},{6,2},{7,3},{8,12},{9,13},{10,... | collective-permute-start | bytes 331784 | tf_op jit(solution)/shard_map/ppermute | solution.py:342
  58.4 9.4 %collective-permute-start.11 = (bf16[32,1728]{1,0:T(8,128)(2,1)S(1)}, bf16[32,1728]{1,0:T(8,128)(2,1)S(1)}, u32[]{:S(2)}, u32[]{:S(2)}) collective-permute-start(bf16[32,1728]{1,0:T(8,128)(2,1)S(1)} %get-tuple-element.41), channel_id=1, source_target_pairs={{0,6},{1,7},{2,4},{3,5},{4,2},{5,3},{6,0},{7,1},{8,14},{9,15},{10,... | collective-permute-start | bytes 331784 | tf_op jit(solution)/shard_map/ppermute | solution.py:342
  60.0 11.8 %collective-permute-start.16 = (bf16[72,576]{1,0:T(8,128)(2,1)S(1)}, bf16[72,576]{1,0:T(8,128)(2,1)S(1)}, u32[]{:S(2)}, u32[]{:S(2)}) collective-permute-start(bf16[72,576]{1,0:T(8,128)(2,1)S(1)} %get-tuple-element.54), channel_id=1, source_target_pairs={{0,2},{1,3},{2,0},{3,1},{4,6},{5,7},{6,4},{7,5},{8,10},{9,11},{10,... | collective-permute-start | bytes 248840 | tf_op jit(solution)/shard_map/ppermute | solution.py:342
  62.5 12.1 %collective-permute-start.17 = (bf16[72,576]{1,0:T(8,128)(2,1)S(1)}, bf16[72,576]{1,0:T(8,128)(2,1)S(1)}, u32[]{:S(2)}, u32[]{:S(2)}) collective-permute-start(bf16[72,576]{1,0:T(8,128)(2,1)S(1)} %get-tuple-element.55), channel_id=1, source_target_pairs={{0,4},{1,5},{2,6},{3,7},{4,0},{5,1},{6,2},{7,3},{8,12},{9,13},{10,... | collective-permute-start | bytes 248840 | tf_op jit(solution)/shard_map/ppermute | solution.py:342
  63.6 11.0 %collective-permute-start.18 = (bf16[72,576]{1,0:T(8,128)(2,1)S(1)}, bf16[72,576]{1,0:T(8,128)(2,1)S(1)}, u32[]{:S(2)}, u32[]{:S(2)}) collective-permute-start(bf16[72,576]{1,0:T(8,128)(2,1)S(1)} %get-tuple-element.56), channel_id=1, source_target_pairs={{0,6},{1,7},{2,4},{3,5},{4,2},{5,3},{6,0},{7,1},{8,14},{9,15},{10,... | collective-permute-start | bytes 248840 | tf_op jit(solution)/shard_map/ppermute | solution.py:342

commit v10 on v9

--- a/solution.py
+++ b/solution.py
@@ -204,7 +204,7 @@
 def temporal_kernel(shards, chips, group, near, far, wot, *refs):
     idx = place(chips)
     weights, refs = refs[: len(shards)], refs[len(shards) :]
-    mine, cot, q, k, v, g, p_ref, blocks = refs
+    (mine, *outs), (cot, q, k, v, g, p_ref, blocks) = refs[:chips], refs[chips:]
     inner, width = wot.shape
     heads = inner // DH
     value = [own_patches(ref, idx[1], 2 * group) for ref in (near, far)]
@@ -231,32 +231,38 @@
         lhs = jnp.concatenate([blocks[block] for block in at(idx)], axis=1)
         grad += dot(lhs, w[...])
     mine[:, :width] = (cot[...].astype(F32) + grad.astype(BF16).astype(F32)).astype(BF16)
-
-
-def whole_return_kernel(chips, block, inner, width, mine, other, *refs):
+    half = mine.shape[0] // 2
+    rows = half // chips
+    for q, out in enumerate(outs, 1):
+        out[:rows] = mine[q * rows : (q + 1) * rows]
+        out[rows:] = mine[half + q * rows : half + (q + 1) * rows]
+
+
+def others_kernel(mine, *refs):
+    parts, out = refs[:-1], refs[-1]
+    half = mine.shape[0] // 2
+    rows = half // (1 + len(parts))
+    out[:rows] = mine[half : half + rows]
+    for q, part in enumerate(parts, 1):
+        out[q * rows : (q + 1) * rows] = part[rows:]
+
+
+def whole_parts_kernel(chips, block, inner, width, mine, other, *refs):
     idx = place(chips)
-    held, outs, part = refs[0], refs[1 : 1 + chips], refs[1 + chips]
+    held, part = refs
     cot, so = held[:, width : 2 * width], held[:, 2 * width : 2 * width + inner]
     half = mine.shape[0] // 2
     near = all_patches(mine[:half], other[half:], idx[1], block)
-    for q, out in enumerate(outs):
-        out[...] = near[q * out.shape[0] : (q + 1) * out.shape[0]]
     part[0] = dot_at(near[:, width:], cot).astype(BF16)
     part[1] = dot_at(so, near[:, :width]).astype(BF16)
 
 
-def return_kernel(chips, block, inner, width, mine, other, *refs):
+def parts_kernel(chips, block, inner, width, mine, other, *refs):
     idx = place(chips)
     sent, refs = refs[:2], refs[2:]
-    outs, (keep, send_x, send_y, heads, cols, kept, sem) = refs[:chips], refs[chips:]
+    keep, send_x, send_y, heads, cols = refs
     half = mine.shape[0] // 2
     near = all_patches(mine[:half], other[half:], idx[1], block)
-    rows = kept.shape[0]
-    kept[...] = near[:rows]
-    copy = pltpu.make_async_copy(kept, outs[0], sem.at[0])
-    copy.start()
-    for q in range(1, chips):
-        outs[q][...] = near[q * rows : (q + 1) * rows]
     far = all_patches(mine[half:], other[:half], idx[1], block)
     rows = near.shape[0]
     size = heads.shape[2]
@@ -283,10 +289,9 @@
                 (send_x, send_y)[i][r // 2 if i == 0 else r - 2] = value.astype(BF16)
             else:
                 keep[2 * i + (r > 0)] = value
-    copy.wait()
-
-
-def sum_first_kernel(keep, got_x, got_y, _, own, send_y, send_x):
+
+
+def sum_first_kernel(keep, got_x, got_y, own, send_y, send_x):
     for i, (got, send) in enumerate(((got_x, send_y), (got_y, send_x))):
         own[i] = keep[2 * i] + got[0].astype(F32)
         send[...] = (keep[2 * i + 1] + got[1].astype(F32)).astype(BF16)
@@ -312,15 +317,18 @@
 
 def last_kernel(chips, patches, *refs):
     idx = place(chips)
-    held, (wos, qkv, p_ref, wot, hid), refs = refs[:chips], refs[chips : chips + 5], refs[chips + 5 :]
+    held, got, refs = refs[:chips], refs[chips], refs[chips + 1 :]
+    (wos, qkv, p_ref, wot, hid), refs = refs[:5], refs[5:]
     block_far, out_far, grads_far, rows, block_out, grads, qs, ks, vs, gs, sems = refs
     inner, width = wos.shape
     frames = rows.shape[0] // patches
     block = patches // chips
+    each = frames * block // 2
     for q in range(chips):
+        value = all_patches(held[q][:each], got[q * each : (q + 1) * each], idx[1], block)
         for f in range(frames):
             low = pl.multiple_of(f * patches + (idx[2] ^ q) * block, block)
-            rows[pl.ds(low, block)] = held[q][f * block : (f + 1) * block]
+            rows[pl.ds(low, block)] = value[f * block : (f + 1) * block]
     value = rows[...]
     grad, attended = value[:, :width], value[:, width:]
     stores = started([(rows.at[:, pl.ds(0, width)], out_far)], sems.at[pl.ds(0, 1)])
@@ -391,13 +399,13 @@
     return [parts[0]] + [flip(parts[q], "seq", 2 * q) for q in range(1, len(parts))]
 
 
-def reduced(keep, send_x, send_y, after):
+def reduced(keep, send_x, send_y):
     _, size, width = keep.shape
     step = shape((size, width))
     own, send_t, send_s = call(
         sum_first_kernel,
         [shape((2, size, width), F32), step, step],
-        [keep, flip(send_x, "dp", 1), flip(send_y, "dp", 2), after],
+        [keep, flip(send_x, "dp", 1), flip(send_y, "dp", 2)],
         small=True,
     )
     n = lax.axis_size("seq") // 2
@@ -447,50 +455,47 @@
     )
     near, far, weights, places, count = gather(w_temporal.T, near, chips)
     blocks = pltpu.VMEM((count, rows, 3 * inner // count), BF16)
-    (mine,) = call(
+    mine, *back = call(
         functools.partial(temporal_kernel, places, chips, group),
-        [shape((rows, width + inner))],
+        [shape((rows, width + inner))] + [shape((per_chip, width + inner))] * (chips - 1),
         [near, far, wo_temporal, *weights],
         [held(width)] + [wide] * 4 + [attended, blocks],
         small=True,
     )
     other = flip(mine, "seq", 1)
-    back = [shape((per_chip, width + inner))] * chips
     if n_dp == 4 and n_seq == peers:
         size = inner // n_seq
-        *back, keep, send_x, send_y = call(
-            functools.partial(return_kernel, chips, block, inner, width),
-            back
-            + [shape((n_dp, size, width), F32)]
-            + [shape((2, size, width))] * 2,
+        keep, send_x, send_y = call(
+            functools.partial(parts_kernel, chips, block, inner, width),
+            [shape((n_dp, size, width), F32)] + [shape((2, size, width))] * 2,
             [mine, other, near, far],
             [
                 pltpu.VMEM((n_seq, 2 * rows, size), BF16),
                 pltpu.VMEM((n_dp, 2 * rows, width // n_dp), BF16),
-                pltpu.VMEM((per_chip, width + inner), BF16),
-                sems(1),
             ],
-            far_out=range(1),
             small=True,
         )
     else:
-        *back, both = call(
-            functools.partial(whole_return_kernel, chips, block, inner, width),
-            back + [shape((2, inner, width))],
+        (both,) = call(
+            functools.partial(whole_parts_kernel, chips, block, inner, width),
+            [shape((2, inner, width))],
             [mine, other, near],
             small=True,
         )
-    back = from_chips(back)
+    back = from_chips([mine, *back])
+    (others,) = call(
+        others_kernel, [shape((rows // 2, width + inner))], back, small=True
+    )
     block_out, tokens_grad, qkv_grad = call(
         functools.partial(last_kernel, chips, patches),
         [shape((rows, width)), shape((rows, width)), shape((rows, 3 * inner))],
-        [*back, wo_spatial, qkv_rows, spatial_p, wo_temporal, hidden],
+        [*back, flip(others, "seq", 1), wo_spatial, qkv_rows, spatial_p, wo_temporal, hidden],
         [held(width + inner), held(width), held(3 * inner)] + [wide] * 4 + [sems(3)],
         far_out=range(3),
         small=True,
     )
     if n_dp == 4 and n_seq == peers:
-        temporal_grad, spatial_grad = reduced(keep, send_x, send_y, back[1])
+        temporal_grad, spatial_grad = reduced(keep, send_x, send_y)
     else:
         both = lax.psum_scatter(both, "seq", scatter_dimension=1, tiled=True)
         both = lax.psum_scatter(both, "dp", scatter_dimension=2, tiled=True).astype(F32)

time: 75.5 us -> 71.8 us (0.951)
  starting transfers between devices: 27.7 us -> 25.7 us
  waiting for transfers between devices: 25.8 us -> 24.5 us
    ppermute x17 -> x18, starting transfers between devices: 22.6 us -> 20.6 us  [flip(): lax.ppermute(value, axis, [(i, i ^ bit) for i in range(lax.axis_size(axis...]
    ppermute x17 -> x18, waiting for transfers between devices: 22.7 us -> 21.4 us  [flip(): lax.ppermute(value, axis, [(i, i ^ bit) for i in range(lax.axis_size(axis...]
    pallas_call x9 -> x10, Pallas kernels: 20.1 us -> 19.8 us  [call(): pl.pallas_call(body, out_shape=outs, in_specs=[HBM if i in far_in else sp...]
  transfers between devices with their start and end apart: 19 -> 20, of which waited for: 10 -> 10; matrix products, arithmetic and copies ran while one was open for 0% -> 0% of each run, Pallas kernels for 12% -> 13%
where the time goes in v10:
time: 71.8 us; the launch traced here: 71.7 us
  starting transfers between devices  25.7 us (36%)
  waiting for transfers between devices  24.5 us (34%)
  Pallas kernels  19.8 us (28%)
  local copies, waits for them, and re-layouts  0.95 us (1%)
  between operations  0.78 us (1%)
    ppermute x18, waiting for transfers between devices, flip(): lax.ppermute(value, axis, [(i, i ^ bit) for i in range(lax.axis_size(axis...  21.4 us
    ppermute x18, starting transfers between devices, flip(): lax.ppermute(value, axis, [(i, i ^ bit) for i in range(lax.axis_size(axis...  20.6 us
    pallas_call x10, Pallas kernels, call(): pl.pallas_call(body, out_shape=outs, in_specs=[HBM if i in far_in else sp...  19.8 us
    ppermute x2, starting transfers between devices, across(): return lax.ppermute(value, ('dp', 'seq'), pairs)  5.12 us
    ppermute x2, waiting for transfers between devices, across(): return lax.ppermute(value, ('dp', 'seq'), pairs)  3.14 us
  transfers between devices with their start and end apart: 20, of which 10 were waited for; matrix products, arithmetic and copies ran while one was open for 0% of the time, Pallas kernels for 13%

profile of v10, /device:TPU:0, one launch (start us, length us, event | category | flops | bytes accessed | tf_op | source)
XLA Modules:
  0.0 71.7 jit_solution(994545575708455225)
XLA Ops:
  0.6 3.0 %collective-permute-start = (bf16[432,1152]{1,0:T(8,128)(2,1)}, bf16[432,1152]{1,0:T(8,128)(2,1)S(1)}, u32[]{:S(2)}, u32[]{:S(2)}) collective-permute-start(bf16[432,1152]{1,0:T(8,128)(2,1)} %bitcast.9), channel_id=1, source_target_pairs={{0,8},{1,17},{2,10},{3,19},{4,12},{5,21},{6,14},{7,23},{8,0},{9,25... | collective-permute-start | bytes 2985992 | tf_op jit(solution)/shard_map/ppermute | solution.py:362
  3.6 4.8 %shard_map.101 = (bf16[32,2944]{1,0:T(8,128)(2,1)}, bf16[32,2944]{1,0:T(8,128)(2,1)}, bf16[32,2944]{1,0:T(8,128)(2,1)}, bf16[32,2944]{1,0:T(8,128)(2,1)}, bf16[1...) custom-call(bf16[128,1728]{1,0:T(8,128)(2,1)} %bitcast.7, bf16[128,1152]{1,0:T(8,128)(2,1)} %bitcast.11, ...), custom_call_target="tpu_custom_call" | custom-call | tf_op jit(solution)/shard_map/pallas_call | solution.py:39
  8.5 1.6 %collective-permute-start.1 = (bf16[32,2944]{1,0:T(8,128)(2,1)}, bf16[32,2944]{1,0:T(8,128)(2,1)S(1)}, u32[]{:S(2)}, u32[]{:S(2)}) collective-permute-start(bf16[32,2944]{1,0:T(8,128)(2,1)} %get-tuple-element.34), channel_id=1, source_target_pairs={{0,2},{1,3},{2,0},{3,1},{4,6},{5,7},{6,4},{7,5},{8,10},{9,11},{10,... | collective-permute-start | bytes 565256 | tf_op jit(solution)/shard_map/ppermute | solution.py:350
  10.1 2.6 %collective-permute-start.2 = (bf16[32,2944]{1,0:T(8,128)(2,1)}, bf16[32,2944]{1,0:T(8,128)(2,1)S(1)}, u32[]{:S(2)}, u32[]{:S(2)}) collective-permute-start(bf16[32,2944]{1,0:T(8,128)(2,1)} %get-tuple-element.35), channel_id=1, source_target_pairs={{0,4},{1,5},{2,6},{3,7},{4,0},{5,1},{6,2},{7,3},{8,12},{9,13},{10,... | collective-permute-start | bytes 565256 | tf_op jit(solution)/shard_map/ppermute | solution.py:350
  12.7 0.2 collective-permute-start.3
  12.9 3.1 %collective-permute-done.got.refs_1_ = bf16[432,1152]{1,0:T(8,128)(2,1)S(1)} collective-permute-done((bf16[432,1152]{1,0:T(8,128)(2,1)}, bf16[432,1152]{1,0:T(8,128)(2,1)S(1)}, u32[]{:S(2)}, u32[]{:S(2)}) %collective-permute-start) | collective-permute-done | bytes 995360 | tf_op jit(solution)/shard_map/ppermute | solution.py:362
  16.1 0.9 %copy-done.6 = bf16[32,2944]{1,0:T(8,128)(2,1)S(1)} copy-done((bf16[32,2944]{1,0:T(8,128)(2,1)S(1)}, bf16[32,2944]{1,0:T(8,128)(2,1)}, u32[]{:S(2)}) %copy-start.6) | copy-done | bytes 188440
  17.1 2.1 %collective-permute-start.6 = (bf16[216,1152]{1,0:T(8,128)(2,1)S(1)}, bf16[216,1152]{1,0:T(8,128)(2,1)S(1)}, u32[]{:S(2)}, u32[]{:S(2)}) collective-permute-start(bf16[216,1152]{1,0:T(8,128)(2,1)S(1)} %get-tuple-element.37), channel_id=1, source_target_pairs={{0,16},{1,9},{2,18},{3,11},{4,20},{5,13},{6,22},{7,15},{8,24},{9,1... | collective-permute-start | bytes 1493000 | tf_op jit(solution)/shard_map/ppermute | solution.py:362
  19.2 7.7 %collective-permute-done.2.refs_2_ = bf16[32,2944]{1,0:T(8,128)(2,1)S(1)} collective-permute-done((bf16[32,2944]{1,0:T(8,128)(2,1)}, bf16[32,2944]{1,0:T(8,128)(2,1)S(1)}, u32[]{:S(2)}, u32[]{:S(2)}) %collective-permute-start.2) | collective-permute-done | bytes 188448 | tf_op jit(solution)/shard_map/ppermute | solution.py:350
  27.1 0.5 collective-permute-start.7
  27.6 1.8 %collective-permute-done.4.far.refs_1_ = bf16[128,3200]{1,0:T(8,128)(2,1)S(1)} collective-permute-done((bf16[128,3200]{1,0:T(8,128)(2,1)S(1)}, bf16[128,3200]{1,0:T(8,128)(2,1)S(1)}, u32[]{:S(2)}, u32[]{:S(2)}) %collective-permute-start.4) | collective-permute-done | bytes 819232 | tf_op jit(solution)/shard_map/ppermute | solution.py:350
  29.4 0.7 collective-permute-done.7.refs_4_
  30.1 7.3 %shard_map.104 = (bf16[128,1728]{1,0:T(8,128)(2,1)S(1)}, bf16[32,1728]{1,0:T(8,128)(2,1)S(1)}, bf16[32,1728]{1,0:T(8,128)(2,1)S(1)}, bf16[32,1728]{1,0:T(8,128)(2,1)S(1)}) custom-call(bf16[128,3200]{1,0:T(8,128)(2,1)S(1)} %shard_map.103.near.refs_0_, bf16[128,3200]{1,0:T(8,128)(2,1)S(1)} %collective-permute-done.4.far.refs_1_, ...), custom_call_target="tpu_custom_call" | custom-call | tf_op jit(solution)/shard_map/pallas_call | solution.py:39
  37.4 0.2 collective-permute-start.12
  37.6 1.7 %collective-permute-done.12.other = bf16[128,1728]{1,0:T(8,128)(2,1)S(1)} collective-permute-done((bf16[128,1728]{1,0:T(8,128)(2,1)S(1)}, bf16[128,1728]{1,0:T(8,128)(2,1)S(1)}, u32[]{:S(2)}, u32[]{:S(2)}) %collective-permute-start.12) | collective-permute-done | bytes 442400 | tf_op jit(solution)/shard_map/ppermute | solution.py:350
  39.3 2.4 %shard_map.107 = (f32[4,72,1152]{2,1,0:T(8,128)S(1)}, bf16[2,72,1152]{2,1,0:T(8,128)(2,1)S(1)}, bf16[2,72,1152]{2,1,0:T(8,128)(2,1)S(1)}) custom-call(bf16[128,1728]{1,0:T(8,128)(2,1)S(1)} %get-tuple-element.38.mine.refs_0_, bf16[128,1728]{1,0:T(8,128)(2,1)S(1)} %collective-permute-done.12.other, bf16[128,3200]{1,0:T(8,128)(2,1)S(1)} %shard_map.103.near.refs_0_, ...), custom_call_target="tpu_custom_call" | custom-call | tf_op jit(solution)/shard_map/pallas_call | solution.py:39
  41.7 0.5 collective-permute-start.13
  42.2 1.6 %collective-permute-start.14 = (bf16[2,72,1152]{2,1,0:T(8,128)(2,1)S(1)}, bf16[2,72,1152]{2,1,0:T(8,128)(2,1)S(1)}, u32[]{:S(2)}, u32[]{:S(2)}) collective-permute-start(bf16[2,72,1152]{2,1,0:T(8,128)(2,1)S(1)} %get-tuple-element.49), channel_id=1, source_target_pairs={{0,16},{8,24},{16,0},{24,8},{1,17},{9,25},{17,1},{25,9},{2,18},{10... | collective-permute-start | bytes 995336 | tf_op jit(solution)/shard_map/ppermute | solution.py:350
  43.9 2.9 %collective-permute-start.8 = (bf16[32,1728]{1,0:T(8,128)(2,1)S(1)}, bf16[32,1728]{1,0:T(8,128)(2,1)S(1)}, u32[]{:S(2)}, u32[]{:S(2)}) collective-permute-start(bf16[32,1728]{1,0:T(8,128)(2,1)S(1)} %get-tuple-element.39), channel_id=1, source_target_pairs={{0,2},{1,3},{2,0},{3,1},{4,6},{5,7},{6,4},{7,5},{8,10},{9,11},{10,... | collective-permute-start | bytes 331784 | tf_op jit(solution)/shard_map/ppermute | solution.py:350
  46.7 1.0 %collective-permute-start.9 = (bf16[32,1728]{1,0:T(8,128)(2,1)S(1)}, bf16[32,1728]{1,0:T(8,128)(2,1)S(1)}, u32[]{:S(2)}, u32[]{:S(2)}) collective-permute-start(bf16[32,1728]{1,0:T(8,128)(2,1)S(1)} %get-tuple-element.40), channel_id=1, source_target_pairs={{0,4},{1,5},{2,6},{3,7},{4,0},{5,1},{6,2},{7,3},{8,12},{9,13},{10,... | collective-permute-start | bytes 331784 | tf_op jit(solution)/shard_map/ppermute | solution.py:350
  47.7 1.5 %collective-permute-start.10 = (bf16[32,1728]{1,0:T(8,128)(2,1)S(1)}, bf16[32,1728]{1,0:T(8,128)(2,1)S(1)}, u32[]{:S(2)}, u32[]{:S(2)}) collective-permute-start(bf16[32,1728]{1,0:T(8,128)(2,1)S(1)} %get-tuple-element.41), channel_id=1, source_target_pairs={{0,6},{1,7},{2,4},{3,5},{4,2},{5,3},{6,0},{7,1},{8,14},{9,15},{10,... | collective-permute-start | bytes 331784 | tf_op jit(solution)/shard_map/ppermute | solution.py:350
  49.2 2.4 %collective-permute-done.13.got_x = bf16[2,72,1152]{2,1,0:T(8,128)(2,1)S(1)} collective-permute-done((bf16[2,72,1152]{2,1,0:T(8,128)(2,1)S(1)}, bf16[2,72,1152]{2,1,0:T(8,128)(2,1)S(1)}, u32[]{:S(2)}, u32[]{:S(2)}) %collective-permute-start.13) | collective-permute-done | bytes 331808 | tf_op jit(solution)/shard_map/ppermute | solution.py:350
  52.0 1.7 %collective-permute-start.15 = (bf16[72,1152]{1,0:T(8,128)(2,1)S(1)}, bf16[72,1152]{1,0:T(8,128)(2,1)S(1)}, u32[]{:S(2)}, u32[]{:S(2)}) collective-permute-start(bf16[72,1152]{1,0:T(8,128)(2,1)S(1)} %get-tuple-element.51), channel_id=1, source_target_pairs={{0,16},{8,24},{16,0},{24,8},{1,17},{9,25},{17,1},{25,9},{2,18},{10... | collective-permute-start | bytes 497672 | tf_op jit(solution)/shard_map/ppermute | solution.py:350
  53.6 0.8 %collective-permute-start.16 = (bf16[72,1152]{1,0:T(8,128)(2,1)S(1)}, bf16[72,1152]{1,0:T(8,128)(2,1)S(1)}, u32[]{:S(2)}, u32[]{:S(2)}) collective-permute-start(bf16[72,1152]{1,0:T(8,128)(2,1)S(1)} %get-tuple-element.52), channel_id=1, source_target_pairs={{0,8},{8,0},{16,24},{24,16},{1,9},{9,1},{17,25},{25,17},{2,10},{10... | collective-permute-start | bytes 497672 | tf_op jit(solution)/shard_map/ppermute | solution.py:350
  54.4 3.7 %collective-permute-done.9.refs_1_.refs_2_ = bf16[32,1728]{1,0:T(8,128)(2,1)S(1)} collective-permute-done((bf16[32,1728]{1,0:T(8,128)(2,1)S(1)}, bf16[32,1728]{1,0:T(8,128)(2,1)S(1)}, u32[]{:S(2)}, u32[]{:S(2)}) %collective-permute-start.9) | collective-permute-done | bytes 110624 | tf_op jit(solution)/shard_map/ppermute | solution.py:350
  58.2 0.7 %collective-permute-done.16.got_x = bf16[72,1152]{1,0:T(8,128)(2,1)S(1)} collective-permute-done((bf16[72,1152]{1,0:T(8,128)(2,1)S(1)}, bf16[72,1152]{1,0:T(8,128)(2,1)S(1)}, u32[]{:S(2)}, u32[]{:S(2)}) %collective-permute-start.16) | collective-permute-done | bytes 165920 | tf_op jit(solution)/shard_map/ppermute | solution.py:350
  59.2 2.9 %collective-permute-start.17 = (bf16[72,576]{1,0:T(8,128)(2,1)S(1)}, bf16[72,576]{1,0:T(8,128)(2,1)S(1)}, u32[]{:S(2)}, u32[]{:S(2)}) collective-permute-start(bf16[72,576]{1,0:T(8,128)(2,1)S(1)} %get-tuple-element.54), channel_id=1, source_target_pairs={{0,2},{1,3},{2,0},{3,1},{4,6},{5,7},{6,4},{7,5},{8,10},{9,11},{10,... | collective-permute-start | bytes 248840 | tf_op jit(solution)/shard_map/ppermute | solution.py:350
  62.1 1.1 %collective-permute-start.18 = (bf16[72,576]{1,0:T(8,128)(2,1)S(1)}, bf16[72,576]{1,0:T(8,128)(2,1)S(1)}, u32[]{:S(2)}, u32[]{:S(2)}) collective-permute-start(bf16[72,576]{1,0:T(8,128)(2,1)S(1)} %get-tuple-element.55), channel_id=1, source_target_pairs={{0,4},{1,5},{2,6},{3,7},{4,0},{5,1},{6,2},{7,3},{8,12},{9,13},{10,... | collective-permute-start | bytes 248840 | tf_op jit(solution)/shard_map/ppermute | solution.py:350
  63.2 1.4 %collective-permute-start.19 = (bf16[72,576]{1,0:T(8,128)(2,1)S(1)}, bf16[72,576]{1,0:T(8,128)(2,1)S(1)}, u32[]{:S(2)}, u32[]{:S(2)}) collective-permute-start(bf16[72,576]{1,0:T(8,128)(2,1)S(1)} %get-tuple-element.56), channel_id=1, source_target_pairs={{0,6},{1,7},{2,4},{3,5},{4,2},{5,3},{6,0},{7,1},{8,14},{9,15},{10,... | collective-permute-start | bytes 248840 | tf_op jit(solution)/shard_map/ppermute | solution.py:350
  64.6 4.0 %shard_map.106 = (bf16[128,1152]{1,0:T(8,128)(2,1)}, bf16[128,1152]{1,0:T(8,128)(2,1)}, bf16[128,1728]{1,0:T(8,128)(2,1)}) custom-call(bf16[128,1728]{1,0:T(8,128)(2,1)S(1)} %get-tuple-element.38.mine.refs_0_, bf16[32,1728]{1,0:T(8,128)(2,1)S(1)} %collective-permute-done.8.refs_0_.refs_1_, bf16[32,1728]{1,0:T(8,128)(2,1)S(1)} %collective-permute-done.9.refs_1_.refs_2_, ...), custom_call_target="tpu_custom_call" | custom-call | tf_op jit(solution)/shard_map/pallas_call | solution.py:39
  68.6 2.3 %collective-permute-done.18.refs_1_ = bf16[72,576]{1,0:T(8,128)(2,1)S(1)} collective-permute-done((bf16[72,576]{1,0:T(8,128)(2,1)S(1)}, bf16[72,576]{1,0:T(8,128)(2,1)S(1)}, u32[]{:S(2)}, u32[]{:S(2)}) %collective-permute-start.18) | collective-permute-done | bytes 82976 | tf_op jit(solution)/shard_map/ppermute | solution.py:350
  70.9 0.8 %shard_map.110 = (f32[72,288]{1,0:T(8,128)}, f32[72,288]{1,0:T(8,128)}) custom-call(f32[72,576]{1,0:T(8,128)S(1)} %get-tuple-element.53.own, bf16[72,576]{1,0:T(8,128)(2,1)S(1)} %collective-permute-done.17.refs_0_, bf16[72,576]{1,0:T(8,128)(2,1)S(1)} %collective-permute-done.18.refs_1_, bf16[72,576]{1,0:T(8,128)(2,1)S(1)} %collective-permute-done.19.refs_2_), custom_call_target="tpu_custom_call" | custom-call | tf_op jit(solution)/shard_map/pallas_call | solution.py:39
  (32 shorter events, 0.9 us)
Async XLA Ops:
  0.6 15.4 %collective-permute-start = (bf16[432,1152]{1,0:T(8,128)(2,1)}, bf16[432,1152]{1,0:T(8,128)(2,1)S(1)}, u32[]{:S(2)}, u32[]{:S(2)}) collective-permute-start(bf16[432,1152]{1,0:T(8,128)(2,1)} %bitcast.9), channel_id=1, source_target_pairs={{0,8},{1,17},{2,10},{3,19},{4,12},{5,21},{6,14},{7,23},{8,0},{9,25... | collective-permute-start | bytes 2985992 | tf_op jit(solution)/shard_map/ppermute | solution.py:362
  8.5 10.8 %collective-permute-start.1 = (bf16[32,2944]{1,0:T(8,128)(2,1)}, bf16[32,2944]{1,0:T(8,128)(2,1)S(1)}, u32[]{:S(2)}, u32[]{:S(2)}) collective-permute-start(bf16[32,2944]{1,0:T(8,128)(2,1)} %get-tuple-element.34), channel_id=1, source_target_pairs={{0,2},{1,3},{2,0},{3,1},{4,6},{5,7},{6,4},{7,5},{8,10},{9,11},{10,... | collective-permute-start | bytes 565256 | tf_op jit(solution)/shard_map/ppermute | solution.py:350
  10.1 16.9 %collective-permute-start.2 = (bf16[32,2944]{1,0:T(8,128)(2,1)}, bf16[32,2944]{1,0:T(8,128)(2,1)S(1)}, u32[]{:S(2)}, u32[]{:S(2)}) collective-permute-start(bf16[32,2944]{1,0:T(8,128)(2,1)} %get-tuple-element.35), channel_id=1, source_target_pairs={{0,4},{1,5},{2,6},{3,7},{4,0},{5,1},{6,2},{7,3},{8,12},{9,13},{10,... | collective-permute-start | bytes 565256 | tf_op jit(solution)/shard_map/ppermute | solution.py:350
  12.7 14.3 %collective-permute-start.3 = (bf16[32,2944]{1,0:T(8,128)(2,1)}, bf16[32,2944]{1,0:T(8,128)(2,1)S(1)}, u32[]{:S(2)}, u32[]{:S(2)}) collective-permute-start(bf16[32,2944]{1,0:T(8,128)(2,1)} %get-tuple-element.36), channel_id=1, source_target_pairs={{0,6},{1,7},{2,4},{3,5},{4,2},{5,3},{6,0},{7,1},{8,14},{9,15},{10,... | collective-permute-start | bytes 565256 | tf_op jit(solution)/shard_map/ppermute | solution.py:350
  16.1 0.9 %copy-start.6 = (bf16[32,2944]{1,0:T(8,128)(2,1)S(1)}, bf16[32,2944]{1,0:T(8,128)(2,1)}, u32[]{:S(2)}) copy-start(bf16[32,2944]{1,0:T(8,128)(2,1)} %get-tuple-element.32.own) | copy-start | bytes 565252
  17.0 13.2 %copy-start.1 = (bf16[576,1152]{1,0:T(8,128)(2,1)S(1)}, bf16[576,1152]{1,0:T(8,128)(2,1)}, u32[]{:S(2)}) copy-start(bf16[576,1152]{1,0:T(8,128)(2,1)} %refs_8_.1) | copy-start | bytes 3981316
  17.0 13.2 %copy-start.3 = (bf16[1152,432]{0,1:T(8,128)(2,1)S(1)}, bf16[1152,432]{0,1:T(8,128)(2,1)}, u32[]{:S(2)}) copy-start(bf16[1152,432]{0,1:T(8,128)(2,1)} %param.9) | copy-start | bytes 2985988
  17.1 10.0 %collective-permute-start.6 = (bf16[216,1152]{1,0:T(8,128)(2,1)S(1)}, bf16[216,1152]{1,0:T(8,128)(2,1)S(1)}, u32[]{:S(2)}, u32[]{:S(2)}) collective-permute-start(bf16[216,1152]{1,0:T(8,128)(2,1)S(1)} %get-tuple-element.37), channel_id=1, source_target_pairs={{0,16},{1,9},{2,18},{3,11},{4,20},{5,13},{6,22},{7,15},{8,24},{9,1... | collective-permute-start | bytes 1493000 | tf_op jit(solution)/shard_map/ppermute | solution.py:362
  19.2 10.2 %collective-permute-start.5 = (bf16[432,1152]{1,0:T(8,128)(2,1)S(1)}, bf16[432,1152]{1,0:T(8,128)(2,1)S(1)}, u32[]{:S(2)}, u32[]{:S(2)}) collective-permute-start(bf16[432,1152]{1,0:T(8,128)(2,1)S(1)} %collective-permute-done.got.refs_1_), channel_id=1, source_target_pairs={{0,1},{1,0},{2,3},{3,2},{4,5},{5,4},{6,7},{7,6},{8,9},{9,8},{10,11... | collective-permute-start | bytes 2985992 | tf_op jit(solution)/shard_map/ppermute | solution.py:350
  27.0 2.4 %collective-permute-start.4 = (bf16[128,3200]{1,0:T(8,128)(2,1)S(1)}, bf16[128,3200]{1,0:T(8,128)(2,1)S(1)}, u32[]{:S(2)}, u32[]{:S(2)}) collective-permute-start(bf16[128,3200]{1,0:T(8,128)(2,1)S(1)} %shard_map.103.near.refs_0_), channel_id=1, source_target_pairs={{0,1},{1,0},{2,3},{3,2},{4,5},{5,4},{6,7},{7,6},{8,9},{9,8},{10,11... | collective-permute-start | bytes 2457608 | tf_op jit(solution)/shard_map/ppermute | solution.py:350
  27.1 3.0 %collective-permute-start.7 = (bf16[216,1152]{1,0:T(8,128)(2,1)S(1)}, bf16[216,1152]{1,0:T(8,128)(2,1)S(1)}, u32[]{:S(2)}, u32[]{:S(2)}) collective-permute-start(bf16[216,1152]{1,0:T(8,128)(2,1)S(1)} %collective-permute-done.6.refs_3_), channel_id=1, source_target_pairs={{0,1},{1,0},{2,3},{3,2},{4,5},{5,4},{6,7},{7,6},{8,9},{9,8},{10,11... | collective-permute-start | bytes 1493000 | tf_op jit(solution)/shard_map/ppermute | solution.py:350
  37.4 1.9 %collective-permute-start.12 = (bf16[128,1728]{1,0:T(8,128)(2,1)S(1)}, bf16[128,1728]{1,0:T(8,128)(2,1)S(1)}, u32[]{:S(2)}, u32[]{:S(2)}) collective-permute-start(bf16[128,1728]{1,0:T(8,128)(2,1)S(1)} %get-tuple-element.38.mine.refs_0_), channel_id=1, source_target_pairs={{0,1},{1,0},{2,3},{3,2},{4,5},{5,4},{6,7},{7,6},{8,9},{9,8},{10,11... | collective-permute-start | bytes 1327112 | tf_op jit(solution)/shard_map/ppermute | solution.py:350
  41.7 9.9 %collective-permute-start.13 = (bf16[2,72,1152]{2,1,0:T(8,128)(2,1)S(1)}, bf16[2,72,1152]{2,1,0:T(8,128)(2,1)S(1)}, u32[]{:S(2)}, u32[]{:S(2)}) collective-permute-start(bf16[2,72,1152]{2,1,0:T(8,128)(2,1)S(1)} %get-tuple-element.48), channel_id=1, source_target_pairs={{0,8},{8,0},{16,24},{24,16},{1,9},{9,1},{17,25},{25,17},{2,10},{10... | collective-permute-start | bytes 995336 | tf_op jit(solution)/shard_map/ppermute | solution.py:350
  42.2 9.6 %collective-permute-start.14 = (bf16[2,72,1152]{2,1,0:T(8,128)(2,1)S(1)}, bf16[2,72,1152]{2,1,0:T(8,128)(2,1)S(1)}, u32[]{:S(2)}, u32[]{:S(2)}) collective-permute-start(bf16[2,72,1152]{2,1,0:T(8,128)(2,1)S(1)} %get-tuple-element.49), channel_id=1, source_target_pairs={{0,16},{8,24},{16,0},{24,8},{1,17},{9,25},{17,1},{25,9},{2,18},{10... | collective-permute-start | bytes 995336 | tf_op jit(solution)/shard_map/ppermute | solution.py:350
  43.9 10.6 %collective-permute-start.8 = (bf16[32,1728]{1,0:T(8,128)(2,1)S(1)}, bf16[32,1728]{1,0:T(8,128)(2,1)S(1)}, u32[]{:S(2)}, u32[]{:S(2)}) collective-permute-start(bf16[32,1728]{1,0:T(8,128)(2,1)S(1)} %get-tuple-element.39), channel_id=1, source_target_pairs={{0,2},{1,3},{2,0},{3,1},{4,6},{5,7},{6,4},{7,5},{8,10},{9,11},{10,... | collective-permute-start | bytes 331784 | tf_op jit(solution)/shard_map/ppermute | solution.py:350
  46.7 11.4 %collective-permute-start.9 = (bf16[32,1728]{1,0:T(8,128)(2,1)S(1)}, bf16[32,1728]{1,0:T(8,128)(2,1)S(1)}, u32[]{:S(2)}, u32[]{:S(2)}) collective-permute-start(bf16[32,1728]{1,0:T(8,128)(2,1)S(1)} %get-tuple-element.40), channel_id=1, source_target_pairs={{0,4},{1,5},{2,6},{3,7},{4,0},{5,1},{6,2},{7,3},{8,12},{9,13},{10,... | collective-permute-start | bytes 331784 | tf_op jit(solution)/shard_map/ppermute | solution.py:350
  47.7 10.4 %collective-permute-start.10 = (bf16[32,1728]{1,0:T(8,128)(2,1)S(1)}, bf16[32,1728]{1,0:T(8,128)(2,1)S(1)}, u32[]{:S(2)}, u32[]{:S(2)}) collective-permute-start(bf16[32,1728]{1,0:T(8,128)(2,1)S(1)} %get-tuple-element.41), channel_id=1, source_target_pairs={{0,6},{1,7},{2,4},{3,5},{4,2},{5,3},{6,0},{7,1},{8,14},{9,15},{10,... | collective-permute-start | bytes 331784 | tf_op jit(solution)/shard_map/ppermute | solution.py:350
  51.8 12.8 %copy-start.4 = (f32[8,128,128]{2,1,0:T(8,128)S(1)}, f32[8,128,128]{2,1,0:T(8,128)}, u32[]{:S(2)}) copy-start(f32[8,128,128]{2,1,0:T(8,128)} %get-tuple-element.42.refs_7_) | copy-start | bytes 1572868
  51.8 12.8 %copy-start.5 = (bf16[128,1152]{1,0:T(8,128)(2,1)S(1)}, bf16[128,1152]{1,0:T(8,128)(2,1)}, u32[]{:S(2)}) copy-start(bf16[128,1152]{1,0:T(8,128)(2,1)} %get-tuple-element.43.refs_9_) | copy-start | bytes 884740
  51.9 12.6 %copy-start = (bf16[576,1152]{1,0:T(8,128)(2,1)S(1)}, bf16[576,1152]{1,0:T(8,128)(2,1)}, u32[]{:S(2)}) copy-start(bf16[576,1152]{1,0:T(8,128)(2,1)} %refs_5_.1) | copy-start | bytes 3981316
  52.0 12.6 %copy-start.2 = (bf16[2,64,1728]{2,1,0:T(8,128)(2,1)S(1)}, bf16[2,64,1728]{2,1,0:T(8,128)(2,1)}, u32[]{:S(2)}) copy-start(bf16[2,64,1728]{2,1,0:T(8,128)(2,1)} %param.7) | copy-start | bytes 1327108
  52.0 6.3 %collective-permute-start.15 = (bf16[72,1152]{1,0:T(8,128)(2,1)S(1)}, bf16[72,1152]{1,0:T(8,128)(2,1)S(1)}, u32[]{:S(2)}, u32[]{:S(2)}) collective-permute-start(bf16[72,1152]{1,0:T(8,128)(2,1)S(1)} %get-tuple-element.51), channel_id=1, source_target_pairs={{0,16},{8,24},{16,0},{24,8},{1,17},{9,25},{17,1},{25,9},{2,18},{10... | collective-permute-start | bytes 497672 | tf_op jit(solution)/shard_map/ppermute | solution.py:350
  53.6 5.3 %collective-permute-start.16 = (bf16[72,1152]{1,0:T(8,128)(2,1)S(1)}, bf16[72,1152]{1,0:T(8,128)(2,1)S(1)}, u32[]{:S(2)}, u32[]{:S(2)}) collective-permute-start(bf16[72,1152]{1,0:T(8,128)(2,1)S(1)} %get-tuple-element.52), channel_id=1, source_target_pairs={{0,8},{8,0},{16,24},{24,16},{1,9},{9,1},{17,25},{25,17},{2,10},{10... | collective-permute-start | bytes 497672 | tf_op jit(solution)/shard_map/ppermute | solution.py:350
  58.2 6.4 %collective-permute-start.11 = (bf16[64,1728]{1,0:T(8,128)(2,1)S(1)}, bf16[64,1728]{1,0:T(8,128)(2,1)S(1)}, u32[]{:S(2)}, u32[]{:S(2)}) collective-permute-start(bf16[64,1728]{1,0:T(8,128)(2,1)S(1)} %shard_map.105), channel_id=1, source_target_pairs={{0,1},{1,0},{2,3},{3,2},{4,5},{5,4},{6,7},{7,6},{8,9},{9,8},{10,11... | collective-permute-start | bytes 663560 | tf_op jit(solution)/shard_map/ppermute | solution.py:350
  59.2 9.4 %collective-permute-start.17 = (bf16[72,576]{1,0:T(8,128)(2,1)S(1)}, bf16[72,576]{1,0:T(8,128)(2,1)S(1)}, u32[]{:S(2)}, u32[]{:S(2)}) collective-permute-start(bf16[72,576]{1,0:T(8,128)(2,1)S(1)} %get-tuple-element.54), channel_id=1, source_target_pairs={{0,2},{1,3},{2,0},{3,1},{4,6},{5,7},{6,4},{7,5},{8,10},{9,11},{10,... | collective-permute-start | bytes 248840 | tf_op jit(solution)/shard_map/ppermute | solution.py:350
  62.1 8.8 %collective-permute-start.18 = (bf16[72,576]{1,0:T(8,128)(2,1)S(1)}, bf16[72,576]{1,0:T(8,128)(2,1)S(1)}, u32[]{:S(2)}, u32[]{:S(2)}) collective-permute-start(bf16[72,576]{1,0:T(8,128)(2,1)S(1)} %get-tuple-element.55), channel_id=1, source_target_pairs={{0,4},{1,5},{2,6},{3,7},{4,0},{5,1},{6,2},{7,3},{8,12},{9,13},{10,... | collective-permute-start | bytes 248840 | tf_op jit(solution)/shard_map/ppermute | solution.py:350
  63.2 7.7 %collective-permute-start.19 = (bf16[72,576]{1,0:T(8,128)(2,1)S(1)}, bf16[72,576]{1,0:T(8,128)(2,1)S(1)}, u32[]{:S(2)}, u32[]{:S(2)}) collective-permute-start(bf16[72,576]{1,0:T(8,128)(2,1)S(1)} %get-tuple-element.56), channel_id=1, source_target_pairs={{0,6},{1,7},{2,4},{3,5},{4,2},{5,3},{6,0},{7,1},{8,14},{9,15},{10,... | collective-permute-start | bytes 248840 | tf_op jit(solution)/shard_map/ppermute | solution.py:350

commit v11 on v10

--- a/solution.py
+++ b/solution.py
@@ -196,7 +196,7 @@
 
 def join_rows_kernel(*refs):
     out, low = refs[-1], 0
-    for ref in refs[:-1]:
+    for ref in refs[-2::-1]:
         out[low : low + ref.shape[0], : ref.shape[1]] = ref[...]
         low += ref.shape[0]
 
@@ -239,7 +239,7 @@
 
 
 def others_kernel(mine, *refs):
-    parts, out = refs[:-1], refs[-1]
+    parts, out = refs[-2::-1], refs[-1]
     half = mine.shape[0] // 2
     rows = half // (1 + len(parts))
     out[:rows] = mine[half : half + rows]
@@ -317,7 +317,7 @@
 
 def last_kernel(chips, patches, *refs):
     idx = place(chips)
-    held, got, refs = refs[:chips], refs[chips], refs[chips + 1 :]
+    held, got, refs = refs[:chips][::-1], refs[chips], refs[chips + 1 :]
     (wos, qkv, p_ref, wot, hid), refs = refs[:5], refs[5:]
     block_far, out_far, grads_far, rows, block_out, grads, qs, ks, vs, gs, sems = refs
     inner, width = wos.shape
@@ -367,7 +367,7 @@
     rows, sent = parts[0].shape
     whole = [shape((len(parts) * rows, sent + PAD))]
     if n != 4:
-        (near,) = call(join_rows_kernel, whole, from_chips(parts), small=True)
+        (near,) = call(join_rows_kernel, whole, from_chips(parts)[::-1], small=True)
         weights = [lax.all_gather(weight, "dp", axis=0, tiled=True)]
         return near, flip(near, "seq", 1), weights, [lambda idx: [0]], 1
     half, width = weight.shape[0] // 2, weight.shape[1]
@@ -379,7 +379,7 @@
         small=True,
     )
     corner = across(corner, (2, 1))
-    (near,) = call(join_rows_kernel, whole, [own, *from_chips(parts)[1:]], small=True)
+    (near,) = call(join_rows_kernel, whole, [*from_chips(parts)[:0:-1], own], small=True)
     weights = [weight, side, flip(side, "seq", 1), corner, flip(corner, "seq", 1)]
 
     def both(shard):
@@ -416,8 +416,8 @@
         [own, flip(send_t, "dp", 2), flip(send_s, "dp", 1)],
         small=True,
     )
-    got = [flip(value, "seq", 2 * (q + 1)) for q, value in enumerate(sends)]
-    return call(sum_kernel, [shape((size, width // n), F32)] * 2, [own, *got], small=True)
+    got = from_chips([own, *sends])[1:]
+    return call(sum_kernel, [shape((size, width // n), F32)] * 2, [own, *got[::-1]], small=True)
 
 
 def shards(tokens, spatial_qkv, wo_spatial, w_temporal, wo_temporal, cotangent):
@@ -484,12 +484,15 @@
         )
     back = from_chips([mine, *back])
     (others,) = call(
-        others_kernel, [shape((rows // 2, width + inner))], back, small=True
+        others_kernel,
+        [shape((rows // 2, width + inner))],
+        [back[0], *back[:0:-1]],
+        small=True,
     )
     block_out, tokens_grad, qkv_grad = call(
         functools.partial(last_kernel, chips, patches),
         [shape((rows, width)), shape((rows, width)), shape((rows, 3 * inner))],
-        [*back, flip(others, "seq", 1), wo_spatial, qkv_rows, spatial_p, wo_temporal, hidden],
+        [*back[::-1], flip(others, "seq", 1), wo_spatial, qkv_rows, spatial_p, wo_temporal, hidden],
         [held(width + inner), held(width), held(3 * inner)] + [wide] * 4 + [sems(3)],
         far_out=range(3),
         small=True,

time: 71.8 us -> 70.4 us (0.981)
  starting transfers between devices: 25.7 us -> 22.5 us
  waiting for transfers between devices: 24.5 us -> 26.3 us
    ppermute x18, starting transfers between devices: 20.6 us -> 17.4 us  [flip(): lax.ppermute(value, axis, [(i, i ^ bit) for i in range(lax.axis_size(axis...]
    ppermute x18, waiting for transfers between devices: 21.4 us -> 23.1 us  [flip(): lax.ppermute(value, axis, [(i, i ^ bit) for i in range(lax.axis_size(axis...]
  transfers between devices with their start and end apart: 20 -> 20, of which waited for: 10 -> 11; matrix products, arithmetic and copies ran while one was open for 0% -> 0% of each run, Pallas kernels for 13% -> 13%
where the time goes in v11:
time: 70.4 us; the launch traced here: 70.2 us
  waiting for transfers between devices  26.3 us (37%)
  starting transfers between devices  22.5 us (32%)
  Pallas kernels  19.8 us (28%)
  local copies, waits for them, and re-layouts  0.95 us (1%)
  between operations  0.76 us (1%)
    ppermute x18, waiting for transfers between devices, flip(): lax.ppermute(value, axis, [(i, i ^ bit) for i in range(lax.axis_size(axis...  23.1 us
    pallas_call x10, Pallas kernels, call(): pl.pallas_call(body, out_shape=outs, in_specs=[HBM if i in far_in else sp...  19.8 us
    ppermute x18, starting transfers between devices, flip(): lax.ppermute(value, axis, [(i, i ^ bit) for i in range(lax.axis_size(axis...  17.4 us
    ppermute x2, starting transfers between devices, across(): return lax.ppermute(value, ('dp', 'seq'), pairs)  5.12 us
    ppermute x2, waiting for transfers between devices, across(): return lax.ppermute(value, ('dp', 'seq'), pairs)  3.13 us
  transfers between devices with their start and end apart: 20, of which 11 were waited for; matrix products, arithmetic and copies ran while one was open for 0% of the time, Pallas kernels for 13%

profile of v11, /device:TPU:0, one launch (start us, length us, event | category | flops | bytes accessed | tf_op | source)
XLA Modules:
  0.0 70.2 jit_solution(453159657339589643)
XLA Ops:
  0.6 3.0 %collective-permute-start.3 = (bf16[432,1152]{1,0:T(8,128)(2,1)}, bf16[432,1152]{1,0:T(8,128)(2,1)S(1)}, u32[]{:S(2)}, u32[]{:S(2)}) collective-permute-start(bf16[432,1152]{1,0:T(8,128)(2,1)} %bitcast.9), channel_id=1, source_target_pairs={{0,8},{1,17},{2,10},{3,19},{4,12},{5,21},{6,14},{7,23},{8,0},{9,25... | collective-permute-start | bytes 2985992 | tf_op jit(solution)/shard_map/ppermute | solution.py:362
  3.6 4.8 %shard_map.101 = (bf16[32,2944]{1,0:T(8,128)(2,1)}, bf16[32,2944]{1,0:T(8,128)(2,1)}, bf16[32,2944]{1,0:T(8,128)(2,1)}, bf16[32,2944]{1,0:T(8,128)(2,1)}, bf16[1...) custom-call(bf16[128,1728]{1,0:T(8,128)(2,1)} %bitcast.7, bf16[128,1152]{1,0:T(8,128)(2,1)} %bitcast.11, ...), custom_call_target="tpu_custom_call" | custom-call | tf_op jit(solution)/shard_map/pallas_call | solution.py:39
  8.5 3.7 %collective-permute-start = (bf16[32,2944]{1,0:T(8,128)(2,1)}, bf16[32,2944]{1,0:T(8,128)(2,1)S(1)}, u32[]{:S(2)}, u32[]{:S(2)}) collective-permute-start(bf16[32,2944]{1,0:T(8,128)(2,1)} %get-tuple-element.32), channel_id=1, source_target_pairs={{0,6},{1,7},{2,4},{3,5},{4,2},{5,3},{6,0},{7,1},{8,14},{9,15},{10,... | collective-permute-start | bytes 565256 | tf_op jit(solution)/shard_map/ppermute | solution.py:350
  12.1 0.8 %collective-permute-start.2 = (bf16[32,2944]{1,0:T(8,128)(2,1)}, bf16[32,2944]{1,0:T(8,128)(2,1)S(1)}, u32[]{:S(2)}, u32[]{:S(2)}) collective-permute-start(bf16[32,2944]{1,0:T(8,128)(2,1)} %get-tuple-element.34), channel_id=1, source_target_pairs={{0,2},{1,3},{2,0},{3,1},{4,6},{5,7},{6,4},{7,5},{8,10},{9,11},{10,... | collective-permute-start | bytes 565256 | tf_op jit(solution)/shard_map/ppermute | solution.py:350
  12.9 3.1 %collective-permute-done.3.got.refs_1_ = bf16[432,1152]{1,0:T(8,128)(2,1)S(1)} collective-permute-done((bf16[432,1152]{1,0:T(8,128)(2,1)}, bf16[432,1152]{1,0:T(8,128)(2,1)S(1)}, u32[]{:S(2)}, u32[]{:S(2)}) %collective-permute-start.3) | collective-permute-done | bytes 995360 | tf_op jit(solution)/shard_map/ppermute | solution.py:362
  16.1 0.9 %copy-done.6 = bf16[32,2944]{1,0:T(8,128)(2,1)S(1)} copy-done((bf16[32,2944]{1,0:T(8,128)(2,1)S(1)}, bf16[32,2944]{1,0:T(8,128)(2,1)}, u32[]{:S(2)}) %copy-start.6) | copy-done | bytes 188440
  17.1 2.1 %collective-permute-start.6 = (bf16[216,1152]{1,0:T(8,128)(2,1)S(1)}, bf16[216,1152]{1,0:T(8,128)(2,1)S(1)}, u32[]{:S(2)}, u32[]{:S(2)}) collective-permute-start(bf16[216,1152]{1,0:T(8,128)(2,1)S(1)} %get-tuple-element.37), channel_id=1, source_target_pairs={{0,16},{1,9},{2,18},{3,11},{4,20},{5,13},{6,22},{7,15},{8,24},{9,1... | collective-permute-start | bytes 1493000 | tf_op jit(solution)/shard_map/ppermute | solution.py:362
  19.2 8.8 %collective-permute-done.1.refs_1_ = bf16[32,2944]{1,0:T(8,128)(2,1)S(1)} collective-permute-done((bf16[32,2944]{1,0:T(8,128)(2,1)}, bf16[32,2944]{1,0:T(8,128)(2,1)S(1)}, u32[]{:S(2)}, u32[]{:S(2)}) %collective-permute-start.1) | collective-permute-done | bytes 188448 | tf_op jit(solution)/shard_map/ppermute | solution.py:350
  28.2 0.5 collective-permute-start.7
  28.7 1.8 %collective-permute-done.4.far.refs_1_ = bf16[128,3200]{1,0:T(8,128)(2,1)S(1)} collective-permute-done((bf16[128,3200]{1,0:T(8,128)(2,1)S(1)}, bf16[128,3200]{1,0:T(8,128)(2,1)S(1)}, u32[]{:S(2)}, u32[]{:S(2)}) %collective-permute-start.4) | collective-permute-done | bytes 819232 | tf_op jit(solution)/shard_map/ppermute | solution.py:350
  30.5 0.7 %collective-permute-done.7.refs_4_ = bf16[216,1152]{1,0:T(8,128)(2,1)S(1)} collective-permute-done((bf16[216,1152]{1,0:T(8,128)(2,1)S(1)}, bf16[216,1152]{1,0:T(8,128)(2,1)S(1)}, u32[]{:S(2)}, u32[]{:S(2)}) %collective-permute-start.7) | collective-permute-done | bytes 497696 | tf_op jit(solution)/shard_map/ppermute | solution.py:350
  31.3 7.3 %shard_map.104 = (bf16[128,1728]{1,0:T(8,128)(2,1)S(1)}, bf16[32,1728]{1,0:T(8,128)(2,1)S(1)}, bf16[32,1728]{1,0:T(8,128)(2,1)S(1)}, bf16[32,1728]{1,0:T(8,128)(2,1)S(1)}) custom-call(bf16[128,3200]{1,0:T(8,128)(2,1)S(1)} %shard_map.103.near.refs_0_, bf16[128,3200]{1,0:T(8,128)(2,1)S(1)} %collective-permute-done.4.far.refs_1_, ...), custom_call_target="tpu_custom_call" | custom-call | tf_op jit(solution)/shard_map/pallas_call | solution.py:39
  38.5 0.2 collective-permute-start.12
  38.7 1.7 %collective-permute-done.12.other = bf16[128,1728]{1,0:T(8,128)(2,1)S(1)} collective-permute-done((bf16[128,1728]{1,0:T(8,128)(2,1)S(1)}, bf16[128,1728]{1,0:T(8,128)(2,1)S(1)}, u32[]{:S(2)}, u32[]{:S(2)}) %collective-permute-start.12) | collective-permute-done | bytes 442400 | tf_op jit(solution)/shard_map/ppermute | solution.py:350
  40.4 2.4 %shard_map.107 = (f32[4,72,1152]{2,1,0:T(8,128)S(1)}, bf16[2,72,1152]{2,1,0:T(8,128)(2,1)S(1)}, bf16[2,72,1152]{2,1,0:T(8,128)(2,1)S(1)}) custom-call(bf16[128,1728]{1,0:T(8,128)(2,1)S(1)} %get-tuple-element.41.mine.refs_3_, bf16[128,1728]{1,0:T(8,128)(2,1)S(1)} %collective-permute-done.12.other, bf16[128,3200]{1,0:T(8,128)(2,1)S(1)} %shard_map.103.near.refs_0_, ...), custom_call_target="tpu_custom_call" | custom-call | tf_op jit(solution)/shard_map/pallas_call | solution.py:39
  42.8 1.6 %collective-permute-start.13 = (bf16[2,72,1152]{2,1,0:T(8,128)(2,1)S(1)}, bf16[2,72,1152]{2,1,0:T(8,128)(2,1)S(1)}, u32[]{:S(2)}, u32[]{:S(2)}) collective-permute-start(bf16[2,72,1152]{2,1,0:T(8,128)(2,1)S(1)} %get-tuple-element.48), channel_id=1, source_target_pairs={{0,8},{8,0},{16,24},{24,16},{1,9},{9,1},{17,25},{25,17},{2,10},{10... | collective-permute-start | bytes 995336 | tf_op jit(solution)/shard_map/ppermute | solution.py:350
  44.4 0.5 collective-permute-start.14
  44.9 2.5 %collective-permute-start.8 = (bf16[32,1728]{1,0:T(8,128)(2,1)S(1)}, bf16[32,1728]{1,0:T(8,128)(2,1)S(1)}, u32[]{:S(2)}, u32[]{:S(2)}) collective-permute-start(bf16[32,1728]{1,0:T(8,128)(2,1)S(1)} %get-tuple-element.38), channel_id=1, source_target_pairs={{0,6},{1,7},{2,4},{3,5},{4,2},{5,3},{6,0},{7,1},{8,14},{9,15},{10,... | collective-permute-start | bytes 331784 | tf_op jit(solution)/shard_map/ppermute | solution.py:350
  47.4 1.9 %collective-permute-start.10 = (bf16[32,1728]{1,0:T(8,128)(2,1)S(1)}, bf16[32,1728]{1,0:T(8,128)(2,1)S(1)}, u32[]{:S(2)}, u32[]{:S(2)}) collective-permute-start(bf16[32,1728]{1,0:T(8,128)(2,1)S(1)} %get-tuple-element.40), channel_id=1, source_target_pairs={{0,2},{1,3},{2,0},{3,1},{4,6},{5,7},{6,4},{7,5},{8,10},{9,11},{10,... | collective-permute-start | bytes 331784 | tf_op jit(solution)/shard_map/ppermute | solution.py:350
  49.3 3.4 %collective-permute-done.13.got_x = bf16[2,72,1152]{2,1,0:T(8,128)(2,1)S(1)} collective-permute-done((bf16[2,72,1152]{2,1,0:T(8,128)(2,1)S(1)}, bf16[2,72,1152]{2,1,0:T(8,128)(2,1)S(1)}, u32[]{:S(2)}, u32[]{:S(2)}) %collective-permute-start.13) | collective-permute-done | bytes 331808 | tf_op jit(solution)/shard_map/ppermute | solution.py:350
  52.7 1.2 %collective-permute-done.14.got_y = bf16[2,72,1152]{2,1,0:T(8,128)(2,1)S(1)} collective-permute-done((bf16[2,72,1152]{2,1,0:T(8,128)(2,1)S(1)}, bf16[2,72,1152]{2,1,0:T(8,128)(2,1)S(1)}, u32[]{:S(2)}, u32[]{:S(2)}) %collective-permute-start.14) | collective-permute-done | bytes 331808 | tf_op jit(solution)/shard_map/ppermute | solution.py:350
  54.1 0.6 collective-permute-start.15
  54.7 0.5 collective-permute-start.16
  55.2 1.1 %collective-permute-done.9.refs_1_ = bf16[32,1728]{1,0:T(8,128)(2,1)S(1)} collective-permute-done((bf16[32,1728]{1,0:T(8,128)(2,1)S(1)}, bf16[32,1728]{1,0:T(8,128)(2,1)S(1)}, u32[]{:S(2)}, u32[]{:S(2)}) %collective-permute-start.9) | collective-permute-done | bytes 110624 | tf_op jit(solution)/shard_map/ppermute | solution.py:350
  56.5 3.0 %collective-permute-done.15.got_y = bf16[72,1152]{1,0:T(8,128)(2,1)S(1)} collective-permute-done((bf16[72,1152]{1,0:T(8,128)(2,1)S(1)}, bf16[72,1152]{1,0:T(8,128)(2,1)S(1)}, u32[]{:S(2)}, u32[]{:S(2)}) %collective-permute-start.15) | collective-permute-done | bytes 165920 | tf_op jit(solution)/shard_map/ppermute | solution.py:350
  59.5 0.5 collective-permute-done.16.got_x
  60.0 0.2 shard_map.109
  60.2 2.5 %collective-permute-start.17 = (bf16[72,576]{1,0:T(8,128)(2,1)S(1)}, bf16[72,576]{1,0:T(8,128)(2,1)S(1)}, u32[]{:S(2)}, u32[]{:S(2)}) collective-permute-start(bf16[72,576]{1,0:T(8,128)(2,1)S(1)} %get-tuple-element.54), channel_id=1, source_target_pairs={{0,6},{1,7},{2,4},{3,5},{4,2},{5,3},{6,0},{7,1},{8,14},{9,15},{10,... | collective-permute-start | bytes 248840 | tf_op jit(solution)/shard_map/ppermute | solution.py:350
  62.8 1.9 %collective-permute-start.19 = (bf16[72,576]{1,0:T(8,128)(2,1)S(1)}, bf16[72,576]{1,0:T(8,128)(2,1)S(1)}, u32[]{:S(2)}, u32[]{:S(2)}) collective-permute-start(bf16[72,576]{1,0:T(8,128)(2,1)S(1)} %get-tuple-element.56), channel_id=1, source_target_pairs={{0,2},{1,3},{2,0},{3,1},{4,6},{5,7},{6,4},{7,5},{8,10},{9,11},{10,... | collective-permute-start | bytes 248840 | tf_op jit(solution)/shard_map/ppermute | solution.py:350
  64.7 4.0 %shard_map.106 = (bf16[128,1152]{1,0:T(8,128)(2,1)}, bf16[128,1152]{1,0:T(8,128)(2,1)}, bf16[128,1728]{1,0:T(8,128)(2,1)}) custom-call(bf16[32,1728]{1,0:T(8,128)(2,1)S(1)} %collective-permute-done.8.refs_0_, bf16[32,1728]{1,0:T(8,128)(2,1)S(1)} %collective-permute-done.9.refs_1_, bf16[32,1728]{1,0:T(8,128)(2,1)S(1)} %collective-permute-done.10.refs_2_, ...), custom_call_target="tpu_custom_call" | custom-call | tf_op jit(solution)/shard_map/pallas_call | solution.py:39
  68.7 0.7 %collective-permute-done.18.refs_1_ = bf16[72,576]{1,0:T(8,128)(2,1)S(1)} collective-permute-done((bf16[72,576]{1,0:T(8,128)(2,1)S(1)}, bf16[72,576]{1,0:T(8,128)(2,1)S(1)}, u32[]{:S(2)}, u32[]{:S(2)}) %collective-permute-start.18) | collective-permute-done | bytes 82976 | tf_op jit(solution)/shard_map/ppermute | solution.py:350
  69.5 0.8 %shard_map.110 = (f32[72,288]{1,0:T(8,128)}, f32[72,288]{1,0:T(8,128)}) custom-call(f32[72,576]{1,0:T(8,128)S(1)} %get-tuple-element.53.own, bf16[72,576]{1,0:T(8,128)(2,1)S(1)} %collective-permute-done.17.refs_0_, bf16[72,576]{1,0:T(8,128)(2,1)S(1)} %collective-permute-done.18.refs_1_, bf16[72,576]{1,0:T(8,128)(2,1)S(1)} %collective-permute-done.19.refs_2_), custom_call_target="tpu_custom_call" | custom-call | tf_op jit(solution)/shard_map/pallas_call | solution.py:39
  (32 shorter events, 0.6 us)
Async XLA Ops:
  0.6 15.4 %collective-permute-start.3 = (bf16[432,1152]{1,0:T(8,128)(2,1)}, bf16[432,1152]{1,0:T(8,128)(2,1)S(1)}, u32[]{:S(2)}, u32[]{:S(2)}) collective-permute-start(bf16[432,1152]{1,0:T(8,128)(2,1)} %bitcast.9), channel_id=1, source_target_pairs={{0,8},{1,17},{2,10},{3,19},{4,12},{5,21},{6,14},{7,23},{8,0},{9,25... | collective-permute-start | bytes 2985992 | tf_op jit(solution)/shard_map/ppermute | solution.py:362
  8.5 10.8 %collective-permute-start = (bf16[32,2944]{1,0:T(8,128)(2,1)}, bf16[32,2944]{1,0:T(8,128)(2,1)S(1)}, u32[]{:S(2)}, u32[]{:S(2)}) collective-permute-start(bf16[32,2944]{1,0:T(8,128)(2,1)} %get-tuple-element.32), channel_id=1, source_target_pairs={{0,6},{1,7},{2,4},{3,5},{4,2},{5,3},{6,0},{7,1},{8,14},{9,15},{10,... | collective-permute-start | bytes 565256 | tf_op jit(solution)/shard_map/ppermute | solution.py:350
  12.1 15.9 %collective-permute-start.1 = (bf16[32,2944]{1,0:T(8,128)(2,1)}, bf16[32,2944]{1,0:T(8,128)(2,1)S(1)}, u32[]{:S(2)}, u32[]{:S(2)}) collective-permute-start(bf16[32,2944]{1,0:T(8,128)(2,1)} %get-tuple-element.33), channel_id=1, source_target_pairs={{0,4},{1,5},{2,6},{3,7},{4,0},{5,1},{6,2},{7,3},{8,12},{9,13},{10,... | collective-permute-start | bytes 565256 | tf_op jit(solution)/shard_map/ppermute | solution.py:350
  12.1 15.9 %collective-permute-start.2 = (bf16[32,2944]{1,0:T(8,128)(2,1)}, bf16[32,2944]{1,0:T(8,128)(2,1)S(1)}, u32[]{:S(2)}, u32[]{:S(2)}) collective-permute-start(bf16[32,2944]{1,0:T(8,128)(2,1)} %get-tuple-element.34), channel_id=1, source_target_pairs={{0,2},{1,3},{2,0},{3,1},{4,6},{5,7},{6,4},{7,5},{8,10},{9,11},{10,... | collective-permute-start | bytes 565256 | tf_op jit(solution)/shard_map/ppermute | solution.py:350
  16.1 0.9 %copy-start.6 = (bf16[32,2944]{1,0:T(8,128)(2,1)S(1)}, bf16[32,2944]{1,0:T(8,128)(2,1)}, u32[]{:S(2)}) copy-start(bf16[32,2944]{1,0:T(8,128)(2,1)} %get-tuple-element.35.own) | copy-start | bytes 565252
  17.0 14.3 %copy-start.1 = (bf16[576,1152]{1,0:T(8,128)(2,1)S(1)}, bf16[576,1152]{1,0:T(8,128)(2,1)}, u32[]{:S(2)}) copy-start(bf16[576,1152]{1,0:T(8,128)(2,1)} %refs_8_.1) | copy-start | bytes 3981316
  17.0 14.3 %copy-start.3 = (bf16[1152,432]{0,1:T(8,128)(2,1)S(1)}, bf16[1152,432]{0,1:T(8,128)(2,1)}, u32[]{:S(2)}) copy-start(bf16[1152,432]{0,1:T(8,128)(2,1)} %param.9) | copy-start | bytes 2985988
  17.1 11.1 %collective-permute-start.6 = (bf16[216,1152]{1,0:T(8,128)(2,1)S(1)}, bf16[216,1152]{1,0:T(8,128)(2,1)S(1)}, u32[]{:S(2)}, u32[]{:S(2)}) collective-permute-start(bf16[216,1152]{1,0:T(8,128)(2,1)S(1)} %get-tuple-element.37), channel_id=1, source_target_pairs={{0,16},{1,9},{2,18},{3,11},{4,20},{5,13},{6,22},{7,15},{8,24},{9,1... | collective-permute-start | bytes 1493000 | tf_op jit(solution)/shard_map/ppermute | solution.py:362
  19.2 11.3 %collective-permute-start.5 = (bf16[432,1152]{1,0:T(8,128)(2,1)S(1)}, bf16[432,1152]{1,0:T(8,128)(2,1)S(1)}, u32[]{:S(2)}, u32[]{:S(2)}) collective-permute-start(bf16[432,1152]{1,0:T(8,128)(2,1)S(1)} %collective-permute-done.3.got.refs_1_), channel_id=1, source_target_pairs={{0,1},{1,0},{2,3},{3,2},{4,5},{5,4},{6,7},{7,6},{8,9},{9,8},{10,11... | collective-permute-start | bytes 2985992 | tf_op jit(solution)/shard_map/ppermute | solution.py:350
  28.1 2.4 %collective-permute-start.4 = (bf16[128,3200]{1,0:T(8,128)(2,1)S(1)}, bf16[128,3200]{1,0:T(8,128)(2,1)S(1)}, u32[]{:S(2)}, u32[]{:S(2)}) collective-permute-start(bf16[128,3200]{1,0:T(8,128)(2,1)S(1)} %shard_map.103.near.refs_0_), channel_id=1, source_target_pairs={{0,1},{1,0},{2,3},{3,2},{4,5},{5,4},{6,7},{7,6},{8,9},{9,8},{10,11... | collective-permute-start | bytes 2457608 | tf_op jit(solution)/shard_map/ppermute | solution.py:350
  28.2 3.0 %collective-permute-start.7 = (bf16[216,1152]{1,0:T(8,128)(2,1)S(1)}, bf16[216,1152]{1,0:T(8,128)(2,1)S(1)}, u32[]{:S(2)}, u32[]{:S(2)}) collective-permute-start(bf16[216,1152]{1,0:T(8,128)(2,1)S(1)} %collective-permute-done.6.refs_3_), channel_id=1, source_target_pairs={{0,1},{1,0},{2,3},{3,2},{4,5},{5,4},{6,7},{7,6},{8,9},{9,8},{10,11... | collective-permute-start | bytes 1493000 | tf_op jit(solution)/shard_map/ppermute | solution.py:350
  38.5 1.9 %collective-permute-start.12 = (bf16[128,1728]{1,0:T(8,128)(2,1)S(1)}, bf16[128,1728]{1,0:T(8,128)(2,1)S(1)}, u32[]{:S(2)}, u32[]{:S(2)}) collective-permute-start(bf16[128,1728]{1,0:T(8,128)(2,1)S(1)} %get-tuple-element.41.mine.refs_3_), channel_id=1, source_target_pairs={{0,1},{1,0},{2,3},{3,2},{4,5},{5,4},{6,7},{7,6},{8,9},{9,8},{10,11... | collective-permute-start | bytes 1327112 | tf_op jit(solution)/shard_map/ppermute | solution.py:350
  42.8 9.9 %collective-permute-start.13 = (bf16[2,72,1152]{2,1,0:T(8,128)(2,1)S(1)}, bf16[2,72,1152]{2,1,0:T(8,128)(2,1)S(1)}, u32[]{:S(2)}, u32[]{:S(2)}) collective-permute-start(bf16[2,72,1152]{2,1,0:T(8,128)(2,1)S(1)} %get-tuple-element.48), channel_id=1, source_target_pairs={{0,8},{8,0},{16,24},{24,16},{1,9},{9,1},{17,25},{25,17},{2,10},{10... | collective-permute-start | bytes 995336 | tf_op jit(solution)/shard_map/ppermute | solution.py:350
  44.4 9.6 %collective-permute-start.14 = (bf16[2,72,1152]{2,1,0:T(8,128)(2,1)S(1)}, bf16[2,72,1152]{2,1,0:T(8,128)(2,1)S(1)}, u32[]{:S(2)}, u32[]{:S(2)}) collective-permute-start(bf16[2,72,1152]{2,1,0:T(8,128)(2,1)S(1)} %get-tuple-element.49), channel_id=1, source_target_pairs={{0,16},{8,24},{16,0},{24,8},{1,17},{9,25},{17,1},{25,9},{2,18},{10... | collective-permute-start | bytes 995336 | tf_op jit(solution)/shard_map/ppermute | solution.py:350
  44.9 10.3 %collective-permute-start.8 = (bf16[32,1728]{1,0:T(8,128)(2,1)S(1)}, bf16[32,1728]{1,0:T(8,128)(2,1)S(1)}, u32[]{:S(2)}, u32[]{:S(2)}) collective-permute-start(bf16[32,1728]{1,0:T(8,128)(2,1)S(1)} %get-tuple-element.38), channel_id=1, source_target_pairs={{0,6},{1,7},{2,4},{3,5},{4,2},{5,3},{6,0},{7,1},{8,14},{9,15},{10,... | collective-permute-start | bytes 331784 | tf_op jit(solution)/shard_map/ppermute | solution.py:350
  47.4 8.9 %collective-permute-start.9 = (bf16[32,1728]{1,0:T(8,128)(2,1)S(1)}, bf16[32,1728]{1,0:T(8,128)(2,1)S(1)}, u32[]{:S(2)}, u32[]{:S(2)}) collective-permute-start(bf16[32,1728]{1,0:T(8,128)(2,1)S(1)} %get-tuple-element.39), channel_id=1, source_target_pairs={{0,4},{1,5},{2,6},{3,7},{4,0},{5,1},{6,2},{7,3},{8,12},{9,13},{10,... | collective-permute-start | bytes 331784 | tf_op jit(solution)/shard_map/ppermute | solution.py:350
  47.4 8.9 %collective-permute-start.10 = (bf16[32,1728]{1,0:T(8,128)(2,1)S(1)}, bf16[32,1728]{1,0:T(8,128)(2,1)S(1)}, u32[]{:S(2)}, u32[]{:S(2)}) collective-permute-start(bf16[32,1728]{1,0:T(8,128)(2,1)S(1)} %get-tuple-element.40), channel_id=1, source_target_pairs={{0,2},{1,3},{2,0},{3,1},{4,6},{5,7},{6,4},{7,5},{8,10},{9,11},{10,... | collective-permute-start | bytes 331784 | tf_op jit(solution)/shard_map/ppermute | solution.py:350
  54.0 10.7 %copy-start.4 = (f32[8,128,128]{2,1,0:T(8,128)S(1)}, f32[8,128,128]{2,1,0:T(8,128)}, u32[]{:S(2)}) copy-start(f32[8,128,128]{2,1,0:T(8,128)} %get-tuple-element.42.refs_7_) | copy-start | bytes 1572868
  54.0 10.7 %copy-start.5 = (bf16[128,1152]{1,0:T(8,128)(2,1)S(1)}, bf16[128,1152]{1,0:T(8,128)(2,1)}, u32[]{:S(2)}) copy-start(bf16[128,1152]{1,0:T(8,128)(2,1)} %get-tuple-element.43.refs_9_) | copy-start | bytes 884740
  54.1 10.6 %copy-start = (bf16[576,1152]{1,0:T(8,128)(2,1)S(1)}, bf16[576,1152]{1,0:T(8,128)(2,1)}, u32[]{:S(2)}) copy-start(bf16[576,1152]{1,0:T(8,128)(2,1)} %refs_5_.1) | copy-start | bytes 3981316
  54.1 10.6 %copy-start.2 = (bf16[2,64,1728]{2,1,0:T(8,128)(2,1)S(1)}, bf16[2,64,1728]{2,1,0:T(8,128)(2,1)}, u32[]{:S(2)}) copy-start(bf16[2,64,1728]{2,1,0:T(8,128)(2,1)} %param.7) | copy-start | bytes 1327108
  54.1 5.4 %collective-permute-start.15 = (bf16[72,1152]{1,0:T(8,128)(2,1)S(1)}, bf16[72,1152]{1,0:T(8,128)(2,1)S(1)}, u32[]{:S(2)}, u32[]{:S(2)}) collective-permute-start(bf16[72,1152]{1,0:T(8,128)(2,1)S(1)} %get-tuple-element.51), channel_id=1, source_target_pairs={{0,16},{8,24},{16,0},{24,8},{1,17},{9,25},{17,1},{25,9},{2,18},{10... | collective-permute-start | bytes 497672 | tf_op jit(solution)/shard_map/ppermute | solution.py:350
  54.7 5.3 %collective-permute-start.16 = (bf16[72,1152]{1,0:T(8,128)(2,1)S(1)}, bf16[72,1152]{1,0:T(8,128)(2,1)S(1)}, u32[]{:S(2)}, u32[]{:S(2)}) collective-permute-start(bf16[72,1152]{1,0:T(8,128)(2,1)S(1)} %get-tuple-element.52), channel_id=1, source_target_pairs={{0,8},{8,0},{16,24},{24,16},{1,9},{9,1},{17,25},{25,17},{2,10},{10... | collective-permute-start | bytes 497672 | tf_op jit(solution)/shard_map/ppermute | solution.py:350
  56.4 8.3 %collective-permute-start.11 = (bf16[64,1728]{1,0:T(8,128)(2,1)S(1)}, bf16[64,1728]{1,0:T(8,128)(2,1)S(1)}, u32[]{:S(2)}, u32[]{:S(2)}) collective-permute-start(bf16[64,1728]{1,0:T(8,128)(2,1)S(1)} %shard_map.105), channel_id=1, source_target_pairs={{0,1},{1,0},{2,3},{3,2},{4,5},{5,4},{6,7},{7,6},{8,9},{9,8},{10,11... | collective-permute-start | bytes 663560 | tf_op jit(solution)/shard_map/ppermute | solution.py:350
  60.2 8.5 %collective-permute-start.17 = (bf16[72,576]{1,0:T(8,128)(2,1)S(1)}, bf16[72,576]{1,0:T(8,128)(2,1)S(1)}, u32[]{:S(2)}, u32[]{:S(2)}) collective-permute-start(bf16[72,576]{1,0:T(8,128)(2,1)S(1)} %get-tuple-element.54), channel_id=1, source_target_pairs={{0,6},{1,7},{2,4},{3,5},{4,2},{5,3},{6,0},{7,1},{8,14},{9,15},{10,... | collective-permute-start | bytes 248840 | tf_op jit(solution)/shard_map/ppermute | solution.py:350
  62.8 6.7 %collective-permute-start.18 = (bf16[72,576]{1,0:T(8,128)(2,1)S(1)}, bf16[72,576]{1,0:T(8,128)(2,1)S(1)}, u32[]{:S(2)}, u32[]{:S(2)}) collective-permute-start(bf16[72,576]{1,0:T(8,128)(2,1)S(1)} %get-tuple-element.55), channel_id=1, source_target_pairs={{0,4},{1,5},{2,6},{3,7},{4,0},{5,1},{6,2},{7,3},{8,12},{9,13},{10,... | collective-permute-start | bytes 248840 | tf_op jit(solution)/shard_map/ppermute | solution.py:350
  62.8 6.7 %collective-permute-start.19 = (bf16[72,576]{1,0:T(8,128)(2,1)S(1)}, bf16[72,576]{1,0:T(8,128)(2,1)S(1)}, u32[]{:S(2)}, u32[]{:S(2)}) collective-permute-start(bf16[72,576]{1,0:T(8,128)(2,1)S(1)} %get-tuple-element.56), channel_id=1, source_target_pairs={{0,2},{1,3},{2,0},{3,1},{4,6},{5,7},{6,4},{7,5},{8,10},{9,11},{10,... | collective-permute-start | bytes 248840 | tf_op jit(solution)/shard_map/ppermute | solution.py:350

commit v12 on v11

--- a/solution.py
+++ b/solution.py
@@ -66,28 +66,18 @@
 TOKEN = shape((1,), jnp.int32)
 
 
-def window(head):
-    low = head * DH // LANES * LANES
-    high = -(-(head + 1) * DH // LANES) * LANES
-    return low, high
-
-
-def head_only(block, head):
-    low, high = window(head)
-    lane = lax.broadcasted_iota(jnp.int32, (1, high - low), 1) + low
-    keep = (lane >= head * DH) & (lane < (head + 1) * DH)
-    return jnp.where(keep, block, jnp.zeros_like(block))
-
-
-def add_tiles(tiles, head, value):
-    low, high = window(head)
-    for at in range(low // LANES, high // LANES):
-        part = value[:, at * LANES - low : (at + 1) * LANES - low]
-        tiles[at] = part if tiles[at] is None else tiles[at] + part
+def tile(value, head):
+    piece = value[:, head * DH : (head + 1) * DH]
+    return jnp.concatenate([piece, jnp.zeros((piece.shape[0], LANES - DH), piece.dtype)], axis=1)
+
+
+def spread(value, ref):
+    for head in range(ref.shape[0]):
+        ref[head] = tile(value, head)
 
 
 def joined(tiles):
-    return jnp.concatenate([tile.astype(BF16) for tile in tiles], axis=1)
+    return jnp.concatenate([part[:, :DH].astype(BF16) for part in tiles], axis=1)
 
 
 def same_group(rows, kind):
@@ -97,43 +87,30 @@
     return row // size == col // size if how == "block" else row % size == col % size
 
 
-def softmax_forward(q_ref, k_ref, v_ref, p_ref, heads, kind):
-    rows = q_ref.shape[0]
-    mask = same_group(rows, kind)
-    tiles = [None] * (q_ref.shape[1] // LANES)
+def softmax_forward(qkv, p_ref, kind):
+    heads = qkv.shape[0] // 3
+    mask = same_group(qkv.shape[1], kind)
+    outs = []
     for head in range(heads):
-        low, high = window(head)
-        s = dot_bt(q_ref[:, low:high], head_only(k_ref[:, low:high], head)) * (1.0 / math.sqrt(DH))
+        s = dot_bt(qkv[head], qkv[heads + head]) * (1.0 / math.sqrt(DH))
         s = jnp.where(mask, s, -jnp.inf)
         e = jnp.exp(s - jnp.max(s, axis=1, keepdims=True))
         p = e / jnp.sum(e, axis=1, keepdims=True)
         p_ref[head] = p
-        add_tiles(tiles, head, dot(p.astype(BF16), head_only(v_ref[:, low:high], head)))
-    return joined(tiles)
-
-
-def softmax_backward(q_ref, k_ref, v_ref, g_ref, p_ref, heads):
-    count = q_ref.shape[1] // LANES
-    dq, dk, dv = [None] * count, [None] * count, [None] * count
+        outs.append(dot(p.astype(BF16), qkv[2 * heads + head]))
+    return joined(outs)
+
+
+def softmax_backward(qkv, g_ref, p_ref, grads):
+    heads = qkv.shape[0] // 3
     for head in range(heads):
-        low, high = window(head)
-        p = p_ref[head]
-        g = head_only(g_ref[:, low:high], head)
-        add_tiles(dv, head, dot_at(p.astype(BF16), g))
-        dp = dot_bt(g, v_ref[:, low:high])
+        p, g = p_ref[head], g_ref[head]
+        grads[2 * heads + head] = dot_at(p.astype(BF16), g).astype(BF16)
+        dp = dot_bt(g, qkv[2 * heads + head])
         ds = p * (dp - jnp.sum(p * dp, axis=1, keepdims=True)) * (1.0 / math.sqrt(DH))
         ds = ds.astype(BF16)
-        add_tiles(dq, head, dot(ds, head_only(k_ref[:, low:high], head)))
-        add_tiles(dk, head, dot_at(ds, head_only(q_ref[:, low:high], head)))
-    return joined(dq), joined(dk), joined(dv)
-
-
-def put(ref, value):
-    width = value.shape[1]
-    ref[:, width // LANES * LANES :] = jnp.zeros(
-        (ref.shape[0], ref.shape[1] - width // LANES * LANES), ref.dtype
-    )
-    ref[:, :width] = value
+        grads[head] = dot(ds, qkv[heads + head]).astype(BF16)
+        grads[heads + head] = dot_at(ds, qkv[head]).astype(BF16)
 
 
 def place(chips):
@@ -144,16 +121,13 @@
 def spatial_kernel(chips, patches, *refs):
     idx = place(chips)
     far, outs, refs = refs[:4], refs[4 : 4 + chips], refs[4 + chips :]
-    hid_far, p_far, tok, cot, qkv, wos, held, hid, p_ref, qs, ks, vs, sems = refs
+    hid_far, p_far, tok, cot, qkv, wos, held, hid, p_ref, tiles, sems = refs
     inner, width = wos.shape
     count, block, _ = held.shape
     loads = started(zip(far, (qkv, tok, wos, cot)), sems)
     loads[0].wait()
-    x = qkv[...]
-    put(qs, x[:, :inner])
-    put(ks, x[:, inner : 2 * inner])
-    put(vs, x[:, 2 * inner :])
-    o = softmax_forward(qs, ks, vs, p_ref, inner // DH, ("block", patches))[:, :inner]
+    spread(qkv[...], tiles)
+    o = softmax_forward(tiles, p_ref, ("block", patches))
     stores = started([(p_ref, p_far)], sems.at[pl.ds(4, 1)])
     for at in range(3):
         loads[1 + at].wait()
@@ -196,39 +170,32 @@
 
 def join_rows_kernel(*refs):
     out, low = refs[-1], 0
-    for ref in refs[-2::-1]:
+    for ref in refs[:-1]:
         out[low : low + ref.shape[0], : ref.shape[1]] = ref[...]
         low += ref.shape[0]
 
 
-def temporal_kernel(shards, chips, group, near, far, wot, *refs):
+def temporal_kernel(shards, blocks, chips, group, near, far, wot, *refs):
     idx = place(chips)
     weights, refs = refs[: len(shards)], refs[len(shards) :]
-    (mine, *outs), (cot, q, k, v, g, p_ref, blocks) = refs[:chips], refs[chips:]
-    inner, width = wot.shape
-    heads = inner // DH
+    (mine, *outs), (cot, qkv, g, p_ref, grads) = refs[:chips], refs[chips:]
+    width = wot.shape[1]
     value = [own_patches(ref, idx[1], 2 * group) for ref in (near, far)]
     value = jnp.concatenate(value, axis=0).astype(BF16)
     hidden = value[:, :width]
     cot[...] = value[:, width : 2 * width]
-    size = blocks.shape[2]
+    count = qkv.shape[0] // blocks
     for at, w in zip(shards, weights):
         value = dot_bt(hidden, w[...]).astype(BF16)
         for i, block in enumerate(at(idx)):
-            blocks[block] = value[:, i * size : (i + 1) * size]
-    whole = jnp.concatenate([blocks[i] for i in range(blocks.shape[0])], axis=1)
-    put(q, whole[:, :inner])
-    put(k, whole[:, inner : 2 * inner])
-    put(v, whole[:, 2 * inner :])
-    mine[:, width:] = softmax_forward(q, k, v, p_ref, heads, ("cycle", group))[:, :inner]
-    put(g, dot_bt(cot[...], wot[...]).astype(BF16))
-    dq, dk, dv = softmax_backward(q, k, v, g, p_ref, heads)
-    whole = jnp.concatenate([dq[:, :inner], dk[:, :inner], dv[:, :inner]], axis=1)
-    for i in range(blocks.shape[0]):
-        blocks[i] = whole[:, i * size : (i + 1) * size]
+            for t in range(count):
+                qkv[block * count + t] = tile(value, i * count + t)
+    mine[:, width:] = softmax_forward(qkv, p_ref, ("cycle", group))
+    spread(dot_bt(cot[...], wot[...]).astype(BF16), g)
+    softmax_backward(qkv, g, p_ref, grads)
     grad = jnp.zeros(cot.shape, F32)
     for at, w in zip(shards, weights):
-        lhs = jnp.concatenate([blocks[block] for block in at(idx)], axis=1)
+        lhs = joined([grads[block * count + t] for block in at(idx) for t in range(count)])
         grad += dot(lhs, w[...])
     mine[:, :width] = (cot[...].astype(F32) + grad.astype(BF16).astype(F32)).astype(BF16)
     half = mine.shape[0] // 2
@@ -319,7 +286,7 @@
     idx = place(chips)
     held, got, refs = refs[:chips][::-1], refs[chips], refs[chips + 1 :]
     (wos, qkv, p_ref, wot, hid), refs = refs[:5], refs[5:]
-    block_far, out_far, grads_far, rows, block_out, grads, qs, ks, vs, gs, sems = refs
+    block_far, out_far, grads_far, rows, block_out, grads, tiles, gs, parts, sems = refs
     inner, width = wos.shape
     frames = rows.shape[0] // patches
     block = patches // chips
@@ -334,13 +301,10 @@
     stores = started([(rows.at[:, pl.ds(0, width)], out_far)], sems.at[pl.ds(0, 1)])
     block_out[...] = (hid[...].astype(F32) + dot(attended, wot[...])).astype(BF16)
     stores += started([(block_out, block_far)], sems.at[pl.ds(1, 1)])
-    put(gs, dot_bt(grad, wos[...]).astype(BF16))
-    x = qkv[...]
-    put(qs, x[:, :inner])
-    put(ks, x[:, inner : 2 * inner])
-    put(vs, x[:, 2 * inner :])
-    dq, dk, dv = softmax_backward(qs, ks, vs, gs, p_ref, inner // DH)
-    grads[...] = jnp.concatenate([dq[:, :inner], dk[:, :inner], dv[:, :inner]], axis=1)
+    spread(dot_bt(grad, wos[...]).astype(BF16), gs)
+    spread(qkv[...], tiles)
+    softmax_backward(tiles, gs, p_ref, parts)
+    grads[...] = joined([parts[i] for i in range(parts.shape[0])])
     stores += started([(grads, grads_far)], sems.at[pl.ds(2, 1)])
     for copy in stores:
         copy.wait()
@@ -367,7 +331,7 @@
     rows, sent = parts[0].shape
     whole = [shape((len(parts) * rows, sent + PAD))]
     if n != 4:
-        (near,) = call(join_rows_kernel, whole, from_chips(parts)[::-1], small=True)
+        (near,) = call(join_rows_kernel, whole, from_chips(parts), small=True)
         weights = [lax.all_gather(weight, "dp", axis=0, tiled=True)]
         return near, flip(near, "seq", 1), weights, [lambda idx: [0]], 1
     half, width = weight.shape[0] // 2, weight.shape[1]
@@ -379,7 +343,7 @@
         small=True,
     )
     corner = across(corner, (2, 1))
-    (near,) = call(join_rows_kernel, whole, [*from_chips(parts)[:0:-1], own], small=True)
+    (near,) = call(join_rows_kernel, whole, [own, *from_chips(parts)[1:]], small=True)
     weights = [weight, side, flip(side, "seq", 1), corner, flip(corner, "seq", 1)]
 
     def both(shard):
@@ -424,7 +388,6 @@
     frames, patches, width = tokens.shape
     inner = wo_spatial.shape[0]
     heads = inner // DH
-    padded = -(-inner // LANES) * LANES
     rows = frames * patches
     peers = FRAMES // frames
     chips = peers // 2
@@ -432,10 +395,12 @@
     block = 2 * group
     n_dp, n_seq = lax.axis_size("dp"), lax.axis_size("seq")
 
-    def held(columns, dtype=BF16):
-        return pltpu.VMEM((rows, columns), dtype)
-
-    wide = held(padded)
+    def held(columns):
+        return pltpu.VMEM((rows, columns), BF16)
+
+    def tiles(parts):
+        return pltpu.VMEM((parts * heads, rows, LANES), BF16)
+
     attended = pltpu.VMEM((heads, rows, rows), F32)
     projection = pltpu.VMEM((inner, width), BF16)
     per_chip = rows // chips
@@ -448,18 +413,16 @@
         [qkv_rows, tokens.reshape(rows, width), wo_spatial, cotangent.reshape(rows, width)],
         [held(width), held(width), held(3 * inner), projection]
         + [pltpu.VMEM((frames * chips, block, sent), BF16), held(width), attended]
-        + [wide] * 3
-        + [sems(6)],
+        + [tiles(3), sems(6)],
         far_in=range(4),
         far_out=(chips, chips + 1),
     )
     near, far, weights, places, count = gather(w_temporal.T, near, chips)
-    blocks = pltpu.VMEM((count, rows, 3 * inner // count), BF16)
     mine, *back = call(
-        functools.partial(temporal_kernel, places, chips, group),
+        functools.partial(temporal_kernel, places, count, chips, group),
         [shape((rows, width + inner))] + [shape((per_chip, width + inner))] * (chips - 1),
         [near, far, wo_temporal, *weights],
-        [held(width)] + [wide] * 4 + [attended, blocks],
+        [held(width), tiles(3), tiles(1), attended, tiles(3)],
         small=True,
     )
     other = flip(mine, "seq", 1)
@@ -493,7 +456,8 @@
         functools.partial(last_kernel, chips, patches),
         [shape((rows, width)), shape((rows, width)), shape((rows, 3 * inner))],
         [*back[::-1], flip(others, "seq", 1), wo_spatial, qkv_rows, spatial_p, wo_temporal, hidden],
-        [held(width + inner), held(width), held(3 * inner)] + [wide] * 4 + [sems(3)],
+        [held(width + inner), held(width), held(3 * inner)]
+        + [tiles(3), tiles(1), tiles(3), sems(3)],
         far_out=range(3),
         small=True,
     )

time: 70.4 us -> 72 us (1.023)
  Pallas kernels: 19.8 us -> 21.3 us
  waiting for transfers between devices: 26.3 us -> 24.9 us
  starting transfers between devices: 22.5 us -> 23.9 us
    pallas_call x10, Pallas kernels: 19.8 us -> 21.3 us  [call(): pl.pallas_call(body, out_shape=outs, in_specs=[HBM if i in far_in else sp...]
    ppermute x18, starting transfers between devices: 17.4 us -> 18.8 us  [flip(): lax.ppermute(value, axis, [(i, i ^ bit) for i in range(lax.axis_size(axis...]
    ppermute x2, waiting for transfers between devices: 3.13 us -> 1.85 us  [across(): return lax.ppermute(value, ('dp', 'seq'), pairs)]
  transfers between devices with their start and end apart: 20 -> 20, of which waited for: 11 -> 10; matrix products, arithmetic and copies ran while one was open for 0% -> 0% of each run, Pallas kernels for 13% -> 15%
where the time goes in v12:
time: 72 us; the launch traced here: 71.9 us
  waiting for transfers between devices  24.9 us (35%)
  starting transfers between devices  23.9 us (33%)
  Pallas kernels  21.3 us (30%)
  local copies, waits for them, and re-layouts  0.95 us (1%)
  between operations  0.78 us (1%)
    ppermute x18, waiting for transfers between devices, flip(): lax.ppermute(value, axis, [(i, i ^ bit) for i in range(lax.axis_size(axis...  23.1 us
    pallas_call x10, Pallas kernels, call(): pl.pallas_call(body, out_shape=outs, in_specs=[HBM if i in far_in else sp...  21.3 us
    ppermute x18, starting transfers between devices, flip(): lax.ppermute(value, axis, [(i, i ^ bit) for i in range(lax.axis_size(axis...  18.8 us
    ppermute x2, starting transfers between devices, across(): return lax.ppermute(value, ('dp', 'seq'), pairs)  5.12 us
    ppermute x2, waiting for transfers between devices, across(): return lax.ppermute(value, ('dp', 'seq'), pairs)  1.85 us
  transfers between devices with their start and end apart: 20, of which 10 were waited for; matrix products, arithmetic and copies ran while one was open for 0% of the time, Pallas kernels for 15%

profile of v12, /device:TPU:0, one launch (start us, length us, event | category | flops | bytes accessed | tf_op | source)
XLA Modules:
  0.0 71.9 jit_solution(8663731531255034282)
XLA Ops:
  0.6 3.0 %collective-permute-start = (bf16[432,1152]{1,0:T(8,128)(2,1)}, bf16[432,1152]{1,0:T(8,128)(2,1)S(1)}, u32[]{:S(2)}, u32[]{:S(2)}) collective-permute-start(bf16[432,1152]{1,0:T(8,128)(2,1)} %bitcast.9), channel_id=1, source_target_pairs={{0,8},{1,17},{2,10},{3,19},{4,12},{5,21},{6,14},{7,23},{8,0},{9,25... | collective-permute-start | bytes 2985992 | tf_op jit(solution)/shard_map/ppermute | solution.py:326
  3.6 6.1 %shard_map.101 = (bf16[32,2944]{1,0:T(8,128)(2,1)}, bf16[32,2944]{1,0:T(8,128)(2,1)}, bf16[32,2944]{1,0:T(8,128)(2,1)}, bf16[32,2944]{1,0:T(8,128)(2,1)}, bf16[1...) custom-call(bf16[128,1728]{1,0:T(8,128)(2,1)} %bitcast.7, bf16[128,1152]{1,0:T(8,128)(2,1)} %bitcast.11, ...), custom_call_target="tpu_custom_call" | custom-call | tf_op jit(solution)/shard_map/pallas_call | solution.py:39
  9.8 1.6 %collective-permute-start.1 = (bf16[32,2944]{1,0:T(8,128)(2,1)}, bf16[32,2944]{1,0:T(8,128)(2,1)S(1)}, u32[]{:S(2)}, u32[]{:S(2)}) collective-permute-start(bf16[32,2944]{1,0:T(8,128)(2,1)} %get-tuple-element.34), channel_id=1, source_target_pairs={{0,2},{1,3},{2,0},{3,1},{4,6},{5,7},{6,4},{7,5},{8,10},{9,11},{10,... | collective-permute-start | bytes 565256 | tf_op jit(solution)/shard_map/ppermute | solution.py:314
  11.4 2.6 %collective-permute-start.2 = (bf16[32,2944]{1,0:T(8,128)(2,1)}, bf16[32,2944]{1,0:T(8,128)(2,1)S(1)}, u32[]{:S(2)}, u32[]{:S(2)}) collective-permute-start(bf16[32,2944]{1,0:T(8,128)(2,1)} %get-tuple-element.35), channel_id=1, source_target_pairs={{0,4},{1,5},{2,6},{3,7},{4,0},{5,1},{6,2},{7,3},{8,12},{9,13},{10,... | collective-permute-start | bytes 565256 | tf_op jit(solution)/shard_map/ppermute | solution.py:314
  14.0 0.2 collective-permute-start.3
  14.2 1.8 %collective-permute-done.got.refs_1_ = bf16[432,1152]{1,0:T(8,128)(2,1)S(1)} collective-permute-done((bf16[432,1152]{1,0:T(8,128)(2,1)}, bf16[432,1152]{1,0:T(8,128)(2,1)S(1)}, u32[]{:S(2)}, u32[]{:S(2)}) %collective-permute-start) | collective-permute-done | bytes 995360 | tf_op jit(solution)/shard_map/ppermute | solution.py:326
  16.1 0.9 %copy-done.6 = bf16[32,2944]{1,0:T(8,128)(2,1)S(1)} copy-done((bf16[32,2944]{1,0:T(8,128)(2,1)S(1)}, bf16[32,2944]{1,0:T(8,128)(2,1)}, u32[]{:S(2)}) %copy-start.6) | copy-done | bytes 188440
  17.1 2.1 %collective-permute-start.6 = (bf16[216,1152]{1,0:T(8,128)(2,1)S(1)}, bf16[216,1152]{1,0:T(8,128)(2,1)S(1)}, u32[]{:S(2)}, u32[]{:S(2)}) collective-permute-start(bf16[216,1152]{1,0:T(8,128)(2,1)S(1)} %get-tuple-element.37), channel_id=1, source_target_pairs={{0,16},{1,9},{2,18},{3,11},{4,20},{5,13},{6,22},{7,15},{8,24},{9,1... | collective-permute-start | bytes 1493000 | tf_op jit(solution)/shard_map/ppermute | solution.py:326
  19.2 9.0 %collective-permute-done.2.refs_2_ = bf16[32,2944]{1,0:T(8,128)(2,1)S(1)} collective-permute-done((bf16[32,2944]{1,0:T(8,128)(2,1)}, bf16[32,2944]{1,0:T(8,128)(2,1)S(1)}, u32[]{:S(2)}, u32[]{:S(2)}) %collective-permute-start.2) | collective-permute-done | bytes 188448 | tf_op jit(solution)/shard_map/ppermute | solution.py:314
  28.4 0.5 collective-permute-start.7
  28.9 1.8 %collective-permute-done.4.far.refs_1_ = bf16[128,3200]{1,0:T(8,128)(2,1)S(1)} collective-permute-done((bf16[128,3200]{1,0:T(8,128)(2,1)S(1)}, bf16[128,3200]{1,0:T(8,128)(2,1)S(1)}, u32[]{:S(2)}, u32[]{:S(2)}) %collective-permute-start.4) | collective-permute-done | bytes 819232 | tf_op jit(solution)/shard_map/ppermute | solution.py:314
  30.7 0.7 collective-permute-done.7.refs_4_
  31.4 7.2 %shard_map.104 = (bf16[128,1728]{1,0:T(8,128)(2,1)S(1)}, bf16[32,1728]{1,0:T(8,128)(2,1)S(1)}, bf16[32,1728]{1,0:T(8,128)(2,1)S(1)}, bf16[32,1728]{1,0:T(8,128)(2,1)S(1)}) custom-call(bf16[128,3200]{1,0:T(8,128)(2,1)S(1)} %shard_map.103.near.refs_0_, bf16[128,3200]{1,0:T(8,128)(2,1)S(1)} %collective-permute-done.4.far.refs_1_, ...), custom_call_target="tpu_custom_call" | custom-call | tf_op jit(solution)/shard_map/pallas_call | solution.py:39
  38.6 0.2 collective-permute-start.12
  38.8 1.7 %collective-permute-done.12.other = bf16[128,1728]{1,0:T(8,128)(2,1)S(1)} collective-permute-done((bf16[128,1728]{1,0:T(8,128)(2,1)S(1)}, bf16[128,1728]{1,0:T(8,128)(2,1)S(1)}, u32[]{:S(2)}, u32[]{:S(2)}) %collective-permute-start.12) | collective-permute-done | bytes 442400 | tf_op jit(solution)/shard_map/ppermute | solution.py:314
  40.5 2.4 %shard_map.107 = (f32[4,72,1152]{2,1,0:T(8,128)S(1)}, bf16[2,72,1152]{2,1,0:T(8,128)(2,1)S(1)}, bf16[2,72,1152]{2,1,0:T(8,128)(2,1)S(1)}) custom-call(bf16[128,1728]{1,0:T(8,128)(2,1)S(1)} %get-tuple-element.41.mine.refs_3_, bf16[128,1728]{1,0:T(8,128)(2,1)S(1)} %collective-permute-done.12.other, bf16[128,3200]{1,0:T(8,128)(2,1)S(1)} %shard_map.103.near.refs_0_, ...), custom_call_target="tpu_custom_call" | custom-call | tf_op jit(solution)/shard_map/pallas_call | solution.py:39
  43.0 0.5 collective-permute-start.13
  43.5 1.6 %collective-permute-start.14 = (bf16[2,72,1152]{2,1,0:T(8,128)(2,1)S(1)}, bf16[2,72,1152]{2,1,0:T(8,128)(2,1)S(1)}, u32[]{:S(2)}, u32[]{:S(2)}) collective-permute-start(bf16[2,72,1152]{2,1,0:T(8,128)(2,1)S(1)} %get-tuple-element.49), channel_id=1, source_target_pairs={{0,16},{8,24},{16,0},{24,8},{1,17},{9,25},{17,1},{25,9},{2,18},{10... | collective-permute-start | bytes 995336 | tf_op jit(solution)/shard_map/ppermute | solution.py:314
  45.1 2.2 %collective-permute-start.8 = (bf16[32,1728]{1,0:T(8,128)(2,1)S(1)}, bf16[32,1728]{1,0:T(8,128)(2,1)S(1)}, u32[]{:S(2)}, u32[]{:S(2)}) collective-permute-start(bf16[32,1728]{1,0:T(8,128)(2,1)S(1)} %get-tuple-element.38), channel_id=1, source_target_pairs={{0,6},{1,7},{2,4},{3,5},{4,2},{5,3},{6,0},{7,1},{8,14},{9,15},{10,... | collective-permute-start | bytes 331784 | tf_op jit(solution)/shard_map/ppermute | solution.py:314
  47.3 2.1 %collective-permute-start.9 = (bf16[32,1728]{1,0:T(8,128)(2,1)S(1)}, bf16[32,1728]{1,0:T(8,128)(2,1)S(1)}, u32[]{:S(2)}, u32[]{:S(2)}) collective-permute-start(bf16[32,1728]{1,0:T(8,128)(2,1)S(1)} %get-tuple-element.39), channel_id=1, source_target_pairs={{0,4},{1,5},{2,6},{3,7},{4,0},{5,1},{6,2},{7,3},{8,12},{9,13},{10,... | collective-permute-start | bytes 331784 | tf_op jit(solution)/shard_map/ppermute | solution.py:314
  49.5 3.3 %collective-permute-done.13.got_x = bf16[2,72,1152]{2,1,0:T(8,128)(2,1)S(1)} collective-permute-done((bf16[2,72,1152]{2,1,0:T(8,128)(2,1)S(1)}, bf16[2,72,1152]{2,1,0:T(8,128)(2,1)S(1)}, u32[]{:S(2)}, u32[]{:S(2)}) %collective-permute-start.13) | collective-permute-done | bytes 331808 | tf_op jit(solution)/shard_map/ppermute | solution.py:314
  52.9 0.2 collective-permute-done.14.got_y
  53.2 1.7 %collective-permute-start.15 = (bf16[72,1152]{1,0:T(8,128)(2,1)S(1)}, bf16[72,1152]{1,0:T(8,128)(2,1)S(1)}, u32[]{:S(2)}, u32[]{:S(2)}) collective-permute-start(bf16[72,1152]{1,0:T(8,128)(2,1)S(1)} %get-tuple-element.51), channel_id=1, source_target_pairs={{0,16},{8,24},{16,0},{24,8},{1,17},{9,25},{17,1},{25,9},{2,18},{10... | collective-permute-start | bytes 497672 | tf_op jit(solution)/shard_map/ppermute | solution.py:314
  54.9 0.8 %collective-permute-start.16 = (bf16[72,1152]{1,0:T(8,128)(2,1)S(1)}, bf16[72,1152]{1,0:T(8,128)(2,1)S(1)}, u32[]{:S(2)}, u32[]{:S(2)}) collective-permute-start(bf16[72,1152]{1,0:T(8,128)(2,1)S(1)} %get-tuple-element.52), channel_id=1, source_target_pairs={{0,8},{8,0},{16,24},{24,16},{1,9},{9,1},{17,25},{25,17},{2,10},{10... | collective-permute-start | bytes 497672 | tf_op jit(solution)/shard_map/ppermute | solution.py:314
  55.7 3.2 %collective-permute-done.9.refs_1_ = bf16[32,1728]{1,0:T(8,128)(2,1)S(1)} collective-permute-done((bf16[32,1728]{1,0:T(8,128)(2,1)S(1)}, bf16[32,1728]{1,0:T(8,128)(2,1)S(1)}, u32[]{:S(2)}, u32[]{:S(2)}) %collective-permute-start.9) | collective-permute-done | bytes 110624 | tf_op jit(solution)/shard_map/ppermute | solution.py:314
  59.0 1.2 %collective-permute-done.16.got_x = bf16[72,1152]{1,0:T(8,128)(2,1)S(1)} collective-permute-done((bf16[72,1152]{1,0:T(8,128)(2,1)S(1)}, bf16[72,1152]{1,0:T(8,128)(2,1)S(1)}, u32[]{:S(2)}, u32[]{:S(2)}) %collective-permute-start.16) | collective-permute-done | bytes 165920 | tf_op jit(solution)/shard_map/ppermute | solution.py:314
  60.2 0.2 shard_map.109
  60.4 2.3 %collective-permute-start.17 = (bf16[72,576]{1,0:T(8,128)(2,1)S(1)}, bf16[72,576]{1,0:T(8,128)(2,1)S(1)}, u32[]{:S(2)}, u32[]{:S(2)}) collective-permute-start(bf16[72,576]{1,0:T(8,128)(2,1)S(1)} %get-tuple-element.54), channel_id=1, source_target_pairs={{0,6},{1,7},{2,4},{3,5},{4,2},{5,3},{6,0},{7,1},{8,14},{9,15},{10,... | collective-permute-start | bytes 248840 | tf_op jit(solution)/shard_map/ppermute | solution.py:314
  62.7 2.1 %collective-permute-start.18 = (bf16[72,576]{1,0:T(8,128)(2,1)S(1)}, bf16[72,576]{1,0:T(8,128)(2,1)S(1)}, u32[]{:S(2)}, u32[]{:S(2)}) collective-permute-start(bf16[72,576]{1,0:T(8,128)(2,1)S(1)} %get-tuple-element.55), channel_id=1, source_target_pairs={{0,4},{1,5},{2,6},{3,7},{4,0},{5,1},{6,2},{7,3},{8,12},{9,13},{10,... | collective-permute-start | bytes 248840 | tf_op jit(solution)/shard_map/ppermute | solution.py:314
  64.9 4.3 %shard_map.106 = (bf16[128,1152]{1,0:T(8,128)(2,1)}, bf16[128,1152]{1,0:T(8,128)(2,1)}, bf16[128,1728]{1,0:T(8,128)(2,1)}) custom-call(bf16[32,1728]{1,0:T(8,128)(2,1)S(1)} %collective-permute-done.8.refs_0_, bf16[32,1728]{1,0:T(8,128)(2,1)S(1)} %collective-permute-done.9.refs_1_, bf16[32,1728]{1,0:T(8,128)(2,1)S(1)} %collective-permute-done.10.refs_2_, ...), custom_call_target="tpu_custom_call" | custom-call | tf_op jit(solution)/shard_map/pallas_call | solution.py:39
  69.3 1.8 %collective-permute-done.18.refs_1_ = bf16[72,576]{1,0:T(8,128)(2,1)S(1)} collective-permute-done((bf16[72,576]{1,0:T(8,128)(2,1)S(1)}, bf16[72,576]{1,0:T(8,128)(2,1)S(1)}, u32[]{:S(2)}, u32[]{:S(2)}) %collective-permute-start.18) | collective-permute-done | bytes 82976 | tf_op jit(solution)/shard_map/ppermute | solution.py:314
  71.1 0.8 %shard_map.110 = (f32[72,288]{1,0:T(8,128)}, f32[72,288]{1,0:T(8,128)}) custom-call(f32[72,576]{1,0:T(8,128)S(1)} %get-tuple-element.53.own, bf16[72,576]{1,0:T(8,128)(2,1)S(1)} %collective-permute-done.17.refs_0_, bf16[72,576]{1,0:T(8,128)(2,1)S(1)} %collective-permute-done.18.refs_1_, bf16[72,576]{1,0:T(8,128)(2,1)S(1)} %collective-permute-done.19.refs_2_), custom_call_target="tpu_custom_call" | custom-call | tf_op jit(solution)/shard_map/pallas_call | solution.py:39
  (32 shorter events, 0.8 us)
Async XLA Ops:
  0.6 15.4 %collective-permute-start = (bf16[432,1152]{1,0:T(8,128)(2,1)}, bf16[432,1152]{1,0:T(8,128)(2,1)S(1)}, u32[]{:S(2)}, u32[]{:S(2)}) collective-permute-start(bf16[432,1152]{1,0:T(8,128)(2,1)} %bitcast.9), channel_id=1, source_target_pairs={{0,8},{1,17},{2,10},{3,19},{4,12},{5,21},{6,14},{7,23},{8,0},{9,25... | collective-permute-start | bytes 2985992 | tf_op jit(solution)/shard_map/ppermute | solution.py:326
  9.8 9.5 %collective-permute-start.1 = (bf16[32,2944]{1,0:T(8,128)(2,1)}, bf16[32,2944]{1,0:T(8,128)(2,1)S(1)}, u32[]{:S(2)}, u32[]{:S(2)}) collective-permute-start(bf16[32,2944]{1,0:T(8,128)(2,1)} %get-tuple-element.34), channel_id=1, source_target_pairs={{0,2},{1,3},{2,0},{3,1},{4,6},{5,7},{6,4},{7,5},{8,10},{9,11},{10,... | collective-permute-start | bytes 565256 | tf_op jit(solution)/shard_map/ppermute | solution.py:314
  11.4 16.9 %collective-permute-start.2 = (bf16[32,2944]{1,0:T(8,128)(2,1)}, bf16[32,2944]{1,0:T(8,128)(2,1)S(1)}, u32[]{:S(2)}, u32[]{:S(2)}) collective-permute-start(bf16[32,2944]{1,0:T(8,128)(2,1)} %get-tuple-element.35), channel_id=1, source_target_pairs={{0,4},{1,5},{2,6},{3,7},{4,0},{5,1},{6,2},{7,3},{8,12},{9,13},{10,... | collective-permute-start | bytes 565256 | tf_op jit(solution)/shard_map/ppermute | solution.py:314
  14.0 14.3 %collective-permute-start.3 = (bf16[32,2944]{1,0:T(8,128)(2,1)}, bf16[32,2944]{1,0:T(8,128)(2,1)S(1)}, u32[]{:S(2)}, u32[]{:S(2)}) collective-permute-start(bf16[32,2944]{1,0:T(8,128)(2,1)} %get-tuple-element.36), channel_id=1, source_target_pairs={{0,6},{1,7},{2,4},{3,5},{4,2},{5,3},{6,0},{7,1},{8,14},{9,15},{10,... | collective-permute-start | bytes 565256 | tf_op jit(solution)/shard_map/ppermute | solution.py:314
  16.1 0.9 %copy-start.6 = (bf16[32,2944]{1,0:T(8,128)(2,1)S(1)}, bf16[32,2944]{1,0:T(8,128)(2,1)}, u32[]{:S(2)}) copy-start(bf16[32,2944]{1,0:T(8,128)(2,1)} %get-tuple-element.32.own) | copy-start | bytes 565252
  17.0 14.4 %copy-start.1 = (bf16[576,1152]{1,0:T(8,128)(2,1)S(1)}, bf16[576,1152]{1,0:T(8,128)(2,1)}, u32[]{:S(2)}) copy-start(bf16[576,1152]{1,0:T(8,128)(2,1)} %refs_8_.1) | copy-start | bytes 3981316
  17.0 14.4 %copy-start.3 = (bf16[1152,432]{0,1:T(8,128)(2,1)S(1)}, bf16[1152,432]{0,1:T(8,128)(2,1)}, u32[]{:S(2)}) copy-start(bf16[1152,432]{0,1:T(8,128)(2,1)} %param.9) | copy-start | bytes 2985988
  17.1 11.3 %collective-permute-start.6 = (bf16[216,1152]{1,0:T(8,128)(2,1)S(1)}, bf16[216,1152]{1,0:T(8,128)(2,1)S(1)}, u32[]{:S(2)}, u32[]{:S(2)}) collective-permute-start(bf16[216,1152]{1,0:T(8,128)(2,1)S(1)} %get-tuple-element.37), channel_id=1, source_target_pairs={{0,16},{1,9},{2,18},{3,11},{4,20},{5,13},{6,22},{7,15},{8,24},{9,1... | collective-permute-start | bytes 1493000 | tf_op jit(solution)/shard_map/ppermute | solution.py:326
  19.2 11.5 %collective-permute-start.5 = (bf16[432,1152]{1,0:T(8,128)(2,1)S(1)}, bf16[432,1152]{1,0:T(8,128)(2,1)S(1)}, u32[]{:S(2)}, u32[]{:S(2)}) collective-permute-start(bf16[432,1152]{1,0:T(8,128)(2,1)S(1)} %collective-permute-done.got.refs_1_), channel_id=1, source_target_pairs={{0,1},{1,0},{2,3},{3,2},{4,5},{5,4},{6,7},{7,6},{8,9},{9,8},{10,11... | collective-permute-start | bytes 2985992 | tf_op jit(solution)/shard_map/ppermute | solution.py:314
  28.3 2.4 %collective-permute-start.4 = (bf16[128,3200]{1,0:T(8,128)(2,1)S(1)}, bf16[128,3200]{1,0:T(8,128)(2,1)S(1)}, u32[]{:S(2)}, u32[]{:S(2)}) collective-permute-start(bf16[128,3200]{1,0:T(8,128)(2,1)S(1)} %shard_map.103.near.refs_0_), channel_id=1, source_target_pairs={{0,1},{1,0},{2,3},{3,2},{4,5},{5,4},{6,7},{7,6},{8,9},{9,8},{10,11... | collective-permute-start | bytes 2457608 | tf_op jit(solution)/shard_map/ppermute | solution.py:314
  28.4 3.0 %collective-permute-start.7 = (bf16[216,1152]{1,0:T(8,128)(2,1)S(1)}, bf16[216,1152]{1,0:T(8,128)(2,1)S(1)}, u32[]{:S(2)}, u32[]{:S(2)}) collective-permute-start(bf16[216,1152]{1,0:T(8,128)(2,1)S(1)} %collective-permute-done.6.refs_3_), channel_id=1, source_target_pairs={{0,1},{1,0},{2,3},{3,2},{4,5},{5,4},{6,7},{7,6},{8,9},{9,8},{10,11... | collective-permute-start | bytes 1493000 | tf_op jit(solution)/shard_map/ppermute | solution.py:314
  38.6 1.9 %collective-permute-start.12 = (bf16[128,1728]{1,0:T(8,128)(2,1)S(1)}, bf16[128,1728]{1,0:T(8,128)(2,1)S(1)}, u32[]{:S(2)}, u32[]{:S(2)}) collective-permute-start(bf16[128,1728]{1,0:T(8,128)(2,1)S(1)} %get-tuple-element.41.mine.refs_3_), channel_id=1, source_target_pairs={{0,1},{1,0},{2,3},{3,2},{4,5},{5,4},{6,7},{7,6},{8,9},{9,8},{10,11... | collective-permute-start | bytes 1327112 | tf_op jit(solution)/shard_map/ppermute | solution.py:314
  43.0 9.9 %collective-permute-start.13 = (bf16[2,72,1152]{2,1,0:T(8,128)(2,1)S(1)}, bf16[2,72,1152]{2,1,0:T(8,128)(2,1)S(1)}, u32[]{:S(2)}, u32[]{:S(2)}) collective-permute-start(bf16[2,72,1152]{2,1,0:T(8,128)(2,1)S(1)} %get-tuple-element.48), channel_id=1, source_target_pairs={{0,8},{8,0},{16,24},{24,16},{1,9},{9,1},{17,25},{25,17},{2,10},{10... | collective-permute-start | bytes 995336 | tf_op jit(solution)/shard_map/ppermute | solution.py:314
  43.5 9.6 %collective-permute-start.14 = (bf16[2,72,1152]{2,1,0:T(8,128)(2,1)S(1)}, bf16[2,72,1152]{2,1,0:T(8,128)(2,1)S(1)}, u32[]{:S(2)}, u32[]{:S(2)}) collective-permute-start(bf16[2,72,1152]{2,1,0:T(8,128)(2,1)S(1)} %get-tuple-element.49), channel_id=1, source_target_pairs={{0,16},{8,24},{16,0},{24,8},{1,17},{9,25},{17,1},{25,9},{2,18},{10... | collective-permute-start | bytes 995336 | tf_op jit(solution)/shard_map/ppermute | solution.py:314
  45.1 10.6 %collective-permute-start.8 = (bf16[32,1728]{1,0:T(8,128)(2,1)S(1)}, bf16[32,1728]{1,0:T(8,128)(2,1)S(1)}, u32[]{:S(2)}, u32[]{:S(2)}) collective-permute-start(bf16[32,1728]{1,0:T(8,128)(2,1)S(1)} %get-tuple-element.38), channel_id=1, source_target_pairs={{0,6},{1,7},{2,4},{3,5},{4,2},{5,3},{6,0},{7,1},{8,14},{9,15},{10,... | collective-permute-start | bytes 331784 | tf_op jit(solution)/shard_map/ppermute | solution.py:314
  47.3 11.6 %collective-permute-start.9 = (bf16[32,1728]{1,0:T(8,128)(2,1)S(1)}, bf16[32,1728]{1,0:T(8,128)(2,1)S(1)}, u32[]{:S(2)}, u32[]{:S(2)}) collective-permute-start(bf16[32,1728]{1,0:T(8,128)(2,1)S(1)} %get-tuple-element.39), channel_id=1, source_target_pairs={{0,4},{1,5},{2,6},{3,7},{4,0},{5,1},{6,2},{7,3},{8,12},{9,13},{10,... | collective-permute-start | bytes 331784 | tf_op jit(solution)/shard_map/ppermute | solution.py:314
  49.4 9.5 %collective-permute-start.10 = (bf16[32,1728]{1,0:T(8,128)(2,1)S(1)}, bf16[32,1728]{1,0:T(8,128)(2,1)S(1)}, u32[]{:S(2)}, u32[]{:S(2)}) collective-permute-start(bf16[32,1728]{1,0:T(8,128)(2,1)S(1)} %get-tuple-element.40), channel_id=1, source_target_pairs={{0,2},{1,3},{2,0},{3,1},{4,6},{5,7},{6,4},{7,5},{8,10},{9,11},{10,... | collective-permute-start | bytes 331784 | tf_op jit(solution)/shard_map/ppermute | solution.py:314
  53.1 11.9 %copy-start.4 = (f32[8,128,128]{2,1,0:T(8,128)S(1)}, f32[8,128,128]{2,1,0:T(8,128)}, u32[]{:S(2)}) copy-start(f32[8,128,128]{2,1,0:T(8,128)} %get-tuple-element.42.refs_7_) | copy-start | bytes 1572868
  53.1 11.9 %copy-start.5 = (bf16[128,1152]{1,0:T(8,128)(2,1)S(1)}, bf16[128,1152]{1,0:T(8,128)(2,1)}, u32[]{:S(2)}) copy-start(bf16[128,1152]{1,0:T(8,128)(2,1)} %get-tuple-element.43.refs_9_) | copy-start | bytes 884740
  53.2 11.7 %copy-start = (bf16[576,1152]{1,0:T(8,128)(2,1)S(1)}, bf16[576,1152]{1,0:T(8,128)(2,1)}, u32[]{:S(2)}) copy-start(bf16[576,1152]{1,0:T(8,128)(2,1)} %refs_5_.1) | copy-start | bytes 3981316
  53.2 11.7 %copy-start.2 = (bf16[2,64,1728]{2,1,0:T(8,128)(2,1)S(1)}, bf16[2,64,1728]{2,1,0:T(8,128)(2,1)}, u32[]{:S(2)}) copy-start(bf16[2,64,1728]{2,1,0:T(8,128)(2,1)} %param.7) | copy-start | bytes 1327108
  53.2 5.8 %collective-permute-start.15 = (bf16[72,1152]{1,0:T(8,128)(2,1)S(1)}, bf16[72,1152]{1,0:T(8,128)(2,1)S(1)}, u32[]{:S(2)}, u32[]{:S(2)}) collective-permute-start(bf16[72,1152]{1,0:T(8,128)(2,1)S(1)} %get-tuple-element.51), channel_id=1, source_target_pairs={{0,16},{8,24},{16,0},{24,8},{1,17},{9,25},{17,1},{25,9},{2,18},{10... | collective-permute-start | bytes 497672 | tf_op jit(solution)/shard_map/ppermute | solution.py:314
  54.9 5.3 %collective-permute-start.16 = (bf16[72,1152]{1,0:T(8,128)(2,1)S(1)}, bf16[72,1152]{1,0:T(8,128)(2,1)S(1)}, u32[]{:S(2)}, u32[]{:S(2)}) collective-permute-start(bf16[72,1152]{1,0:T(8,128)(2,1)S(1)} %get-tuple-element.52), channel_id=1, source_target_pairs={{0,8},{8,0},{16,24},{24,16},{1,9},{9,1},{17,25},{25,17},{2,10},{10... | collective-permute-start | bytes 497672 | tf_op jit(solution)/shard_map/ppermute | solution.py:314
  58.9 6.0 %collective-permute-start.11 = (bf16[64,1728]{1,0:T(8,128)(2,1)S(1)}, bf16[64,1728]{1,0:T(8,128)(2,1)S(1)}, u32[]{:S(2)}, u32[]{:S(2)}) collective-permute-start(bf16[64,1728]{1,0:T(8,128)(2,1)S(1)} %shard_map.105), channel_id=1, source_target_pairs={{0,1},{1,0},{2,3},{3,2},{4,5},{5,4},{6,7},{7,6},{8,9},{9,8},{10,11... | collective-permute-start | bytes 663560 | tf_op jit(solution)/shard_map/ppermute | solution.py:314
  60.4 8.9 %collective-permute-start.17 = (bf16[72,576]{1,0:T(8,128)(2,1)S(1)}, bf16[72,576]{1,0:T(8,128)(2,1)S(1)}, u32[]{:S(2)}, u32[]{:S(2)}) collective-permute-start(bf16[72,576]{1,0:T(8,128)(2,1)S(1)} %get-tuple-element.54), channel_id=1, source_target_pairs={{0,6},{1,7},{2,4},{3,5},{4,2},{5,3},{6,0},{7,1},{8,14},{9,15},{10,... | collective-permute-start | bytes 248840 | tf_op jit(solution)/shard_map/ppermute | solution.py:314
  62.7 8.4 %collective-permute-start.18 = (bf16[72,576]{1,0:T(8,128)(2,1)S(1)}, bf16[72,576]{1,0:T(8,128)(2,1)S(1)}, u32[]{:S(2)}, u32[]{:S(2)}) collective-permute-start(bf16[72,576]{1,0:T(8,128)(2,1)S(1)} %get-tuple-element.55), channel_id=1, source_target_pairs={{0,4},{1,5},{2,6},{3,7},{4,0},{5,1},{6,2},{7,3},{8,12},{9,13},{10,... | collective-permute-start | bytes 248840 | tf_op jit(solution)/shard_map/ppermute | solution.py:314
  64.8 6.3 %collective-permute-start.19 = (bf16[72,576]{1,0:T(8,128)(2,1)S(1)}, bf16[72,576]{1,0:T(8,128)(2,1)S(1)}, u32[]{:S(2)}, u32[]{:S(2)}) collective-permute-start(bf16[72,576]{1,0:T(8,128)(2,1)S(1)} %get-tuple-element.56), channel_id=1, source_target_pairs={{0,2},{1,3},{2,0},{3,1},{4,6},{5,7},{6,4},{7,5},{8,10},{9,11},{10,... | collective-permute-start | bytes 248840 | tf_op jit(solution)/shard_map/ppermute | solution.py:314

commit v13 on v11

--- a/solution.py
+++ b/solution.py
@@ -18,7 +18,7 @@
 HBM = pl.BlockSpec(memory_space=pltpu.HBM)
 PAD = 2 * LANES
 LIMIT = 16 * 1024 * 1024
-MOST = 60 * 1024 * 1024
+MOST = 53 * 1024 * 1024
 
 
 def dot(left, right):
@@ -196,7 +196,7 @@
 
 def join_rows_kernel(*refs):
     out, low = refs[-1], 0
-    for ref in refs[-2::-1]:
+    for ref in refs[:-1]:
         out[low : low + ref.shape[0], : ref.shape[1]] = ref[...]
         low += ref.shape[0]
 
@@ -367,7 +367,7 @@
     rows, sent = parts[0].shape
     whole = [shape((len(parts) * rows, sent + PAD))]
     if n != 4:
-        (near,) = call(join_rows_kernel, whole, from_chips(parts)[::-1], small=True)
+        (near,) = call(join_rows_kernel, whole, from_chips(parts), small=True)
         weights = [lax.all_gather(weight, "dp", axis=0, tiled=True)]
         return near, flip(near, "seq", 1), weights, [lambda idx: [0]], 1
     half, width = weight.shape[0] // 2, weight.shape[1]
@@ -379,7 +379,7 @@
         small=True,
     )
     corner = across(corner, (2, 1))
-    (near,) = call(join_rows_kernel, whole, [*from_chips(parts)[:0:-1], own], small=True)
+    (near,) = call(join_rows_kernel, whole, [own, *from_chips(parts)[1:]], small=True)
     weights = [weight, side, flip(side, "seq", 1), corner, flip(corner, "seq", 1)]
 
     def both(shard):

time: 70.4 us -> 69.9 us (level)
  starting transfers between devices: 22.5 us -> 23.9 us
  local copies, waits for them, and re-layouts: 0.95 us -> 0.03 us
  Pallas kernels: 19.8 us -> 18.9 us
    ppermute x18, starting transfers between devices: 17.4 us -> 18.8 us  [flip(): lax.ppermute(value, axis, [(i, i ^ bit) for i in range(lax.axis_size(axis...]
    unnamed x14 -> x12, local copies, waits for them, and re-layouts: 0.95 us -> 0.03 us
    ppermute x18, waiting for transfers between devices: 23.1 us -> 22.2 us  [flip(): lax.ppermute(value, axis, [(i, i ^ bit) for i in range(lax.axis_size(axis...]
    ppermute x2, waiting for transfers between devices: 3.13 us -> 4 us  [across(): return lax.ppermute(value, ('dp', 'seq'), pairs)]
    pallas_call x10, Pallas kernels: 19.8 us -> 18.9 us  [call(): pl.pallas_call(body, out_shape=outs, in_specs=[HBM if i in far_in else sp...]
  transfers between devices with their start and end apart: 20 -> 20, of which waited for: 11 -> 10; matrix products, arithmetic and copies ran while one was open for 0% -> 0% of each run, Pallas kernels for 13% -> 12%
where the time goes in v13:
time: 69.9 us; the launch traced here: 69.8 us
  waiting for transfers between devices  26.2 us (37%)
  starting transfers between devices  23.9 us (34%)
  Pallas kernels  18.9 us (27%)
  between operations  0.78 us (1%)
    ppermute x18, waiting for transfers between devices, flip(): lax.ppermute(value, axis, [(i, i ^ bit) for i in range(lax.axis_size(axis...  22.2 us
    pallas_call x10, Pallas kernels, call(): pl.pallas_call(body, out_shape=outs, in_specs=[HBM if i in far_in else sp...  18.9 us
    ppermute x18, starting transfers between devices, flip(): lax.ppermute(value, axis, [(i, i ^ bit) for i in range(lax.axis_size(axis...  18.8 us
    ppermute x2, starting transfers between devices, across(): return lax.ppermute(value, ('dp', 'seq'), pairs)  5.12 us
    ppermute x2, waiting for transfers between devices, across(): return lax.ppermute(value, ('dp', 'seq'), pairs)  4 us
  transfers between devices with their start and end apart: 20, of which 10 were waited for; matrix products, arithmetic and copies ran while one was open for 0% of the time, Pallas kernels for 12%

profile of v13, /device:TPU:0, one launch (start us, length us, event | category | flops | bytes accessed | tf_op | source)
XLA Modules:
  0.0 69.8 jit_solution(6523772144990662633)
XLA Ops:
  0.6 3.0 %collective-permute-start = (bf16[432,1152]{1,0:T(8,128)(2,1)}, bf16[432,1152]{1,0:T(8,128)(2,1)S(1)}, u32[]{:S(2)}, u32[]{:S(2)}) collective-permute-start(bf16[432,1152]{1,0:T(8,128)(2,1)} %bitcast.9), channel_id=1, source_target_pairs={{0,8},{1,17},{2,10},{3,19},{4,12},{5,21},{6,14},{7,23},{8,0},{9,25... | collective-permute-start | bytes 2985992 | tf_op jit(solution)/shard_map/ppermute | solution.py:362
  3.6 4.0 %shard_map.101 = (bf16[32,2944]{1,0:T(8,128)(2,1)S(1)}, bf16[32,2944]{1,0:T(8,128)(2,1)S(1)}, bf16[32,2944]{1,0:T(8,128)(2,1)S(1)}, bf16[32,2944]{1,0:T(8,128)(2...) custom-call(bf16[128,1728]{1,0:T(8,128)(2,1)} %bitcast.7, bf16[128,1152]{1,0:T(8,128)(2,1)} %bitcast.11, ...), custom_call_target="tpu_custom_call" | custom-call | tf_op jit(solution)/shard_map/pallas_call | solution.py:39
  7.6 1.6 %collective-permute-start.1 = (bf16[32,2944]{1,0:T(8,128)(2,1)S(1)}, bf16[32,2944]{1,0:T(8,128)(2,1)S(1)}, u32[]{:S(2)}, u32[]{:S(2)}) collective-permute-start(bf16[32,2944]{1,0:T(8,128)(2,1)S(1)} %get-tuple-element.34), channel_id=1, source_target_pairs={{0,2},{1,3},{2,0},{3,1},{4,6},{5,7},{6,4},{7,5},{8,10},{9,11},{10,... | collective-permute-start | bytes 565256 | tf_op jit(solution)/shard_map/ppermute | solution.py:350
  9.2 2.6 %collective-permute-start.2 = (bf16[32,2944]{1,0:T(8,128)(2,1)S(1)}, bf16[32,2944]{1,0:T(8,128)(2,1)S(1)}, u32[]{:S(2)}, u32[]{:S(2)}) collective-permute-start(bf16[32,2944]{1,0:T(8,128)(2,1)S(1)} %get-tuple-element.35), channel_id=1, source_target_pairs={{0,4},{1,5},{2,6},{3,7},{4,0},{5,1},{6,2},{7,3},{8,12},{9,13},{10,... | collective-permute-start | bytes 565256 | tf_op jit(solution)/shard_map/ppermute | solution.py:350
  11.8 0.2 collective-permute-start.3
  12.1 4.0 %collective-permute-done.got.refs_1_ = bf16[432,1152]{1,0:T(8,128)(2,1)S(1)} collective-permute-done((bf16[432,1152]{1,0:T(8,128)(2,1)}, bf16[432,1152]{1,0:T(8,128)(2,1)S(1)}, u32[]{:S(2)}, u32[]{:S(2)}) %collective-permute-start) | collective-permute-done | bytes 995360 | tf_op jit(solution)/shard_map/ppermute | solution.py:362
  16.2 2.1 %collective-permute-start.6 = (bf16[216,1152]{1,0:T(8,128)(2,1)S(1)}, bf16[216,1152]{1,0:T(8,128)(2,1)S(1)}, u32[]{:S(2)}, u32[]{:S(2)}) collective-permute-start(bf16[216,1152]{1,0:T(8,128)(2,1)S(1)} %get-tuple-element.37), channel_id=1, source_target_pairs={{0,16},{1,9},{2,18},{3,11},{4,20},{5,13},{6,22},{7,15},{8,24},{9,1... | collective-permute-start | bytes 1493000 | tf_op jit(solution)/shard_map/ppermute | solution.py:362
  18.3 7.6 %collective-permute-done.2.refs_2_ = bf16[32,2944]{1,0:T(8,128)(2,1)S(1)} collective-permute-done((bf16[32,2944]{1,0:T(8,128)(2,1)S(1)}, bf16[32,2944]{1,0:T(8,128)(2,1)S(1)}, u32[]{:S(2)}, u32[]{:S(2)}) %collective-permute-start.2) | collective-permute-done | bytes 188448 | tf_op jit(solution)/shard_map/ppermute | solution.py:350
  26.0 0.5 collective-permute-start.7
  26.5 1.8 %collective-permute-done.4.far.refs_1_ = bf16[128,3200]{1,0:T(8,128)(2,1)S(1)} collective-permute-done((bf16[128,3200]{1,0:T(8,128)(2,1)S(1)}, bf16[128,3200]{1,0:T(8,128)(2,1)S(1)}, u32[]{:S(2)}, u32[]{:S(2)}) %collective-permute-start.4) | collective-permute-done | bytes 819232 | tf_op jit(solution)/shard_map/ppermute | solution.py:350
  28.3 0.7 %collective-permute-done.7.refs_4_ = bf16[216,1152]{1,0:T(8,128)(2,1)S(1)} collective-permute-done((bf16[216,1152]{1,0:T(8,128)(2,1)S(1)}, bf16[216,1152]{1,0:T(8,128)(2,1)S(1)}, u32[]{:S(2)}, u32[]{:S(2)}) %collective-permute-start.7) | collective-permute-done | bytes 497696 | tf_op jit(solution)/shard_map/ppermute | solution.py:350
  29.1 7.3 %shard_map.104 = (bf16[128,1728]{1,0:T(8,128)(2,1)S(1)}, bf16[32,1728]{1,0:T(8,128)(2,1)S(1)}, bf16[32,1728]{1,0:T(8,128)(2,1)S(1)}, bf16[32,1728]{1,0:T(8,128)(2,1)S(1)}) custom-call(bf16[128,3200]{1,0:T(8,128)(2,1)S(1)} %shard_map.103.near.refs_0_, bf16[128,3200]{1,0:T(8,128)(2,1)S(1)} %collective-permute-done.4.far.refs_1_, ...), custom_call_target="tpu_custom_call" | custom-call | tf_op jit(solution)/shard_map/pallas_call | solution.py:39
  36.3 0.2 collective-permute-start.12
  36.5 1.7 %collective-permute-done.12.other = bf16[128,1728]{1,0:T(8,128)(2,1)S(1)} collective-permute-done((bf16[128,1728]{1,0:T(8,128)(2,1)S(1)}, bf16[128,1728]{1,0:T(8,128)(2,1)S(1)}, u32[]{:S(2)}, u32[]{:S(2)}) %collective-permute-start.12) | collective-permute-done | bytes 442400 | tf_op jit(solution)/shard_map/ppermute | solution.py:350
  38.2 2.4 %shard_map.107 = (f32[4,72,1152]{2,1,0:T(8,128)S(1)}, bf16[2,72,1152]{2,1,0:T(8,128)(2,1)S(1)}, bf16[2,72,1152]{2,1,0:T(8,128)(2,1)S(1)}) custom-call(bf16[128,1728]{1,0:T(8,128)(2,1)S(1)} %get-tuple-element.41.mine.refs_3_, bf16[128,1728]{1,0:T(8,128)(2,1)S(1)} %collective-permute-done.12.other, bf16[128,3200]{1,0:T(8,128)(2,1)S(1)} %shard_map.103.near.refs_0_, ...), custom_call_target="tpu_custom_call" | custom-call | tf_op jit(solution)/shard_map/pallas_call | solution.py:39
  40.6 0.5 collective-permute-start.13
  41.2 1.6 %collective-permute-start.14 = (bf16[2,72,1152]{2,1,0:T(8,128)(2,1)S(1)}, bf16[2,72,1152]{2,1,0:T(8,128)(2,1)S(1)}, u32[]{:S(2)}, u32[]{:S(2)}) collective-permute-start(bf16[2,72,1152]{2,1,0:T(8,128)(2,1)S(1)} %get-tuple-element.49), channel_id=1, source_target_pairs={{0,16},{8,24},{16,0},{24,8},{1,17},{9,25},{17,1},{25,9},{2,18},{10... | collective-permute-start | bytes 995336 | tf_op jit(solution)/shard_map/ppermute | solution.py:350
  42.8 3.1 %collective-permute-start.8 = (bf16[32,1728]{1,0:T(8,128)(2,1)S(1)}, bf16[32,1728]{1,0:T(8,128)(2,1)S(1)}, u32[]{:S(2)}, u32[]{:S(2)}) collective-permute-start(bf16[32,1728]{1,0:T(8,128)(2,1)S(1)} %get-tuple-element.38), channel_id=1, source_target_pairs={{0,6},{1,7},{2,4},{3,5},{4,2},{5,3},{6,0},{7,1},{8,14},{9,15},{10,... | collective-permute-start | bytes 331784 | tf_op jit(solution)/shard_map/ppermute | solution.py:350
  45.8 1.3 %collective-permute-start.9 = (bf16[32,1728]{1,0:T(8,128)(2,1)S(1)}, bf16[32,1728]{1,0:T(8,128)(2,1)S(1)}, u32[]{:S(2)}, u32[]{:S(2)}) collective-permute-start(bf16[32,1728]{1,0:T(8,128)(2,1)S(1)} %get-tuple-element.39), channel_id=1, source_target_pairs={{0,4},{1,5},{2,6},{3,7},{4,0},{5,1},{6,2},{7,3},{8,12},{9,13},{10,... | collective-permute-start | bytes 331784 | tf_op jit(solution)/shard_map/ppermute | solution.py:350
  47.2 3.3 %collective-permute-done.13.got_x = bf16[2,72,1152]{2,1,0:T(8,128)(2,1)S(1)} collective-permute-done((bf16[2,72,1152]{2,1,0:T(8,128)(2,1)S(1)}, bf16[2,72,1152]{2,1,0:T(8,128)(2,1)S(1)}, u32[]{:S(2)}, u32[]{:S(2)}) %collective-permute-start.13) | collective-permute-done | bytes 331808 | tf_op jit(solution)/shard_map/ppermute | solution.py:350
  50.5 0.2 collective-permute-done.14.got_y
  50.7 0.1 shard_map.108
  50.9 1.6 %collective-permute-start.15 = (bf16[72,1152]{1,0:T(8,128)(2,1)S(1)}, bf16[72,1152]{1,0:T(8,128)(2,1)S(1)}, u32[]{:S(2)}, u32[]{:S(2)}) collective-permute-start(bf16[72,1152]{1,0:T(8,128)(2,1)S(1)} %get-tuple-element.51), channel_id=1, source_target_pairs={{0,16},{8,24},{16,0},{24,8},{1,17},{9,25},{17,1},{25,9},{2,18},{10... | collective-permute-start | bytes 497672 | tf_op jit(solution)/shard_map/ppermute | solution.py:350
  52.6 0.8 %collective-permute-start.16 = (bf16[72,1152]{1,0:T(8,128)(2,1)S(1)}, bf16[72,1152]{1,0:T(8,128)(2,1)S(1)}, u32[]{:S(2)}, u32[]{:S(2)}) collective-permute-start(bf16[72,1152]{1,0:T(8,128)(2,1)S(1)} %get-tuple-element.52), channel_id=1, source_target_pairs={{0,8},{8,0},{16,24},{24,16},{1,9},{9,1},{17,25},{25,17},{2,10},{10... | collective-permute-start | bytes 497672 | tf_op jit(solution)/shard_map/ppermute | solution.py:350
  53.3 3.2 %collective-permute-done.9.refs_1_ = bf16[32,1728]{1,0:T(8,128)(2,1)S(1)} collective-permute-done((bf16[32,1728]{1,0:T(8,128)(2,1)S(1)}, bf16[32,1728]{1,0:T(8,128)(2,1)S(1)}, u32[]{:S(2)}, u32[]{:S(2)}) %collective-permute-start.9) | collective-permute-done | bytes 110624 | tf_op jit(solution)/shard_map/ppermute | solution.py:350
  56.7 1.2 %collective-permute-done.16.got_x = bf16[72,1152]{1,0:T(8,128)(2,1)S(1)} collective-permute-done((bf16[72,1152]{1,0:T(8,128)(2,1)S(1)}, bf16[72,1152]{1,0:T(8,128)(2,1)S(1)}, u32[]{:S(2)}, u32[]{:S(2)}) %collective-permute-start.16) | collective-permute-done | bytes 165920 | tf_op jit(solution)/shard_map/ppermute | solution.py:350
  57.9 0.2 shard_map.109
  58.1 3.1 %collective-permute-start.17 = (bf16[72,576]{1,0:T(8,128)(2,1)S(1)}, bf16[72,576]{1,0:T(8,128)(2,1)S(1)}, u32[]{:S(2)}, u32[]{:S(2)}) collective-permute-start(bf16[72,576]{1,0:T(8,128)(2,1)S(1)} %get-tuple-element.54), channel_id=1, source_target_pairs={{0,6},{1,7},{2,4},{3,5},{4,2},{5,3},{6,0},{7,1},{8,14},{9,15},{10,... | collective-permute-start | bytes 248840 | tf_op jit(solution)/shard_map/ppermute | solution.py:350
  61.2 1.3 %collective-permute-start.18 = (bf16[72,576]{1,0:T(8,128)(2,1)S(1)}, bf16[72,576]{1,0:T(8,128)(2,1)S(1)}, u32[]{:S(2)}, u32[]{:S(2)}) collective-permute-start(bf16[72,576]{1,0:T(8,128)(2,1)S(1)} %get-tuple-element.55), channel_id=1, source_target_pairs={{0,4},{1,5},{2,6},{3,7},{4,0},{5,1},{6,2},{7,3},{8,12},{9,13},{10,... | collective-permute-start | bytes 248840 | tf_op jit(solution)/shard_map/ppermute | solution.py:350
  62.6 4.0 %shard_map.106 = (bf16[128,1152]{1,0:T(8,128)(2,1)}, bf16[128,1152]{1,0:T(8,128)(2,1)}, bf16[128,1728]{1,0:T(8,128)(2,1)}) custom-call(bf16[32,1728]{1,0:T(8,128)(2,1)S(1)} %collective-permute-done.8.refs_0_, bf16[32,1728]{1,0:T(8,128)(2,1)S(1)} %collective-permute-done.9.refs_1_, bf16[32,1728]{1,0:T(8,128)(2,1)S(1)} %collective-permute-done.10.refs_2_, ...), custom_call_target="tpu_custom_call" | custom-call | tf_op jit(solution)/shard_map/pallas_call | solution.py:39
  66.6 2.4 %collective-permute-done.18.refs_1_ = bf16[72,576]{1,0:T(8,128)(2,1)S(1)} collective-permute-done((bf16[72,576]{1,0:T(8,128)(2,1)S(1)}, bf16[72,576]{1,0:T(8,128)(2,1)S(1)}, u32[]{:S(2)}, u32[]{:S(2)}) %collective-permute-start.18) | collective-permute-done | bytes 82976 | tf_op jit(solution)/shard_map/ppermute | solution.py:350
  69.0 0.8 %shard_map.110 = (f32[72,288]{1,0:T(8,128)}, f32[72,288]{1,0:T(8,128)}) custom-call(f32[72,576]{1,0:T(8,128)S(1)} %get-tuple-element.53.own, bf16[72,576]{1,0:T(8,128)(2,1)S(1)} %collective-permute-done.17.refs_0_, bf16[72,576]{1,0:T(8,128)(2,1)S(1)} %collective-permute-done.18.refs_1_, bf16[72,576]{1,0:T(8,128)(2,1)S(1)} %collective-permute-done.19.refs_2_), custom_call_target="tpu_custom_call" | custom-call | tf_op jit(solution)/shard_map/pallas_call | solution.py:39
  (30 shorter events, 0.6 us)
Async XLA Ops:
  0.6 15.4 %collective-permute-start = (bf16[432,1152]{1,0:T(8,128)(2,1)}, bf16[432,1152]{1,0:T(8,128)(2,1)S(1)}, u32[]{:S(2)}, u32[]{:S(2)}) collective-permute-start(bf16[432,1152]{1,0:T(8,128)(2,1)} %bitcast.9), channel_id=1, source_target_pairs={{0,8},{1,17},{2,10},{3,19},{4,12},{5,21},{6,14},{7,23},{8,0},{9,25... | collective-permute-start | bytes 2985992 | tf_op jit(solution)/shard_map/ppermute | solution.py:362
  7.6 10.7 %collective-permute-start.1 = (bf16[32,2944]{1,0:T(8,128)(2,1)S(1)}, bf16[32,2944]{1,0:T(8,128)(2,1)S(1)}, u32[]{:S(2)}, u32[]{:S(2)}) collective-permute-start(bf16[32,2944]{1,0:T(8,128)(2,1)S(1)} %get-tuple-element.34), channel_id=1, source_target_pairs={{0,2},{1,3},{2,0},{3,1},{4,6},{5,7},{6,4},{7,5},{8,10},{9,11},{10,... | collective-permute-start | bytes 565256 | tf_op jit(solution)/shard_map/ppermute | solution.py:350
  9.2 16.6 %collective-permute-start.2 = (bf16[32,2944]{1,0:T(8,128)(2,1)S(1)}, bf16[32,2944]{1,0:T(8,128)(2,1)S(1)}, u32[]{:S(2)}, u32[]{:S(2)}) collective-permute-start(bf16[32,2944]{1,0:T(8,128)(2,1)S(1)} %get-tuple-element.35), channel_id=1, source_target_pairs={{0,4},{1,5},{2,6},{3,7},{4,0},{5,1},{6,2},{7,3},{8,12},{9,13},{10,... | collective-permute-start | bytes 565256 | tf_op jit(solution)/shard_map/ppermute | solution.py:350
  11.8 14.1 %collective-permute-start.3 = (bf16[32,2944]{1,0:T(8,128)(2,1)S(1)}, bf16[32,2944]{1,0:T(8,128)(2,1)S(1)}, u32[]{:S(2)}, u32[]{:S(2)}) collective-permute-start(bf16[32,2944]{1,0:T(8,128)(2,1)S(1)} %get-tuple-element.36), channel_id=1, source_target_pairs={{0,6},{1,7},{2,4},{3,5},{4,2},{5,3},{6,0},{7,1},{8,14},{9,15},{10,... | collective-permute-start | bytes 565256 | tf_op jit(solution)/shard_map/ppermute | solution.py:350
  16.1 13.0 %copy-start.1 = (bf16[576,1152]{1,0:T(8,128)(2,1)S(1)}, bf16[576,1152]{1,0:T(8,128)(2,1)}, u32[]{:S(2)}) copy-start(bf16[576,1152]{1,0:T(8,128)(2,1)} %refs_8_.1) | copy-start | bytes 3981316
  16.1 13.0 %copy-start.3 = (bf16[1152,432]{0,1:T(8,128)(2,1)S(1)}, bf16[1152,432]{0,1:T(8,128)(2,1)}, u32[]{:S(2)}) copy-start(bf16[1152,432]{0,1:T(8,128)(2,1)} %param.9) | copy-start | bytes 2985988
  16.2 9.8 %collective-permute-start.6 = (bf16[216,1152]{1,0:T(8,128)(2,1)S(1)}, bf16[216,1152]{1,0:T(8,128)(2,1)S(1)}, u32[]{:S(2)}, u32[]{:S(2)}) collective-permute-start(bf16[216,1152]{1,0:T(8,128)(2,1)S(1)} %get-tuple-element.37), channel_id=1, source_target_pairs={{0,16},{1,9},{2,18},{3,11},{4,20},{5,13},{6,22},{7,15},{8,24},{9,1... | collective-permute-start | bytes 1493000 | tf_op jit(solution)/shard_map/ppermute | solution.py:362
  18.3 10.0 %collective-permute-start.5 = (bf16[432,1152]{1,0:T(8,128)(2,1)S(1)}, bf16[432,1152]{1,0:T(8,128)(2,1)S(1)}, u32[]{:S(2)}, u32[]{:S(2)}) collective-permute-start(bf16[432,1152]{1,0:T(8,128)(2,1)S(1)} %collective-permute-done.got.refs_1_), channel_id=1, source_target_pairs={{0,1},{1,0},{2,3},{3,2},{4,5},{5,4},{6,7},{7,6},{8,9},{9,8},{10,11... | collective-permute-start | bytes 2985992 | tf_op jit(solution)/shard_map/ppermute | solution.py:350
  25.9 2.4 %collective-permute-start.4 = (bf16[128,3200]{1,0:T(8,128)(2,1)S(1)}, bf16[128,3200]{1,0:T(8,128)(2,1)S(1)}, u32[]{:S(2)}, u32[]{:S(2)}) collective-permute-start(bf16[128,3200]{1,0:T(8,128)(2,1)S(1)} %shard_map.103.near.refs_0_), channel_id=1, source_target_pairs={{0,1},{1,0},{2,3},{3,2},{4,5},{5,4},{6,7},{7,6},{8,9},{9,8},{10,11... | collective-permute-start | bytes 2457608 | tf_op jit(solution)/shard_map/ppermute | solution.py:350
  26.0 3.0 %collective-permute-start.7 = (bf16[216,1152]{1,0:T(8,128)(2,1)S(1)}, bf16[216,1152]{1,0:T(8,128)(2,1)S(1)}, u32[]{:S(2)}, u32[]{:S(2)}) collective-permute-start(bf16[216,1152]{1,0:T(8,128)(2,1)S(1)} %collective-permute-done.6.refs_3_), channel_id=1, source_target_pairs={{0,1},{1,0},{2,3},{3,2},{4,5},{5,4},{6,7},{7,6},{8,9},{9,8},{10,11... | collective-permute-start | bytes 1493000 | tf_op jit(solution)/shard_map/ppermute | solution.py:350
  36.3 1.9 %collective-permute-start.12 = (bf16[128,1728]{1,0:T(8,128)(2,1)S(1)}, bf16[128,1728]{1,0:T(8,128)(2,1)S(1)}, u32[]{:S(2)}, u32[]{:S(2)}) collective-permute-start(bf16[128,1728]{1,0:T(8,128)(2,1)S(1)} %get-tuple-element.41.mine.refs_3_), channel_id=1, source_target_pairs={{0,1},{1,0},{2,3},{3,2},{4,5},{5,4},{6,7},{7,6},{8,9},{9,8},{10,11... | collective-permute-start | bytes 1327112 | tf_op jit(solution)/shard_map/ppermute | solution.py:350
  40.6 9.9 %collective-permute-start.13 = (bf16[2,72,1152]{2,1,0:T(8,128)(2,1)S(1)}, bf16[2,72,1152]{2,1,0:T(8,128)(2,1)S(1)}, u32[]{:S(2)}, u32[]{:S(2)}) collective-permute-start(bf16[2,72,1152]{2,1,0:T(8,128)(2,1)S(1)} %get-tuple-element.48), channel_id=1, source_target_pairs={{0,8},{8,0},{16,24},{24,16},{1,9},{9,1},{17,25},{25,17},{2,10},{10... | collective-permute-start | bytes 995336 | tf_op jit(solution)/shard_map/ppermute | solution.py:350
  41.2 9.6 %collective-permute-start.14 = (bf16[2,72,1152]{2,1,0:T(8,128)(2,1)S(1)}, bf16[2,72,1152]{2,1,0:T(8,128)(2,1)S(1)}, u32[]{:S(2)}, u32[]{:S(2)}) collective-permute-start(bf16[2,72,1152]{2,1,0:T(8,128)(2,1)S(1)} %get-tuple-element.49), channel_id=1, source_target_pairs={{0,16},{8,24},{16,0},{24,8},{1,17},{9,25},{17,1},{25,9},{2,18},{10... | collective-permute-start | bytes 995336 | tf_op jit(solution)/shard_map/ppermute | solution.py:350
  42.8 10.6 %collective-permute-start.8 = (bf16[32,1728]{1,0:T(8,128)(2,1)S(1)}, bf16[32,1728]{1,0:T(8,128)(2,1)S(1)}, u32[]{:S(2)}, u32[]{:S(2)}) collective-permute-start(bf16[32,1728]{1,0:T(8,128)(2,1)S(1)} %get-tuple-element.38), channel_id=1, source_target_pairs={{0,6},{1,7},{2,4},{3,5},{4,2},{5,3},{6,0},{7,1},{8,14},{9,15},{10,... | collective-permute-start | bytes 331784 | tf_op jit(solution)/shard_map/ppermute | solution.py:350
  45.8 10.7 %collective-permute-start.9 = (bf16[32,1728]{1,0:T(8,128)(2,1)S(1)}, bf16[32,1728]{1,0:T(8,128)(2,1)S(1)}, u32[]{:S(2)}, u32[]{:S(2)}) collective-permute-start(bf16[32,1728]{1,0:T(8,128)(2,1)S(1)} %get-tuple-element.39), channel_id=1, source_target_pairs={{0,4},{1,5},{2,6},{3,7},{4,0},{5,1},{6,2},{7,3},{8,12},{9,13},{10,... | collective-permute-start | bytes 331784 | tf_op jit(solution)/shard_map/ppermute | solution.py:350
  47.1 9.5 %collective-permute-start.10 = (bf16[32,1728]{1,0:T(8,128)(2,1)S(1)}, bf16[32,1728]{1,0:T(8,128)(2,1)S(1)}, u32[]{:S(2)}, u32[]{:S(2)}) collective-permute-start(bf16[32,1728]{1,0:T(8,128)(2,1)S(1)} %get-tuple-element.40), channel_id=1, source_target_pairs={{0,2},{1,3},{2,0},{3,1},{4,6},{5,7},{6,4},{7,5},{8,10},{9,11},{10,... | collective-permute-start | bytes 331784 | tf_op jit(solution)/shard_map/ppermute | solution.py:350
  50.7 11.9 %copy-start.4 = (f32[8,128,128]{2,1,0:T(8,128)S(1)}, f32[8,128,128]{2,1,0:T(8,128)}, u32[]{:S(2)}) copy-start(f32[8,128,128]{2,1,0:T(8,128)} %get-tuple-element.42.refs_7_) | copy-start | bytes 1572868
  50.7 11.9 %copy-start.5 = (bf16[128,1152]{1,0:T(8,128)(2,1)S(1)}, bf16[128,1152]{1,0:T(8,128)(2,1)}, u32[]{:S(2)}) copy-start(bf16[128,1152]{1,0:T(8,128)(2,1)} %get-tuple-element.43.refs_9_) | copy-start | bytes 884740
  50.9 11.7 %copy-start = (bf16[576,1152]{1,0:T(8,128)(2,1)S(1)}, bf16[576,1152]{1,0:T(8,128)(2,1)}, u32[]{:S(2)}) copy-start(bf16[576,1152]{1,0:T(8,128)(2,1)} %refs_5_.1) | copy-start | bytes 3981316
  50.9 11.7 %copy-start.2 = (bf16[2,64,1728]{2,1,0:T(8,128)(2,1)S(1)}, bf16[2,64,1728]{2,1,0:T(8,128)(2,1)}, u32[]{:S(2)}) copy-start(bf16[2,64,1728]{2,1,0:T(8,128)(2,1)} %param.7) | copy-start | bytes 1327108
  50.9 5.8 %collective-permute-start.15 = (bf16[72,1152]{1,0:T(8,128)(2,1)S(1)}, bf16[72,1152]{1,0:T(8,128)(2,1)S(1)}, u32[]{:S(2)}, u32[]{:S(2)}) collective-permute-start(bf16[72,1152]{1,0:T(8,128)(2,1)S(1)} %get-tuple-element.51), channel_id=1, source_target_pairs={{0,16},{8,24},{16,0},{24,8},{1,17},{9,25},{17,1},{25,9},{2,18},{10... | collective-permute-start | bytes 497672 | tf_op jit(solution)/shard_map/ppermute | solution.py:350
  52.6 5.3 %collective-permute-start.16 = (bf16[72,1152]{1,0:T(8,128)(2,1)S(1)}, bf16[72,1152]{1,0:T(8,128)(2,1)S(1)}, u32[]{:S(2)}, u32[]{:S(2)}) collective-permute-start(bf16[72,1152]{1,0:T(8,128)(2,1)S(1)} %get-tuple-element.52), channel_id=1, source_target_pairs={{0,8},{8,0},{16,24},{24,16},{1,9},{9,1},{17,25},{25,17},{2,10},{10... | collective-permute-start | bytes 497672 | tf_op jit(solution)/shard_map/ppermute | solution.py:350
  56.6 6.0 %collective-permute-start.11 = (bf16[64,1728]{1,0:T(8,128)(2,1)S(1)}, bf16[64,1728]{1,0:T(8,128)(2,1)S(1)}, u32[]{:S(2)}, u32[]{:S(2)}) collective-permute-start(bf16[64,1728]{1,0:T(8,128)(2,1)S(1)} %shard_map.105), channel_id=1, source_target_pairs={{0,1},{1,0},{2,3},{3,2},{4,5},{5,4},{6,7},{7,6},{8,9},{9,8},{10,11... | collective-permute-start | bytes 663560 | tf_op jit(solution)/shard_map/ppermute | solution.py:350
  58.1 8.5 %collective-permute-start.17 = (bf16[72,576]{1,0:T(8,128)(2,1)S(1)}, bf16[72,576]{1,0:T(8,128)(2,1)S(1)}, u32[]{:S(2)}, u32[]{:S(2)}) collective-permute-start(bf16[72,576]{1,0:T(8,128)(2,1)S(1)} %get-tuple-element.54), channel_id=1, source_target_pairs={{0,6},{1,7},{2,4},{3,5},{4,2},{5,3},{6,0},{7,1},{8,14},{9,15},{10,... | collective-permute-start | bytes 248840 | tf_op jit(solution)/shard_map/ppermute | solution.py:350
  61.2 7.8 %collective-permute-start.18 = (bf16[72,576]{1,0:T(8,128)(2,1)S(1)}, bf16[72,576]{1,0:T(8,128)(2,1)S(1)}, u32[]{:S(2)}, u32[]{:S(2)}) collective-permute-start(bf16[72,576]{1,0:T(8,128)(2,1)S(1)} %get-tuple-element.55), channel_id=1, source_target_pairs={{0,4},{1,5},{2,6},{3,7},{4,0},{5,1},{6,2},{7,3},{8,12},{9,13},{10,... | collective-permute-start | bytes 248840 | tf_op jit(solution)/shard_map/ppermute | solution.py:350
  62.5 6.6 %collective-permute-start.19 = (bf16[72,576]{1,0:T(8,128)(2,1)S(1)}, bf16[72,576]{1,0:T(8,128)(2,1)S(1)}, u32[]{:S(2)}, u32[]{:S(2)}) collective-permute-start(bf16[72,576]{1,0:T(8,128)(2,1)S(1)} %get-tuple-element.56), channel_id=1, source_target_pairs={{0,2},{1,3},{2,0},{3,1},{4,6},{5,7},{6,4},{7,5},{8,10},{9,11},{10,... | collective-permute-start | bytes 248840 | tf_op jit(solution)/shard_map/ppermute | solution.py:350

commit v14 on v13

--- a/solution.py
+++ b/solution.py
@@ -27,6 +27,10 @@
 
 def dot_bt(left, right):
     return lax.dot_general(left, right, (((1,), (1,)), ((), ())), preferred_element_type=F32)
+
+
+def dot_weight(rows, weight):
+    return dot_bt(weight, rows).T
 
 
 def dot_at(left, right):
@@ -213,7 +217,7 @@
     cot[...] = value[:, width : 2 * width]
     size = blocks.shape[2]
     for at, w in zip(shards, weights):
-        value = dot_bt(hidden, w[...]).astype(BF16)
+        value = dot_weight(hidden, w[...]).astype(BF16)
         for i, block in enumerate(at(idx)):
             blocks[block] = value[:, i * size : (i + 1) * size]
     whole = jnp.concatenate([blocks[i] for i in range(blocks.shape[0])], axis=1)
@@ -221,7 +225,7 @@
     put(k, whole[:, inner : 2 * inner])
     put(v, whole[:, 2 * inner :])
     mine[:, width:] = softmax_forward(q, k, v, p_ref, heads, ("cycle", group))[:, :inner]
-    put(g, dot_bt(cot[...], wot[...]).astype(BF16))
+    put(g, dot_weight(cot[...], wot[...]).astype(BF16))
     dq, dk, dv = softmax_backward(q, k, v, g, p_ref, heads)
     whole = jnp.concatenate([dq[:, :inner], dk[:, :inner], dv[:, :inner]], axis=1)
     for i in range(blocks.shape[0]):
@@ -334,7 +338,7 @@
     stores = started([(rows.at[:, pl.ds(0, width)], out_far)], sems.at[pl.ds(0, 1)])
     block_out[...] = (hid[...].astype(F32) + dot(attended, wot[...])).astype(BF16)
     stores += started([(block_out, block_far)], sems.at[pl.ds(1, 1)])
-    put(gs, dot_bt(grad, wos[...]).astype(BF16))
+    put(gs, dot_weight(grad, wos[...]).astype(BF16))
     x = qkv[...]
     put(qs, x[:, :inner])
     put(ks, x[:, inner : 2 * inner])

time: 69.9 us -> 69.8 us (level)
  transfers between devices with their start and end apart: 20 -> 20, of which waited for: 10 -> 10; matrix products, arithmetic and copies ran while one was open for 0% -> 0% of each run, Pallas kernels for 12% -> 13%
where the time goes in v14:
time: 69.8 us; the launch traced here: 69.6 us
  waiting for transfers between devices  25.7 us (37%)
  starting transfers between devices  23.9 us (34%)
  Pallas kernels  19.2 us (28%)
  between operations  0.78 us (1%)
    ppermute x18, waiting for transfers between devices, flip(): lax.ppermute(value, axis, [(i, i ^ bit) for i in range(lax.axis_size(axis...  21.7 us
    pallas_call x10, Pallas kernels, call(): pl.pallas_call(body, out_shape=outs, in_specs=[HBM if i in far_in else sp...  19.2 us
    ppermute x18, starting transfers between devices, flip(): lax.ppermute(value, axis, [(i, i ^ bit) for i in range(lax.axis_size(axis...  18.8 us
    ppermute x2, starting transfers between devices, across(): return lax.ppermute(value, ('dp', 'seq'), pairs)  5.12 us
    ppermute x2, waiting for transfers between devices, across(): return lax.ppermute(value, ('dp', 'seq'), pairs)  4 us
  transfers between devices with their start and end apart: 20, of which 10 were waited for; matrix products, arithmetic and copies ran while one was open for 0% of the time, Pallas kernels for 13%

profile of v14, /device:TPU:0, one launch (start us, length us, event | category | flops | bytes accessed | tf_op | source)
XLA Modules:
  0.0 69.6 jit_solution(5888661421200089209)
XLA Ops:
  0.6 3.0 %collective-permute-start = (bf16[432,1152]{1,0:T(8,128)(2,1)}, bf16[432,1152]{1,0:T(8,128)(2,1)S(1)}, u32[]{:S(2)}, u32[]{:S(2)}) collective-permute-start(bf16[432,1152]{1,0:T(8,128)(2,1)} %bitcast.9), channel_id=1, source_target_pairs={{0,8},{1,17},{2,10},{3,19},{4,12},{5,21},{6,14},{7,23},{8,0},{9,25... | collective-permute-start | bytes 2985992 | tf_op jit(solution)/shard_map/ppermute | solution.py:366
  3.6 4.0 %shard_map.101 = (bf16[32,2944]{1,0:T(8,128)(2,1)S(1)}, bf16[32,2944]{1,0:T(8,128)(2,1)S(1)}, bf16[32,2944]{1,0:T(8,128)(2,1)S(1)}, bf16[32,2944]{1,0:T(8,128)(2...) custom-call(bf16[128,1728]{1,0:T(8,128)(2,1)} %bitcast.7, bf16[128,1152]{1,0:T(8,128)(2,1)} %bitcast.11, ...), custom_call_target="tpu_custom_call" | custom-call | tf_op jit(solution)/shard_map/pallas_call | solution.py:43
  7.6 1.6 %collective-permute-start.1 = (bf16[32,2944]{1,0:T(8,128)(2,1)S(1)}, bf16[32,2944]{1,0:T(8,128)(2,1)S(1)}, u32[]{:S(2)}, u32[]{:S(2)}) collective-permute-start(bf16[32,2944]{1,0:T(8,128)(2,1)S(1)} %get-tuple-element.34), channel_id=1, source_target_pairs={{0,2},{1,3},{2,0},{3,1},{4,6},{5,7},{6,4},{7,5},{8,10},{9,11},{10,... | collective-permute-start | bytes 565256 | tf_op jit(solution)/shard_map/ppermute | solution.py:354
  9.2 2.6 %collective-permute-start.2 = (bf16[32,2944]{1,0:T(8,128)(2,1)S(1)}, bf16[32,2944]{1,0:T(8,128)(2,1)S(1)}, u32[]{:S(2)}, u32[]{:S(2)}) collective-permute-start(bf16[32,2944]{1,0:T(8,128)(2,1)S(1)} %get-tuple-element.35), channel_id=1, source_target_pairs={{0,4},{1,5},{2,6},{3,7},{4,0},{5,1},{6,2},{7,3},{8,12},{9,13},{10,... | collective-permute-start | bytes 565256 | tf_op jit(solution)/shard_map/ppermute | solution.py:354
  11.8 0.2 collective-permute-start.3
  12.1 4.0 %collective-permute-done.got.refs_1_ = bf16[432,1152]{1,0:T(8,128)(2,1)S(1)} collective-permute-done((bf16[432,1152]{1,0:T(8,128)(2,1)}, bf16[432,1152]{1,0:T(8,128)(2,1)S(1)}, u32[]{:S(2)}, u32[]{:S(2)}) %collective-permute-start) | collective-permute-done | bytes 995360 | tf_op jit(solution)/shard_map/ppermute | solution.py:366
  16.2 2.1 %collective-permute-start.6 = (bf16[216,1152]{1,0:T(8,128)(2,1)S(1)}, bf16[216,1152]{1,0:T(8,128)(2,1)S(1)}, u32[]{:S(2)}, u32[]{:S(2)}) collective-permute-start(bf16[216,1152]{1,0:T(8,128)(2,1)S(1)} %get-tuple-element.37), channel_id=1, source_target_pairs={{0,16},{1,9},{2,18},{3,11},{4,20},{5,13},{6,22},{7,15},{8,24},{9,1... | collective-permute-start | bytes 1493000 | tf_op jit(solution)/shard_map/ppermute | solution.py:366
  18.3 7.6 %collective-permute-done.2.refs_2_ = bf16[32,2944]{1,0:T(8,128)(2,1)S(1)} collective-permute-done((bf16[32,2944]{1,0:T(8,128)(2,1)S(1)}, bf16[32,2944]{1,0:T(8,128)(2,1)S(1)}, u32[]{:S(2)}, u32[]{:S(2)}) %collective-permute-start.2) | collective-permute-done | bytes 188448 | tf_op jit(solution)/shard_map/ppermute | solution.py:354
  26.0 0.5 collective-permute-start.7
  26.5 1.8 %collective-permute-done.4.far.refs_1_ = bf16[128,3200]{1,0:T(8,128)(2,1)S(1)} collective-permute-done((bf16[128,3200]{1,0:T(8,128)(2,1)S(1)}, bf16[128,3200]{1,0:T(8,128)(2,1)S(1)}, u32[]{:S(2)}, u32[]{:S(2)}) %collective-permute-start.4) | collective-permute-done | bytes 819232 | tf_op jit(solution)/shard_map/ppermute | solution.py:354
  28.3 0.7 %collective-permute-done.7.refs_4_ = bf16[216,1152]{1,0:T(8,128)(2,1)S(1)} collective-permute-done((bf16[216,1152]{1,0:T(8,128)(2,1)S(1)}, bf16[216,1152]{1,0:T(8,128)(2,1)S(1)}, u32[]{:S(2)}, u32[]{:S(2)}) %collective-permute-start.7) | collective-permute-done | bytes 497696 | tf_op jit(solution)/shard_map/ppermute | solution.py:354
  29.1 7.1 %shard_map.104 = (bf16[128,1728]{1,0:T(8,128)(2,1)S(1)}, bf16[32,1728]{1,0:T(8,128)(2,1)S(1)}, bf16[32,1728]{1,0:T(8,128)(2,1)S(1)}, bf16[32,1728]{1,0:T(8,128)(2,1)S(1)}) custom-call(bf16[128,3200]{1,0:T(8,128)(2,1)S(1)} %shard_map.103.near.refs_0_, bf16[128,3200]{1,0:T(8,128)(2,1)S(1)} %collective-permute-done.4.far.refs_1_, ...), custom_call_target="tpu_custom_call" | custom-call | tf_op jit(solution)/shard_map/pallas_call | solution.py:43
  36.1 0.2 collective-permute-start.12
  36.3 1.7 %collective-permute-done.12.other = bf16[128,1728]{1,0:T(8,128)(2,1)S(1)} collective-permute-done((bf16[128,1728]{1,0:T(8,128)(2,1)S(1)}, bf16[128,1728]{1,0:T(8,128)(2,1)S(1)}, u32[]{:S(2)}, u32[]{:S(2)}) %collective-permute-start.12) | collective-permute-done | bytes 442400 | tf_op jit(solution)/shard_map/ppermute | solution.py:354
  38.0 2.4 %shard_map.107 = (f32[4,72,1152]{2,1,0:T(8,128)S(1)}, bf16[2,72,1152]{2,1,0:T(8,128)(2,1)S(1)}, bf16[2,72,1152]{2,1,0:T(8,128)(2,1)S(1)}) custom-call(bf16[128,1728]{1,0:T(8,128)(2,1)S(1)} %get-tuple-element.41.mine.refs_3_, bf16[128,1728]{1,0:T(8,128)(2,1)S(1)} %collective-permute-done.12.other, bf16[128,3200]{1,0:T(8,128)(2,1)S(1)} %shard_map.103.near.refs_0_, ...), custom_call_target="tpu_custom_call" | custom-call | tf_op jit(solution)/shard_map/pallas_call | solution.py:43
  40.5 0.5 collective-permute-start.13
  41.0 1.6 %collective-permute-start.14 = (bf16[2,72,1152]{2,1,0:T(8,128)(2,1)S(1)}, bf16[2,72,1152]{2,1,0:T(8,128)(2,1)S(1)}, u32[]{:S(2)}, u32[]{:S(2)}) collective-permute-start(bf16[2,72,1152]{2,1,0:T(8,128)(2,1)S(1)} %get-tuple-element.49), channel_id=1, source_target_pairs={{0,16},{8,24},{16,0},{24,8},{1,17},{9,25},{17,1},{25,9},{2,18},{10... | collective-permute-start | bytes 995336 | tf_op jit(solution)/shard_map/ppermute | solution.py:354
  42.6 3.0 %collective-permute-start.8 = (bf16[32,1728]{1,0:T(8,128)(2,1)S(1)}, bf16[32,1728]{1,0:T(8,128)(2,1)S(1)}, u32[]{:S(2)}, u32[]{:S(2)}) collective-permute-start(bf16[32,1728]{1,0:T(8,128)(2,1)S(1)} %get-tuple-element.38), channel_id=1, source_target_pairs={{0,6},{1,7},{2,4},{3,5},{4,2},{5,3},{6,0},{7,1},{8,14},{9,15},{10,... | collective-permute-start | bytes 331784 | tf_op jit(solution)/shard_map/ppermute | solution.py:354
  45.6 1.3 %collective-permute-start.9 = (bf16[32,1728]{1,0:T(8,128)(2,1)S(1)}, bf16[32,1728]{1,0:T(8,128)(2,1)S(1)}, u32[]{:S(2)}, u32[]{:S(2)}) collective-permute-start(bf16[32,1728]{1,0:T(8,128)(2,1)S(1)} %get-tuple-element.39), channel_id=1, source_target_pairs={{0,4},{1,5},{2,6},{3,7},{4,0},{5,1},{6,2},{7,3},{8,12},{9,13},{10,... | collective-permute-start | bytes 331784 | tf_op jit(solution)/shard_map/ppermute | solution.py:354
  47.0 3.3 %collective-permute-done.13.got_x = bf16[2,72,1152]{2,1,0:T(8,128)(2,1)S(1)} collective-permute-done((bf16[2,72,1152]{2,1,0:T(8,128)(2,1)S(1)}, bf16[2,72,1152]{2,1,0:T(8,128)(2,1)S(1)}, u32[]{:S(2)}, u32[]{:S(2)}) %collective-permute-start.13) | collective-permute-done | bytes 331808 | tf_op jit(solution)/shard_map/ppermute | solution.py:354
  50.4 0.2 collective-permute-done.14.got_y
  50.6 0.1 shard_map.108
  50.7 1.7 %collective-permute-start.15 = (bf16[72,1152]{1,0:T(8,128)(2,1)S(1)}, bf16[72,1152]{1,0:T(8,128)(2,1)S(1)}, u32[]{:S(2)}, u32[]{:S(2)}) collective-permute-start(bf16[72,1152]{1,0:T(8,128)(2,1)S(1)} %get-tuple-element.51), channel_id=1, source_target_pairs={{0,16},{8,24},{16,0},{24,8},{1,17},{9,25},{17,1},{25,9},{2,18},{10... | collective-permute-start | bytes 497672 | tf_op jit(solution)/shard_map/ppermute | solution.py:354
  52.4 0.8 %collective-permute-start.16 = (bf16[72,1152]{1,0:T(8,128)(2,1)S(1)}, bf16[72,1152]{1,0:T(8,128)(2,1)S(1)}, u32[]{:S(2)}, u32[]{:S(2)}) collective-permute-start(bf16[72,1152]{1,0:T(8,128)(2,1)S(1)} %get-tuple-element.52), channel_id=1, source_target_pairs={{0,8},{8,0},{16,24},{24,16},{1,9},{9,1},{17,25},{25,17},{2,10},{10... | collective-permute-start | bytes 497672 | tf_op jit(solution)/shard_map/ppermute | solution.py:354
  53.1 3.3 %collective-permute-done.9.refs_1_ = bf16[32,1728]{1,0:T(8,128)(2,1)S(1)} collective-permute-done((bf16[32,1728]{1,0:T(8,128)(2,1)S(1)}, bf16[32,1728]{1,0:T(8,128)(2,1)S(1)}, u32[]{:S(2)}, u32[]{:S(2)}) %collective-permute-start.9) | collective-permute-done | bytes 110624 | tf_op jit(solution)/shard_map/ppermute | solution.py:354
  56.5 1.2 %collective-permute-done.16.got_x = bf16[72,1152]{1,0:T(8,128)(2,1)S(1)} collective-permute-done((bf16[72,1152]{1,0:T(8,128)(2,1)S(1)}, bf16[72,1152]{1,0:T(8,128)(2,1)S(1)}, u32[]{:S(2)}, u32[]{:S(2)}) %collective-permute-start.16) | collective-permute-done | bytes 165920 | tf_op jit(solution)/shard_map/ppermute | solution.py:354
  57.7 0.2 shard_map.109
  57.9 3.1 %collective-permute-start.17 = (bf16[72,576]{1,0:T(8,128)(2,1)S(1)}, bf16[72,576]{1,0:T(8,128)(2,1)S(1)}, u32[]{:S(2)}, u32[]{:S(2)}) collective-permute-start(bf16[72,576]{1,0:T(8,128)(2,1)S(1)} %get-tuple-element.54), channel_id=1, source_target_pairs={{0,6},{1,7},{2,4},{3,5},{4,2},{5,3},{6,0},{7,1},{8,14},{9,15},{10,... | collective-permute-start | bytes 248840 | tf_op jit(solution)/shard_map/ppermute | solution.py:354
  61.0 1.2 %collective-permute-start.18 = (bf16[72,576]{1,0:T(8,128)(2,1)S(1)}, bf16[72,576]{1,0:T(8,128)(2,1)S(1)}, u32[]{:S(2)}, u32[]{:S(2)}) collective-permute-start(bf16[72,576]{1,0:T(8,128)(2,1)S(1)} %get-tuple-element.55), channel_id=1, source_target_pairs={{0,4},{1,5},{2,6},{3,7},{4,0},{5,1},{6,2},{7,3},{8,12},{9,13},{10,... | collective-permute-start | bytes 248840 | tf_op jit(solution)/shard_map/ppermute | solution.py:354
  62.4 4.5 %shard_map.106 = (bf16[128,1152]{1,0:T(8,128)(2,1)}, bf16[128,1152]{1,0:T(8,128)(2,1)}, bf16[128,1728]{1,0:T(8,128)(2,1)}) custom-call(bf16[32,1728]{1,0:T(8,128)(2,1)S(1)} %collective-permute-done.8.refs_0_, bf16[32,1728]{1,0:T(8,128)(2,1)S(1)} %collective-permute-done.9.refs_1_, bf16[32,1728]{1,0:T(8,128)(2,1)S(1)} %collective-permute-done.10.refs_2_, ...), custom_call_target="tpu_custom_call" | custom-call | tf_op jit(solution)/shard_map/pallas_call | solution.py:43
  66.9 1.9 %collective-permute-done.18.refs_1_ = bf16[72,576]{1,0:T(8,128)(2,1)S(1)} collective-permute-done((bf16[72,576]{1,0:T(8,128)(2,1)S(1)}, bf16[72,576]{1,0:T(8,128)(2,1)S(1)}, u32[]{:S(2)}, u32[]{:S(2)}) %collective-permute-start.18) | collective-permute-done | bytes 82976 | tf_op jit(solution)/shard_map/ppermute | solution.py:354
  68.8 0.8 %shard_map.110 = (f32[72,288]{1,0:T(8,128)}, f32[72,288]{1,0:T(8,128)}) custom-call(f32[72,576]{1,0:T(8,128)S(1)} %get-tuple-element.53.own, bf16[72,576]{1,0:T(8,128)(2,1)S(1)} %collective-permute-done.17.refs_0_, bf16[72,576]{1,0:T(8,128)(2,1)S(1)} %collective-permute-done.18.refs_1_, bf16[72,576]{1,0:T(8,128)(2,1)S(1)} %collective-permute-done.19.refs_2_), custom_call_target="tpu_custom_call" | custom-call | tf_op jit(solution)/shard_map/pallas_call | solution.py:43
  (30 shorter events, 0.6 us)
Async XLA Ops:
  0.6 15.4 %collective-permute-start = (bf16[432,1152]{1,0:T(8,128)(2,1)}, bf16[432,1152]{1,0:T(8,128)(2,1)S(1)}, u32[]{:S(2)}, u32[]{:S(2)}) collective-permute-start(bf16[432,1152]{1,0:T(8,128)(2,1)} %bitcast.9), channel_id=1, source_target_pairs={{0,8},{1,17},{2,10},{3,19},{4,12},{5,21},{6,14},{7,23},{8,0},{9,25... | collective-permute-start | bytes 2985992 | tf_op jit(solution)/shard_map/ppermute | solution.py:366
  7.6 10.7 %collective-permute-start.1 = (bf16[32,2944]{1,0:T(8,128)(2,1)S(1)}, bf16[32,2944]{1,0:T(8,128)(2,1)S(1)}, u32[]{:S(2)}, u32[]{:S(2)}) collective-permute-start(bf16[32,2944]{1,0:T(8,128)(2,1)S(1)} %get-tuple-element.34), channel_id=1, source_target_pairs={{0,2},{1,3},{2,0},{3,1},{4,6},{5,7},{6,4},{7,5},{8,10},{9,11},{10,... | collective-permute-start | bytes 565256 | tf_op jit(solution)/shard_map/ppermute | solution.py:354
  9.2 16.6 %collective-permute-start.2 = (bf16[32,2944]{1,0:T(8,128)(2,1)S(1)}, bf16[32,2944]{1,0:T(8,128)(2,1)S(1)}, u32[]{:S(2)}, u32[]{:S(2)}) collective-permute-start(bf16[32,2944]{1,0:T(8,128)(2,1)S(1)} %get-tuple-element.35), channel_id=1, source_target_pairs={{0,4},{1,5},{2,6},{3,7},{4,0},{5,1},{6,2},{7,3},{8,12},{9,13},{10,... | collective-permute-start | bytes 565256 | tf_op jit(solution)/shard_map/ppermute | solution.py:354
  11.8 14.1 %collective-permute-start.3 = (bf16[32,2944]{1,0:T(8,128)(2,1)S(1)}, bf16[32,2944]{1,0:T(8,128)(2,1)S(1)}, u32[]{:S(2)}, u32[]{:S(2)}) collective-permute-start(bf16[32,2944]{1,0:T(8,128)(2,1)S(1)} %get-tuple-element.36), channel_id=1, source_target_pairs={{0,6},{1,7},{2,4},{3,5},{4,2},{5,3},{6,0},{7,1},{8,14},{9,15},{10,... | collective-permute-start | bytes 565256 | tf_op jit(solution)/shard_map/ppermute | solution.py:354
  16.1 13.0 %copy-start.1 = (bf16[576,1152]{1,0:T(8,128)(2,1)S(1)}, bf16[576,1152]{1,0:T(8,128)(2,1)}, u32[]{:S(2)}) copy-start(bf16[576,1152]{1,0:T(8,128)(2,1)} %refs_8_.1) | copy-start | bytes 3981316
  16.1 13.0 %copy-start.3 = (bf16[1152,432]{0,1:T(8,128)(2,1)S(1)}, bf16[1152,432]{0,1:T(8,128)(2,1)}, u32[]{:S(2)}) copy-start(bf16[1152,432]{0,1:T(8,128)(2,1)} %param.9) | copy-start | bytes 2985988
  16.2 9.8 %collective-permute-start.6 = (bf16[216,1152]{1,0:T(8,128)(2,1)S(1)}, bf16[216,1152]{1,0:T(8,128)(2,1)S(1)}, u32[]{:S(2)}, u32[]{:S(2)}) collective-permute-start(bf16[216,1152]{1,0:T(8,128)(2,1)S(1)} %get-tuple-element.37), channel_id=1, source_target_pairs={{0,16},{1,9},{2,18},{3,11},{4,20},{5,13},{6,22},{7,15},{8,24},{9,1... | collective-permute-start | bytes 1493000 | tf_op jit(solution)/shard_map/ppermute | solution.py:366
  18.3 10.0 %collective-permute-start.5 = (bf16[432,1152]{1,0:T(8,128)(2,1)S(1)}, bf16[432,1152]{1,0:T(8,128)(2,1)S(1)}, u32[]{:S(2)}, u32[]{:S(2)}) collective-permute-start(bf16[432,1152]{1,0:T(8,128)(2,1)S(1)} %collective-permute-done.got.refs_1_), channel_id=1, source_target_pairs={{0,1},{1,0},{2,3},{3,2},{4,5},{5,4},{6,7},{7,6},{8,9},{9,8},{10,11... | collective-permute-start | bytes 2985992 | tf_op jit(solution)/shard_map/ppermute | solution.py:354
  25.9 2.4 %collective-permute-start.4 = (bf16[128,3200]{1,0:T(8,128)(2,1)S(1)}, bf16[128,3200]{1,0:T(8,128)(2,1)S(1)}, u32[]{:S(2)}, u32[]{:S(2)}) collective-permute-start(bf16[128,3200]{1,0:T(8,128)(2,1)S(1)} %shard_map.103.near.refs_0_), channel_id=1, source_target_pairs={{0,1},{1,0},{2,3},{3,2},{4,5},{5,4},{6,7},{7,6},{8,9},{9,8},{10,11... | collective-permute-start | bytes 2457608 | tf_op jit(solution)/shard_map/ppermute | solution.py:354
  26.0 3.0 %collective-permute-start.7 = (bf16[216,1152]{1,0:T(8,128)(2,1)S(1)}, bf16[216,1152]{1,0:T(8,128)(2,1)S(1)}, u32[]{:S(2)}, u32[]{:S(2)}) collective-permute-start(bf16[216,1152]{1,0:T(8,128)(2,1)S(1)} %collective-permute-done.6.refs_3_), channel_id=1, source_target_pairs={{0,1},{1,0},{2,3},{3,2},{4,5},{5,4},{6,7},{7,6},{8,9},{9,8},{10,11... | collective-permute-start | bytes 1493000 | tf_op jit(solution)/shard_map/ppermute | solution.py:354
  36.1 1.9 %collective-permute-start.12 = (bf16[128,1728]{1,0:T(8,128)(2,1)S(1)}, bf16[128,1728]{1,0:T(8,128)(2,1)S(1)}, u32[]{:S(2)}, u32[]{:S(2)}) collective-permute-start(bf16[128,1728]{1,0:T(8,128)(2,1)S(1)} %get-tuple-element.41.mine.refs_3_), channel_id=1, source_target_pairs={{0,1},{1,0},{2,3},{3,2},{4,5},{5,4},{6,7},{7,6},{8,9},{9,8},{10,11... | collective-permute-start | bytes 1327112 | tf_op jit(solution)/shard_map/ppermute | solution.py:354
  40.5 9.9 %collective-permute-start.13 = (bf16[2,72,1152]{2,1,0:T(8,128)(2,1)S(1)}, bf16[2,72,1152]{2,1,0:T(8,128)(2,1)S(1)}, u32[]{:S(2)}, u32[]{:S(2)}) collective-permute-start(bf16[2,72,1152]{2,1,0:T(8,128)(2,1)S(1)} %get-tuple-element.48), channel_id=1, source_target_pairs={{0,8},{8,0},{16,24},{24,16},{1,9},{9,1},{17,25},{25,17},{2,10},{10... | collective-permute-start | bytes 995336 | tf_op jit(solution)/shard_map/ppermute | solution.py:354
  41.0 9.6 %collective-permute-start.14 = (bf16[2,72,1152]{2,1,0:T(8,128)(2,1)S(1)}, bf16[2,72,1152]{2,1,0:T(8,128)(2,1)S(1)}, u32[]{:S(2)}, u32[]{:S(2)}) collective-permute-start(bf16[2,72,1152]{2,1,0:T(8,128)(2,1)S(1)} %get-tuple-element.49), channel_id=1, source_target_pairs={{0,16},{8,24},{16,0},{24,8},{1,17},{9,25},{17,1},{25,9},{2,18},{10... | collective-permute-start | bytes 995336 | tf_op jit(solution)/shard_map/ppermute | solution.py:354
  42.6 10.5 %collective-permute-start.8 = (bf16[32,1728]{1,0:T(8,128)(2,1)S(1)}, bf16[32,1728]{1,0:T(8,128)(2,1)S(1)}, u32[]{:S(2)}, u32[]{:S(2)}) collective-permute-start(bf16[32,1728]{1,0:T(8,128)(2,1)S(1)} %get-tuple-element.38), channel_id=1, source_target_pairs={{0,6},{1,7},{2,4},{3,5},{4,2},{5,3},{6,0},{7,1},{8,14},{9,15},{10,... | collective-permute-start | bytes 331784 | tf_op jit(solution)/shard_map/ppermute | solution.py:354
  45.6 10.8 %collective-permute-start.9 = (bf16[32,1728]{1,0:T(8,128)(2,1)S(1)}, bf16[32,1728]{1,0:T(8,128)(2,1)S(1)}, u32[]{:S(2)}, u32[]{:S(2)}) collective-permute-start(bf16[32,1728]{1,0:T(8,128)(2,1)S(1)} %get-tuple-element.39), channel_id=1, source_target_pairs={{0,4},{1,5},{2,6},{3,7},{4,0},{5,1},{6,2},{7,3},{8,12},{9,13},{10,... | collective-permute-start | bytes 331784 | tf_op jit(solution)/shard_map/ppermute | solution.py:354
  46.9 9.5 %collective-permute-start.10 = (bf16[32,1728]{1,0:T(8,128)(2,1)S(1)}, bf16[32,1728]{1,0:T(8,128)(2,1)S(1)}, u32[]{:S(2)}, u32[]{:S(2)}) collective-permute-start(bf16[32,1728]{1,0:T(8,128)(2,1)S(1)} %get-tuple-element.40), channel_id=1, source_target_pairs={{0,2},{1,3},{2,0},{3,1},{4,6},{5,7},{6,4},{7,5},{8,10},{9,11},{10,... | collective-permute-start | bytes 331784 | tf_op jit(solution)/shard_map/ppermute | solution.py:354
  50.5 11.9 %copy-start.4 = (f32[8,128,128]{2,1,0:T(8,128)S(1)}, f32[8,128,128]{2,1,0:T(8,128)}, u32[]{:S(2)}) copy-start(f32[8,128,128]{2,1,0:T(8,128)} %get-tuple-element.42.refs_7_) | copy-start | bytes 1572868
  50.5 11.9 %copy-start.5 = (bf16[128,1152]{1,0:T(8,128)(2,1)S(1)}, bf16[128,1152]{1,0:T(8,128)(2,1)}, u32[]{:S(2)}) copy-start(bf16[128,1152]{1,0:T(8,128)(2,1)} %get-tuple-element.43.refs_9_) | copy-start | bytes 884740
  50.7 11.7 %copy-start = (bf16[576,1152]{1,0:T(8,128)(2,1)S(1)}, bf16[576,1152]{1,0:T(8,128)(2,1)}, u32[]{:S(2)}) copy-start(bf16[576,1152]{1,0:T(8,128)(2,1)} %refs_5_.1) | copy-start | bytes 3981316
  50.7 11.7 %copy-start.2 = (bf16[2,64,1728]{2,1,0:T(8,128)(2,1)S(1)}, bf16[2,64,1728]{2,1,0:T(8,128)(2,1)}, u32[]{:S(2)}) copy-start(bf16[2,64,1728]{2,1,0:T(8,128)(2,1)} %param.7) | copy-start | bytes 1327108
  50.7 5.8 %collective-permute-start.15 = (bf16[72,1152]{1,0:T(8,128)(2,1)S(1)}, bf16[72,1152]{1,0:T(8,128)(2,1)S(1)}, u32[]{:S(2)}, u32[]{:S(2)}) collective-permute-start(bf16[72,1152]{1,0:T(8,128)(2,1)S(1)} %get-tuple-element.51), channel_id=1, source_target_pairs={{0,16},{8,24},{16,0},{24,8},{1,17},{9,25},{17,1},{25,9},{2,18},{10... | collective-permute-start | bytes 497672 | tf_op jit(solution)/shard_map/ppermute | solution.py:354
  52.4 5.3 %collective-permute-start.16 = (bf16[72,1152]{1,0:T(8,128)(2,1)S(1)}, bf16[72,1152]{1,0:T(8,128)(2,1)S(1)}, u32[]{:S(2)}, u32[]{:S(2)}) collective-permute-start(bf16[72,1152]{1,0:T(8,128)(2,1)S(1)} %get-tuple-element.52), channel_id=1, source_target_pairs={{0,8},{8,0},{16,24},{24,16},{1,9},{9,1},{17,25},{25,17},{2,10},{10... | collective-permute-start | bytes 497672 | tf_op jit(solution)/shard_map/ppermute | solution.py:354
  56.4 6.0 %collective-permute-start.11 = (bf16[64,1728]{1,0:T(8,128)(2,1)S(1)}, bf16[64,1728]{1,0:T(8,128)(2,1)S(1)}, u32[]{:S(2)}, u32[]{:S(2)}) collective-permute-start(bf16[64,1728]{1,0:T(8,128)(2,1)S(1)} %shard_map.105), channel_id=1, source_target_pairs={{0,1},{1,0},{2,3},{3,2},{4,5},{5,4},{6,7},{7,6},{8,9},{9,8},{10,11... | collective-permute-start | bytes 663560 | tf_op jit(solution)/shard_map/ppermute | solution.py:354
  57.9 9.0 %collective-permute-start.17 = (bf16[72,576]{1,0:T(8,128)(2,1)S(1)}, bf16[72,576]{1,0:T(8,128)(2,1)S(1)}, u32[]{:S(2)}, u32[]{:S(2)}) collective-permute-start(bf16[72,576]{1,0:T(8,128)(2,1)S(1)} %get-tuple-element.54), channel_id=1, source_target_pairs={{0,6},{1,7},{2,4},{3,5},{4,2},{5,3},{6,0},{7,1},{8,14},{9,15},{10,... | collective-permute-start | bytes 248840 | tf_op jit(solution)/shard_map/ppermute | solution.py:354
  61.0 7.8 %collective-permute-start.18 = (bf16[72,576]{1,0:T(8,128)(2,1)S(1)}, bf16[72,576]{1,0:T(8,128)(2,1)S(1)}, u32[]{:S(2)}, u32[]{:S(2)}) collective-permute-start(bf16[72,576]{1,0:T(8,128)(2,1)S(1)} %get-tuple-element.55), channel_id=1, source_target_pairs={{0,4},{1,5},{2,6},{3,7},{4,0},{5,1},{6,2},{7,3},{8,12},{9,13},{10,... | collective-permute-start | bytes 248840 | tf_op jit(solution)/shard_map/ppermute | solution.py:354
  62.3 6.5 %collective-permute-start.19 = (bf16[72,576]{1,0:T(8,128)(2,1)S(1)}, bf16[72,576]{1,0:T(8,128)(2,1)S(1)}, u32[]{:S(2)}, u32[]{:S(2)}) collective-permute-start(bf16[72,576]{1,0:T(8,128)(2,1)S(1)} %get-tuple-element.56), channel_id=1, source_target_pairs={{0,2},{1,3},{2,0},{3,1},{4,6},{5,7},{6,4},{7,5},{8,10},{9,11},{10,... | collective-permute-start | bytes 248840 | tf_op jit(solution)/shard_map/ppermute | solution.py:354

commit v15 on v14

--- a/solution.py
+++ b/solution.py
@@ -17,6 +17,7 @@
 SMEM = pl.BlockSpec(memory_space=pltpu.SMEM)
 HBM = pl.BlockSpec(memory_space=pltpu.HBM)
 PAD = 2 * LANES
+WIDER = 1088
 LIMIT = 16 * 1024 * 1024
 MOST = 53 * 1024 * 1024
 
@@ -246,9 +247,10 @@
     parts, out = refs[-2::-1], refs[-1]
     half = mine.shape[0] // 2
     rows = half // (1 + len(parts))
-    out[:rows] = mine[half : half + rows]
+    width = mine.shape[1]
+    out[:rows, :width] = mine[half : half + rows]
     for q, part in enumerate(parts, 1):
-        out[q * rows : (q + 1) * rows] = part[rows:]
+        out[q * rows : (q + 1) * rows, :width] = part[rows:]
 
 
 def whole_parts_kernel(chips, block, inner, width, mine, other, *refs):
@@ -264,7 +266,7 @@
 def parts_kernel(chips, block, inner, width, mine, other, *refs):
     idx = place(chips)
     sent, refs = refs[:2], refs[2:]
-    keep, send_x, send_y, heads, cols = refs
+    keep, send, heads, cols = refs
     half = mine.shape[0] // 2
     near = all_patches(mine[:half], other[half:], idx[1], block)
     far = all_patches(mine[half:], other[:half], idx[1], block)
@@ -285,24 +287,23 @@
             for r in range(count):
                 cols[r, held] = rights[at][:, r * wide : (r + 1) * wide]
         left = jnp.concatenate([heads[idx[3] ^ (2 * q)] for q in range(chips)], axis=1)
-        first = 1 if i == 0 else 2
-        for r in range(count):
+        for at, r in enumerate((0, 2 - idx[1], 1 + idx[1], 3)):
             full = dot_at(left, cols[idx[0] ^ r])
             value = jnp.concatenate([full[q * size : (q + 1) * size] for q in range(chips)], axis=1)
-            if r & first:
-                (send_x, send_y)[i][r // 2 if i == 0 else r - 2] = value.astype(BF16)
+            if at < 2:
+                keep[2 * i + at] = value
             else:
-                keep[2 * i + (r > 0)] = value
-
-
-def sum_first_kernel(keep, got_x, got_y, own, send_y, send_x):
-    for i, (got, send) in enumerate(((got_x, send_y), (got_y, send_x))):
-        own[i] = keep[2 * i] + got[0].astype(F32)
-        send[...] = (keep[2 * i + 1] + got[1].astype(F32)).astype(BF16)
-
-
-def sum_second_kernel(own, got_y, got_x, kept, *outs):
-    totals = [own[0] + got_y[...].astype(F32), own[1] + got_x[...].astype(F32)]
+                send[2 * i + at - 2] = value.astype(BF16)
+
+
+def sum_first_kernel(keep, got, own, send):
+    for i in range(2):
+        own[i] = keep[2 * i] + got[2 * i].astype(F32)
+        send[i] = (keep[2 * i + 1] + got[2 * i + 1].astype(F32)).astype(BF16)
+
+
+def sum_second_kernel(own, got, kept, *outs):
+    totals = [own[i] + got[i].astype(F32) for i in range(2)]
     size = totals[0].shape[1] // (1 + len(outs))
     for q, out in enumerate((kept, *outs)):
         cut = [total[:, q * size : (q + 1) * size] for total in totals]
@@ -329,7 +330,8 @@
     block = patches // chips
     each = frames * block // 2
     for q in range(chips):
-        value = all_patches(held[q][:each], got[q * each : (q + 1) * each], idx[1], block)
+        other = got[q * each : (q + 1) * each, : rows.shape[1]]
+        value = all_patches(held[q][:each], other, idx[1], block)
         for f in range(frames):
             low = pl.multiple_of(f * patches + (idx[2] ^ q) * block, block)
             rows[pl.ds(low, block)] = value[f * block : (f + 1) * block]
@@ -338,7 +340,7 @@
     stores = started([(rows.at[:, pl.ds(0, width)], out_far)], sems.at[pl.ds(0, 1)])
     block_out[...] = (hid[...].astype(F32) + dot(attended, wot[...])).astype(BF16)
     stores += started([(block_out, block_far)], sems.at[pl.ds(1, 1)])
-    put(gs, dot_weight(grad, wos[...]).astype(BF16))
+    put(gs, dot_bt(grad, wos[...]).astype(BF16))
     x = qkv[...]
     put(qs, x[:, :inner])
     put(ks, x[:, inner : 2 * inner])
@@ -403,13 +405,13 @@
     return [parts[0]] + [flip(parts[q], "seq", 2 * q) for q in range(1, len(parts))]
 
 
-def reduced(keep, send_x, send_y):
+def reduced(keep, send):
     _, size, width = keep.shape
-    step = shape((size, width))
-    own, send_t, send_s = call(
+    step = (2, size, width)
+    own, send = call(
         sum_first_kernel,
-        [shape((2, size, width), F32), step, step],
-        [keep, flip(send_x, "dp", 1), flip(send_y, "dp", 2)],
+        [shape(step, F32), shape(step)],
+        [keep, across(send, (1, 2))],
         small=True,
     )
     n = lax.axis_size("seq") // 2
@@ -417,7 +419,7 @@
     own, *sends = call(
         sum_second_kernel,
         [shape(block, F32)] + [shape(block)] * (n - 1),
-        [own, flip(send_t, "dp", 2), flip(send_s, "dp", 1)],
+        [own, across(send, (2, 1))],
         small=True,
     )
     got = from_chips([own, *sends])[1:]
@@ -469,9 +471,9 @@
     other = flip(mine, "seq", 1)
     if n_dp == 4 and n_seq == peers:
         size = inner // n_seq
-        keep, send_x, send_y = call(
+        keep, send = call(
             functools.partial(parts_kernel, chips, block, inner, width),
-            [shape((n_dp, size, width), F32)] + [shape((2, size, width))] * 2,
+            [shape((4, size, width), F32), shape((4, size, width))],
             [mine, other, near, far],
             [
                 pltpu.VMEM((n_seq, 2 * rows, size), BF16),
@@ -489,7 +491,7 @@
     back = from_chips([mine, *back])
     (others,) = call(
         others_kernel,
-        [shape((rows // 2, width + inner))],
+        [shape((rows // 2, width + inner + WIDER))],
         [back[0], *back[:0:-1]],
         small=True,
     )
@@ -502,7 +504,7 @@
         small=True,
     )
     if n_dp == 4 and n_seq == peers:
-        temporal_grad, spatial_grad = reduced(keep, send_x, send_y)
+        temporal_grad, spatial_grad = reduced(keep, send)
     else:
         both = lax.psum_scatter(both, "seq", scatter_dimension=1, tiled=True)
         both = lax.psum_scatter(both, "dp", scatter_dimension=2, tiled=True).astype(F32)

time: 69.8 us -> 70.3 us (level)
  waiting for transfers between devices: 25.7 us -> 28.9 us
  starting transfers between devices: 23.9 us -> 21.9 us
    ppermute x2 -> x4, waiting for transfers between devices: 4 us -> 11.7 us  [across(): return lax.ppermute(value, ('dp', 'seq'), pairs)]
    ppermute x18 -> x14, waiting for transfers between devices: 21.7 us -> 17.2 us  [flip(): lax.ppermute(value, axis, [(i, i ^ bit) for i in range(lax.axis_size(axis...]
    ppermute x18 -> x14, starting transfers between devices: 18.8 us -> 15.4 us  [flip(): lax.ppermute(value, axis, [(i, i ^ bit) for i in range(lax.axis_size(axis...]
    ppermute x2 -> x4, starting transfers between devices: 5.12 us -> 6.53 us  [across(): return lax.ppermute(value, ('dp', 'seq'), pairs)]
  transfers between devices with their start and end apart: 20 -> 18, of which waited for: 10 -> 9; matrix products, arithmetic and copies ran while one was open for 0% -> 0% of each run, Pallas kernels for 13% -> 12%
where the time goes in v15:
time: 70.3 us; the launch traced here: 70.2 us
  waiting for transfers between devices  28.9 us (41%)
  starting transfers between devices  21.9 us (31%)
  Pallas kernels  18.6 us (26%)
  between operations  0.77 us (1%)
    pallas_call x10, Pallas kernels, call(): pl.pallas_call(body, out_shape=outs, in_specs=[HBM if i in far_in else sp...  18.6 us
    ppermute x14, waiting for transfers between devices, flip(): lax.ppermute(value, axis, [(i, i ^ bit) for i in range(lax.axis_size(axis...  17.2 us
    ppermute x14, starting transfers between devices, flip(): lax.ppermute(value, axis, [(i, i ^ bit) for i in range(lax.axis_size(axis...  15.4 us
    ppermute x4, waiting for transfers between devices, across(): return lax.ppermute(value, ('dp', 'seq'), pairs)  11.7 us
    ppermute x4, starting transfers between devices, across(): return lax.ppermute(value, ('dp', 'seq'), pairs)  6.53 us
  transfers between devices with their start and end apart: 18, of which 9 were waited for; matrix products, arithmetic and copies ran while one was open for 0% of the time, Pallas kernels for 12%

profile of v15, /device:TPU:0, one launch (start us, length us, event | category | flops | bytes accessed | tf_op | source)
XLA Modules:
  0.0 70.2 jit_solution(8351073845844174273)
XLA Ops:
  0.6 3.0 %collective-permute-start = (bf16[432,1152]{1,0:T(8,128)(2,1)}, bf16[432,1152]{1,0:T(8,128)(2,1)S(1)}, u32[]{:S(2)}, u32[]{:S(2)}) collective-permute-start(bf16[432,1152]{1,0:T(8,128)(2,1)} %bitcast.9), channel_id=1, source_target_pairs={{0,8},{1,17},{2,10},{3,19},{4,12},{5,21},{6,14},{7,23},{8,0},{9,25... | collective-permute-start | bytes 2985992 | tf_op jit(solution)/shard_map/ppermute | solution.py:368
  3.6 4.0 %shard_map.101 = (bf16[32,2944]{1,0:T(8,128)(2,1)S(1)}, bf16[32,2944]{1,0:T(8,128)(2,1)S(1)}, bf16[32,2944]{1,0:T(8,128)(2,1)S(1)}, bf16[32,2944]{1,0:T(8,128)(2...) custom-call(bf16[128,1728]{1,0:T(8,128)(2,1)} %bitcast.7, bf16[128,1152]{1,0:T(8,128)(2,1)} %bitcast.11, ...), custom_call_target="tpu_custom_call" | custom-call | tf_op jit(solution)/shard_map/pallas_call | solution.py:44
  7.6 1.6 %collective-permute-start.1 = (bf16[32,2944]{1,0:T(8,128)(2,1)S(1)}, bf16[32,2944]{1,0:T(8,128)(2,1)S(1)}, u32[]{:S(2)}, u32[]{:S(2)}) collective-permute-start(bf16[32,2944]{1,0:T(8,128)(2,1)S(1)} %get-tuple-element.32), channel_id=1, source_target_pairs={{0,2},{1,3},{2,0},{3,1},{4,6},{5,7},{6,4},{7,5},{8,10},{9,11},{10,... | collective-permute-start | bytes 565256 | tf_op jit(solution)/shard_map/ppermute | solution.py:356
  9.2 2.6 %collective-permute-start.2 = (bf16[32,2944]{1,0:T(8,128)(2,1)S(1)}, bf16[32,2944]{1,0:T(8,128)(2,1)S(1)}, u32[]{:S(2)}, u32[]{:S(2)}) collective-permute-start(bf16[32,2944]{1,0:T(8,128)(2,1)S(1)} %get-tuple-element.33), channel_id=1, source_target_pairs={{0,4},{1,5},{2,6},{3,7},{4,0},{5,1},{6,2},{7,3},{8,12},{9,13},{10,... | collective-permute-start | bytes 565256 | tf_op jit(solution)/shard_map/ppermute | solution.py:356
  11.8 0.2 collective-permute-start.3
  12.1 4.0 %collective-permute-done.got.refs_1_ = bf16[432,1152]{1,0:T(8,128)(2,1)S(1)} collective-permute-done((bf16[432,1152]{1,0:T(8,128)(2,1)}, bf16[432,1152]{1,0:T(8,128)(2,1)S(1)}, u32[]{:S(2)}, u32[]{:S(2)}) %collective-permute-start) | collective-permute-done | bytes 995360 | tf_op jit(solution)/shard_map/ppermute | solution.py:368
  16.1 0.1 shard_map.102
  16.2 2.1 %collective-permute-start.6 = (bf16[216,1152]{1,0:T(8,128)(2,1)S(1)}, bf16[216,1152]{1,0:T(8,128)(2,1)S(1)}, u32[]{:S(2)}, u32[]{:S(2)}) collective-permute-start(bf16[216,1152]{1,0:T(8,128)(2,1)S(1)} %get-tuple-element.35), channel_id=1, source_target_pairs={{0,16},{1,9},{2,18},{3,11},{4,20},{5,13},{6,22},{7,15},{8,24},{9,1... | collective-permute-start | bytes 1493000 | tf_op jit(solution)/shard_map/ppermute | solution.py:368
  18.3 7.6 %collective-permute-done.2.refs_2_ = bf16[32,2944]{1,0:T(8,128)(2,1)S(1)} collective-permute-done((bf16[32,2944]{1,0:T(8,128)(2,1)S(1)}, bf16[32,2944]{1,0:T(8,128)(2,1)S(1)}, u32[]{:S(2)}, u32[]{:S(2)}) %collective-permute-start.2) | collective-permute-done | bytes 188448 | tf_op jit(solution)/shard_map/ppermute | solution.py:356
  26.0 0.5 collective-permute-start.7
  26.5 1.8 %collective-permute-done.4.far.refs_1_ = bf16[128,3200]{1,0:T(8,128)(2,1)S(1)} collective-permute-done((bf16[128,3200]{1,0:T(8,128)(2,1)S(1)}, bf16[128,3200]{1,0:T(8,128)(2,1)S(1)}, u32[]{:S(2)}, u32[]{:S(2)}) %collective-permute-start.4) | collective-permute-done | bytes 819232 | tf_op jit(solution)/shard_map/ppermute | solution.py:356
  28.3 0.7 %collective-permute-done.7.refs_4_ = bf16[216,1152]{1,0:T(8,128)(2,1)S(1)} collective-permute-done((bf16[216,1152]{1,0:T(8,128)(2,1)S(1)}, bf16[216,1152]{1,0:T(8,128)(2,1)S(1)}, u32[]{:S(2)}, u32[]{:S(2)}) %collective-permute-start.7) | collective-permute-done | bytes 497696 | tf_op jit(solution)/shard_map/ppermute | solution.py:356
  29.1 7.1 %shard_map.104 = (bf16[128,1728]{1,0:T(8,128)(2,1)S(1)}, bf16[32,1728]{1,0:T(8,128)(2,1)S(1)}, bf16[32,1728]{1,0:T(8,128)(2,1)S(1)}, bf16[32,1728]{1,0:T(8,128)(2,1)S(1)}) custom-call(bf16[128,3200]{1,0:T(8,128)(2,1)S(1)} %shard_map.103.near.refs_0_, bf16[128,3200]{1,0:T(8,128)(2,1)S(1)} %collective-permute-done.4.far.refs_1_, ...), custom_call_target="tpu_custom_call" | custom-call | tf_op jit(solution)/shard_map/pallas_call | solution.py:44
  36.1 0.2 collective-permute-start.12
  36.3 1.7 %collective-permute-done.12.other = bf16[128,1728]{1,0:T(8,128)(2,1)S(1)} collective-permute-done((bf16[128,1728]{1,0:T(8,128)(2,1)S(1)}, bf16[128,1728]{1,0:T(8,128)(2,1)S(1)}, u32[]{:S(2)}, u32[]{:S(2)}) %collective-permute-start.12) | collective-permute-done | bytes 442400 | tf_op jit(solution)/shard_map/ppermute | solution.py:356
  38.0 2.3 %shard_map.107 = (f32[4,72,1152]{2,1,0:T(8,128)S(1)}, bf16[4,72,1152]{2,1,0:T(8,128)(2,1)S(1)}) custom-call(bf16[128,1728]{1,0:T(8,128)(2,1)S(1)} %get-tuple-element.39.mine.refs_3_, bf16[128,1728]{1,0:T(8,128)(2,1)S(1)} %collective-permute-done.12.other, bf16[128,3200]{1,0:T(8,128)(2,1)S(1)} %shard_map.103.near.refs_0_, ...), custom_call_target="tpu_custom_call" | custom-call | tf_op jit(solution)/shard_map/pallas_call | solution.py:44
  40.4 0.5 collective-permute-start.13
  40.9 3.1 %collective-permute-start.8 = (bf16[32,1728]{1,0:T(8,128)(2,1)S(1)}, bf16[32,1728]{1,0:T(8,128)(2,1)S(1)}, u32[]{:S(2)}, u32[]{:S(2)}) collective-permute-start(bf16[32,1728]{1,0:T(8,128)(2,1)S(1)} %get-tuple-element.36), channel_id=1, source_target_pairs={{0,6},{1,7},{2,4},{3,5},{4,2},{5,3},{6,0},{7,1},{8,14},{9,15},{10,... | collective-permute-start | bytes 331784 | tf_op jit(solution)/shard_map/ppermute | solution.py:356
  44.0 2.3 %collective-permute-start.9 = (bf16[32,1728]{1,0:T(8,128)(2,1)S(1)}, bf16[32,1728]{1,0:T(8,128)(2,1)S(1)}, u32[]{:S(2)}, u32[]{:S(2)}) collective-permute-start(bf16[32,1728]{1,0:T(8,128)(2,1)S(1)} %get-tuple-element.37), channel_id=1, source_target_pairs={{0,4},{1,5},{2,6},{3,7},{4,0},{5,1},{6,2},{7,3},{8,12},{9,13},{10,... | collective-permute-start | bytes 331784 | tf_op jit(solution)/shard_map/ppermute | solution.py:356
  46.3 0.1 collective-permute-start.10
  46.4 4.7 %collective-permute-done.13.got = bf16[4,72,1152]{2,1,0:T(8,128)(2,1)S(1)} collective-permute-done((bf16[4,72,1152]{2,1,0:T(8,128)(2,1)S(1)}, bf16[4,72,1152]{2,1,0:T(8,128)(2,1)S(1)}, u32[]{:S(2)}, u32[]{:S(2)}) %collective-permute-start.13) | collective-permute-done | bytes 663584 | tf_op jit(solution)/shard_map/ppermute | solution.py:368
  51.1 0.1 shard_map.108
  51.2 0.9 %collective-permute-start.14 = (bf16[2,72,1152]{2,1,0:T(8,128)(2,1)S(1)}, bf16[2,72,1152]{2,1,0:T(8,128)(2,1)S(1)}, u32[]{:S(2)}, u32[]{:S(2)}) collective-permute-start(bf16[2,72,1152]{2,1,0:T(8,128)(2,1)S(1)} %get-tuple-element.48), channel_id=1, source_target_pairs={{0,16},{1,9},{2,18},{3,11},{4,20},{5,13},{6,22},{7,15},{8,24},{9,1... | collective-permute-start | bytes 995336 | tf_op jit(solution)/shard_map/ppermute | solution.py:368
  52.1 3.2 %collective-permute-done.9.refs_1_ = bf16[32,1728]{1,0:T(8,128)(2,1)S(1)} collective-permute-done((bf16[32,1728]{1,0:T(8,128)(2,1)S(1)}, bf16[32,1728]{1,0:T(8,128)(2,1)S(1)}, u32[]{:S(2)}, u32[]{:S(2)}) %collective-permute-start.9) | collective-permute-done | bytes 110624 | tf_op jit(solution)/shard_map/ppermute | solution.py:356
  55.4 3.0 %collective-permute-done.14.got = bf16[2,72,1152]{2,1,0:T(8,128)(2,1)S(1)} collective-permute-done((bf16[2,72,1152]{2,1,0:T(8,128)(2,1)S(1)}, bf16[2,72,1152]{2,1,0:T(8,128)(2,1)S(1)}, u32[]{:S(2)}, u32[]{:S(2)}) %collective-permute-start.14) | collective-permute-done | bytes 331808 | tf_op jit(solution)/shard_map/ppermute | solution.py:368
  58.4 0.2 shard_map.109
  58.6 2.4 %collective-permute-start.15 = (bf16[72,576]{1,0:T(8,128)(2,1)S(1)}, bf16[72,576]{1,0:T(8,128)(2,1)S(1)}, u32[]{:S(2)}, u32[]{:S(2)}) collective-permute-start(bf16[72,576]{1,0:T(8,128)(2,1)S(1)} %get-tuple-element.50), channel_id=1, source_target_pairs={{0,6},{1,7},{2,4},{3,5},{4,2},{5,3},{6,0},{7,1},{8,14},{9,15},{10,... | collective-permute-start | bytes 248840 | tf_op jit(solution)/shard_map/ppermute | solution.py:356
  61.0 2.1 %collective-permute-start.16 = (bf16[72,576]{1,0:T(8,128)(2,1)S(1)}, bf16[72,576]{1,0:T(8,128)(2,1)S(1)}, u32[]{:S(2)}, u32[]{:S(2)}) collective-permute-start(bf16[72,576]{1,0:T(8,128)(2,1)S(1)} %get-tuple-element.51), channel_id=1, source_target_pairs={{0,4},{1,5},{2,6},{3,7},{4,0},{5,1},{6,2},{7,3},{8,12},{9,13},{10,... | collective-permute-start | bytes 248840 | tf_op jit(solution)/shard_map/ppermute | solution.py:356
  63.1 0.1 collective-permute-start.17
  63.2 4.0 %shard_map.106 = (bf16[128,1152]{1,0:T(8,128)(2,1)}, bf16[128,1152]{1,0:T(8,128)(2,1)}, bf16[128,1728]{1,0:T(8,128)(2,1)}) custom-call(bf16[32,1728]{1,0:T(8,128)(2,1)S(1)} %collective-permute-done.8.refs_0_, bf16[32,1728]{1,0:T(8,128)(2,1)S(1)} %collective-permute-done.9.refs_1_, bf16[32,1728]{1,0:T(8,128)(2,1)S(1)} %collective-permute-done.10.refs_2_, ...), custom_call_target="tpu_custom_call" | custom-call | tf_op jit(solution)/shard_map/pallas_call | solution.py:44
  67.2 2.2 %collective-permute-done.16.refs_1_ = bf16[72,576]{1,0:T(8,128)(2,1)S(1)} collective-permute-done((bf16[72,576]{1,0:T(8,128)(2,1)S(1)}, bf16[72,576]{1,0:T(8,128)(2,1)S(1)}, u32[]{:S(2)}, u32[]{:S(2)}) %collective-permute-start.16) | collective-permute-done | bytes 82976 | tf_op jit(solution)/shard_map/ppermute | solution.py:356
  69.4 0.8 %shard_map.110 = (f32[72,288]{1,0:T(8,128)}, f32[72,288]{1,0:T(8,128)}) custom-call(f32[72,576]{1,0:T(8,128)S(1)} %get-tuple-element.49.own, bf16[72,576]{1,0:T(8,128)(2,1)S(1)} %collective-permute-done.15.refs_0_, bf16[72,576]{1,0:T(8,128)(2,1)S(1)} %collective-permute-done.16.refs_1_, bf16[72,576]{1,0:T(8,128)(2,1)S(1)} %collective-permute-done.17.refs_2_), custom_call_target="tpu_custom_call" | custom-call | tf_op jit(solution)/shard_map/pallas_call | solution.py:44
  (26 shorter events, 0.3 us)
Async XLA Ops:
  0.6 15.4 %collective-permute-start = (bf16[432,1152]{1,0:T(8,128)(2,1)}, bf16[432,1152]{1,0:T(8,128)(2,1)S(1)}, u32[]{:S(2)}, u32[]{:S(2)}) collective-permute-start(bf16[432,1152]{1,0:T(8,128)(2,1)} %bitcast.9), channel_id=1, source_target_pairs={{0,8},{1,17},{2,10},{3,19},{4,12},{5,21},{6,14},{7,23},{8,0},{9,25... | collective-permute-start | bytes 2985992 | tf_op jit(solution)/shard_map/ppermute | solution.py:368
  7.6 10.7 %collective-permute-start.1 = (bf16[32,2944]{1,0:T(8,128)(2,1)S(1)}, bf16[32,2944]{1,0:T(8,128)(2,1)S(1)}, u32[]{:S(2)}, u32[]{:S(2)}) collective-permute-start(bf16[32,2944]{1,0:T(8,128)(2,1)S(1)} %get-tuple-element.32), channel_id=1, source_target_pairs={{0,2},{1,3},{2,0},{3,1},{4,6},{5,7},{6,4},{7,5},{8,10},{9,11},{10,... | collective-permute-start | bytes 565256 | tf_op jit(solution)/shard_map/ppermute | solution.py:356
  9.2 16.6 %collective-permute-start.2 = (bf16[32,2944]{1,0:T(8,128)(2,1)S(1)}, bf16[32,2944]{1,0:T(8,128)(2,1)S(1)}, u32[]{:S(2)}, u32[]{:S(2)}) collective-permute-start(bf16[32,2944]{1,0:T(8,128)(2,1)S(1)} %get-tuple-element.33), channel_id=1, source_target_pairs={{0,4},{1,5},{2,6},{3,7},{4,0},{5,1},{6,2},{7,3},{8,12},{9,13},{10,... | collective-permute-start | bytes 565256 | tf_op jit(solution)/shard_map/ppermute | solution.py:356
  11.8 14.1 %collective-permute-start.3 = (bf16[32,2944]{1,0:T(8,128)(2,1)S(1)}, bf16[32,2944]{1,0:T(8,128)(2,1)S(1)}, u32[]{:S(2)}, u32[]{:S(2)}) collective-permute-start(bf16[32,2944]{1,0:T(8,128)(2,1)S(1)} %get-tuple-element.34), channel_id=1, source_target_pairs={{0,6},{1,7},{2,4},{3,5},{4,2},{5,3},{6,0},{7,1},{8,14},{9,15},{10,... | collective-permute-start | bytes 565256 | tf_op jit(solution)/shard_map/ppermute | solution.py:356
  16.1 13.0 %copy-start.1 = (bf16[576,1152]{1,0:T(8,128)(2,1)S(1)}, bf16[576,1152]{1,0:T(8,128)(2,1)}, u32[]{:S(2)}) copy-start(bf16[576,1152]{1,0:T(8,128)(2,1)} %refs_8_.1) | copy-start | bytes 3981316
  16.1 13.0 %copy-start.3 = (bf16[1152,432]{0,1:T(8,128)(2,1)S(1)}, bf16[1152,432]{0,1:T(8,128)(2,1)}, u32[]{:S(2)}) copy-start(bf16[1152,432]{0,1:T(8,128)(2,1)} %param.9) | copy-start | bytes 2985988
  16.2 9.8 %collective-permute-start.6 = (bf16[216,1152]{1,0:T(8,128)(2,1)S(1)}, bf16[216,1152]{1,0:T(8,128)(2,1)S(1)}, u32[]{:S(2)}, u32[]{:S(2)}) collective-permute-start(bf16[216,1152]{1,0:T(8,128)(2,1)S(1)} %get-tuple-element.35), channel_id=1, source_target_pairs={{0,16},{1,9},{2,18},{3,11},{4,20},{5,13},{6,22},{7,15},{8,24},{9,1... | collective-permute-start | bytes 1493000 | tf_op jit(solution)/shard_map/ppermute | solution.py:368
  18.3 10.0 %collective-permute-start.5 = (bf16[432,1152]{1,0:T(8,128)(2,1)S(1)}, bf16[432,1152]{1,0:T(8,128)(2,1)S(1)}, u32[]{:S(2)}, u32[]{:S(2)}) collective-permute-start(bf16[432,1152]{1,0:T(8,128)(2,1)S(1)} %collective-permute-done.got.refs_1_), channel_id=1, source_target_pairs={{0,1},{1,0},{2,3},{3,2},{4,5},{5,4},{6,7},{7,6},{8,9},{9,8},{10,11... | collective-permute-start | bytes 2985992 | tf_op jit(solution)/shard_map/ppermute | solution.py:356
  25.9 2.4 %collective-permute-start.4 = (bf16[128,3200]{1,0:T(8,128)(2,1)S(1)}, bf16[128,3200]{1,0:T(8,128)(2,1)S(1)}, u32[]{:S(2)}, u32[]{:S(2)}) collective-permute-start(bf16[128,3200]{1,0:T(8,128)(2,1)S(1)} %shard_map.103.near.refs_0_), channel_id=1, source_target_pairs={{0,1},{1,0},{2,3},{3,2},{4,5},{5,4},{6,7},{7,6},{8,9},{9,8},{10,11... | collective-permute-start | bytes 2457608 | tf_op jit(solution)/shard_map/ppermute | solution.py:356
  26.0 3.0 %collective-permute-start.7 = (bf16[216,1152]{1,0:T(8,128)(2,1)S(1)}, bf16[216,1152]{1,0:T(8,128)(2,1)S(1)}, u32[]{:S(2)}, u32[]{:S(2)}) collective-permute-start(bf16[216,1152]{1,0:T(8,128)(2,1)S(1)} %collective-permute-done.6.refs_3_), channel_id=1, source_target_pairs={{0,1},{1,0},{2,3},{3,2},{4,5},{5,4},{6,7},{7,6},{8,9},{9,8},{10,11... | collective-permute-start | bytes 1493000 | tf_op jit(solution)/shard_map/ppermute | solution.py:356
  36.1 1.9 %collective-permute-start.12 = (bf16[128,1728]{1,0:T(8,128)(2,1)S(1)}, bf16[128,1728]{1,0:T(8,128)(2,1)S(1)}, u32[]{:S(2)}, u32[]{:S(2)}) collective-permute-start(bf16[128,1728]{1,0:T(8,128)(2,1)S(1)} %get-tuple-element.39.mine.refs_3_), channel_id=1, source_target_pairs={{0,1},{1,0},{2,3},{3,2},{4,5},{5,4},{6,7},{7,6},{8,9},{9,8},{10,11... | collective-permute-start | bytes 1327112 | tf_op jit(solution)/shard_map/ppermute | solution.py:356
  40.4 10.7 %collective-permute-start.13 = (bf16[4,72,1152]{2,1,0:T(8,128)(2,1)S(1)}, bf16[4,72,1152]{2,1,0:T(8,128)(2,1)S(1)}, u32[]{:S(2)}, u32[]{:S(2)}) collective-permute-start(bf16[4,72,1152]{2,1,0:T(8,128)(2,1)S(1)} %get-tuple-element.46), channel_id=1, source_target_pairs={{0,8},{1,17},{2,10},{3,19},{4,12},{5,21},{6,14},{7,23},{8,0},{9,25... | collective-permute-start | bytes 1990664 | tf_op jit(solution)/shard_map/ppermute | solution.py:368
  40.9 11.2 %collective-permute-start.8 = (bf16[32,1728]{1,0:T(8,128)(2,1)S(1)}, bf16[32,1728]{1,0:T(8,128)(2,1)S(1)}, u32[]{:S(2)}, u32[]{:S(2)}) collective-permute-start(bf16[32,1728]{1,0:T(8,128)(2,1)S(1)} %get-tuple-element.36), channel_id=1, source_target_pairs={{0,6},{1,7},{2,4},{3,5},{4,2},{5,3},{6,0},{7,1},{8,14},{9,15},{10,... | collective-permute-start | bytes 331784 | tf_op jit(solution)/shard_map/ppermute | solution.py:356
  44.0 11.3 %collective-permute-start.9 = (bf16[32,1728]{1,0:T(8,128)(2,1)S(1)}, bf16[32,1728]{1,0:T(8,128)(2,1)S(1)}, u32[]{:S(2)}, u32[]{:S(2)}) collective-permute-start(bf16[32,1728]{1,0:T(8,128)(2,1)S(1)} %get-tuple-element.37), channel_id=1, source_target_pairs={{0,4},{1,5},{2,6},{3,7},{4,0},{5,1},{6,2},{7,3},{8,12},{9,13},{10,... | collective-permute-start | bytes 331784 | tf_op jit(solution)/shard_map/ppermute | solution.py:356
  46.3 9.0 %collective-permute-start.10 = (bf16[32,1728]{1,0:T(8,128)(2,1)S(1)}, bf16[32,1728]{1,0:T(8,128)(2,1)S(1)}, u32[]{:S(2)}, u32[]{:S(2)}) collective-permute-start(bf16[32,1728]{1,0:T(8,128)(2,1)S(1)} %get-tuple-element.38), channel_id=1, source_target_pairs={{0,2},{1,3},{2,0},{3,1},{4,6},{5,7},{6,4},{7,5},{8,10},{9,11},{10,... | collective-permute-start | bytes 331784 | tf_op jit(solution)/shard_map/ppermute | solution.py:356
  51.1 12.1 %copy-start.4 = (f32[8,128,128]{2,1,0:T(8,128)S(1)}, f32[8,128,128]{2,1,0:T(8,128)}, u32[]{:S(2)}) copy-start(f32[8,128,128]{2,1,0:T(8,128)} %get-tuple-element.40.refs_7_) | copy-start | bytes 1572868
  51.2 12.0 %copy-start = (bf16[576,1152]{1,0:T(8,128)(2,1)S(1)}, bf16[576,1152]{1,0:T(8,128)(2,1)}, u32[]{:S(2)}) copy-start(bf16[576,1152]{1,0:T(8,128)(2,1)} %refs_5_.1) | copy-start | bytes 3981316
  51.2 12.0 %copy-start.2 = (bf16[2,64,1728]{2,1,0:T(8,128)(2,1)S(1)}, bf16[2,64,1728]{2,1,0:T(8,128)(2,1)}, u32[]{:S(2)}) copy-start(bf16[2,64,1728]{2,1,0:T(8,128)(2,1)} %param.7) | copy-start | bytes 1327108
  51.2 12.0 %copy-start.5 = (bf16[128,1152]{1,0:T(8,128)(2,1)S(1)}, bf16[128,1152]{1,0:T(8,128)(2,1)}, u32[]{:S(2)}) copy-start(bf16[128,1152]{1,0:T(8,128)(2,1)} %get-tuple-element.41.refs_9_) | copy-start | bytes 884740
  51.2 7.2 %collective-permute-start.14 = (bf16[2,72,1152]{2,1,0:T(8,128)(2,1)S(1)}, bf16[2,72,1152]{2,1,0:T(8,128)(2,1)S(1)}, u32[]{:S(2)}, u32[]{:S(2)}) collective-permute-start(bf16[2,72,1152]{2,1,0:T(8,128)(2,1)S(1)} %get-tuple-element.48), channel_id=1, source_target_pairs={{0,16},{1,9},{2,18},{3,11},{4,20},{5,13},{6,22},{7,15},{8,24},{9,1... | collective-permute-start | bytes 995336 | tf_op jit(solution)/shard_map/ppermute | solution.py:368
  55.3 7.8 %collective-permute-start.11 = (bf16[64,2816]{1,0:T(8,128)(2,1)S(1)}, bf16[64,2816]{1,0:T(8,128)(2,1)S(1)}, u32[]{:S(2)}, u32[]{:S(2)}) collective-permute-start(bf16[64,2816]{1,0:T(8,128)(2,1)S(1)} %shard_map.105), channel_id=1, source_target_pairs={{0,1},{1,0},{2,3},{3,2},{4,5},{5,4},{6,7},{7,6},{8,9},{9,8},{10,11... | collective-permute-start | bytes 1081352 | tf_op jit(solution)/shard_map/ppermute | solution.py:356
  58.6 8.6 %collective-permute-start.15 = (bf16[72,576]{1,0:T(8,128)(2,1)S(1)}, bf16[72,576]{1,0:T(8,128)(2,1)S(1)}, u32[]{:S(2)}, u32[]{:S(2)}) collective-permute-start(bf16[72,576]{1,0:T(8,128)(2,1)S(1)} %get-tuple-element.50), channel_id=1, source_target_pairs={{0,6},{1,7},{2,4},{3,5},{4,2},{5,3},{6,0},{7,1},{8,14},{9,15},{10,... | collective-permute-start | bytes 248840 | tf_op jit(solution)/shard_map/ppermute | solution.py:356
  61.0 8.4 %collective-permute-start.16 = (bf16[72,576]{1,0:T(8,128)(2,1)S(1)}, bf16[72,576]{1,0:T(8,128)(2,1)S(1)}, u32[]{:S(2)}, u32[]{:S(2)}) collective-permute-start(bf16[72,576]{1,0:T(8,128)(2,1)S(1)} %get-tuple-element.51), channel_id=1, source_target_pairs={{0,4},{1,5},{2,6},{3,7},{4,0},{5,1},{6,2},{7,3},{8,12},{9,13},{10,... | collective-permute-start | bytes 248840 | tf_op jit(solution)/shard_map/ppermute | solution.py:356
  63.1 6.3 %collective-permute-start.17 = (bf16[72,576]{1,0:T(8,128)(2,1)S(1)}, bf16[72,576]{1,0:T(8,128)(2,1)S(1)}, u32[]{:S(2)}, u32[]{:S(2)}) collective-permute-start(bf16[72,576]{1,0:T(8,128)(2,1)S(1)} %get-tuple-element.52), channel_id=1, source_target_pairs={{0,2},{1,3},{2,0},{3,1},{4,6},{5,7},{6,4},{7,5},{8,10},{9,11},{10,... | collective-permute-start | bytes 248840 | tf_op jit(solution)/shard_map/ppermute | solution.py:356

commit v16 on v14

--- a/solution.py
+++ b/solution.py
@@ -261,38 +261,42 @@
     part[1] = dot_at(so, near[:, :width]).astype(BF16)
 
 
-def parts_kernel(chips, block, inner, width, mine, other, *refs):
-    idx = place(chips)
-    sent, refs = refs[:2], refs[2:]
-    keep, send_x, send_y, heads, cols = refs
-    half = mine.shape[0] // 2
-    near = all_patches(mine[:half], other[half:], idx[1], block)
-    far = all_patches(mine[half:], other[:half], idx[1], block)
-    rows = near.shape[0]
+def products(idx, core, chips, block, inner, width, rows, first, second, heads, cols):
+    held = [own_patches(ref, core, block)[:, width:] for ref in (first, second)]
+    held = jnp.concatenate(held, axis=0).astype(BF16)
     size = heads.shape[2]
     count, _, wide = cols.shape
     for i in range(2):
-        if i == 0:
-            lefts = [near[:, width:], far[:, width:]]
-            rights = [part[:, width : 2 * width] for part in sent]
-        else:
-            lefts = [part[:, 2 * width : 2 * width + inner] for part in sent]
-            rights = [near[:, :width], far[:, :width]]
-        for at in range(2):
-            held = slice(at * rows, (at + 1) * rows)
-            for h in range(heads.shape[0]):
-                heads[h, held] = lefts[at][:, h * size : (h + 1) * size]
-            for r in range(count):
-                cols[r, held] = rights[at][:, r * wide : (r + 1) * wide]
+        left = rows[:, width:] if i == 0 else held[:, width : width + inner]
+        right = held[:, :width] if i == 0 else rows[:, :width]
+        for h in range(heads.shape[0]):
+            heads[h] = left[:, h * size : (h + 1) * size]
+        for r in range(count):
+            cols[r] = right[:, r * wide : (r + 1) * wide]
         left = jnp.concatenate([heads[idx[3] ^ (2 * q)] for q in range(chips)], axis=1)
-        first = 1 if i == 0 else 2
         for r in range(count):
             full = dot_at(left, cols[idx[0] ^ r])
-            value = jnp.concatenate([full[q * size : (q + 1) * size] for q in range(chips)], axis=1)
-            if r & first:
-                (send_x, send_y)[i][r // 2 if i == 0 else r - 2] = value.astype(BF16)
-            else:
-                keep[2 * i + (r > 0)] = value
+            value = [full[q * size : (q + 1) * size] for q in range(chips)]
+            yield i, r, jnp.concatenate(value, axis=1)
+
+
+def own_parts_kernel(chips, block, inner, width, mine, near, far, part, heads, cols):
+    idx = place(chips)
+    sizes = (chips, block, inner, width)
+    for i, r, value in products(idx, idx[1], *sizes, mine, near, far, heads, cols):
+        part[4 * i + r] = value
+
+
+def parts_kernel(chips, block, inner, width, other, near, far, part, *refs):
+    keep, send_x, send_y, heads, cols = refs
+    idx = place(chips)
+    sizes = (chips, block, inner, width)
+    for i, r, value in products(idx, 1 - idx[1], *sizes, other, far, near, heads, cols):
+        value += part[4 * i + r]
+        if r & (1 if i == 0 else 2):
+            (send_x, send_y)[i][r // 2 if i == 0 else r - 2] = value.astype(BF16)
+        else:
+            keep[2 * i + (r > 0)] = value
 
 
 def sum_first_kernel(keep, got_x, got_y, own, send_y, send_x):
@@ -338,7 +342,7 @@
     stores = started([(rows.at[:, pl.ds(0, width)], out_far)], sems.at[pl.ds(0, 1)])
     block_out[...] = (hid[...].astype(F32) + dot(attended, wot[...])).astype(BF16)
     stores += started([(block_out, block_far)], sems.at[pl.ds(1, 1)])
-    put(gs, dot_weight(grad, wos[...]).astype(BF16))
+    put(gs, dot_bt(grad, wos[...]).astype(BF16))
     x = qkv[...]
     put(qs, x[:, :inner])
     put(ks, x[:, inner : 2 * inner])
@@ -469,14 +473,22 @@
     other = flip(mine, "seq", 1)
     if n_dp == 4 and n_seq == peers:
         size = inner // n_seq
+        work = [
+            pltpu.VMEM((n_seq, rows, size), BF16),
+            pltpu.VMEM((n_dp, rows, width // n_dp), BF16),
+        ]
+        (part,) = call(
+            functools.partial(own_parts_kernel, chips, block, inner, width),
+            [shape((2 * n_dp, size, width), F32)],
+            [mine, near, far],
+            work,
+            small=True,
+        )
         keep, send_x, send_y = call(
             functools.partial(parts_kernel, chips, block, inner, width),
             [shape((n_dp, size, width), F32)] + [shape((2, size, width))] * 2,
-            [mine, other, near, far],
-            [
-                pltpu.VMEM((n_seq, 2 * rows, size), BF16),
-                pltpu.VMEM((n_dp, 2 * rows, width // n_dp), BF16),
-            ],
+            [other, near, far, part],
+            work,
             small=True,
         )
     else:

time: 69.8 us -> 69.7 us (level)
  waiting for transfers between devices: 25.7 us -> 24.9 us
    ppermute x18, waiting for transfers between devices: 21.7 us -> 20.9 us  [flip(): lax.ppermute(value, axis, [(i, i ^ bit) for i in range(lax.axis_size(axis...]
    pallas_call x10 -> x11, Pallas kernels: 19.2 us -> 19.8 us  [call(): pl.pallas_call(body, out_shape=outs, in_specs=[HBM if i in far_in else sp...]
  transfers between devices with their start and end apart: 20 -> 20, of which waited for: 10 -> 9; matrix products, arithmetic and copies ran while one was open for 0% -> 0% of each run, Pallas kernels for 13% -> 15%
where the time goes in v16:
time: 69.7 us; the launch traced here: 69.5 us
  waiting for transfers between devices  24.9 us (36%)
  starting transfers between devices  23.9 us (34%)
  Pallas kernels  19.8 us (28%)
  between operations  0.78 us (1%)
    ppermute x18, waiting for transfers between devices, flip(): lax.ppermute(value, axis, [(i, i ^ bit) for i in range(lax.axis_size(axis...  20.9 us
    pallas_call x11, Pallas kernels, call(): pl.pallas_call(body, out_shape=outs, in_specs=[HBM if i in far_in else sp...  19.8 us
    ppermute x18, starting transfers between devices, flip(): lax.ppermute(value, axis, [(i, i ^ bit) for i in range(lax.axis_size(axis...  18.8 us
    ppermute x2, starting transfers between devices, across(): return lax.ppermute(value, ('dp', 'seq'), pairs)  5.12 us
    ppermute x2, waiting for transfers between devices, across(): return lax.ppermute(value, ('dp', 'seq'), pairs)  4 us
  transfers between devices with their start and end apart: 20, of which 9 were waited for; matrix products, arithmetic and copies ran while one was open for 0% of the time, Pallas kernels for 15%

profile of v16, /device:TPU:0, one launch (start us, length us, event | category | flops | bytes accessed | tf_op | source)
XLA Modules:
  0.0 69.5 jit_solution(15548860281314635139)
XLA Ops:
  0.6 3.0 %collective-permute-start = (bf16[432,1152]{1,0:T(8,128)(2,1)}, bf16[432,1152]{1,0:T(8,128)(2,1)S(1)}, u32[]{:S(2)}, u32[]{:S(2)}) collective-permute-start(bf16[432,1152]{1,0:T(8,128)(2,1)} %bitcast.9), channel_id=1, source_target_pairs={{0,8},{1,17},{2,10},{3,19},{4,12},{5,21},{6,14},{7,23},{8,0},{9,25... | collective-permute-start | bytes 2985992 | tf_op jit(solution)/shard_map/ppermute | solution.py:370
  3.6 4.0 %shard_map.101 = (bf16[32,2944]{1,0:T(8,128)(2,1)S(1)}, bf16[32,2944]{1,0:T(8,128)(2,1)S(1)}, bf16[32,2944]{1,0:T(8,128)(2,1)S(1)}, bf16[32,2944]{1,0:T(8,128)(2...) custom-call(bf16[128,1728]{1,0:T(8,128)(2,1)} %bitcast.7, bf16[128,1152]{1,0:T(8,128)(2,1)} %bitcast.11, ...), custom_call_target="tpu_custom_call" | custom-call | tf_op jit(solution)/shard_map/pallas_call | solution.py:43
  7.6 1.6 %collective-permute-start.1 = (bf16[32,2944]{1,0:T(8,128)(2,1)S(1)}, bf16[32,2944]{1,0:T(8,128)(2,1)S(1)}, u32[]{:S(2)}, u32[]{:S(2)}) collective-permute-start(bf16[32,2944]{1,0:T(8,128)(2,1)S(1)} %get-tuple-element.34), channel_id=1, source_target_pairs={{0,2},{1,3},{2,0},{3,1},{4,6},{5,7},{6,4},{7,5},{8,10},{9,11},{10,... | collective-permute-start | bytes 565256 | tf_op jit(solution)/shard_map/ppermute | solution.py:358
  9.2 2.6 %collective-permute-start.2 = (bf16[32,2944]{1,0:T(8,128)(2,1)S(1)}, bf16[32,2944]{1,0:T(8,128)(2,1)S(1)}, u32[]{:S(2)}, u32[]{:S(2)}) collective-permute-start(bf16[32,2944]{1,0:T(8,128)(2,1)S(1)} %get-tuple-element.35), channel_id=1, source_target_pairs={{0,4},{1,5},{2,6},{3,7},{4,0},{5,1},{6,2},{7,3},{8,12},{9,13},{10,... | collective-permute-start | bytes 565256 | tf_op jit(solution)/shard_map/ppermute | solution.py:358
  11.8 0.2 collective-permute-start.3
  12.1 4.0 %collective-permute-done.got.refs_1_ = bf16[432,1152]{1,0:T(8,128)(2,1)S(1)} collective-permute-done((bf16[432,1152]{1,0:T(8,128)(2,1)}, bf16[432,1152]{1,0:T(8,128)(2,1)S(1)}, u32[]{:S(2)}, u32[]{:S(2)}) %collective-permute-start) | collective-permute-done | bytes 995360 | tf_op jit(solution)/shard_map/ppermute | solution.py:370
  16.2 2.1 %collective-permute-start.6 = (bf16[216,1152]{1,0:T(8,128)(2,1)S(1)}, bf16[216,1152]{1,0:T(8,128)(2,1)S(1)}, u32[]{:S(2)}, u32[]{:S(2)}) collective-permute-start(bf16[216,1152]{1,0:T(8,128)(2,1)S(1)} %get-tuple-element.37), channel_id=1, source_target_pairs={{0,16},{1,9},{2,18},{3,11},{4,20},{5,13},{6,22},{7,15},{8,24},{9,1... | collective-permute-start | bytes 1493000 | tf_op jit(solution)/shard_map/ppermute | solution.py:370
  18.3 7.6 %collective-permute-done.2.refs_2_ = bf16[32,2944]{1,0:T(8,128)(2,1)S(1)} collective-permute-done((bf16[32,2944]{1,0:T(8,128)(2,1)S(1)}, bf16[32,2944]{1,0:T(8,128)(2,1)S(1)}, u32[]{:S(2)}, u32[]{:S(2)}) %collective-permute-start.2) | collective-permute-done | bytes 188448 | tf_op jit(solution)/shard_map/ppermute | solution.py:358
  26.0 0.5 collective-permute-start.7
  26.5 1.8 %collective-permute-done.4.far = bf16[128,3200]{1,0:T(8,128)(2,1)S(1)} collective-permute-done((bf16[128,3200]{1,0:T(8,128)(2,1)S(1)}, bf16[128,3200]{1,0:T(8,128)(2,1)S(1)}, u32[]{:S(2)}, u32[]{:S(2)}) %collective-permute-start.4) | collective-permute-done | bytes 819232 | tf_op jit(solution)/shard_map/ppermute | solution.py:358
  28.3 0.7 %collective-permute-done.7.refs_4_ = bf16[216,1152]{1,0:T(8,128)(2,1)S(1)} collective-permute-done((bf16[216,1152]{1,0:T(8,128)(2,1)S(1)}, bf16[216,1152]{1,0:T(8,128)(2,1)S(1)}, u32[]{:S(2)}, u32[]{:S(2)}) %collective-permute-start.7) | collective-permute-done | bytes 497696 | tf_op jit(solution)/shard_map/ppermute | solution.py:358
  29.1 7.1 %shard_map.104 = (bf16[128,1728]{1,0:T(8,128)(2,1)S(1)}, bf16[32,1728]{1,0:T(8,128)(2,1)S(1)}, bf16[32,1728]{1,0:T(8,128)(2,1)S(1)}, bf16[32,1728]{1,0:T(8,128)(2,1)S(1)}) custom-call(bf16[128,3200]{1,0:T(8,128)(2,1)S(1)} %shard_map.103.near, bf16[128,3200]{1,0:T(8,128)(2,1)S(1)} %collective-permute-done.4.far, bf16[576,1152]{1,0:T(8,128)(2,1)S(1)} %copy-done.1, ...), custom_call_target="tpu_custom_call" | custom-call | tf_op jit(solution)/shard_map/pallas_call | solution.py:43
  36.1 0.2 collective-permute-start.12
  36.3 1.8 %shard_map.107.part = f32[8,72,1152]{2,1,0:T(8,128)S(1)} custom-call(bf16[128,1728]{1,0:T(8,128)(2,1)S(1)} %get-tuple-element.41.mine.refs_3_, bf16[128,3200]{1,0:T(8,128)(2,1)S(1)} %shard_map.103.near, bf16[128,3200]{1,0:T(8,128)(2,1)S(1)} %collective-permute-done.4.far), custom_call_target="tpu_custom_call" | custom-call | tf_op jit(solution)/shard_map/pallas_call | solution.py:43
  38.1 1.8 %shard_map.108 = (f32[4,72,1152]{2,1,0:T(8,128)S(1)}, bf16[2,72,1152]{2,1,0:T(8,128)(2,1)S(1)}, bf16[2,72,1152]{2,1,0:T(8,128)(2,1)S(1)}) custom-call(bf16[128,1728]{1,0:T(8,128)(2,1)S(1)} %collective-permute-done.12.other, bf16[128,3200]{1,0:T(8,128)(2,1)S(1)} %shard_map.103.near, bf16[128,3200]{1,0:T(8,128)(2,1)S(1)} %collective-permute-done.4.far, ...), custom_call_target="tpu_custom_call" | custom-call | tf_op jit(solution)/shard_map/pallas_call | solution.py:43
  39.9 0.5 collective-permute-start.13
  40.5 1.6 %collective-permute-start.14 = (bf16[2,72,1152]{2,1,0:T(8,128)(2,1)S(1)}, bf16[2,72,1152]{2,1,0:T(8,128)(2,1)S(1)}, u32[]{:S(2)}, u32[]{:S(2)}) collective-permute-start(bf16[2,72,1152]{2,1,0:T(8,128)(2,1)S(1)} %get-tuple-element.49), channel_id=1, source_target_pairs={{0,16},{8,24},{16,0},{24,8},{1,17},{9,25},{17,1},{25,9},{2,18},{10... | collective-permute-start | bytes 995336 | tf_op jit(solution)/shard_map/ppermute | solution.py:358
  42.1 3.1 %collective-permute-start.8 = (bf16[32,1728]{1,0:T(8,128)(2,1)S(1)}, bf16[32,1728]{1,0:T(8,128)(2,1)S(1)}, u32[]{:S(2)}, u32[]{:S(2)}) collective-permute-start(bf16[32,1728]{1,0:T(8,128)(2,1)S(1)} %get-tuple-element.38), channel_id=1, source_target_pairs={{0,6},{1,7},{2,4},{3,5},{4,2},{5,3},{6,0},{7,1},{8,14},{9,15},{10,... | collective-permute-start | bytes 331784 | tf_op jit(solution)/shard_map/ppermute | solution.py:358
  45.1 1.3 %collective-permute-start.9 = (bf16[32,1728]{1,0:T(8,128)(2,1)S(1)}, bf16[32,1728]{1,0:T(8,128)(2,1)S(1)}, u32[]{:S(2)}, u32[]{:S(2)}) collective-permute-start(bf16[32,1728]{1,0:T(8,128)(2,1)S(1)} %get-tuple-element.39), channel_id=1, source_target_pairs={{0,4},{1,5},{2,6},{3,7},{4,0},{5,1},{6,2},{7,3},{8,12},{9,13},{10,... | collective-permute-start | bytes 331784 | tf_op jit(solution)/shard_map/ppermute | solution.py:358
  46.5 3.6 %collective-permute-done.13.got_x = bf16[2,72,1152]{2,1,0:T(8,128)(2,1)S(1)} collective-permute-done((bf16[2,72,1152]{2,1,0:T(8,128)(2,1)S(1)}, bf16[2,72,1152]{2,1,0:T(8,128)(2,1)S(1)}, u32[]{:S(2)}, u32[]{:S(2)}) %collective-permute-start.13) | collective-permute-done | bytes 331808 | tf_op jit(solution)/shard_map/ppermute | solution.py:358
  50.1 0.2 collective-permute-done.14.got_y
  50.3 0.1 shard_map.109
  50.4 1.6 %collective-permute-start.15 = (bf16[72,1152]{1,0:T(8,128)(2,1)S(1)}, bf16[72,1152]{1,0:T(8,128)(2,1)S(1)}, u32[]{:S(2)}, u32[]{:S(2)}) collective-permute-start(bf16[72,1152]{1,0:T(8,128)(2,1)S(1)} %get-tuple-element.51), channel_id=1, source_target_pairs={{0,16},{8,24},{16,0},{24,8},{1,17},{9,25},{17,1},{25,9},{2,18},{10... | collective-permute-start | bytes 497672 | tf_op jit(solution)/shard_map/ppermute | solution.py:358
  52.1 0.8 %collective-permute-start.16 = (bf16[72,1152]{1,0:T(8,128)(2,1)S(1)}, bf16[72,1152]{1,0:T(8,128)(2,1)S(1)}, u32[]{:S(2)}, u32[]{:S(2)}) collective-permute-start(bf16[72,1152]{1,0:T(8,128)(2,1)S(1)} %get-tuple-element.52), channel_id=1, source_target_pairs={{0,8},{8,0},{16,24},{24,16},{1,9},{9,1},{17,25},{25,17},{2,10},{10... | collective-permute-start | bytes 497672 | tf_op jit(solution)/shard_map/ppermute | solution.py:358
  52.9 3.2 %collective-permute-done.9.refs_1_ = bf16[32,1728]{1,0:T(8,128)(2,1)S(1)} collective-permute-done((bf16[32,1728]{1,0:T(8,128)(2,1)S(1)}, bf16[32,1728]{1,0:T(8,128)(2,1)S(1)}, u32[]{:S(2)}, u32[]{:S(2)}) %collective-permute-start.9) | collective-permute-done | bytes 110624 | tf_op jit(solution)/shard_map/ppermute | solution.py:358
  56.2 1.2 %collective-permute-done.16.got_x = bf16[72,1152]{1,0:T(8,128)(2,1)S(1)} collective-permute-done((bf16[72,1152]{1,0:T(8,128)(2,1)S(1)}, bf16[72,1152]{1,0:T(8,128)(2,1)S(1)}, u32[]{:S(2)}, u32[]{:S(2)}) %collective-permute-start.16) | collective-permute-done | bytes 165920 | tf_op jit(solution)/shard_map/ppermute | solution.py:358
  57.4 0.2 shard_map.110
  57.6 3.1 %collective-permute-start.17 = (bf16[72,576]{1,0:T(8,128)(2,1)S(1)}, bf16[72,576]{1,0:T(8,128)(2,1)S(1)}, u32[]{:S(2)}, u32[]{:S(2)}) collective-permute-start(bf16[72,576]{1,0:T(8,128)(2,1)S(1)} %get-tuple-element.54), channel_id=1, source_target_pairs={{0,6},{1,7},{2,4},{3,5},{4,2},{5,3},{6,0},{7,1},{8,14},{9,15},{10,... | collective-permute-start | bytes 248840 | tf_op jit(solution)/shard_map/ppermute | solution.py:358
  60.7 1.3 %collective-permute-start.18 = (bf16[72,576]{1,0:T(8,128)(2,1)S(1)}, bf16[72,576]{1,0:T(8,128)(2,1)S(1)}, u32[]{:S(2)}, u32[]{:S(2)}) collective-permute-start(bf16[72,576]{1,0:T(8,128)(2,1)S(1)} %get-tuple-element.55), channel_id=1, source_target_pairs={{0,4},{1,5},{2,6},{3,7},{4,0},{5,1},{6,2},{7,3},{8,12},{9,13},{10,... | collective-permute-start | bytes 248840 | tf_op jit(solution)/shard_map/ppermute | solution.py:358
  62.1 4.0 %shard_map.106 = (bf16[128,1152]{1,0:T(8,128)(2,1)}, bf16[128,1152]{1,0:T(8,128)(2,1)}, bf16[128,1728]{1,0:T(8,128)(2,1)}) custom-call(bf16[32,1728]{1,0:T(8,128)(2,1)S(1)} %collective-permute-done.8.refs_0_, bf16[32,1728]{1,0:T(8,128)(2,1)S(1)} %collective-permute-done.9.refs_1_, bf16[32,1728]{1,0:T(8,128)(2,1)S(1)} %collective-permute-done.10.refs_2_, ...), custom_call_target="tpu_custom_call" | custom-call | tf_op jit(solution)/shard_map/pallas_call | solution.py:43
  66.1 2.6 %collective-permute-done.18.refs_1_ = bf16[72,576]{1,0:T(8,128)(2,1)S(1)} collective-permute-done((bf16[72,576]{1,0:T(8,128)(2,1)S(1)}, bf16[72,576]{1,0:T(8,128)(2,1)S(1)}, u32[]{:S(2)}, u32[]{:S(2)}) %collective-permute-start.18) | collective-permute-done | bytes 82976 | tf_op jit(solution)/shard_map/ppermute | solution.py:358
  68.8 0.8 %shard_map.111 = (f32[72,288]{1,0:T(8,128)}, f32[72,288]{1,0:T(8,128)}) custom-call(f32[72,576]{1,0:T(8,128)S(1)} %get-tuple-element.53.own, bf16[72,576]{1,0:T(8,128)(2,1)S(1)} %collective-permute-done.17.refs_0_, bf16[72,576]{1,0:T(8,128)(2,1)S(1)} %collective-permute-done.18.refs_1_, bf16[72,576]{1,0:T(8,128)(2,1)S(1)} %collective-permute-done.19.refs_2_), custom_call_target="tpu_custom_call" | custom-call | tf_op jit(solution)/shard_map/pallas_call | solution.py:43
  (31 shorter events, 0.6 us)
Async XLA Ops:
  0.6 15.4 %collective-permute-start = (bf16[432,1152]{1,0:T(8,128)(2,1)}, bf16[432,1152]{1,0:T(8,128)(2,1)S(1)}, u32[]{:S(2)}, u32[]{:S(2)}) collective-permute-start(bf16[432,1152]{1,0:T(8,128)(2,1)} %bitcast.9), channel_id=1, source_target_pairs={{0,8},{1,17},{2,10},{3,19},{4,12},{5,21},{6,14},{7,23},{8,0},{9,25... | collective-permute-start | bytes 2985992 | tf_op jit(solution)/shard_map/ppermute | solution.py:370
  7.6 10.7 %collective-permute-start.1 = (bf16[32,2944]{1,0:T(8,128)(2,1)S(1)}, bf16[32,2944]{1,0:T(8,128)(2,1)S(1)}, u32[]{:S(2)}, u32[]{:S(2)}) collective-permute-start(bf16[32,2944]{1,0:T(8,128)(2,1)S(1)} %get-tuple-element.34), channel_id=1, source_target_pairs={{0,2},{1,3},{2,0},{3,1},{4,6},{5,7},{6,4},{7,5},{8,10},{9,11},{10,... | collective-permute-start | bytes 565256 | tf_op jit(solution)/shard_map/ppermute | solution.py:358
  9.2 16.6 %collective-permute-start.2 = (bf16[32,2944]{1,0:T(8,128)(2,1)S(1)}, bf16[32,2944]{1,0:T(8,128)(2,1)S(1)}, u32[]{:S(2)}, u32[]{:S(2)}) collective-permute-start(bf16[32,2944]{1,0:T(8,128)(2,1)S(1)} %get-tuple-element.35), channel_id=1, source_target_pairs={{0,4},{1,5},{2,6},{3,7},{4,0},{5,1},{6,2},{7,3},{8,12},{9,13},{10,... | collective-permute-start | bytes 565256 | tf_op jit(solution)/shard_map/ppermute | solution.py:358
  11.8 14.1 %collective-permute-start.3 = (bf16[32,2944]{1,0:T(8,128)(2,1)S(1)}, bf16[32,2944]{1,0:T(8,128)(2,1)S(1)}, u32[]{:S(2)}, u32[]{:S(2)}) collective-permute-start(bf16[32,2944]{1,0:T(8,128)(2,1)S(1)} %get-tuple-element.36), channel_id=1, source_target_pairs={{0,6},{1,7},{2,4},{3,5},{4,2},{5,3},{6,0},{7,1},{8,14},{9,15},{10,... | collective-permute-start | bytes 565256 | tf_op jit(solution)/shard_map/ppermute | solution.py:358
  16.1 13.0 %copy-start.1 = (bf16[576,1152]{1,0:T(8,128)(2,1)S(1)}, bf16[576,1152]{1,0:T(8,128)(2,1)}, u32[]{:S(2)}) copy-start(bf16[576,1152]{1,0:T(8,128)(2,1)} %refs_8_.1) | copy-start | bytes 3981316
  16.1 13.0 %copy-start.3 = (bf16[1152,432]{0,1:T(8,128)(2,1)S(1)}, bf16[1152,432]{0,1:T(8,128)(2,1)}, u32[]{:S(2)}) copy-start(bf16[1152,432]{0,1:T(8,128)(2,1)} %param.9) | copy-start | bytes 2985988
  16.2 9.8 %collective-permute-start.6 = (bf16[216,1152]{1,0:T(8,128)(2,1)S(1)}, bf16[216,1152]{1,0:T(8,128)(2,1)S(1)}, u32[]{:S(2)}, u32[]{:S(2)}) collective-permute-start(bf16[216,1152]{1,0:T(8,128)(2,1)S(1)} %get-tuple-element.37), channel_id=1, source_target_pairs={{0,16},{1,9},{2,18},{3,11},{4,20},{5,13},{6,22},{7,15},{8,24},{9,1... | collective-permute-start | bytes 1493000 | tf_op jit(solution)/shard_map/ppermute | solution.py:370
  18.3 10.0 %collective-permute-start.5 = (bf16[432,1152]{1,0:T(8,128)(2,1)S(1)}, bf16[432,1152]{1,0:T(8,128)(2,1)S(1)}, u32[]{:S(2)}, u32[]{:S(2)}) collective-permute-start(bf16[432,1152]{1,0:T(8,128)(2,1)S(1)} %collective-permute-done.got.refs_1_), channel_id=1, source_target_pairs={{0,1},{1,0},{2,3},{3,2},{4,5},{5,4},{6,7},{7,6},{8,9},{9,8},{10,11... | collective-permute-start | bytes 2985992 | tf_op jit(solution)/shard_map/ppermute | solution.py:358
  25.9 2.4 %collective-permute-start.4 = (bf16[128,3200]{1,0:T(8,128)(2,1)S(1)}, bf16[128,3200]{1,0:T(8,128)(2,1)S(1)}, u32[]{:S(2)}, u32[]{:S(2)}) collective-permute-start(bf16[128,3200]{1,0:T(8,128)(2,1)S(1)} %shard_map.103.near), channel_id=1, source_target_pairs={{0,1},{1,0},{2,3},{3,2},{4,5},{5,4},{6,7},{7,6},{8,9},{9,8},{10,11... | collective-permute-start | bytes 2457608 | tf_op jit(solution)/shard_map/ppermute | solution.py:358
  26.0 3.0 %collective-permute-start.7 = (bf16[216,1152]{1,0:T(8,128)(2,1)S(1)}, bf16[216,1152]{1,0:T(8,128)(2,1)S(1)}, u32[]{:S(2)}, u32[]{:S(2)}) collective-permute-start(bf16[216,1152]{1,0:T(8,128)(2,1)S(1)} %collective-permute-done.6.refs_3_), channel_id=1, source_target_pairs={{0,1},{1,0},{2,3},{3,2},{4,5},{5,4},{6,7},{7,6},{8,9},{9,8},{10,11... | collective-permute-start | bytes 1493000 | tf_op jit(solution)/shard_map/ppermute | solution.py:358
  36.1 2.0 %collective-permute-start.12 = (bf16[128,1728]{1,0:T(8,128)(2,1)S(1)}, bf16[128,1728]{1,0:T(8,128)(2,1)S(1)}, u32[]{:S(2)}, u32[]{:S(2)}) collective-permute-start(bf16[128,1728]{1,0:T(8,128)(2,1)S(1)} %get-tuple-element.41.mine.refs_3_), channel_id=1, source_target_pairs={{0,1},{1,0},{2,3},{3,2},{4,5},{5,4},{6,7},{7,6},{8,9},{9,8},{10,11... | collective-permute-start | bytes 1327112 | tf_op jit(solution)/shard_map/ppermute | solution.py:358
  39.9 10.1 %collective-permute-start.13 = (bf16[2,72,1152]{2,1,0:T(8,128)(2,1)S(1)}, bf16[2,72,1152]{2,1,0:T(8,128)(2,1)S(1)}, u32[]{:S(2)}, u32[]{:S(2)}) collective-permute-start(bf16[2,72,1152]{2,1,0:T(8,128)(2,1)S(1)} %get-tuple-element.48), channel_id=1, source_target_pairs={{0,8},{8,0},{16,24},{24,16},{1,9},{9,1},{17,25},{25,17},{2,10},{10... | collective-permute-start | bytes 995336 | tf_op jit(solution)/shard_map/ppermute | solution.py:358
  40.5 9.8 %collective-permute-start.14 = (bf16[2,72,1152]{2,1,0:T(8,128)(2,1)S(1)}, bf16[2,72,1152]{2,1,0:T(8,128)(2,1)S(1)}, u32[]{:S(2)}, u32[]{:S(2)}) collective-permute-start(bf16[2,72,1152]{2,1,0:T(8,128)(2,1)S(1)} %get-tuple-element.49), channel_id=1, source_target_pairs={{0,16},{8,24},{16,0},{24,8},{1,17},{9,25},{17,1},{25,9},{2,18},{10... | collective-permute-start | bytes 995336 | tf_op jit(solution)/shard_map/ppermute | solution.py:358
  42.1 10.8 %collective-permute-start.8 = (bf16[32,1728]{1,0:T(8,128)(2,1)S(1)}, bf16[32,1728]{1,0:T(8,128)(2,1)S(1)}, u32[]{:S(2)}, u32[]{:S(2)}) collective-permute-start(bf16[32,1728]{1,0:T(8,128)(2,1)S(1)} %get-tuple-element.38), channel_id=1, source_target_pairs={{0,6},{1,7},{2,4},{3,5},{4,2},{5,3},{6,0},{7,1},{8,14},{9,15},{10,... | collective-permute-start | bytes 331784 | tf_op jit(solution)/shard_map/ppermute | solution.py:358
  45.1 11.0 %collective-permute-start.9 = (bf16[32,1728]{1,0:T(8,128)(2,1)S(1)}, bf16[32,1728]{1,0:T(8,128)(2,1)S(1)}, u32[]{:S(2)}, u32[]{:S(2)}) collective-permute-start(bf16[32,1728]{1,0:T(8,128)(2,1)S(1)} %get-tuple-element.39), channel_id=1, source_target_pairs={{0,4},{1,5},{2,6},{3,7},{4,0},{5,1},{6,2},{7,3},{8,12},{9,13},{10,... | collective-permute-start | bytes 331784 | tf_op jit(solution)/shard_map/ppermute | solution.py:358
  46.4 9.7 %collective-permute-start.10 = (bf16[32,1728]{1,0:T(8,128)(2,1)S(1)}, bf16[32,1728]{1,0:T(8,128)(2,1)S(1)}, u32[]{:S(2)}, u32[]{:S(2)}) collective-permute-start(bf16[32,1728]{1,0:T(8,128)(2,1)S(1)} %get-tuple-element.40), channel_id=1, source_target_pairs={{0,2},{1,3},{2,0},{3,1},{4,6},{5,7},{6,4},{7,5},{8,10},{9,11},{10,... | collective-permute-start | bytes 331784 | tf_op jit(solution)/shard_map/ppermute | solution.py:358
  50.3 11.9 %copy-start.4 = (f32[8,128,128]{2,1,0:T(8,128)S(1)}, f32[8,128,128]{2,1,0:T(8,128)}, u32[]{:S(2)}) copy-start(f32[8,128,128]{2,1,0:T(8,128)} %get-tuple-element.42.refs_7_) | copy-start | bytes 1572868
  50.3 11.9 %copy-start.5 = (bf16[128,1152]{1,0:T(8,128)(2,1)S(1)}, bf16[128,1152]{1,0:T(8,128)(2,1)}, u32[]{:S(2)}) copy-start(bf16[128,1152]{1,0:T(8,128)(2,1)} %get-tuple-element.43.refs_9_) | copy-start | bytes 884740
  50.4 11.7 %copy-start = (bf16[576,1152]{1,0:T(8,128)(2,1)S(1)}, bf16[576,1152]{1,0:T(8,128)(2,1)}, u32[]{:S(2)}) copy-start(bf16[576,1152]{1,0:T(8,128)(2,1)} %refs_5_.1) | copy-start | bytes 3981316
  50.4 11.7 %copy-start.2 = (bf16[2,64,1728]{2,1,0:T(8,128)(2,1)S(1)}, bf16[2,64,1728]{2,1,0:T(8,128)(2,1)}, u32[]{:S(2)}) copy-start(bf16[2,64,1728]{2,1,0:T(8,128)(2,1)} %param.7) | copy-start | bytes 1327108
  50.4 5.8 %collective-permute-start.15 = (bf16[72,1152]{1,0:T(8,128)(2,1)S(1)}, bf16[72,1152]{1,0:T(8,128)(2,1)S(1)}, u32[]{:S(2)}, u32[]{:S(2)}) collective-permute-start(bf16[72,1152]{1,0:T(8,128)(2,1)S(1)} %get-tuple-element.51), channel_id=1, source_target_pairs={{0,16},{8,24},{16,0},{24,8},{1,17},{9,25},{17,1},{25,9},{2,18},{10... | collective-permute-start | bytes 497672 | tf_op jit(solution)/shard_map/ppermute | solution.py:358
  52.1 5.3 %collective-permute-start.16 = (bf16[72,1152]{1,0:T(8,128)(2,1)S(1)}, bf16[72,1152]{1,0:T(8,128)(2,1)S(1)}, u32[]{:S(2)}, u32[]{:S(2)}) collective-permute-start(bf16[72,1152]{1,0:T(8,128)(2,1)S(1)} %get-tuple-element.52), channel_id=1, source_target_pairs={{0,8},{8,0},{16,24},{24,16},{1,9},{9,1},{17,25},{25,17},{2,10},{10... | collective-permute-start | bytes 497672 | tf_op jit(solution)/shard_map/ppermute | solution.py:358
  56.1 6.0 %collective-permute-start.11 = (bf16[64,1728]{1,0:T(8,128)(2,1)S(1)}, bf16[64,1728]{1,0:T(8,128)(2,1)S(1)}, u32[]{:S(2)}, u32[]{:S(2)}) collective-permute-start(bf16[64,1728]{1,0:T(8,128)(2,1)S(1)} %shard_map.105), channel_id=1, source_target_pairs={{0,1},{1,0},{2,3},{3,2},{4,5},{5,4},{6,7},{7,6},{8,9},{9,8},{10,11... | collective-permute-start | bytes 663560 | tf_op jit(solution)/shard_map/ppermute | solution.py:358
  57.6 8.5 %collective-permute-start.17 = (bf16[72,576]{1,0:T(8,128)(2,1)S(1)}, bf16[72,576]{1,0:T(8,128)(2,1)S(1)}, u32[]{:S(2)}, u32[]{:S(2)}) collective-permute-start(bf16[72,576]{1,0:T(8,128)(2,1)S(1)} %get-tuple-element.54), channel_id=1, source_target_pairs={{0,6},{1,7},{2,4},{3,5},{4,2},{5,3},{6,0},{7,1},{8,14},{9,15},{10,... | collective-permute-start | bytes 248840 | tf_op jit(solution)/shard_map/ppermute | solution.py:358
  60.7 8.0 %collective-permute-start.18 = (bf16[72,576]{1,0:T(8,128)(2,1)S(1)}, bf16[72,576]{1,0:T(8,128)(2,1)S(1)}, u32[]{:S(2)}, u32[]{:S(2)}) collective-permute-start(bf16[72,576]{1,0:T(8,128)(2,1)S(1)} %get-tuple-element.55), channel_id=1, source_target_pairs={{0,4},{1,5},{2,6},{3,7},{4,0},{5,1},{6,2},{7,3},{8,12},{9,13},{10,... | collective-permute-start | bytes 248840 | tf_op jit(solution)/shard_map/ppermute | solution.py:358
  62.0 6.8 %collective-permute-start.19 = (bf16[72,576]{1,0:T(8,128)(2,1)S(1)}, bf16[72,576]{1,0:T(8,128)(2,1)S(1)}, u32[]{:S(2)}, u32[]{:S(2)}) collective-permute-start(bf16[72,576]{1,0:T(8,128)(2,1)S(1)} %get-tuple-element.56), channel_id=1, source_target_pairs={{0,2},{1,3},{2,0},{3,1},{4,6},{5,7},{6,4},{7,5},{8,10},{9,11},{10,... | collective-permute-start | bytes 248840 | tf_op jit(solution)/shard_map/ppermute | solution.py:358

commit v17 on v16

--- a/solution.py
+++ b/solution.py
@@ -308,8 +308,10 @@
 def sum_second_kernel(own, got_y, got_x, kept, *outs):
     totals = [own[0] + got_y[...].astype(F32), own[1] + got_x[...].astype(F32)]
     size = totals[0].shape[1] // (1 + len(outs))
+    rows = kept.shape[0]
     for q, out in enumerate((kept, *outs)):
-        cut = [total[:, q * size : (q + 1) * size] for total in totals]
+        cut = jnp.concatenate([total[:, q * size : (q + 1) * size] for total in totals], axis=0)
+        cut = [cut[i * rows : (i + 1) * rows] for i in range(3)]
         out[...] = jnp.concatenate(cut, axis=1).astype(out.dtype)
 
 
@@ -318,9 +320,10 @@
     total = own[...]
     for part in got:
         total += part[...].astype(F32)
-    size = outs[0].shape[1]
+    rows, size = outs[0].shape
+    total = jnp.concatenate([total[:, i * size : (i + 1) * size] for i in range(3)], axis=0)
     for i, out in enumerate(outs):
-        out[...] = total[:, i * size : (i + 1) * size]
+        out[...] = total[i * rows : (i + 1) * rows]
 
 
 def last_kernel(chips, patches, *refs):
@@ -417,7 +420,7 @@
         small=True,
     )
     n = lax.axis_size("seq") // 2
-    block = (size, 2 * width // n)
+    block = (2 * size // 3, 3 * width // n)
     own, *sends = call(
         sum_second_kernel,
         [shape(block, F32)] + [shape(block)] * (n - 1),

time: 69.7 us -> 69.3 us (level)
  no operation moved by 1% of the time
where the time goes in v17:
time: 69.3 us; the launch traced here: 69.2 us
  waiting for transfers between devices  24.6 us (35%)
  starting transfers between devices  23.9 us (34%)
  Pallas kernels  19.9 us (29%)
  between operations  0.77 us (1%)
    ppermute x18, waiting for transfers between devices, flip(): lax.ppermute(value, axis, [(i, i ^ bit) for i in range(lax.axis_size(axis...  20.6 us
    pallas_call x11, Pallas kernels, call(): pl.pallas_call(body, out_shape=outs, in_specs=[HBM if i in far_in else sp...  19.9 us
    ppermute x18, starting transfers between devices, flip(): lax.ppermute(value, axis, [(i, i ^ bit) for i in range(lax.axis_size(axis...  18.8 us
    ppermute x2, starting transfers between devices, across(): return lax.ppermute(value, ('dp', 'seq'), pairs)  5.12 us
    ppermute x2, waiting for transfers between devices, across(): return lax.ppermute(value, ('dp', 'seq'), pairs)  4 us
  transfers between devices with their start and end apart: 20, of which 9 were waited for; matrix products, arithmetic and copies ran while one was open for 0% of the time, Pallas kernels for 15%

profile of v17, /device:TPU:0, one launch (start us, length us, event | category | flops | bytes accessed | tf_op | source)
XLA Modules:
  0.0 69.2 jit_solution(10080341003412790471)
XLA Ops:
  0.6 3.0 %collective-permute-start = (bf16[432,1152]{1,0:T(8,128)(2,1)}, bf16[432,1152]{1,0:T(8,128)(2,1)S(1)}, u32[]{:S(2)}, u32[]{:S(2)}) collective-permute-start(bf16[432,1152]{1,0:T(8,128)(2,1)} %bitcast.9), channel_id=1, source_target_pairs={{0,8},{1,17},{2,10},{3,19},{4,12},{5,21},{6,14},{7,23},{8,0},{9,25... | collective-permute-start | bytes 2985992 | tf_op jit(solution)/shard_map/ppermute | solution.py:373
  3.6 4.0 %shard_map.101 = (bf16[32,2944]{1,0:T(8,128)(2,1)S(1)}, bf16[32,2944]{1,0:T(8,128)(2,1)S(1)}, bf16[32,2944]{1,0:T(8,128)(2,1)S(1)}, bf16[32,2944]{1,0:T(8,128)(2...) custom-call(bf16[128,1728]{1,0:T(8,128)(2,1)} %bitcast.7, bf16[128,1152]{1,0:T(8,128)(2,1)} %bitcast.11, ...), custom_call_target="tpu_custom_call" | custom-call | tf_op jit(solution)/shard_map/pallas_call | solution.py:43
  7.6 1.6 %collective-permute-start.1 = (bf16[32,2944]{1,0:T(8,128)(2,1)S(1)}, bf16[32,2944]{1,0:T(8,128)(2,1)S(1)}, u32[]{:S(2)}, u32[]{:S(2)}) collective-permute-start(bf16[32,2944]{1,0:T(8,128)(2,1)S(1)} %get-tuple-element.34), channel_id=1, source_target_pairs={{0,2},{1,3},{2,0},{3,1},{4,6},{5,7},{6,4},{7,5},{8,10},{9,11},{10,... | collective-permute-start | bytes 565256 | tf_op jit(solution)/shard_map/ppermute | solution.py:361
  9.2 2.6 %collective-permute-start.2 = (bf16[32,2944]{1,0:T(8,128)(2,1)S(1)}, bf16[32,2944]{1,0:T(8,128)(2,1)S(1)}, u32[]{:S(2)}, u32[]{:S(2)}) collective-permute-start(bf16[32,2944]{1,0:T(8,128)(2,1)S(1)} %get-tuple-element.35), channel_id=1, source_target_pairs={{0,4},{1,5},{2,6},{3,7},{4,0},{5,1},{6,2},{7,3},{8,12},{9,13},{10,... | collective-permute-start | bytes 565256 | tf_op jit(solution)/shard_map/ppermute | solution.py:361
  11.8 0.2 collective-permute-start.3
  12.1 4.0 %collective-permute-done.got.refs_1_ = bf16[432,1152]{1,0:T(8,128)(2,1)S(1)} collective-permute-done((bf16[432,1152]{1,0:T(8,128)(2,1)}, bf16[432,1152]{1,0:T(8,128)(2,1)S(1)}, u32[]{:S(2)}, u32[]{:S(2)}) %collective-permute-start) | collective-permute-done | bytes 995360 | tf_op jit(solution)/shard_map/ppermute | solution.py:373
  16.2 2.1 %collective-permute-start.6 = (bf16[216,1152]{1,0:T(8,128)(2,1)S(1)}, bf16[216,1152]{1,0:T(8,128)(2,1)S(1)}, u32[]{:S(2)}, u32[]{:S(2)}) collective-permute-start(bf16[216,1152]{1,0:T(8,128)(2,1)S(1)} %get-tuple-element.37), channel_id=1, source_target_pairs={{0,16},{1,9},{2,18},{3,11},{4,20},{5,13},{6,22},{7,15},{8,24},{9,1... | collective-permute-start | bytes 1493000 | tf_op jit(solution)/shard_map/ppermute | solution.py:373
  18.3 7.6 %collective-permute-done.2.refs_2_ = bf16[32,2944]{1,0:T(8,128)(2,1)S(1)} collective-permute-done((bf16[32,2944]{1,0:T(8,128)(2,1)S(1)}, bf16[32,2944]{1,0:T(8,128)(2,1)S(1)}, u32[]{:S(2)}, u32[]{:S(2)}) %collective-permute-start.2) | collective-permute-done | bytes 188448 | tf_op jit(solution)/shard_map/ppermute | solution.py:361
  26.0 0.5 collective-permute-start.7
  26.5 1.8 %collective-permute-done.4.far = bf16[128,3200]{1,0:T(8,128)(2,1)S(1)} collective-permute-done((bf16[128,3200]{1,0:T(8,128)(2,1)S(1)}, bf16[128,3200]{1,0:T(8,128)(2,1)S(1)}, u32[]{:S(2)}, u32[]{:S(2)}) %collective-permute-start.4) | collective-permute-done | bytes 819232 | tf_op jit(solution)/shard_map/ppermute | solution.py:361
  28.3 0.7 %collective-permute-done.7.refs_4_ = bf16[216,1152]{1,0:T(8,128)(2,1)S(1)} collective-permute-done((bf16[216,1152]{1,0:T(8,128)(2,1)S(1)}, bf16[216,1152]{1,0:T(8,128)(2,1)S(1)}, u32[]{:S(2)}, u32[]{:S(2)}) %collective-permute-start.7) | collective-permute-done | bytes 497696 | tf_op jit(solution)/shard_map/ppermute | solution.py:361
  29.1 7.1 %shard_map.104 = (bf16[128,1728]{1,0:T(8,128)(2,1)S(1)}, bf16[32,1728]{1,0:T(8,128)(2,1)S(1)}, bf16[32,1728]{1,0:T(8,128)(2,1)S(1)}, bf16[32,1728]{1,0:T(8,128)(2,1)S(1)}) custom-call(bf16[128,3200]{1,0:T(8,128)(2,1)S(1)} %shard_map.103.near, bf16[128,3200]{1,0:T(8,128)(2,1)S(1)} %collective-permute-done.4.far, bf16[576,1152]{1,0:T(8,128)(2,1)S(1)} %copy-done.1, ...), custom_call_target="tpu_custom_call" | custom-call | tf_op jit(solution)/shard_map/pallas_call | solution.py:43
  36.1 0.2 collective-permute-start.12
  36.3 1.8 %shard_map.107.part = f32[8,72,1152]{2,1,0:T(8,128)S(1)} custom-call(bf16[128,1728]{1,0:T(8,128)(2,1)S(1)} %get-tuple-element.41.mine.refs_3_, bf16[128,3200]{1,0:T(8,128)(2,1)S(1)} %shard_map.103.near, bf16[128,3200]{1,0:T(8,128)(2,1)S(1)} %collective-permute-done.4.far), custom_call_target="tpu_custom_call" | custom-call | tf_op jit(solution)/shard_map/pallas_call | solution.py:43
  38.1 1.8 %shard_map.108 = (f32[4,72,1152]{2,1,0:T(8,128)S(1)}, bf16[2,72,1152]{2,1,0:T(8,128)(2,1)S(1)}, bf16[2,72,1152]{2,1,0:T(8,128)(2,1)S(1)}) custom-call(bf16[128,1728]{1,0:T(8,128)(2,1)S(1)} %collective-permute-done.12.other, bf16[128,3200]{1,0:T(8,128)(2,1)S(1)} %shard_map.103.near, bf16[128,3200]{1,0:T(8,128)(2,1)S(1)} %collective-permute-done.4.far, ...), custom_call_target="tpu_custom_call" | custom-call | tf_op jit(solution)/shard_map/pallas_call | solution.py:43
  39.9 0.5 collective-permute-start.13
  40.5 1.6 %collective-permute-start.14 = (bf16[2,72,1152]{2,1,0:T(8,128)(2,1)S(1)}, bf16[2,72,1152]{2,1,0:T(8,128)(2,1)S(1)}, u32[]{:S(2)}, u32[]{:S(2)}) collective-permute-start(bf16[2,72,1152]{2,1,0:T(8,128)(2,1)S(1)} %get-tuple-element.49), channel_id=1, source_target_pairs={{0,16},{8,24},{16,0},{24,8},{1,17},{9,25},{17,1},{25,9},{2,18},{10... | collective-permute-start | bytes 995336 | tf_op jit(solution)/shard_map/ppermute | solution.py:361
  42.1 3.1 %collective-permute-start.8 = (bf16[32,1728]{1,0:T(8,128)(2,1)S(1)}, bf16[32,1728]{1,0:T(8,128)(2,1)S(1)}, u32[]{:S(2)}, u32[]{:S(2)}) collective-permute-start(bf16[32,1728]{1,0:T(8,128)(2,1)S(1)} %get-tuple-element.38), channel_id=1, source_target_pairs={{0,6},{1,7},{2,4},{3,5},{4,2},{5,3},{6,0},{7,1},{8,14},{9,15},{10,... | collective-permute-start | bytes 331784 | tf_op jit(solution)/shard_map/ppermute | solution.py:361
  45.1 1.3 %collective-permute-start.9 = (bf16[32,1728]{1,0:T(8,128)(2,1)S(1)}, bf16[32,1728]{1,0:T(8,128)(2,1)S(1)}, u32[]{:S(2)}, u32[]{:S(2)}) collective-permute-start(bf16[32,1728]{1,0:T(8,128)(2,1)S(1)} %get-tuple-element.39), channel_id=1, source_target_pairs={{0,4},{1,5},{2,6},{3,7},{4,0},{5,1},{6,2},{7,3},{8,12},{9,13},{10,... | collective-permute-start | bytes 331784 | tf_op jit(solution)/shard_map/ppermute | solution.py:361
  46.5 3.6 %collective-permute-done.13.got_x = bf16[2,72,1152]{2,1,0:T(8,128)(2,1)S(1)} collective-permute-done((bf16[2,72,1152]{2,1,0:T(8,128)(2,1)S(1)}, bf16[2,72,1152]{2,1,0:T(8,128)(2,1)S(1)}, u32[]{:S(2)}, u32[]{:S(2)}) %collective-permute-start.13) | collective-permute-done | bytes 331808 | tf_op jit(solution)/shard_map/ppermute | solution.py:361
  50.1 0.2 collective-permute-done.14.got_y
  50.3 0.1 shard_map.109
  50.4 1.6 %collective-permute-start.15 = (bf16[72,1152]{1,0:T(8,128)(2,1)S(1)}, bf16[72,1152]{1,0:T(8,128)(2,1)S(1)}, u32[]{:S(2)}, u32[]{:S(2)}) collective-permute-start(bf16[72,1152]{1,0:T(8,128)(2,1)S(1)} %get-tuple-element.51), channel_id=1, source_target_pairs={{0,16},{8,24},{16,0},{24,8},{1,17},{9,25},{17,1},{25,9},{2,18},{10... | collective-permute-start | bytes 497672 | tf_op jit(solution)/shard_map/ppermute | solution.py:361
  52.1 0.8 %collective-permute-start.16 = (bf16[72,1152]{1,0:T(8,128)(2,1)S(1)}, bf16[72,1152]{1,0:T(8,128)(2,1)S(1)}, u32[]{:S(2)}, u32[]{:S(2)}) collective-permute-start(bf16[72,1152]{1,0:T(8,128)(2,1)S(1)} %get-tuple-element.52), channel_id=1, source_target_pairs={{0,8},{8,0},{16,24},{24,16},{1,9},{9,1},{17,25},{25,17},{2,10},{10... | collective-permute-start | bytes 497672 | tf_op jit(solution)/shard_map/ppermute | solution.py:361
  52.9 3.2 %collective-permute-done.9.refs_1_ = bf16[32,1728]{1,0:T(8,128)(2,1)S(1)} collective-permute-done((bf16[32,1728]{1,0:T(8,128)(2,1)S(1)}, bf16[32,1728]{1,0:T(8,128)(2,1)S(1)}, u32[]{:S(2)}, u32[]{:S(2)}) %collective-permute-start.9) | collective-permute-done | bytes 110624 | tf_op jit(solution)/shard_map/ppermute | solution.py:361
  56.2 1.2 %collective-permute-done.16.got_x = bf16[72,1152]{1,0:T(8,128)(2,1)S(1)} collective-permute-done((bf16[72,1152]{1,0:T(8,128)(2,1)S(1)}, bf16[72,1152]{1,0:T(8,128)(2,1)S(1)}, u32[]{:S(2)}, u32[]{:S(2)}) %collective-permute-start.16) | collective-permute-done | bytes 165920 | tf_op jit(solution)/shard_map/ppermute | solution.py:361
  57.4 0.2 shard_map.110
  57.6 3.1 %collective-permute-start.17 = (bf16[48,864]{1,0:T(8,128)(2,1)S(1)}, bf16[48,864]{1,0:T(8,128)(2,1)S(1)}, u32[]{:S(2)}, u32[]{:S(2)}) collective-permute-start(bf16[48,864]{1,0:T(8,128)(2,1)S(1)} %get-tuple-element.54), channel_id=1, source_target_pairs={{0,6},{1,7},{2,4},{3,5},{4,2},{5,3},{6,0},{7,1},{8,14},{9,15},{10,... | collective-permute-start | bytes 248840 | tf_op jit(solution)/shard_map/ppermute | solution.py:361
  60.7 1.3 %collective-permute-start.18 = (bf16[48,864]{1,0:T(8,128)(2,1)S(1)}, bf16[48,864]{1,0:T(8,128)(2,1)S(1)}, u32[]{:S(2)}, u32[]{:S(2)}) collective-permute-start(bf16[48,864]{1,0:T(8,128)(2,1)S(1)} %get-tuple-element.55), channel_id=1, source_target_pairs={{0,4},{1,5},{2,6},{3,7},{4,0},{5,1},{6,2},{7,3},{8,12},{9,13},{10,... | collective-permute-start | bytes 248840 | tf_op jit(solution)/shard_map/ppermute | solution.py:361
  62.1 4.0 %shard_map.106 = (bf16[128,1152]{1,0:T(8,128)(2,1)}, bf16[128,1152]{1,0:T(8,128)(2,1)}, bf16[128,1728]{1,0:T(8,128)(2,1)}) custom-call(bf16[32,1728]{1,0:T(8,128)(2,1)S(1)} %collective-permute-done.8.refs_0_, bf16[32,1728]{1,0:T(8,128)(2,1)S(1)} %collective-permute-done.9.refs_1_, bf16[32,1728]{1,0:T(8,128)(2,1)S(1)} %collective-permute-done.10.refs_2_, ...), custom_call_target="tpu_custom_call" | custom-call | tf_op jit(solution)/shard_map/pallas_call | solution.py:43
  66.1 2.2 %collective-permute-done.18.refs_1_ = bf16[48,864]{1,0:T(8,128)(2,1)S(1)} collective-permute-done((bf16[48,864]{1,0:T(8,128)(2,1)S(1)}, bf16[48,864]{1,0:T(8,128)(2,1)S(1)}, u32[]{:S(2)}, u32[]{:S(2)}) %collective-permute-start.18) | collective-permute-done | bytes 82976 | tf_op jit(solution)/shard_map/ppermute | solution.py:361
  68.4 0.8 %shard_map.111 = (f32[72,288]{1,0:T(8,128)}, f32[72,288]{1,0:T(8,128)}) custom-call(f32[48,864]{1,0:T(8,128)S(1)} %get-tuple-element.53.own, bf16[48,864]{1,0:T(8,128)(2,1)S(1)} %collective-permute-done.17.refs_0_, bf16[48,864]{1,0:T(8,128)(2,1)S(1)} %collective-permute-done.18.refs_1_, bf16[48,864]{1,0:T(8,128)(2,1)S(1)} %collective-permute-done.19.refs_2_), custom_call_target="tpu_custom_call" | custom-call | tf_op jit(solution)/shard_map/pallas_call | solution.py:43
  (31 shorter events, 0.6 us)
Async XLA Ops:
  0.6 15.4 %collective-permute-start = (bf16[432,1152]{1,0:T(8,128)(2,1)}, bf16[432,1152]{1,0:T(8,128)(2,1)S(1)}, u32[]{:S(2)}, u32[]{:S(2)}) collective-permute-start(bf16[432,1152]{1,0:T(8,128)(2,1)} %bitcast.9), channel_id=1, source_target_pairs={{0,8},{1,17},{2,10},{3,19},{4,12},{5,21},{6,14},{7,23},{8,0},{9,25... | collective-permute-start | bytes 2985992 | tf_op jit(solution)/shard_map/ppermute | solution.py:373
  7.6 10.7 %collective-permute-start.1 = (bf16[32,2944]{1,0:T(8,128)(2,1)S(1)}, bf16[32,2944]{1,0:T(8,128)(2,1)S(1)}, u32[]{:S(2)}, u32[]{:S(2)}) collective-permute-start(bf16[32,2944]{1,0:T(8,128)(2,1)S(1)} %get-tuple-element.34), channel_id=1, source_target_pairs={{0,2},{1,3},{2,0},{3,1},{4,6},{5,7},{6,4},{7,5},{8,10},{9,11},{10,... | collective-permute-start | bytes 565256 | tf_op jit(solution)/shard_map/ppermute | solution.py:361
  9.2 16.6 %collective-permute-start.2 = (bf16[32,2944]{1,0:T(8,128)(2,1)S(1)}, bf16[32,2944]{1,0:T(8,128)(2,1)S(1)}, u32[]{:S(2)}, u32[]{:S(2)}) collective-permute-start(bf16[32,2944]{1,0:T(8,128)(2,1)S(1)} %get-tuple-element.35), channel_id=1, source_target_pairs={{0,4},{1,5},{2,6},{3,7},{4,0},{5,1},{6,2},{7,3},{8,12},{9,13},{10,... | collective-permute-start | bytes 565256 | tf_op jit(solution)/shard_map/ppermute | solution.py:361
  11.8 14.1 %collective-permute-start.3 = (bf16[32,2944]{1,0:T(8,128)(2,1)S(1)}, bf16[32,2944]{1,0:T(8,128)(2,1)S(1)}, u32[]{:S(2)}, u32[]{:S(2)}) collective-permute-start(bf16[32,2944]{1,0:T(8,128)(2,1)S(1)} %get-tuple-element.36), channel_id=1, source_target_pairs={{0,6},{1,7},{2,4},{3,5},{4,2},{5,3},{6,0},{7,1},{8,14},{9,15},{10,... | collective-permute-start | bytes 565256 | tf_op jit(solution)/shard_map/ppermute | solution.py:361
  16.1 13.0 %copy-start.1 = (bf16[576,1152]{1,0:T(8,128)(2,1)S(1)}, bf16[576,1152]{1,0:T(8,128)(2,1)}, u32[]{:S(2)}) copy-start(bf16[576,1152]{1,0:T(8,128)(2,1)} %refs_8_.1) | copy-start | bytes 3981316
  16.1 13.0 %copy-start.3 = (bf16[1152,432]{0,1:T(8,128)(2,1)S(1)}, bf16[1152,432]{0,1:T(8,128)(2,1)}, u32[]{:S(2)}) copy-start(bf16[1152,432]{0,1:T(8,128)(2,1)} %param.9) | copy-start | bytes 2985988
  16.2 9.8 %collective-permute-start.6 = (bf16[216,1152]{1,0:T(8,128)(2,1)S(1)}, bf16[216,1152]{1,0:T(8,128)(2,1)S(1)}, u32[]{:S(2)}, u32[]{:S(2)}) collective-permute-start(bf16[216,1152]{1,0:T(8,128)(2,1)S(1)} %get-tuple-element.37), channel_id=1, source_target_pairs={{0,16},{1,9},{2,18},{3,11},{4,20},{5,13},{6,22},{7,15},{8,24},{9,1... | collective-permute-start | bytes 1493000 | tf_op jit(solution)/shard_map/ppermute | solution.py:373
  18.3 10.0 %collective-permute-start.5 = (bf16[432,1152]{1,0:T(8,128)(2,1)S(1)}, bf16[432,1152]{1,0:T(8,128)(2,1)S(1)}, u32[]{:S(2)}, u32[]{:S(2)}) collective-permute-start(bf16[432,1152]{1,0:T(8,128)(2,1)S(1)} %collective-permute-done.got.refs_1_), channel_id=1, source_target_pairs={{0,1},{1,0},{2,3},{3,2},{4,5},{5,4},{6,7},{7,6},{8,9},{9,8},{10,11... | collective-permute-start | bytes 2985992 | tf_op jit(solution)/shard_map/ppermute | solution.py:361
  25.9 2.4 %collective-permute-start.4 = (bf16[128,3200]{1,0:T(8,128)(2,1)S(1)}, bf16[128,3200]{1,0:T(8,128)(2,1)S(1)}, u32[]{:S(2)}, u32[]{:S(2)}) collective-permute-start(bf16[128,3200]{1,0:T(8,128)(2,1)S(1)} %shard_map.103.near), channel_id=1, source_target_pairs={{0,1},{1,0},{2,3},{3,2},{4,5},{5,4},{6,7},{7,6},{8,9},{9,8},{10,11... | collective-permute-start | bytes 2457608 | tf_op jit(solution)/shard_map/ppermute | solution.py:361
  26.0 3.0 %collective-permute-start.7 = (bf16[216,1152]{1,0:T(8,128)(2,1)S(1)}, bf16[216,1152]{1,0:T(8,128)(2,1)S(1)}, u32[]{:S(2)}, u32[]{:S(2)}) collective-permute-start(bf16[216,1152]{1,0:T(8,128)(2,1)S(1)} %collective-permute-done.6.refs_3_), channel_id=1, source_target_pairs={{0,1},{1,0},{2,3},{3,2},{4,5},{5,4},{6,7},{7,6},{8,9},{9,8},{10,11... | collective-permute-start | bytes 1493000 | tf_op jit(solution)/shard_map/ppermute | solution.py:361
  36.1 2.0 %collective-permute-start.12 = (bf16[128,1728]{1,0:T(8,128)(2,1)S(1)}, bf16[128,1728]{1,0:T(8,128)(2,1)S(1)}, u32[]{:S(2)}, u32[]{:S(2)}) collective-permute-start(bf16[128,1728]{1,0:T(8,128)(2,1)S(1)} %get-tuple-element.41.mine.refs_3_), channel_id=1, source_target_pairs={{0,1},{1,0},{2,3},{3,2},{4,5},{5,4},{6,7},{7,6},{8,9},{9,8},{10,11... | collective-permute-start | bytes 1327112 | tf_op jit(solution)/shard_map/ppermute | solution.py:361
  39.9 10.1 %collective-permute-start.13 = (bf16[2,72,1152]{2,1,0:T(8,128)(2,1)S(1)}, bf16[2,72,1152]{2,1,0:T(8,128)(2,1)S(1)}, u32[]{:S(2)}, u32[]{:S(2)}) collective-permute-start(bf16[2,72,1152]{2,1,0:T(8,128)(2,1)S(1)} %get-tuple-element.48), channel_id=1, source_target_pairs={{0,8},{8,0},{16,24},{24,16},{1,9},{9,1},{17,25},{25,17},{2,10},{10... | collective-permute-start | bytes 995336 | tf_op jit(solution)/shard_map/ppermute | solution.py:361
  40.5 9.8 %collective-permute-start.14 = (bf16[2,72,1152]{2,1,0:T(8,128)(2,1)S(1)}, bf16[2,72,1152]{2,1,0:T(8,128)(2,1)S(1)}, u32[]{:S(2)}, u32[]{:S(2)}) collective-permute-start(bf16[2,72,1152]{2,1,0:T(8,128)(2,1)S(1)} %get-tuple-element.49), channel_id=1, source_target_pairs={{0,16},{8,24},{16,0},{24,8},{1,17},{9,25},{17,1},{25,9},{2,18},{10... | collective-permute-start | bytes 995336 | tf_op jit(solution)/shard_map/ppermute | solution.py:361
  42.1 10.8 %collective-permute-start.8 = (bf16[32,1728]{1,0:T(8,128)(2,1)S(1)}, bf16[32,1728]{1,0:T(8,128)(2,1)S(1)}, u32[]{:S(2)}, u32[]{:S(2)}) collective-permute-start(bf16[32,1728]{1,0:T(8,128)(2,1)S(1)} %get-tuple-element.38), channel_id=1, source_target_pairs={{0,6},{1,7},{2,4},{3,5},{4,2},{5,3},{6,0},{7,1},{8,14},{9,15},{10,... | collective-permute-start | bytes 331784 | tf_op jit(solution)/shard_map/ppermute | solution.py:361
  45.1 11.0 %collective-permute-start.9 = (bf16[32,1728]{1,0:T(8,128)(2,1)S(1)}, bf16[32,1728]{1,0:T(8,128)(2,1)S(1)}, u32[]{:S(2)}, u32[]{:S(2)}) collective-permute-start(bf16[32,1728]{1,0:T(8,128)(2,1)S(1)} %get-tuple-element.39), channel_id=1, source_target_pairs={{0,4},{1,5},{2,6},{3,7},{4,0},{5,1},{6,2},{7,3},{8,12},{9,13},{10,... | collective-permute-start | bytes 331784 | tf_op jit(solution)/shard_map/ppermute | solution.py:361
  46.4 9.7 %collective-permute-start.10 = (bf16[32,1728]{1,0:T(8,128)(2,1)S(1)}, bf16[32,1728]{1,0:T(8,128)(2,1)S(1)}, u32[]{:S(2)}, u32[]{:S(2)}) collective-permute-start(bf16[32,1728]{1,0:T(8,128)(2,1)S(1)} %get-tuple-element.40), channel_id=1, source_target_pairs={{0,2},{1,3},{2,0},{3,1},{4,6},{5,7},{6,4},{7,5},{8,10},{9,11},{10,... | collective-permute-start | bytes 331784 | tf_op jit(solution)/shard_map/ppermute | solution.py:361
  50.3 11.9 %copy-start.4 = (f32[8,128,128]{2,1,0:T(8,128)S(1)}, f32[8,128,128]{2,1,0:T(8,128)}, u32[]{:S(2)}) copy-start(f32[8,128,128]{2,1,0:T(8,128)} %get-tuple-element.42.refs_7_) | copy-start | bytes 1572868
  50.3 11.9 %copy-start.5 = (bf16[128,1152]{1,0:T(8,128)(2,1)S(1)}, bf16[128,1152]{1,0:T(8,128)(2,1)}, u32[]{:S(2)}) copy-start(bf16[128,1152]{1,0:T(8,128)(2,1)} %get-tuple-element.43.refs_9_) | copy-start | bytes 884740
  50.4 11.7 %copy-start = (bf16[576,1152]{1,0:T(8,128)(2,1)S(1)}, bf16[576,1152]{1,0:T(8,128)(2,1)}, u32[]{:S(2)}) copy-start(bf16[576,1152]{1,0:T(8,128)(2,1)} %refs_5_.1) | copy-start | bytes 3981316
  50.4 11.7 %copy-start.2 = (bf16[2,64,1728]{2,1,0:T(8,128)(2,1)S(1)}, bf16[2,64,1728]{2,1,0:T(8,128)(2,1)}, u32[]{:S(2)}) copy-start(bf16[2,64,1728]{2,1,0:T(8,128)(2,1)} %param.7) | copy-start | bytes 1327108
  50.4 5.8 %collective-permute-start.15 = (bf16[72,1152]{1,0:T(8,128)(2,1)S(1)}, bf16[72,1152]{1,0:T(8,128)(2,1)S(1)}, u32[]{:S(2)}, u32[]{:S(2)}) collective-permute-start(bf16[72,1152]{1,0:T(8,128)(2,1)S(1)} %get-tuple-element.51), channel_id=1, source_target_pairs={{0,16},{8,24},{16,0},{24,8},{1,17},{9,25},{17,1},{25,9},{2,18},{10... | collective-permute-start | bytes 497672 | tf_op jit(solution)/shard_map/ppermute | solution.py:361
  52.1 5.3 %collective-permute-start.16 = (bf16[72,1152]{1,0:T(8,128)(2,1)S(1)}, bf16[72,1152]{1,0:T(8,128)(2,1)S(1)}, u32[]{:S(2)}, u32[]{:S(2)}) collective-permute-start(bf16[72,1152]{1,0:T(8,128)(2,1)S(1)} %get-tuple-element.52), channel_id=1, source_target_pairs={{0,8},{8,0},{16,24},{24,16},{1,9},{9,1},{17,25},{25,17},{2,10},{10... | collective-permute-start | bytes 497672 | tf_op jit(solution)/shard_map/ppermute | solution.py:361
  56.1 6.0 %collective-permute-start.11 = (bf16[64,1728]{1,0:T(8,128)(2,1)S(1)}, bf16[64,1728]{1,0:T(8,128)(2,1)S(1)}, u32[]{:S(2)}, u32[]{:S(2)}) collective-permute-start(bf16[64,1728]{1,0:T(8,128)(2,1)S(1)} %shard_map.105), channel_id=1, source_target_pairs={{0,1},{1,0},{2,3},{3,2},{4,5},{5,4},{6,7},{7,6},{8,9},{9,8},{10,11... | collective-permute-start | bytes 663560 | tf_op jit(solution)/shard_map/ppermute | solution.py:361
  57.6 8.5 %collective-permute-start.17 = (bf16[48,864]{1,0:T(8,128)(2,1)S(1)}, bf16[48,864]{1,0:T(8,128)(2,1)S(1)}, u32[]{:S(2)}, u32[]{:S(2)}) collective-permute-start(bf16[48,864]{1,0:T(8,128)(2,1)S(1)} %get-tuple-element.54), channel_id=1, source_target_pairs={{0,6},{1,7},{2,4},{3,5},{4,2},{5,3},{6,0},{7,1},{8,14},{9,15},{10,... | collective-permute-start | bytes 248840 | tf_op jit(solution)/shard_map/ppermute | solution.py:361
  60.7 7.6 %collective-permute-start.18 = (bf16[48,864]{1,0:T(8,128)(2,1)S(1)}, bf16[48,864]{1,0:T(8,128)(2,1)S(1)}, u32[]{:S(2)}, u32[]{:S(2)}) collective-permute-start(bf16[48,864]{1,0:T(8,128)(2,1)S(1)} %get-tuple-element.55), channel_id=1, source_target_pairs={{0,4},{1,5},{2,6},{3,7},{4,0},{5,1},{6,2},{7,3},{8,12},{9,13},{10,... | collective-permute-start | bytes 248840 | tf_op jit(solution)/shard_map/ppermute | solution.py:361
  62.0 6.4 %collective-permute-start.19 = (bf16[48,864]{1,0:T(8,128)(2,1)S(1)}, bf16[48,864]{1,0:T(8,128)(2,1)S(1)}, u32[]{:S(2)}, u32[]{:S(2)}) collective-permute-start(bf16[48,864]{1,0:T(8,128)(2,1)S(1)} %get-tuple-element.56), channel_id=1, source_target_pairs={{0,2},{1,3},{2,0},{3,1},{4,6},{5,7},{6,4},{7,5},{8,10},{9,11},{10,... | collective-permute-start | bytes 248840 | tf_op jit(solution)/shard_map/ppermute | solution.py:361
